TPU v7x, 32 devices: a whole 2x2x4 slice. The times are simulated.
32 devices in a mesh: wide: 4 (over y, core), node: 8 (over z, x).
Axes of the slice: x: 2, y: 2, z: 4, core: 2. Of those that a mesh axis runs over, the one named last changes fastest.
Arguments:
- tokens: bfloat16 [16384, 4096], P(('wide', 'node')), may hold values from -6 to 6
- key_weight: bfloat16 [4096, 512], P(('node', 'wide')), may hold values from -0.09375 to 0.09375
- cotangent: bfloat16 [16384, 512], P(('wide', 'node')), may hold values from -6 to 6
Outputs:
- keys: bfloat16 [16384, 512], P(('wide', 'node'))
- input_grad: bfloat16 [16384, 4096], P(('wide', 'node'))
- weight_grad: float32 [4096, 512], P(('node', 'wide'))
All inputs are finite; a program needn't handle non-finite values.
Results may differ from a plain program's by a relative error of at most 0.001.
Values may be sent and summed in bfloat16 or wider, within the bound.
No kernel may reach another device: no remote copies, remote signals or barrier semaphores. Data moves between devices by JAX's collectives and lax.ppermute only.
A program may use at most 64 MiB of HBM per device.

v0:
```python
import jax
import jax.numpy as jnp
from jax import lax
from jax.sharding import PartitionSpec as P


def on_device(tokens, key_weight, cotangent):
    secondary = lax.all_gather(key_weight, "wide", axis=0, tiled=True)
    rows_tok = tokens.shape[0]
    contract_cols = (((1,), (1,)), ((), ()))
    columns = tokens
    keys_acc = jnp.dot(
        columns,
        lax.all_gather(secondary, "node", axis=0, tiled=True),
        preferred_element_type=jnp.float32,
    )
    grad_acc = lax.dot_general(
        cotangent,
        lax.all_gather(secondary, "node", axis=0, tiled=True),
        contract_cols,
        preferred_element_type=jnp.float32,
    )
    keys = keys_acc.astype(jnp.bfloat16)
    input_grad = grad_acc.astype(jnp.bfloat16)
    columns = tokens
    node_sums = lax.psum_scatter(
        lax.dot_general(
            columns, cotangent, (((0,), (0,)), ((), ())), preferred_element_type=jnp.float32
        ),
        "node",
        scatter_dimension=0,
        tiled=True,
    )
    wide_sums = lax.psum_scatter(node_sums, "wide", scatter_dimension=0, tiled=True)
    total_tokens = rows_tok * lax.axis_size("wide") * lax.axis_size("node")
    weight_grad = wide_sums * (1.0 / jnp.sqrt(jnp.float32(total_tokens)))
    return (keys, input_grad, weight_grad)


def solution(mesh):
    placed = (P(("wide", "node"), None), P(("node", "wide"), None), P(("wide", "node"), None))
    return jax.shard_map(
        on_device,
        mesh=mesh,
        in_specs=placed,
        out_specs=(P(("wide", "node"), None), P(("wide", "node"), None), P(("node", "wide"), None)),
        check_vma=False,
    )
```

profile of v0, /device:TPU:0, one launch (start us, length us, event | category | flops | bytes accessed | tf_op | source)
XLA Modules:
  0.0 276.8 jit_solution(17902633112124176011)
XLA Ops:
  7.2 0.0 copy-start
  7.2 0.0 reduce-scatter.3.cloned.1.call-start
  7.2 1.0 copy-done
  8.2 7.8 %fusion = f32[4096,512]{1,0:T(8,128)} fusion(bf16[512,4096]{1,0:T(8,128)(2,1)} %param.3, bf16[512,512]{1,0:T(8,128)(2,1)S(1)} %copy-done), kind=kOutput, calls=%fused_computation.3 | convolution fusion | flops 2147483648 | bytes 13107200 | tf_op jit(solution)/shard_map/dot_general | solution.py:27
  16.0 0.0 copy-start.2
  16.0 0.0 reduce-scatter.3.cloned.1.call-update
  16.0 0.0 all-gather.2.cloned.1.call-start
  16.1 0.8 copy-done.2
  16.9 9.1 %all_gather.7 = bf16[512,512]{1,0:T(8,128)(2,1)} all-gather(bf16[128,512]{1,0:T(8,128)(2,1)S(1)} %copy-done.2), channel_id=1, replica_groups=mesh['wide'=4,'node'=8] {'wide'}, dimensions={0}, use_global_device_ids=true | all-gather | bytes 655360 | tf_op jit(solution)/shard_map/all_gather | solution.py:8
  26.0 0.0 all-gather.2.cloned.1.call-update
  26.0 0.0 reduce-scatter.5.cloned.1.call-start
  26.1 141.8 %reduce-scatter.3.cloned.1.call-done = f32[512,512]{1,0:T(8,128)} async-done(((f32[4096,512]{1,0:T(8,128)}), f32[512,512]{1,0:T(8,128)}) %reduce-scatter.3.cloned.1.call-update) | async-done | bytes 1048592 | tf_op jit(solution)/shard_map/reduce_scatter | solution.py:26
  167.9 0.0 reduce-scatter.5.cloned.1.call-update
  167.9 74.7 %all-gather.2.cloned.1.call-done = bf16[4096,512]{1,0:T(8,128)(2,1)} async-done(((bf16[512,512]{1,0:T(8,128)(2,1)}), bf16[4096,512]{1,0:T(8,128)(2,1)}) %all-gather.2.cloned.1.call-update) | async-done | bytes 4194320 | tf_op jit(solution)/shard_map/all_gather | solution.py:14
  242.7 0.0 copy-start.1
  242.7 0.0 copy-start.3
  242.7 6.7 %convolution_convert_fusion = bf16[512,4096]{1,0:T(8,128)(2,1)} fusion(bf16[512,512]{1,0:T(8,128)(2,1)S(1)} %copy-done, bf16[4096,512]{1,0:T(8,128)(2,1)} %all-gather.2.cloned.1.call-done), kind=kOutput, calls=%fused_computation | convolution fusion | flops 2149580800 | bytes 8912896 | tf_op jit(solution)/shard_map/dot_general | solution.py:17
  249.4 0.0 copy-done.1
  249.4 0.0 copy-done.3
  249.4 3.1 %convolution_convert_fusion.1 = bf16[512,512]{1,0:T(8,128)(2,1)} fusion(bf16[512,4096]{1,0:T(8,128)(2,1)S(1)} %copy-done.1, bf16[4096,512]{1,0:T(8,128)(2,1)S(1)} %copy-done.3), kind=kOutput, calls=%fused_computation.1 | convolution fusion | flops 2147745792 | bytes 8912896 | tf_op jit(solution)/shard_map/dot_general | solution.py:12
  252.5 16.0 %reduce-scatter.5.cloned.1.call-done = f32[128,512]{1,0:T(8,128)} async-done(((f32[512,512]{1,0:T(8,128)}), f32[128,512]{1,0:T(8,128)}) %reduce-scatter.5.cloned.1.call-update) | async-done | bytes 262160 | tf_op jit(solution)/shard_map/reduce_scatter | solution.py:34
  268.6 1.7 broadcast_multiply_fusion
Async XLA Ops:
  7.2 1.0 copy-start
  7.2 160.7 %reduce-scatter.3.cloned.1.call-start = ((), (), s32[]{:S(2)}) async-start(), calls=%async_computation.3 | async-start | bytes 9437184 | tf_op jit(solution)/shard_map/reduce_scatter | solution.py:26
  16.0 0.9 copy-start.2
  16.0 226.6 %all-gather.2.cloned.1.call-start = ((), (), s32[]{:S(2)}) async-start(), calls=%async_computation.2 | async-start | bytes 4718592 | tf_op jit(solution)/shard_map/all_gather | solution.py:14
  26.0 242.5 %reduce-scatter.5.cloned.1.call-start = ((), (), s32[]{:S(2)}) async-start(), calls=%async_computation.4 | async-start | bytes 1310720 | tf_op jit(solution)/shard_map/reduce_scatter | solution.py:34
  242.7 6.7 %copy-start.1 = (bf16[512,4096]{1,0:T(8,128)(2,1)S(1)}, bf16[512,4096]{1,0:T(8,128)(2,1)}, u32[]{:S(2)}) copy-start(bf16[512,4096]{1,0:T(8,128)(2,1)} %param.3) | copy-start | bytes 12582916
  242.7 6.7 %copy-start.3 = (bf16[4096,512]{1,0:T(8,128)(2,1)S(1)}, bf16[4096,512]{1,0:T(8,128)(2,1)}, u32[]{:S(2)}) copy-start(bf16[4096,512]{1,0:T(8,128)(2,1)} %all-gather.2.cloned.1.call-done) | copy-start | bytes 12582916
Sparse Core Ops, SparseCore 0:
  16.2 151.6 reduce-scatter.2
  170.2 72.3 all-gather.1
  245.4 23.1 reduce-scatter.4
where the time goes:
time: 277 us
  waiting for transfers between devices  233 us (84%)
  matrix products  17.7 us (6%)
  between operations  13.8 us (5%)
  blocking collectives  9.08 us (3%)
    reduce_scatter x1, waiting for transfers between devices, on_device(): lax.psum_scatter(lax.dot_general(columns, cotangent, (((0,), (0,)), ((),...  142 us
    all_gather x1, waiting for transfers between devices, on_device(): lax.all_gather(secondary, 'node', axis=0, tiled=True)  74.7 us
    reduce_scatter x1, waiting for transfers between devices, on_device(): lax.psum_scatter(node_sums, 'wide', scatter_dimension=0, tiled=True)  16 us
    all_gather x1, blocking collectives, on_device(): secondary = lax.all_gather(key_weight, 'wide', axis=0, tiled=True)  9.08 us
    dot_general x1, matrix products, on_device(): lax.dot_general(columns, cotangent, (((0,), (0,)), ((), ())), preferred_e...  7.81 us
    dot_general x1, matrix products, on_device(): lax.dot_general(cotangent, lax.all_gather(secondary, 'node', axis=0, tile...  6.73 us
  transfers between devices with their start and end apart: 3, of which 3 were waited for; matrix products, arithmetic and copies ran while one was open for 4% of the time, Pallas kernels for 0%

commit v1 on v0

v1 whole, which is shorter than its diff:
```python
import jax
import jax.numpy as jnp
from jax import lax
from jax.sharding import PartitionSpec as P

AXES = ("wide", "node")


def on_device(tokens, key_weight, cotangent):
    wide, node = lax.axis_size("wide"), lax.axis_size("node")
    w_me, n_me = lax.axis_index("wide"), lax.axis_index("node")
    rows, kd = key_weight.shape
    half = rows // 2
    ny, nx, nz = wide // 2, 2, node // 2
    core, y_me = w_me % 2, w_me // 2
    x_me, z_me = n_me % 2, n_me // 2

    def swap(value, name, j):
        mask = {"core": j * node, "y": 2 * j * node, "x": j, "z": 2 * j}[name]
        return lax.ppermute(value, AXES, [(i, i ^ mask) for i in range(wide * node)])

    def gathered(value, name, size, me):
        parts = [value] + [swap(value, name, j) for j in range(1, size)]
        out = jnp.zeros((size,) + value.shape, value.dtype)
        for j in range(size):
            out = lax.dynamic_update_index_in_dim(out, parts[j], me ^ j, 0)
        return out

    def pick(value, axis, index):
        return lax.dynamic_index_in_dim(value, index, axis, keepdims=False)

    def summed(value, axis, name, size, me, scale):
        total = pick(value, axis, me).astype(jnp.float32)
        for j in range(1, size):
            sent = pick(value, axis, me ^ j)
            total = total + swap(sent, name, j).astype(jnp.float32)
        return total * scale

    tok_top = jnp.max(jnp.abs(tokens), axis=1).astype(jnp.float32)
    cot_top = jnp.max(jnp.abs(cotangent), axis=1).astype(jnp.float32)
    bound = jnp.full((8, 128), jnp.sum(tok_top * cot_top))
    pair = bound + swap(bound, "core", 1)
    whole = pair
    for name, size in (("x", nx), ("y", ny), ("z", nz)):
        bit = 1
        while bit < size:
            whole = whole + swap(whole, name, bit)
            bit *= 2
    pair = jnp.maximum(pair[0, 0], 1e-33)
    whole = jnp.maximum(whole[0, 0], 1e-33)

    gz = gathered(key_weight, "z", nz, z_me).reshape(nz, 2, half, kd)
    one = gathered(gathered(gz[:, 0], "x", nx, x_me), "y", ny, y_me)
    two = gathered(gathered(gz[:, 1], "y", ny, y_me), "x", nx, x_me)
    both = jnp.stack([one.transpose(2, 1, 0, 3, 4), two.transpose(2, 0, 1, 3, 4)], axis=3)
    weight = gathered(both, "core", 2, core)
    weight = weight.transpose(1, 2, 3, 0, 4, 5, 6).reshape(node * wide * rows, kd)

    part = lax.dot_general(
        tokens, cotangent, (((0,), (0,)), ((), ())), preferred_element_type=jnp.float32
    )
    part = (part * (32768.0 / pair)).astype(jnp.float16)
    part = part.reshape(nz * nx * ny, 2, rows, kd)
    part = summed(part, 1, "core", 2, core, pair / whole).astype(jnp.float16)
    part = part.reshape(nz, nx, ny, 2, half, kd)
    one = summed(part[:, :, :, 0], 1, "x", nx, x_me, 1.0).astype(jnp.float16)
    one = summed(one, 1, "y", ny, y_me, 1.0)
    two = summed(part[:, :, :, 1], 2, "y", ny, y_me, 1.0).astype(jnp.float16)
    two = summed(two, 1, "x", nx, x_me, 1.0)
    part = jnp.concatenate([one, two], axis=1).astype(jnp.float16)
    total_tokens = tokens.shape[0] * wide * node
    weight_grad = summed(
        part, 0, "z", nz, z_me, (whole / 32768.0) * (1.0 / jnp.sqrt(jnp.float32(total_tokens)))
    )

    keys = jnp.dot(tokens, weight, preferred_element_type=jnp.float32).astype(jnp.bfloat16)
    input_grad = lax.dot_general(
        cotangent, weight, (((1,), (1,)), ((), ())), preferred_element_type=jnp.float32
    ).astype(jnp.bfloat16)
    return (keys, input_grad, weight_grad)


def solution(mesh):
    placed = (P(AXES, None), P(("node", "wide"), None), P(AXES, None))
    return jax.shard_map(
        on_device,
        mesh=mesh,
        in_specs=placed,
        out_specs=(P(AXES, None), P(AXES, None), P(("node", "wide"), None)),
        check_vma=False,
    )
```

time: 277 us -> 98.1 us (0.35)
  waiting for transfers between devices: 233 us -> 36.8 us
  starting transfers between devices: 0.12 us -> 27.1 us
  between operations: 13.8 us -> 2.5 us
  local copies, waits for them, and re-layouts: 1.83 us -> 12 us
  blocking collectives: 9.08 us -> 0 us
  other arithmetic: 1.67 us -> 7.96 us
  matrix products: 17.7 us -> 11.5 us
    reduce_scatter x2 -> x0, waiting for transfers between devices: 158 us -> none  [the longest x1 142 us: on_device(): lax.psum_scatter(lax.dot_general(columns, cotangent, (((0,), (0,)), ((),...]
    all_gather x1 -> x0, waiting for transfers between devices: 74.7 us -> none  [on_device(): lax.all_gather(secondary, 'node', axis=0, tiled=True)]
    ppermute x0 -> x21, waiting for transfers between devices: none -> 36.8 us  [swap(): lax.ppermute(value, AXES, [(i, i ^ mask) for i in range(wide * node)])]
    ppermute x0 -> x21, starting transfers between devices: none -> 27.1 us  [swap(): lax.ppermute(value, AXES, [(i, i ^ mask) for i in range(wide * node)])]
    all_gather x1 -> x0, blocking collectives: 9.08 us -> none  [on_device(): secondary = lax.all_gather(key_weight, 'wide', axis=0, tiled=True)]
    dot_general x3, matrix products: 17.7 us -> 11.5 us  [the longest x1 4.57 us: on_device(): lax.dot_general(tokens, cotangent, (((0,), (0,)), ((), ())), preferred_el...]
    unnamed x8 -> x9, local copies, waits for them, and re-layouts: 1.83 us -> 7.43 us
    reduce_max x0 -> x2, other arithmetic: none -> 3.3 us  [the longest x1 3.12 us: on_device(): tok_top = jnp.max(jnp.abs(tokens), axis=1).astype(jnp.float32)]
  transfers between devices with their start and end apart: 3 -> 21, of which waited for: 3 -> 10; matrix products, arithmetic and copies ran while one was open for 4% -> 24% of each run, Pallas kernels for 0% -> 0%
where the time goes in v1:
time: 98.1 us; the launch traced here: 97.8 us
  waiting for transfers between devices  36.8 us (38%)
  starting transfers between devices  27.1 us (28%)
  local copies, waits for them, and re-layouts  12 us (12%)
  matrix products  11.5 us (12%)
  other arithmetic  7.96 us (8%)
  between operations  2.5 us (3%)
    ppermute x21, waiting for transfers between devices, swap(): lax.ppermute(value, AXES, [(i, i ^ mask) for i in range(wide * node)])  36.8 us
    ppermute x21, starting transfers between devices, swap(): lax.ppermute(value, AXES, [(i, i ^ mask) for i in range(wide * node)])  27.1 us
    unnamed x9, local copies, waits for them, and re-layouts  7.43 us
    dot_general x1, matrix products, on_device(): lax.dot_general(tokens, cotangent, (((0,), (0,)), ((), ())), preferred_el...  4.57 us
    dot_general x1, matrix products, on_device(): lax.dot_general(cotangent, weight, (((1,), (1,)), ((), ())), preferred_el...  4.34 us
    reduce_max x1, other arithmetic, on_device(): tok_top = jnp.max(jnp.abs(tokens), axis=1).astype(jnp.float32)  3.12 us
    dot_general x1, matrix products, on_device(): jnp.dot(tokens, weight, preferred_element_type=jnp.float32)  2.58 us
  transfers between devices with their start and end apart: 21, of which 10 were waited for; matrix products, arithmetic and copies ran while one was open for 24% of the time, Pallas kernels for 0%

profile of v1, /device:TPU:0, one launch (start us, length us, event | category | flops | bytes accessed | tf_op | source)
XLA Modules:
  0.0 97.8 jit_solution(1065357235051958247)
XLA Ops:
  0.7 3.1 %abs_reduce_fusion = bf16[512]{0:T(512)(128)(2,1)S(1)} fusion(bf16[512,4096]{1,0:T(8,128)(2,1)} %param.3), kind=kLoop, calls=%fused_computation.6 | loop fusion | flops 4193792 | bytes 4195328 | tf_op jit(solution)/shard_map/reduce_max | solution.py:39
  7.2 2.9 %collective-permute-start.10 = (f32[8,128]{1,0:T(8,128)S(1)}, f32[8,128]{1,0:T(8,128)S(1)}, u32[]{:S(2)}, u32[]{:S(2)}) collective-permute-start(f32[8,128]{1,0:T(8,128)S(1)} %broadcast_add_fusion), channel_id=1, source_target_pairs={{0,1},{1,0},{2,3},{3,2},{4,5},{5,4},{6,7},{7,6},{8,9},{9,8},{10,11... | collective-permute-start | bytes 12296 | tf_op jit(solution)/shard_map/ppermute | solution.py:20
  10.1 1.6 %collective-permute-start = (bf16[128,512]{1,0:T(8,128)(2,1)S(1)}, bf16[128,512]{1,0:T(8,128)(2,1)S(1)}, u32[]{:S(2)}, u32[]{:S(2)}) collective-permute-start(bf16[128,512]{1,0:T(8,128)(2,1)S(1)} %copy-done.2), channel_id=1, source_target_pairs={{0,2},{1,3},{2,0},{3,1},{4,6},{5,7},{6,4},{7,5},{8,10},{9,11},{10,... | collective-permute-start | bytes 393224 | tf_op jit(solution)/shard_map/ppermute | solution.py:20
  11.7 2.5 %collective-permute-start.2 = (bf16[128,512]{1,0:T(8,128)(2,1)S(1)}, bf16[128,512]{1,0:T(8,128)(2,1)S(1)}, u32[]{:S(2)}, u32[]{:S(2)}) collective-permute-start(bf16[128,512]{1,0:T(8,128)(2,1)S(1)} %copy-done.2), channel_id=1, source_target_pairs={{0,6},{1,7},{2,4},{3,5},{4,2},{5,3},{6,0},{7,1},{8,14},{9,15},{10,... | collective-permute-start | bytes 393224 | tf_op jit(solution)/shard_map/ppermute | solution.py:20
  14.9 1.6 %collective-permute-start.11 = (f32[8,128]{1,0:T(8,128)S(1)}, f32[8,128]{1,0:T(8,128)S(1)}, u32[]{:S(2)}, u32[]{:S(2)}) collective-permute-start(f32[8,128]{1,0:T(8,128)S(1)} %fusion.26), channel_id=1, source_target_pairs={{0,16},{1,17},{2,18},{3,19},{4,20},{5,21},{6,22},{7,23},{8,24},{9,... | collective-permute-start | bytes 12296 | tf_op jit(solution)/shard_map/ppermute | solution.py:20
  18.6 1.8 %collective-permute-start.12 = (f32[8,128]{1,0:T(8,128)S(1)}, f32[8,128]{1,0:T(8,128)S(1)}, u32[]{:S(2)}, u32[]{:S(2)}) collective-permute-start(f32[8,128]{1,0:T(8,128)S(1)} %add.120), channel_id=1, source_target_pairs={{0,2},{1,3},{2,0},{3,1},{4,6},{5,7},{6,4},{7,5},{8,10},{9,11},{10,... | collective-permute-start | bytes 12296 | tf_op jit(solution)/shard_map/ppermute | solution.py:20
  20.4 4.6 %multiply_convert_fusion = f16[4096,512]{1,0:T(8,128)(2,1)S(1)} fusion(bf16[512,4096]{1,0:T(8,128)(2,1)} %param.3, bf16[512,512]{1,0:T(8,128)(2,1)S(1)} %copy-done.1, f32[]{:T(128)} %bitcast.34), kind=kOutput, calls=%fused_computation | convolution fusion | flops 2151677952 | bytes 8912900 | tf_op jit(solution)/shard_map/dot_general | solution.py:59
  25.0 1.8 %collective-permute-start.13 = (f32[8,128]{1,0:T(8,128)S(1)}, f32[8,128]{1,0:T(8,128)S(1)}, u32[]{:S(2)}, u32[]{:S(2)}) collective-permute-start(f32[8,128]{1,0:T(8,128)S(1)} %add.121), channel_id=1, source_target_pairs={{0,4},{1,5},{2,6},{3,7},{4,0},{5,1},{6,2},{7,3},{8,12},{9,13},{10,... | collective-permute-start | bytes 12296 | tf_op jit(solution)/shard_map/ppermute | solution.py:20
  27.3 2.2 %collective-permute-done.13 = f32[8,128]{1,0:T(8,128)S(1)} collective-permute-done((f32[8,128]{1,0:T(8,128)S(1)}, f32[8,128]{1,0:T(8,128)S(1)}, u32[]{:S(2)}, u32[]{:S(2)}) %collective-permute-start.13) | collective-permute-done | bytes 4128 | tf_op jit(solution)/shard_map/ppermute | solution.py:20
  31.6 1.5 %collective-permute-start.5 = (bf16[4,64,512]{2,1,0:T(8,128)(2,1)S(1)}, bf16[4,64,512]{2,1,0:T(8,128)(2,1)S(1)}, u32[]{:S(2)}, u32[]{:S(2)}) collective-permute-start(bf16[4,64,512]{2,1,0:T(8,128)(2,1)S(1)} %get-tuple-element.20), channel_id=1, source_target_pairs={{0,16},{1,17},{2,18},{3,19},{4,20},{5,21},{6,22},{7,23},{8,24},{9,... | collective-permute-start | bytes 786440 | tf_op jit(solution)/shard_map/ppermute | solution.py:20
  33.2 4.7 %collective-permute-done.5 = bf16[4,64,512]{2,1,0:T(8,128)(2,1)S(1)} collective-permute-done((bf16[4,64,512]{2,1,0:T(8,128)(2,1)S(1)}, bf16[4,64,512]{2,1,0:T(8,128)(2,1)S(1)}, u32[]{:S(2)}, u32[]{:S(2)}) %collective-permute-start.5) | collective-permute-done | bytes 262176 | tf_op jit(solution)/shard_map/ppermute | solution.py:20
  38.0 1.6 %collective-permute-start.6 = (bf16[2,4,64,512]{3,2,0,1:T(8,128)(2,1)S(1)}, bf16[2,4,64,512]{3,2,0,1:T(8,128)(2,1)S(1)}, u32[]{:S(2)}, u32[]{:S(2)}) collective-permute-start(bf16[2,4,64,512]{3,2,0,1:T(8,128)(2,1)S(1)} %bitcast_dynamic-update-slice_fusion.6), channel_id=1, source_target_pairs={{0,1},{1,0},{2,3},{3,2},{4,5},{5,4},{6,7},{7,6},{8,9},{9,8},{10,11... | collective-permute-start | bytes 1572872 | tf_op jit(solution)/shard_map/ppermute | solution.py:20
  39.5 1.6 %collective-permute-start.4 = (bf16[2,4,64,512]{3,2,0,1:T(8,128)(2,1)S(1)}, bf16[2,4,64,512]{3,2,0,1:T(8,128)(2,1)S(1)}, u32[]{:S(2)}, u32[]{:S(2)}) collective-permute-start(bf16[2,4,64,512]{3,2,0,1:T(8,128)(2,1)S(1)} %bitcast_dynamic-update-slice_fusion.8), channel_id=1, source_target_pairs={{0,16},{1,17},{2,18},{3,19},{4,20},{5,21},{6,22},{7,23},{8,24},{9,... | collective-permute-start | bytes 1572872 | tf_op jit(solution)/shard_map/ppermute | solution.py:20
  41.4 7.5 %collective-permute-done.6 = bf16[2,4,64,512]{3,2,0,1:T(8,128)(2,1)S(1)} collective-permute-done((bf16[2,4,64,512]{3,2,0,1:T(8,128)(2,1)S(1)}, bf16[2,4,64,512]{3,2,0,1:T(8,128)(2,1)S(1)}, u32[]{:S(2)}, u32[]{:S(2)}) %collective-permute-start.6) | collective-permute-done | bytes 524320 | tf_op jit(solution)/shard_map/ppermute | solution.py:20
  51.9 1.6 %collective-permute-start.16 = (f16[4,2,64,512]{3,2,1,0:T(8,128)(2,1)S(1)}, f16[4,2,64,512]{3,2,1,0:T(8,128)(2,1)S(1)}, u32[]{:S(2)}, u32[]{:S(2)}) collective-permute-start(f16[4,2,64,512]{3,2,1,0:T(8,128)(2,1)S(1)} %dynamic-slice_bitcast_fusion.1), channel_id=1, source_target_pairs={{0,16},{1,17},{2,18},{3,19},{4,20},{5,21},{6,22},{7,23},{8,24},{9,... | collective-permute-start | bytes 1572872 | tf_op jit(solution)/shard_map/ppermute | solution.py:20
  54.6 7.0 %collective-permute-done.16 = f16[4,2,64,512]{3,2,1,0:T(8,128)(2,1)S(1)} collective-permute-done((f16[4,2,64,512]{3,2,1,0:T(8,128)(2,1)S(1)}, f16[4,2,64,512]{3,2,1,0:T(8,128)(2,1)S(1)}, u32[]{:S(2)}, u32[]{:S(2)}) %collective-permute-start.16) | collective-permute-done | bytes 524320 | tf_op jit(solution)/shard_map/ppermute | solution.py:20
  62.6 6.3 %collective-permute-done.14 = f16[4,2,64,512]{3,2,0,1:T(8,128)(2,1)S(1)} collective-permute-done((f16[4,2,64,512]{3,2,0,1:T(8,128)(2,1)S(1)}, f16[4,2,64,512]{3,2,0,1:T(8,128)(2,1)S(1)}, u32[]{:S(2)}, u32[]{:S(2)}) %collective-permute-start.14) | collective-permute-done | bytes 524320 | tf_op jit(solution)/shard_map/ppermute | solution.py:20
  70.4 3.6 %collective-permute-done.17 = f16[4,64,512]{2,1,0:T(8,128)(2,1)S(1)} collective-permute-done((f16[4,64,512]{2,1,0:T(8,128)(2,1)S(1)}, f16[4,64,512]{2,1,0:T(8,128)(2,1)S(1)}, u32[]{:S(2)}, u32[]{:S(2)}) %collective-permute-start.17) | collective-permute-done | bytes 262176 | tf_op jit(solution)/shard_map/ppermute | solution.py:20
  74.1 2.5 %collective-permute-done.15 = f16[4,64,512]{2,1,0:T(8,128)(2,1)S(1)} collective-permute-done((f16[4,64,512]{2,1,0:T(8,128)(2,1)S(1)}, f16[4,64,512]{2,1,0:T(8,128)(2,1)S(1)}, u32[]{:S(2)}, u32[]{:S(2)}) %collective-permute-start.15) | collective-permute-done | bytes 262176 | tf_op jit(solution)/shard_map/ppermute | solution.py:20
  76.8 2.3 %collective-permute-start.18 = (f16[128,512]{1,0:T(8,128)(2,1)S(1)}, f16[128,512]{1,0:T(8,128)(2,1)S(1)}, u32[]{:S(2)}, u32[]{:S(2)}) collective-permute-start(f16[128,512]{1,0:T(8,128)(2,1)S(1)} %get-tuple-element.16), channel_id=1, source_target_pairs={{0,2},{1,3},{2,0},{3,1},{4,6},{5,7},{6,4},{7,5},{8,10},{9,11},{10,... | collective-permute-start | bytes 393224 | tf_op jit(solution)/shard_map/ppermute | solution.py:20
  79.1 3.3 %collective-permute-start.19 = (f16[128,512]{1,0:T(8,128)(2,1)S(1)}, f16[128,512]{1,0:T(8,128)(2,1)S(1)}, u32[]{:S(2)}, u32[]{:S(2)}) collective-permute-start(f16[128,512]{1,0:T(8,128)(2,1)S(1)} %get-tuple-element.17), channel_id=1, source_target_pairs={{0,4},{1,5},{2,6},{3,7},{4,0},{5,1},{6,2},{7,3},{8,12},{9,13},{10,... | collective-permute-start | bytes 393224 | tf_op jit(solution)/shard_map/ppermute | solution.py:20
  82.8 2.6 %fusion.3 = bf16[512,512]{0,1:T(8,128)(2,1)S(1)} fusion(bf16[4096,512]{1,0:T(8,128)(2,1)S(1)} %bitcast.128, bf16[512,4096]{1,0:T(8,128)(2,1)S(1)} %copy-done), kind=kOutput, calls=%fused_computation.12 | convolution fusion | flops 2147745792 | bytes 8912896 | tf_op jit(solution)/shard_map/dot_general | solution.py:76
  85.4 4.3 %fusion = bf16[512,4096]{0,1:T(8,128)(2,1)} fusion(bf16[4096,512]{1,0:T(8,128)(2,1)S(1)} %bitcast.129, bf16[512,512]{1,0:T(8,128)(2,1)S(1)} %copy-done.1), kind=kOutput, calls=%fused_computation.2 | convolution fusion | flops 2149580800 | bytes 8912896 | tf_op jit(solution)/shard_map/dot_general | solution.py:77
  89.7 6.3 %copy.35 = bf16[512,4096]{1,0:T(8,128)(2,1)} copy(bf16[512,4096]{0,1:T(8,128)(2,1)} %fusion) | data formatting | bytes 8388608
  (76 shorter events, 16.5 us)
Async XLA Ops:
  0.6 3.1 %copy-start.1 = (bf16[512,512]{1,0:T(8,128)(2,1)S(1)}, bf16[512,512]{1,0:T(8,128)(2,1)}, u32[]{:S(2)}) copy-start(bf16[512,512]{1,0:T(8,128)(2,1)} %param.5) | copy-start | bytes 1572868
  0.6 9.5 %copy-start.2 = (bf16[128,512]{1,0:T(8,128)(2,1)S(1)}, bf16[128,512]{1,0:T(8,128)(2,1)}, u32[]{:S(2)}) copy-start(bf16[128,512]{1,0:T(8,128)(2,1)} %param.4) | copy-start | bytes 393220
  5.2 1.3 %collective-permute-start.8 = (f32[8,128]{1,0:T(8,128)S(1)}, f32[8,128]{1,0:T(8,128)S(1)}, u32[]{:S(2)}, u32[]{:S(2)}) collective-permute-start(f32[8,128]{1,0:T(8,128)S(1)} %broadcast_in_dim.71), channel_id=1, source_target_pairs={{0,8},{1,9},{2,10},{3,11},{4,12},{5,13},{6,14},{7,15},{8,0},{9,1},... | collective-permute-start | bytes 12296 | tf_op jit(solution)/shard_map/ppermute | solution.py:20
  7.2 7.1 %collective-permute-start.10 = (f32[8,128]{1,0:T(8,128)S(1)}, f32[8,128]{1,0:T(8,128)S(1)}, u32[]{:S(2)}, u32[]{:S(2)}) collective-permute-start(f32[8,128]{1,0:T(8,128)S(1)} %broadcast_add_fusion), channel_id=1, source_target_pairs={{0,1},{1,0},{2,3},{3,2},{4,5},{5,4},{6,7},{7,6},{8,9},{9,8},{10,11... | collective-permute-start | bytes 12296 | tf_op jit(solution)/shard_map/ppermute | solution.py:20
  10.1 20.7 %collective-permute-start = (bf16[128,512]{1,0:T(8,128)(2,1)S(1)}, bf16[128,512]{1,0:T(8,128)(2,1)S(1)}, u32[]{:S(2)}, u32[]{:S(2)}) collective-permute-start(bf16[128,512]{1,0:T(8,128)(2,1)S(1)} %copy-done.2), channel_id=1, source_target_pairs={{0,2},{1,3},{2,0},{3,1},{4,6},{5,7},{6,4},{7,5},{8,10},{9,11},{10,... | collective-permute-start | bytes 393224 | tf_op jit(solution)/shard_map/ppermute | solution.py:20
  11.7 19.2 %collective-permute-start.2 = (bf16[128,512]{1,0:T(8,128)(2,1)S(1)}, bf16[128,512]{1,0:T(8,128)(2,1)S(1)}, u32[]{:S(2)}, u32[]{:S(2)}) collective-permute-start(bf16[128,512]{1,0:T(8,128)(2,1)S(1)} %copy-done.2), channel_id=1, source_target_pairs={{0,6},{1,7},{2,4},{3,5},{4,2},{5,3},{6,0},{7,1},{8,14},{9,15},{10,... | collective-permute-start | bytes 393224 | tf_op jit(solution)/shard_map/ppermute | solution.py:20
  14.2 16.7 %collective-permute-start.1 = (bf16[128,512]{1,0:T(8,128)(2,1)S(1)}, bf16[128,512]{1,0:T(8,128)(2,1)S(1)}, u32[]{:S(2)}, u32[]{:S(2)}) collective-permute-start(bf16[128,512]{1,0:T(8,128)(2,1)S(1)} %copy-done.2), channel_id=1, source_target_pairs={{0,4},{1,5},{2,6},{3,7},{4,0},{5,1},{6,2},{7,3},{8,12},{9,13},{10,... | collective-permute-start | bytes 393224 | tf_op jit(solution)/shard_map/ppermute | solution.py:20
  14.9 3.7 %collective-permute-start.11 = (f32[8,128]{1,0:T(8,128)S(1)}, f32[8,128]{1,0:T(8,128)S(1)}, u32[]{:S(2)}, u32[]{:S(2)}) collective-permute-start(f32[8,128]{1,0:T(8,128)S(1)} %fusion.26), channel_id=1, source_target_pairs={{0,16},{1,17},{2,18},{3,19},{4,20},{5,21},{6,22},{7,23},{8,24},{9,... | collective-permute-start | bytes 12296 | tf_op jit(solution)/shard_map/ppermute | solution.py:20
  18.6 6.4 %collective-permute-start.12 = (f32[8,128]{1,0:T(8,128)S(1)}, f32[8,128]{1,0:T(8,128)S(1)}, u32[]{:S(2)}, u32[]{:S(2)}) collective-permute-start(f32[8,128]{1,0:T(8,128)S(1)} %add.120), channel_id=1, source_target_pairs={{0,2},{1,3},{2,0},{3,1},{4,6},{5,7},{6,4},{7,5},{8,10},{9,11},{10,... | collective-permute-start | bytes 12296 | tf_op jit(solution)/shard_map/ppermute | solution.py:20
  25.0 4.6 %collective-permute-start.13 = (f32[8,128]{1,0:T(8,128)S(1)}, f32[8,128]{1,0:T(8,128)S(1)}, u32[]{:S(2)}, u32[]{:S(2)}) collective-permute-start(f32[8,128]{1,0:T(8,128)S(1)} %add.121), channel_id=1, source_target_pairs={{0,4},{1,5},{2,6},{3,7},{4,0},{5,1},{6,2},{7,3},{8,12},{9,13},{10,... | collective-permute-start | bytes 12296 | tf_op jit(solution)/shard_map/ppermute | solution.py:20
  27.3 23.1 %collective-permute-start.9 = (f16[16,128,512]{2,1,0:T(8,128)(2,1)S(1)}, f16[16,128,512]{2,1,0:T(8,128)(2,1)S(1)}, u32[]{:S(2)}, u32[]{:S(2)}) collective-permute-start(f16[16,128,512]{2,1,0:T(8,128)(2,1)S(1)} %dynamic-slice_bitcast_fusion), channel_id=1, source_target_pairs={{0,8},{1,9},{2,10},{3,11},{4,12},{5,13},{6,14},{7,15},{8,0},{9,1},... | collective-permute-start | bytes 6291464 | tf_op jit(solution)/shard_map/ppermute | solution.py:20
  31.0 8.6 %collective-permute-start.3 = (bf16[4,64,512]{2,1,0:T(8,128)(2,1)S(1)}, bf16[4,64,512]{2,1,0:T(8,128)(2,1)S(1)}, u32[]{:S(2)}, u32[]{:S(2)}) collective-permute-start(bf16[4,64,512]{2,1,0:T(8,128)(2,1)S(1)} %get-tuple-element.19), channel_id=1, source_target_pairs={{0,1},{1,0},{2,3},{3,2},{4,5},{5,4},{6,7},{7,6},{8,9},{9,8},{10,11... | collective-permute-start | bytes 786440 | tf_op jit(solution)/shard_map/ppermute | solution.py:20
  31.6 6.4 %collective-permute-start.5 = (bf16[4,64,512]{2,1,0:T(8,128)(2,1)S(1)}, bf16[4,64,512]{2,1,0:T(8,128)(2,1)S(1)}, u32[]{:S(2)}, u32[]{:S(2)}) collective-permute-start(bf16[4,64,512]{2,1,0:T(8,128)(2,1)S(1)} %get-tuple-element.20), channel_id=1, source_target_pairs={{0,16},{1,17},{2,18},{3,19},{4,20},{5,21},{6,22},{7,23},{8,24},{9,... | collective-permute-start | bytes 786440 | tf_op jit(solution)/shard_map/ppermute | solution.py:20
  38.0 11.0 %collective-permute-start.6 = (bf16[2,4,64,512]{3,2,0,1:T(8,128)(2,1)S(1)}, bf16[2,4,64,512]{3,2,0,1:T(8,128)(2,1)S(1)}, u32[]{:S(2)}, u32[]{:S(2)}) collective-permute-start(bf16[2,4,64,512]{3,2,0,1:T(8,128)(2,1)S(1)} %bitcast_dynamic-update-slice_fusion.6), channel_id=1, source_target_pairs={{0,1},{1,0},{2,3},{3,2},{4,5},{5,4},{6,7},{7,6},{8,9},{9,8},{10,11... | collective-permute-start | bytes 1572872 | tf_op jit(solution)/shard_map/ppermute | solution.py:20
  39.5 10.7 %collective-permute-start.4 = (bf16[2,4,64,512]{3,2,0,1:T(8,128)(2,1)S(1)}, bf16[2,4,64,512]{3,2,0,1:T(8,128)(2,1)S(1)}, u32[]{:S(2)}, u32[]{:S(2)}) collective-permute-start(bf16[2,4,64,512]{3,2,0,1:T(8,128)(2,1)S(1)} %bitcast_dynamic-update-slice_fusion.8), channel_id=1, source_target_pairs={{0,16},{1,17},{2,18},{3,19},{4,20},{5,21},{6,22},{7,23},{8,24},{9,... | collective-permute-start | bytes 1572872 | tf_op jit(solution)/shard_map/ppermute | solution.py:20
  51.9 9.8 %collective-permute-start.16 = (f16[4,2,64,512]{3,2,1,0:T(8,128)(2,1)S(1)}, f16[4,2,64,512]{3,2,1,0:T(8,128)(2,1)S(1)}, u32[]{:S(2)}, u32[]{:S(2)}) collective-permute-start(f16[4,2,64,512]{3,2,1,0:T(8,128)(2,1)S(1)} %dynamic-slice_bitcast_fusion.1), channel_id=1, source_target_pairs={{0,16},{1,17},{2,18},{3,19},{4,20},{5,21},{6,22},{7,23},{8,24},{9,... | collective-permute-start | bytes 1572872 | tf_op jit(solution)/shard_map/ppermute | solution.py:20
  53.6 28.9 %collective-permute-start.7 = (bf16[4,2,2,2,64,512]{5,4,3,2,1,0:T(8,128)(2,1)S(1)}, bf16[4,2,2,2,64,512]{5,4,3,2,1,0:T(8,128)(2,1)S(1)}, u32[]{:S(2)}, u32[]{:S(2)}) collective-permute-start(bf16[4,2,2,2,64,512]{5,4,3,2,1,0:T(8,128)(2,1)S(1)} %pad_maximum_fusion), channel_id=1, source_target_pairs={{0,8},{1,9},{2,10},{3,11},{4,12},{5,13},{6,14},{7,15},{8,0},{9,1},... | collective-permute-start | bytes 6291464 | tf_op jit(solution)/shard_map/ppermute | solution.py:20
  54.0 14.8 %collective-permute-start.14 = (f16[4,2,64,512]{3,2,0,1:T(8,128)(2,1)S(1)}, f16[4,2,64,512]{3,2,0,1:T(8,128)(2,1)S(1)}, u32[]{:S(2)}, u32[]{:S(2)}) collective-permute-start(f16[4,2,64,512]{3,2,0,1:T(8,128)(2,1)S(1)} %bitcast.130), channel_id=1, source_target_pairs={{0,1},{1,0},{2,3},{3,2},{4,5},{5,4},{6,7},{7,6},{8,9},{9,8},{10,11... | collective-permute-start | bytes 1572872 | tf_op jit(solution)/shard_map/ppermute | solution.py:20
  62.0 12.1 %collective-permute-start.17 = (f16[4,64,512]{2,1,0:T(8,128)(2,1)S(1)}, f16[4,64,512]{2,1,0:T(8,128)(2,1)S(1)}, u32[]{:S(2)}, u32[]{:S(2)}) collective-permute-start(f16[4,64,512]{2,1,0:T(8,128)(2,1)S(1)} %dynamic-slice_bitcast_fusion.2), channel_id=1, source_target_pairs={{0,1},{1,0},{2,3},{3,2},{4,5},{5,4},{6,7},{7,6},{8,9},{9,8},{10,11... | collective-permute-start | bytes 786440 | tf_op jit(solution)/shard_map/ppermute | solution.py:20
  69.1 7.6 %collective-permute-start.15 = (f16[4,64,512]{2,1,0:T(8,128)(2,1)S(1)}, f16[4,64,512]{2,1,0:T(8,128)(2,1)S(1)}, u32[]{:S(2)}, u32[]{:S(2)}) collective-permute-start(f16[4,64,512]{2,1,0:T(8,128)(2,1)S(1)} %dynamic-slice_bitcast_fusion.3), channel_id=1, source_target_pairs={{0,16},{1,17},{2,18},{3,19},{4,20},{5,21},{6,22},{7,23},{8,24},{9,... | collective-permute-start | bytes 786440 | tf_op jit(solution)/shard_map/ppermute | solution.py:20
  70.4 12.4 %copy-start = (bf16[512,4096]{1,0:T(8,128)(2,1)S(1)}, bf16[512,4096]{1,0:T(8,128)(2,1)}, u32[]{:S(2)}) copy-start(bf16[512,4096]{1,0:T(8,128)(2,1)} %param.3) | copy-start | bytes 12582916
  76.8 20.2 %collective-permute-start.18 = (f16[128,512]{1,0:T(8,128)(2,1)S(1)}, f16[128,512]{1,0:T(8,128)(2,1)S(1)}, u32[]{:S(2)}, u32[]{:S(2)}) collective-permute-start(f16[128,512]{1,0:T(8,128)(2,1)S(1)} %get-tuple-element.16), channel_id=1, source_target_pairs={{0,2},{1,3},{2,0},{3,1},{4,6},{5,7},{6,4},{7,5},{8,10},{9,11},{10,... | collective-permute-start | bytes 393224 | tf_op jit(solution)/shard_map/ppermute | solution.py:20
  79.1 17.9 %collective-permute-start.19 = (f16[128,512]{1,0:T(8,128)(2,1)S(1)}, f16[128,512]{1,0:T(8,128)(2,1)S(1)}, u32[]{:S(2)}, u32[]{:S(2)}) collective-permute-start(f16[128,512]{1,0:T(8,128)(2,1)S(1)} %get-tuple-element.17), channel_id=1, source_target_pairs={{0,4},{1,5},{2,6},{3,7},{4,0},{5,1},{6,2},{7,3},{8,12},{9,13},{10,... | collective-permute-start | bytes 393224 | tf_op jit(solution)/shard_map/ppermute | solution.py:20
  82.5 14.6 %collective-permute-start.20 = (f16[128,512]{1,0:T(8,128)(2,1)S(1)}, f16[128,512]{1,0:T(8,128)(2,1)S(1)}, u32[]{:S(2)}, u32[]{:S(2)}) collective-permute-start(f16[128,512]{1,0:T(8,128)(2,1)S(1)} %get-tuple-element.18), channel_id=1, source_target_pairs={{0,6},{1,7},{2,4},{3,5},{4,2},{5,3},{6,0},{7,1},{8,14},{9,15},{10,... | collective-permute-start | bytes 393224 | tf_op jit(solution)/shard_map/ppermute | solution.py:20

commit v2 on v1

v2 whole, which is shorter than its diff:
```python
import functools

import jax
import jax.numpy as jnp
from jax import lax
from jax.experimental import pallas as pl
from jax.experimental.pallas import tpu as pltpu
from jax.sharding import PartitionSpec as P

AXES = ("wide", "node")
TOP = 14.0
NOTE = 8


def products_kernel(place, tok, cot, weight, *rest, first, last):
    keys_in, keys, grad, total = (None if first else rest[0]), *rest[-3:]
    step = pl.program_id(0)

    @pl.when(step == 0)
    def _():
        total[...] = jnp.zeros_like(total) if first else keys_in[...]

    total[...] += jnp.dot(tok[...], weight[0], preferred_element_type=jnp.float32)
    grad[...] = lax.dot_general(
        cot[...], weight[0], (((1,), (1,)), ((), ())), preferred_element_type=jnp.float32
    ).astype(grad.dtype)

    @pl.when(step == pl.num_programs(0) - 1)
    def _():
        keys[...] = total[...].astype(keys.dtype)


def products(tokens, cotangent, weight, z_me, start, before, last):
    steps, depth, kd = weight.shape
    rows = tokens.shape[0]
    whole = pl.BlockSpec((rows, kd), lambda i, z: (0, 0))
    columns = pl.BlockSpec((rows, depth), lambda i, z: (0, z[0] ^ (start + i)))
    in_specs = [columns, whole, pl.BlockSpec((1, depth, kd), lambda i, z: (i, 0, 0))]
    operands = [tokens, cotangent, weight]
    aliases = {}
    if before is not None:
        in_specs += [whole, pl.BlockSpec(memory_space=pl.ANY)]
        operands += list(before)
        aliases = {5: 1}
    return pl.pallas_call(
        functools.partial(products_kernel, first=before is None, last=last),
        grid_spec=pltpu.PrefetchScalarGridSpec(
            num_scalar_prefetch=1,
            grid=(steps,),
            in_specs=in_specs,
            out_specs=[whole, columns],
            scratch_shapes=[pltpu.VMEM((rows, kd), jnp.float32)],
        ),
        out_shape=[
            jax.ShapeDtypeStruct((rows, kd), jnp.bfloat16 if last else jnp.float32),
            jax.ShapeDtypeStruct(tokens.shape, jnp.bfloat16),
        ],
        input_output_aliases=aliases,
        compiler_params=pltpu.CompilerParams(vmem_limit_bytes=24 * 1024 * 1024),
        cost_estimate=pl.CostEstimate(
            flops=4 * rows * steps * depth * kd,
            bytes_accessed=2 * (2 * rows * steps * depth + steps * depth * kd + 3 * rows * kd),
            transcendentals=0,
        ),
    )(jnp.reshape(z_me, (1,)), *operands)


def on_device(tokens, key_weight, cotangent):
    wide, node = lax.axis_size("wide"), lax.axis_size("node")
    w_me, n_me = lax.axis_index("wide"), lax.axis_index("node")
    rows, kd = key_weight.shape
    half = rows // 2
    ny, nx, nz = wide // 2, 2, node // 2
    core, y_me = w_me & 1, w_me >> 1
    x_me, z_me = n_me & 1, n_me >> 1

    def swap(value, name, j):
        mask = {"core": j * node, "y": 2 * j * node, "x": j, "z": 2 * j}[name]
        return lax.ppermute(value, AXES, [(i, i ^ mask) for i in range(wide * node)])

    def gathered(value, name, size, me):
        parts = [value] + [swap(value, name, j) for j in range(1, size)]
        out = jnp.zeros((size,) + value.shape, value.dtype)
        for j in range(size):
            out = lax.dynamic_update_index_in_dim(out, parts[j], me ^ j, 0)
        return out

    def pick(value, axis, index):
        return lax.dynamic_index_in_dim(value, index, axis, keepdims=False)

    def spread(blocks):
        blocks = jnp.stack(blocks).reshape(-1, 2, half, kd)
        one = gathered(gathered(blocks[:, 0], "x", nx, x_me), "y", ny, y_me)
        two = gathered(gathered(blocks[:, 1], "y", ny, y_me), "x", nx, x_me)
        both = jnp.stack([one.transpose(2, 1, 0, 3, 4), two.transpose(2, 0, 1, 3, 4)], axis=3)
        weight = gathered(both, "core", 2, core)
        return weight.transpose(1, 2, 3, 0, 4, 5, 6).reshape(-1, nx * ny * 2 * rows, kd)

    shards = [key_weight] + [swap(key_weight, "z", j) for j in range(1, nz)]
    near = spread(shards[: nz // 2])
    far = spread(shards[nz // 2 :])

    part = lax.dot_general(
        tokens, cotangent, (((0,), (0,)), ((), ())), preferred_element_type=jnp.float32
    )
    top = jnp.maximum(jnp.max(jnp.abs(part), axis=0, keepdims=True), 2.0**-100)
    power = jnp.ceil(jnp.log2(top))
    part = part.reshape(2, nz // 2, nx, ny, 2, rows, kd)

    notes = {}

    def traded(value, power, name, j, key):
        flat = (value.reshape(-1, kd) * jnp.exp2(TOP - power)).astype(jnp.float16)
        if key not in notes:
            note = jnp.broadcast_to(power, (NOTE, kd)).astype(jnp.float16)
            got = swap(jnp.concatenate([flat, note]), name, j)
            notes[key] = got[-NOTE:][:1].astype(jnp.float32)
            got = got[:-NOTE]
        else:
            got = swap(flat, name, j)
        return (got.astype(jnp.float32) * jnp.exp2(notes[key] - TOP)).reshape(value.shape)

    def summed(value, power, axis, name, size, me, key):
        total, bound = pick(value, axis, me), power
        for j in range(1, size):
            total = total + traded(pick(value, axis, me ^ j), power, name, j, (key, j))
            bound = jnp.maximum(bound, notes[key, j])
        return total, bound + (size - 1).bit_length()

    def reduced(slab, power):
        slab, power = summed(slab, power, 3, "core", 2, core, "core")
        one, one_power = summed(slab[:, :, :, :half], power, 1, "x", nx, x_me, "x one")
        two, two_power = summed(slab[:, :, :, half:], power, 2, "y", ny, y_me, "y two")
        one, one_power = summed(one, one_power, 1, "y", ny, y_me, "y one")
        two, two_power = summed(two, two_power, 1, "x", nx, x_me, "x two")
        return jnp.concatenate([one, two], axis=1), jnp.maximum(one_power, two_power)

    z_top = z_me // (nz // 2)
    z_low = z_me % (nz // 2)
    away, power_z = reduced(pick(part, 0, 1 - z_top), power)
    home, power_z = reduced(pick(part, 0, z_top), power)
    total = pick(home, 0, z_low)
    for j in range(nz // 2, nz):
        total = total + traded(pick(away, 0, z_low ^ (j - nz // 2)), power_z, "z", j, ("z", j))
    for j in range(1, nz // 2):
        total = total + traded(pick(home, 0, z_low ^ j), power_z, "z", j, ("z", j))
    total_tokens = tokens.shape[0] * wide * node
    weight_grad = total * (1.0 / jnp.sqrt(jnp.float32(total_tokens)))

    begun = products(tokens, cotangent, near, z_me, 0, None, False)
    keys, input_grad = products(tokens, cotangent, far, z_me, nz // 2, begun, True)
    return (keys, input_grad, weight_grad)


def solution(mesh):
    placed = (P(AXES, None), P(("node", "wide"), None), P(AXES, None))
    return jax.shard_map(
        on_device,
        mesh=mesh,
        in_specs=placed,
        out_specs=(P(AXES, None), P(AXES, None), P(("node", "wide"), None)),
        check_vma=False,
    )
```

time: 98.1 us -> 84.8 us (0.86)
  waiting for transfers between devices: 36.8 us -> 25.8 us
  Pallas kernels: 0 us -> 7.85 us
  matrix products: 11.5 us -> 4.7 us
  local copies, waits for them, and re-layouts: 12 us -> 5.55 us
  starting transfers between devices: 27.1 us -> 31.2 us
  between operations: 2.5 us -> 1.36 us
    ppermute x21 -> x26, waiting for transfers between devices: 36.8 us -> 25.8 us  [swap(): lax.ppermute(value, AXES, [(i, i ^ mask) for i in range(wide * node)])]
    pallas_call x0 -> x2, Pallas kernels: none -> 7.85 us  [products(): pl.pallas_call(functools.partial(products_kernel, first=before is None, l...]
    dot_general x2 -> x0, matrix products: 6.92 us -> none  [the longest x1 4.34 us: on_device(): lax.dot_general(cotangent, weight, (((1,), (1,)), ((), ())), preferred_el...]
    unnamed x9 -> x12, local copies, waits for them, and re-layouts: 7.43 us -> 2.99 us
    ppermute x21 -> x26, starting transfers between devices: 27.1 us -> 31.2 us  [swap(): lax.ppermute(value, AXES, [(i, i ^ mask) for i in range(wide * node)])]
    reduce_max x2 -> x0, other arithmetic: 3.3 us -> none  [the longest x1 3.12 us: on_device(): tok_top = jnp.max(jnp.abs(tokens), axis=1).astype(jnp.float32)]
    mul x1 -> x6, other arithmetic: 0.79 us -> 3.14 us  [the longest x5 2.32 us: traded(): got.astype(jnp.float32) * jnp.exp2(notes[key] - TOP)]
    slice x3 -> x2, local copies, waits for them, and re-layouts: 1.54 us -> 0.35 us  [reduced(): slab[:, :, :, half:]]
  transfers between devices with their start and end apart: 21 -> 26, of which waited for: 10 -> 12; matrix products, arithmetic and copies ran while one was open for 24% -> 17% of each run, Pallas kernels for 0% -> 9%
where the time goes in v2:
time: 84.8 us; the launch traced here: 84.6 us
  starting transfers between devices  31.2 us (37%)
  waiting for transfers between devices  25.8 us (30%)
  other arithmetic  8.1 us (10%)
  Pallas kernels  7.85 us (9%)
  local copies, waits for them, and re-layouts  5.55 us (7%)
  matrix products  4.7 us (6%)
  between operations  1.36 us (2%)
    ppermute x26, starting transfers between devices, swap(): lax.ppermute(value, AXES, [(i, i ^ mask) for i in range(wide * node)])  31.2 us
    ppermute x26, waiting for transfers between devices, swap(): lax.ppermute(value, AXES, [(i, i ^ mask) for i in range(wide * node)])  25.8 us
    pallas_call x2, Pallas kernels, products(): pl.pallas_call(functools.partial(products_kernel, first=before is None, l...  7.85 us
    dot_general x1, matrix products, on_device(): lax.dot_general(tokens, cotangent, (((0,), (0,)), ((), ())), preferred_el...  4.7 us
    unnamed x12, local copies, waits for them, and re-layouts  2.99 us
    mul x5, other arithmetic, traded(): got.astype(jnp.float32) * jnp.exp2(notes[key] - TOP)  2.32 us
    convert_element_type x5, other arithmetic, traded(): flat = (value.reshape(-1, kd) * jnp.exp2(TOP - power)).astype(jnp.float16)  2.07 us
  transfers between devices with their start and end apart: 26, of which 12 were waited for; matrix products, arithmetic and copies ran while one was open for 17% of the time, Pallas kernels for 9%

profile of v2, /device:TPU:0, one launch (start us, length us, event | category | flops | bytes accessed | tf_op | source)
XLA Modules:
  0.0 84.6 jit_solution(2959082754627358747)
XLA Ops:
  0.6 4.1 %collective-permute-start = (bf16[128,512]{1,0:T(8,128)(2,1)}, bf16[128,512]{1,0:T(8,128)(2,1)S(1)}, u32[]{:S(2)}, u32[]{:S(2)}) collective-permute-start(bf16[128,512]{1,0:T(8,128)(2,1)} %param.4), channel_id=1, source_target_pairs={{0,4},{1,5},{2,6},{3,7},{4,0},{5,1},{6,2},{7,3},{8,12},{9,13},{10,... | collective-permute-start | bytes 393224 | tf_op jit(solution)/shard_map/ppermute | solution.py:79
  6.3 4.7 %abs_reduce_fusion = (f32[512]{0:T(512)S(1)}, f32[4096,512]{1,0:T(8,128)S(1)}) fusion(bf16[512,4096]{1,0:T(8,128)(2,1)} %tok.3, bf16[512,512]{1,0:T(8,128)(2,1)} %cot.3), kind=kOutput, calls=%fused_computation | convolution fusion | flops 2151677440 | bytes 13109248 | tf_op jit(solution)/shard_map/dot_general | solution.py:103
  11.6 2.7 %copy-done.2 = f32[4096,512]{1,0:T(8,128)} copy-done((f32[4096,512]{1,0:T(8,128)}, f32[4096,512]{1,0:T(8,128)S(1)}, u32[]{:S(2)}) %copy-start.2) | copy-done | bytes 8388632
  14.3 1.6 %fusion = (f16[1024,512]{1,0:T(8,128)(2,1)S(1)}, f16[1024,512]{1,0:T(8,128)(2,1)}) fusion(f32[1,2,2,2,1,128,512]{6,5,4,3,2,1,0:T(8,128)S(1)} %get-tuple-element.21, f32[512]{0:T(512)S(1)} %get-tuple-element.66, f32[1,2,2,2,1,128,512]{6,5,4,3,2,1,0:T(8,128)S(1)} %get-tuple-element.22), kind=kLoop, calls=%fused_computation.4 | loop fusion | flops 2097152 | bytes 6293504 | tf_op jit(solution)/shard_map/convert_element_type | solution.py:113
  16.7 1.6 %collective-permute-start.4 = (bf16[2,64,512]{2,1,0:T(8,128)(2,1)S(1)}, bf16[2,64,512]{2,1,0:T(8,128)(2,1)S(1)}, u32[]{:S(2)}, u32[]{:S(2)}) collective-permute-start(bf16[2,64,512]{2,1,0:T(8,128)(2,1)S(1)} %get-tuple-element.36), channel_id=1, source_target_pairs={{0,16},{1,17},{2,18},{3,19},{4,20},{5,21},{6,22},{7,23},{8,24},{9,... | collective-permute-start | bytes 393224 | tf_op jit(solution)/shard_map/ppermute | solution.py:79
  19.0 1.5 %collective-permute-start.8 = (bf16[2,64,512]{2,1,0:T(8,128)(2,1)S(1)}, bf16[2,64,512]{2,1,0:T(8,128)(2,1)S(1)}, u32[]{:S(2)}, u32[]{:S(2)}) collective-permute-start(bf16[2,64,512]{2,1,0:T(8,128)(2,1)S(1)} %get-tuple-element.33), channel_id=1, source_target_pairs={{0,1},{1,0},{2,3},{3,2},{4,5},{5,4},{6,7},{7,6},{8,9},{9,8},{10,11... | collective-permute-start | bytes 393224 | tf_op jit(solution)/shard_map/ppermute | solution.py:79
  20.6 2.5 %collective-permute-done.4 = bf16[2,64,512]{2,1,0:T(8,128)(2,1)S(1)} collective-permute-done((bf16[2,64,512]{2,1,0:T(8,128)(2,1)S(1)}, bf16[2,64,512]{2,1,0:T(8,128)(2,1)S(1)}, u32[]{:S(2)}, u32[]{:S(2)}) %collective-permute-start.4) | collective-permute-done | bytes 131104 | tf_op jit(solution)/shard_map/ppermute | solution.py:79
  27.4 1.9 %collective-permute-done.2 = bf16[2,64,512]{2,1,0:T(8,128)(2,1)S(1)} collective-permute-done((bf16[2,64,512]{2,1,0:T(8,128)(2,1)S(1)}, bf16[2,64,512]{2,1,0:T(8,128)(2,1)S(1)}, u32[]{:S(2)}, u32[]{:S(2)}) %collective-permute-start.2) | collective-permute-done | bytes 131104 | tf_op jit(solution)/shard_map/ppermute | solution.py:79
  29.3 1.5 %collective-permute-start.9 = (bf16[2,2,64,512]{3,2,0,1:T(8,128)(2,1)S(1)}, bf16[2,2,64,512]{3,2,0,1:T(8,128)(2,1)S(1)}, u32[]{:S(2)}, u32[]{:S(2)}) collective-permute-start(bf16[2,2,64,512]{3,2,0,1:T(8,128)(2,1)S(1)} %bitcast_dynamic-update-slice_fusion.11), channel_id=1, source_target_pairs={{0,16},{1,17},{2,18},{3,19},{4,20},{5,21},{6,22},{7,23},{8,24},{9,... | collective-permute-start | bytes 786440 | tf_op jit(solution)/shard_map/ppermute | solution.py:79
  30.9 4.0 %collective-permute-done.5 = bf16[2,2,64,512]{3,2,0,1:T(8,128)(2,1)S(1)} collective-permute-done((bf16[2,2,64,512]{3,2,0,1:T(8,128)(2,1)S(1)}, bf16[2,2,64,512]{3,2,0,1:T(8,128)(2,1)S(1)}, u32[]{:S(2)}, u32[]{:S(2)}) %collective-permute-start.5) | collective-permute-done | bytes 262176 | tf_op jit(solution)/shard_map/ppermute | solution.py:79
  34.9 1.5 %collective-permute-start.3 = (bf16[2,2,64,512]{3,2,0,1:T(8,128)(2,1)S(1)}, bf16[2,2,64,512]{3,2,0,1:T(8,128)(2,1)S(1)}, u32[]{:S(2)}, u32[]{:S(2)}) collective-permute-start(bf16[2,2,64,512]{3,2,0,1:T(8,128)(2,1)S(1)} %bitcast_dynamic-update-slice_fusion.14), channel_id=1, source_target_pairs={{0,16},{1,17},{2,18},{3,19},{4,20},{5,21},{6,22},{7,23},{8,24},{9,... | collective-permute-start | bytes 786440 | tf_op jit(solution)/shard_map/ppermute | solution.py:79
  36.5 2.9 %collective-permute-done.11 = bf16[2,2,64,512]{3,2,0,1:T(8,128)(2,1)S(1)} collective-permute-done((bf16[2,2,64,512]{3,2,0,1:T(8,128)(2,1)S(1)}, bf16[2,2,64,512]{3,2,0,1:T(8,128)(2,1)S(1)}, u32[]{:S(2)}, u32[]{:S(2)}) %collective-permute-start.11) | collective-permute-done | bytes 262176 | tf_op jit(solution)/shard_map/ppermute | solution.py:79
  39.7 1.6 %collective-permute-done.3 = bf16[2,2,64,512]{3,2,0,1:T(8,128)(2,1)S(1)} collective-permute-done((bf16[2,2,64,512]{3,2,0,1:T(8,128)(2,1)S(1)}, bf16[2,2,64,512]{3,2,0,1:T(8,128)(2,1)S(1)}, u32[]{:S(2)}, u32[]{:S(2)}) %collective-permute-start.3) | collective-permute-done | bytes 262176 | tf_op jit(solution)/shard_map/ppermute | solution.py:79
  41.6 2.0 %convert_multiply_fusion = (f32[1024,512]{1,0:T(8,128)S(1)}, f32[1024,512]{1,0:T(8,128)S(1)}) fusion(f16[1032,512]{1,0:T(8,128)(2,1)S(1)} %collective-permute-done.14, f32[512]{0:T(512)S(1)} %bitcast.266, f16[1024,512]{1,0:T(8,128)(2,1)} %collective-permute-done.13), kind=kLoop, calls=%fused_computation.7 | loop fusion | flops 2097152 | bytes 6293504 | tf_op jit(solution)/shard_map/mul | solution.py:121
  46.1 1.6 %collective-permute-start.20 = (f16[264,512]{1,0:T(8,128)(2,1)S(1)}, f16[264,512]{1,0:T(8,128)(2,1)S(1)}, u32[]{:S(2)}, u32[]{:S(2)}) collective-permute-start(f16[264,512]{1,0:T(8,128)(2,1)S(1)} %get-tuple-element.42), channel_id=1, source_target_pairs={{0,16},{1,17},{2,18},{3,19},{4,20},{5,21},{6,22},{7,23},{8,24},{9,... | collective-permute-start | bytes 811016 | tf_op jit(solution)/shard_map/ppermute | solution.py:79
  48.6 1.6 %collective-permute-start.16 = (f16[264,512]{1,0:T(8,128)(2,1)S(1)}, f16[264,512]{1,0:T(8,128)(2,1)S(1)}, u32[]{:S(2)}, u32[]{:S(2)}) collective-permute-start(f16[264,512]{1,0:T(8,128)(2,1)S(1)} %get-tuple-element.43), channel_id=1, source_target_pairs={{0,1},{1,0},{2,3},{3,2},{4,5},{5,4},{6,7},{7,6},{8,9},{9,8},{10,11... | collective-permute-start | bytes 811016 | tf_op jit(solution)/shard_map/ppermute | solution.py:79
  50.1 5.4 %collective-permute-done.20 = f16[264,512]{1,0:T(8,128)(2,1)S(1)} collective-permute-done((f16[264,512]{1,0:T(8,128)(2,1)S(1)}, f16[264,512]{1,0:T(8,128)(2,1)S(1)}, u32[]{:S(2)}, u32[]{:S(2)}) %collective-permute-start.20) | collective-permute-done | bytes 270368 | tf_op jit(solution)/shard_map/ppermute | solution.py:79
  57.0 3.2 %collective-permute-done.19 = f16[256,512]{1,0:T(8,128)(2,1)S(1)} collective-permute-done((f16[256,512]{1,0:T(8,128)(2,1)S(1)}, f16[256,512]{1,0:T(8,128)(2,1)S(1)}, u32[]{:S(2)}, u32[]{:S(2)}) %collective-permute-start.19) | collective-permute-done | bytes 262176 | tf_op jit(solution)/shard_map/ppermute | solution.py:79
  60.8 1.6 %collective-permute-start.22 = (f16[136,512]{1,0:T(8,128)(2,1)S(1)}, f16[136,512]{1,0:T(8,128)(2,1)S(1)}, u32[]{:S(2)}, u32[]{:S(2)}) collective-permute-start(f16[136,512]{1,0:T(8,128)(2,1)S(1)} %pad_maximum_fusion.9), channel_id=1, source_target_pairs={{0,1},{1,0},{2,3},{3,2},{4,5},{5,4},{6,7},{7,6},{8,9},{9,8},{10,11... | collective-permute-start | bytes 417800 | tf_op jit(solution)/shard_map/ppermute | solution.py:79
  62.9 1.6 %collective-permute-start.18 = (f16[136,512]{1,0:T(8,128)(2,1)S(1)}, f16[136,512]{1,0:T(8,128)(2,1)S(1)}, u32[]{:S(2)}, u32[]{:S(2)}) collective-permute-start(f16[136,512]{1,0:T(8,128)(2,1)S(1)} %pad_maximum_fusion.8), channel_id=1, source_target_pairs={{0,16},{1,17},{2,18},{3,19},{4,20},{5,21},{6,22},{7,23},{8,24},{9,... | collective-permute-start | bytes 417800 | tf_op jit(solution)/shard_map/ppermute | solution.py:79
  67.4 1.6 %collective-permute-done.18 = f16[136,512]{1,0:T(8,128)(2,1)S(1)} collective-permute-done((f16[136,512]{1,0:T(8,128)(2,1)S(1)}, f16[136,512]{1,0:T(8,128)(2,1)S(1)}, u32[]{:S(2)}, u32[]{:S(2)}) %collective-permute-start.18) | collective-permute-done | bytes 139296 | tf_op jit(solution)/shard_map/ppermute | solution.py:79
  71.4 3.0 %collective-permute-start.23 = (f16[136,512]{1,0:T(8,128)(2,1)S(1)}, f16[136,512]{1,0:T(8,128)(2,1)S(1)}, u32[]{:S(2)}, u32[]{:S(2)}) collective-permute-start(f16[136,512]{1,0:T(8,128)(2,1)S(1)} %get-tuple-element.39), channel_id=1, source_target_pairs={{0,4},{1,5},{2,6},{3,7},{4,0},{5,1},{6,2},{7,3},{8,12},{9,13},{10,... | collective-permute-start | bytes 417800 | tf_op jit(solution)/shard_map/ppermute | solution.py:79
  75.8 3.8 %shard_map.58 = (f32[512,512]{1,0:T(8,128)S(1)}, bf16[512,4096]{1,0:T(8,128)(2,1)}) custom-call(s32[1]{0:T(128)} %bitcast.place, bf16[512,4096]{1,0:T(8,128)(2,1)S(1)} %copy-done, bf16[512,512]{1,0:T(8,128)(2,1)S(1)} %copy-done.1, bf16[2,1024,512]{2,1,0:T(8,128)(2,1)S(1)} %bitcast.231), custom_call_target="tpu_custom_call" | custom-call | flops 2147483648 | bytes 7864320 | tf_op jit(solution)/shard_map/pallas_call | solution.py:45
  79.7 4.0 %shard_map.59 = (bf16[512,512]{1,0:T(8,128)(2,1)}, bf16[512,4096]{1,0:T(8,128)(2,1)}) custom-call(s32[1]{0:T(128)} %bitcast.place, bf16[512,4096]{1,0:T(8,128)(2,1)S(1)} %copy-done, bf16[512,512]{1,0:T(8,128)(2,1)S(1)} %copy-done.1, bf16[2,1024,512]{2,1,0:T(8,128)(2,1)S(1)} %bitcast.230, ...), custom_call_target="tpu_custom_call", output_to_operand_aliasing={{1}: (5, {})} | custom-call | flops 2147483648 | bytes 7864320 | tf_op jit(solution)/shard_map/pallas_call | solution.py:45
  (131 shorter events, 21.8 us)
Async XLA Ops:
  0.6 16.1 %collective-permute-start = (bf16[128,512]{1,0:T(8,128)(2,1)}, bf16[128,512]{1,0:T(8,128)(2,1)S(1)}, u32[]{:S(2)}, u32[]{:S(2)}) collective-permute-start(bf16[128,512]{1,0:T(8,128)(2,1)} %param.4), channel_id=1, source_target_pairs={{0,4},{1,5},{2,6},{3,7},{4,0},{5,1},{6,2},{7,3},{8,12},{9,13},{10,... | collective-permute-start | bytes 393224 | tf_op jit(solution)/shard_map/ppermute | solution.py:79
  4.7 12.0 %collective-permute-start.1 = (bf16[128,512]{1,0:T(8,128)(2,1)}, bf16[128,512]{1,0:T(8,128)(2,1)S(1)}, u32[]{:S(2)}, u32[]{:S(2)}) collective-permute-start(bf16[128,512]{1,0:T(8,128)(2,1)} %param.4), channel_id=1, source_target_pairs={{0,6},{1,7},{2,4},{3,5},{4,2},{5,3},{6,0},{7,1},{8,14},{9,15},{10,... | collective-permute-start | bytes 393224 | tf_op jit(solution)/shard_map/ppermute | solution.py:79
  6.1 12.3 %collective-permute-start.7 = (bf16[128,512]{1,0:T(8,128)(2,1)}, bf16[128,512]{1,0:T(8,128)(2,1)S(1)}, u32[]{:S(2)}, u32[]{:S(2)}) collective-permute-start(bf16[128,512]{1,0:T(8,128)(2,1)} %param.4), channel_id=1, source_target_pairs={{0,2},{1,3},{2,0},{3,1},{4,6},{5,7},{6,4},{7,5},{8,10},{9,11},{10,... | collective-permute-start | bytes 393224 | tf_op jit(solution)/shard_map/ppermute | solution.py:79
  16.1 25.4 %collective-permute-start.14 = (f16[1032,512]{1,0:T(8,128)(2,1)S(1)}, f16[1032,512]{1,0:T(8,128)(2,1)S(1)}, u32[]{:S(2)}, u32[]{:S(2)}) collective-permute-start(f16[1032,512]{1,0:T(8,128)(2,1)S(1)} %pad_maximum_fusion), channel_id=1, source_target_pairs={{0,8},{1,9},{2,10},{3,11},{4,12},{5,13},{6,14},{7,15},{8,0},{9,1},... | collective-permute-start | bytes 3170312 | tf_op jit(solution)/shard_map/ppermute | solution.py:79
  16.2 25.3 %collective-permute-start.13 = (f16[1024,512]{1,0:T(8,128)(2,1)}, f16[1024,512]{1,0:T(8,128)(2,1)}, u32[]{:S(2)}, u32[]{:S(2)}) collective-permute-start(f16[1024,512]{1,0:T(8,128)(2,1)} %get-tuple-element.69), channel_id=1, source_target_pairs={{0,8},{1,9},{2,10},{3,11},{4,12},{5,13},{6,14},{7,15},{8,0},{9,1},... | collective-permute-start | bytes 3145736 | tf_op jit(solution)/shard_map/ppermute | solution.py:79
  16.7 6.4 %collective-permute-start.4 = (bf16[2,64,512]{2,1,0:T(8,128)(2,1)S(1)}, bf16[2,64,512]{2,1,0:T(8,128)(2,1)S(1)}, u32[]{:S(2)}, u32[]{:S(2)}) collective-permute-start(bf16[2,64,512]{2,1,0:T(8,128)(2,1)S(1)} %get-tuple-element.36), channel_id=1, source_target_pairs={{0,16},{1,17},{2,18},{3,19},{4,20},{5,21},{6,22},{7,23},{8,24},{9,... | collective-permute-start | bytes 393224 | tf_op jit(solution)/shard_map/ppermute | solution.py:79
  18.5 6.6 %collective-permute-start.10 = (bf16[2,64,512]{2,1,0:T(8,128)(2,1)S(1)}, bf16[2,64,512]{2,1,0:T(8,128)(2,1)S(1)}, u32[]{:S(2)}, u32[]{:S(2)}) collective-permute-start(bf16[2,64,512]{2,1,0:T(8,128)(2,1)S(1)} %get-tuple-element.34), channel_id=1, source_target_pairs={{0,16},{1,17},{2,18},{3,19},{4,20},{5,21},{6,22},{7,23},{8,24},{9,... | collective-permute-start | bytes 393224 | tf_op jit(solution)/shard_map/ppermute | solution.py:79
  19.0 7.6 %collective-permute-start.8 = (bf16[2,64,512]{2,1,0:T(8,128)(2,1)S(1)}, bf16[2,64,512]{2,1,0:T(8,128)(2,1)S(1)}, u32[]{:S(2)}, u32[]{:S(2)}) collective-permute-start(bf16[2,64,512]{2,1,0:T(8,128)(2,1)S(1)} %get-tuple-element.33), channel_id=1, source_target_pairs={{0,1},{1,0},{2,3},{3,2},{4,5},{5,4},{6,7},{7,6},{8,9},{9,8},{10,11... | collective-permute-start | bytes 393224 | tf_op jit(solution)/shard_map/ppermute | solution.py:79
  23.2 6.2 %collective-permute-start.2 = (bf16[2,64,512]{2,1,0:T(8,128)(2,1)S(1)}, bf16[2,64,512]{2,1,0:T(8,128)(2,1)S(1)}, u32[]{:S(2)}, u32[]{:S(2)}) collective-permute-start(bf16[2,64,512]{2,1,0:T(8,128)(2,1)S(1)} %get-tuple-element.35), channel_id=1, source_target_pairs={{0,1},{1,0},{2,3},{3,2},{4,5},{5,4},{6,7},{7,6},{8,9},{9,8},{10,11... | collective-permute-start | bytes 393224 | tf_op jit(solution)/shard_map/ppermute | solution.py:79
  25.1 9.8 %collective-permute-start.5 = (bf16[2,2,64,512]{3,2,0,1:T(8,128)(2,1)S(1)}, bf16[2,2,64,512]{3,2,0,1:T(8,128)(2,1)S(1)}, u32[]{:S(2)}, u32[]{:S(2)}) collective-permute-start(bf16[2,2,64,512]{3,2,0,1:T(8,128)(2,1)S(1)} %bitcast_dynamic-update-slice_fusion.17), channel_id=1, source_target_pairs={{0,1},{1,0},{2,3},{3,2},{4,5},{5,4},{6,7},{7,6},{8,9},{9,8},{10,11... | collective-permute-start | bytes 786440 | tf_op jit(solution)/shard_map/ppermute | solution.py:79
  26.7 12.7 %collective-permute-start.11 = (bf16[2,2,64,512]{3,2,0,1:T(8,128)(2,1)S(1)}, bf16[2,2,64,512]{3,2,0,1:T(8,128)(2,1)S(1)}, u32[]{:S(2)}, u32[]{:S(2)}) collective-permute-start(bf16[2,2,64,512]{3,2,0,1:T(8,128)(2,1)S(1)} %bitcast_dynamic-update-slice_fusion.16), channel_id=1, source_target_pairs={{0,1},{1,0},{2,3},{3,2},{4,5},{5,4},{6,7},{7,6},{8,9},{9,8},{10,11... | collective-permute-start | bytes 786440 | tf_op jit(solution)/shard_map/ppermute | solution.py:79
  29.3 10.1 %collective-permute-start.9 = (bf16[2,2,64,512]{3,2,0,1:T(8,128)(2,1)S(1)}, bf16[2,2,64,512]{3,2,0,1:T(8,128)(2,1)S(1)}, u32[]{:S(2)}, u32[]{:S(2)}) collective-permute-start(bf16[2,2,64,512]{3,2,0,1:T(8,128)(2,1)S(1)} %bitcast_dynamic-update-slice_fusion.11), channel_id=1, source_target_pairs={{0,16},{1,17},{2,18},{3,19},{4,20},{5,21},{6,22},{7,23},{8,24},{9,... | collective-permute-start | bytes 786440 | tf_op jit(solution)/shard_map/ppermute | solution.py:79
  34.9 6.4 %collective-permute-start.3 = (bf16[2,2,64,512]{3,2,0,1:T(8,128)(2,1)S(1)}, bf16[2,2,64,512]{3,2,0,1:T(8,128)(2,1)S(1)}, u32[]{:S(2)}, u32[]{:S(2)}) collective-permute-start(bf16[2,2,64,512]{3,2,0,1:T(8,128)(2,1)S(1)} %bitcast_dynamic-update-slice_fusion.14), channel_id=1, source_target_pairs={{0,16},{1,17},{2,18},{3,19},{4,20},{5,21},{6,22},{7,23},{8,24},{9,... | collective-permute-start | bytes 786440 | tf_op jit(solution)/shard_map/ppermute | solution.py:79
  39.6 36.0 %collective-permute-start.12 = (bf16[2,2,2,2,64,512]{5,4,2,1,0,3:T(8,128)(2,1)S(1)}, bf16[2,2,2,2,64,512]{5,4,2,1,0,3:T(8,128)(2,1)S(1)}, u32[]{:S(2)}, u32[]{:S(2)}) collective-permute-start(bf16[2,2,2,2,64,512]{5,4,2,1,0,3:T(8,128)(2,1)S(1)} %get-tuple-element.29), channel_id=1, source_target_pairs={{0,8},{1,9},{2,10},{3,11},{4,12},{5,13},{6,14},{7,15},{8,0},{9,1},... | collective-permute-start | bytes 3145736 | tf_op jit(solution)/shard_map/ppermute | solution.py:79
  41.4 38.2 %collective-permute-start.6 = (bf16[2,2,2,2,64,512]{5,4,3,2,1,0:T(8,128)(2,1)S(1)}, bf16[2,2,2,2,64,512]{5,4,3,2,1,0:T(8,128)(2,1)S(1)}, u32[]{:S(2)}, u32[]{:S(2)}) collective-permute-start(bf16[2,2,2,2,64,512]{5,4,3,2,1,0:T(8,128)(2,1)S(1)} %pad_maximum_fusion.1), channel_id=1, source_target_pairs={{0,8},{1,9},{2,10},{3,11},{4,12},{5,13},{6,14},{7,15},{8,0},{9,1},... | collective-permute-start | bytes 3145736 | tf_op jit(solution)/shard_map/ppermute | solution.py:79
  46.1 9.4 %collective-permute-start.20 = (f16[264,512]{1,0:T(8,128)(2,1)S(1)}, f16[264,512]{1,0:T(8,128)(2,1)S(1)}, u32[]{:S(2)}, u32[]{:S(2)}) collective-permute-start(f16[264,512]{1,0:T(8,128)(2,1)S(1)} %get-tuple-element.42), channel_id=1, source_target_pairs={{0,16},{1,17},{2,18},{3,19},{4,20},{5,21},{6,22},{7,23},{8,24},{9,... | collective-permute-start | bytes 811016 | tf_op jit(solution)/shard_map/ppermute | solution.py:79
  47.7 12.5 %collective-permute-start.19 = (f16[256,512]{1,0:T(8,128)(2,1)S(1)}, f16[256,512]{1,0:T(8,128)(2,1)S(1)}, u32[]{:S(2)}, u32[]{:S(2)}) collective-permute-start(f16[256,512]{1,0:T(8,128)(2,1)S(1)} %get-tuple-element.57), channel_id=1, source_target_pairs={{0,16},{1,17},{2,18},{3,19},{4,20},{5,21},{6,22},{7,23},{8,24},{9,... | collective-permute-start | bytes 786440 | tf_op jit(solution)/shard_map/ppermute | solution.py:79
  48.6 12.1 %collective-permute-start.16 = (f16[264,512]{1,0:T(8,128)(2,1)S(1)}, f16[264,512]{1,0:T(8,128)(2,1)S(1)}, u32[]{:S(2)}, u32[]{:S(2)}) collective-permute-start(f16[264,512]{1,0:T(8,128)(2,1)S(1)} %get-tuple-element.43), channel_id=1, source_target_pairs={{0,1},{1,0},{2,3},{3,2},{4,5},{5,4},{6,7},{7,6},{8,9},{9,8},{10,11... | collective-permute-start | bytes 811016 | tf_op jit(solution)/shard_map/ppermute | solution.py:79
  55.5 6.9 %collective-permute-start.15 = (f16[256,512]{1,0:T(8,128)(2,1)S(1)}, f16[256,512]{1,0:T(8,128)(2,1)S(1)}, u32[]{:S(2)}, u32[]{:S(2)}) collective-permute-start(f16[256,512]{1,0:T(8,128)(2,1)S(1)} %get-tuple-element.58), channel_id=1, source_target_pairs={{0,1},{1,0},{2,3},{3,2},{4,5},{5,4},{6,7},{7,6},{8,9},{9,8},{10,11... | collective-permute-start | bytes 786440 | tf_op jit(solution)/shard_map/ppermute | solution.py:79
  62.9 6.1 %collective-permute-start.18 = (f16[136,512]{1,0:T(8,128)(2,1)S(1)}, f16[136,512]{1,0:T(8,128)(2,1)S(1)}, u32[]{:S(2)}, u32[]{:S(2)}) collective-permute-start(f16[136,512]{1,0:T(8,128)(2,1)S(1)} %pad_maximum_fusion.8), channel_id=1, source_target_pairs={{0,16},{1,17},{2,18},{3,19},{4,20},{5,21},{6,22},{7,23},{8,24},{9,... | collective-permute-start | bytes 417800 | tf_op jit(solution)/shard_map/ppermute | solution.py:79
  64.8 5.6 %collective-permute-start.17 = (f16[128,512]{1,0:T(8,128)(2,1)S(1)}, f16[128,512]{1,0:T(8,128)(2,1)S(1)}, u32[]{:S(2)}, u32[]{:S(2)}) collective-permute-start(f16[128,512]{1,0:T(8,128)(2,1)S(1)} %get-tuple-element.60), channel_id=1, source_target_pairs={{0,16},{1,17},{2,18},{3,19},{4,20},{5,21},{6,22},{7,23},{8,24},{9,... | collective-permute-start | bytes 393224 | tf_op jit(solution)/shard_map/ppermute | solution.py:79
  71.4 12.3 %collective-permute-start.23 = (f16[136,512]{1,0:T(8,128)(2,1)S(1)}, f16[136,512]{1,0:T(8,128)(2,1)S(1)}, u32[]{:S(2)}, u32[]{:S(2)}) collective-permute-start(f16[136,512]{1,0:T(8,128)(2,1)S(1)} %get-tuple-element.39), channel_id=1, source_target_pairs={{0,4},{1,5},{2,6},{3,7},{4,0},{5,1},{6,2},{7,3},{8,12},{9,13},{10,... | collective-permute-start | bytes 417800 | tf_op jit(solution)/shard_map/ppermute | solution.py:79
  74.4 9.4 %collective-permute-start.24 = (f16[136,512]{1,0:T(8,128)(2,1)S(1)}, f16[136,512]{1,0:T(8,128)(2,1)S(1)}, u32[]{:S(2)}, u32[]{:S(2)}) collective-permute-start(f16[136,512]{1,0:T(8,128)(2,1)S(1)} %get-tuple-element.40), channel_id=1, source_target_pairs={{0,6},{1,7},{2,4},{3,5},{4,2},{5,3},{6,0},{7,1},{8,14},{9,15},{10,... | collective-permute-start | bytes 417800 | tf_op jit(solution)/shard_map/ppermute | solution.py:79
  75.6 8.2 %collective-permute-start.25 = (f16[136,512]{1,0:T(8,128)(2,1)S(1)}, f16[136,512]{1,0:T(8,128)(2,1)S(1)}, u32[]{:S(2)}, u32[]{:S(2)}) collective-permute-start(f16[136,512]{1,0:T(8,128)(2,1)S(1)} %get-tuple-element.41), channel_id=1, source_target_pairs={{0,2},{1,3},{2,0},{3,1},{4,6},{5,7},{6,4},{7,5},{8,10},{9,11},{10,... | collective-permute-start | bytes 417800 | tf_op jit(solution)/shard_map/ppermute | solution.py:79
  (8 other events, 43.8 us)

commit v3 on v2

v3 whole, which is shorter than its diff:
```python
import functools

import jax
import jax.numpy as jnp
from jax import lax
from jax.experimental import pallas as pl
from jax.experimental.pallas import tpu as pltpu
from jax.sharding import PartitionSpec as P

AXES = ("wide", "node")
TOP = 14.0


def products_kernel(place, tok, cot, weight, *rest, first, last):
    keys_in, keys, grad, total = (None if first else rest[0]), *rest[-3:]
    step = pl.program_id(0)

    @pl.when(step == 0)
    def _():
        total[...] = jnp.zeros_like(total) if first else keys_in[...]

    total[...] += jnp.dot(tok[...], weight[0], preferred_element_type=jnp.float32)
    grad[...] = lax.dot_general(
        cot[...], weight[0], (((1,), (1,)), ((), ())), preferred_element_type=jnp.float32
    ).astype(grad.dtype)

    @pl.when(step == pl.num_programs(0) - 1)
    def _():
        keys[...] = total[...].astype(keys.dtype)


def products(tokens, cotangent, weight, z_me, start, before, last):
    steps, depth, kd = weight.shape
    rows = tokens.shape[0]
    whole = pl.BlockSpec((rows, kd), lambda i, z: (0, 0))
    columns = pl.BlockSpec((rows, depth), lambda i, z: (0, z[0] ^ (start + i)))
    in_specs = [columns, whole, pl.BlockSpec((1, depth, kd), lambda i, z: (i, 0, 0))]
    operands = [tokens, cotangent, weight]
    aliases = {}
    if before is not None:
        in_specs += [whole, pl.BlockSpec(memory_space=pl.ANY)]
        operands += list(before)
        aliases = {5: 1}
    return pl.pallas_call(
        functools.partial(products_kernel, first=before is None, last=last),
        grid_spec=pltpu.PrefetchScalarGridSpec(
            num_scalar_prefetch=1,
            grid=(steps,),
            in_specs=in_specs,
            out_specs=[whole, columns],
            scratch_shapes=[pltpu.VMEM((rows, kd), jnp.float32)],
        ),
        out_shape=[
            jax.ShapeDtypeStruct((rows, kd), jnp.bfloat16 if last else jnp.float32),
            jax.ShapeDtypeStruct(tokens.shape, jnp.bfloat16),
        ],
        input_output_aliases=aliases,
        compiler_params=pltpu.CompilerParams(vmem_limit_bytes=24 * 1024 * 1024),
        cost_estimate=pl.CostEstimate(
            flops=4 * rows * steps * depth * kd,
            bytes_accessed=2 * (2 * rows * steps * depth + steps * depth * kd + 3 * rows * kd),
            transcendentals=0,
        ),
    )(jnp.reshape(z_me, (1,)), *operands)


def on_device(tokens, key_weight, cotangent):
    wide, node = lax.axis_size("wide"), lax.axis_size("node")
    w_me, n_me = lax.axis_index("wide"), lax.axis_index("node")
    rows, kd = key_weight.shape
    half = rows // 2
    ny, nx, nz = wide // 2, 2, node // 2
    core, y_me = w_me & 1, w_me >> 1
    x_me, z_me = n_me & 1, n_me >> 1

    size = {"core": 2, "y": ny, "x": nx, "z": nz}
    place = {"core": core, "y": y_me, "x": x_me, "z": z_me}
    mask = {"core": node, "y": 2 * node, "x": 1, "z": 2}

    def swap(value, name, j):
        return lax.ppermute(value, AXES, [(i, i ^ (j * mask[name])) for i in range(wide * node)])

    def pick(value, *places):
        start, extent = [0] * value.ndim, list(value.shape)
        for axis, index, *more in places:
            start[axis], extent[axis] = index, (more[0] if more else 1)
        return lax.dynamic_slice(value, start, extent)

    together = lax.optimization_barrier

    def from_all(value, name):
        return [swap(value, name, j) for j in range(1, size[name])]

    def in_order(value, others, name):
        out = jnp.zeros((size[name],) + value.shape, value.dtype)
        for j, part in enumerate([value, *others]):
            out = lax.dynamic_update_index_in_dim(out, part, place[name] ^ j, 0)
        return out

    def top_of(power, name):
        bit = 1
        while bit < size[name]:
            power = jnp.maximum(power, swap(power, name, bit)) + 1.0
            bit *= 2
        return power

    def trade(value, name, axis, *places):
        me = place[name]
        own = pick(value, *places, (axis, me))
        return own, [
            swap(pick(value, *places, (axis, me ^ j)), name, j) for j in range(1, size[name])
        ]

    def added(own, others):
        return sum((other.astype(jnp.float32) for other in others), own.astype(jnp.float32))

    shards = [key_weight] + from_all(key_weight, "z")

    part = lax.dot_general(
        tokens, cotangent, (((0,), (0,)), ((), ())), preferred_element_type=jnp.float32
    )
    top = jnp.maximum(jnp.max(jnp.abs(part), axis=0, keepdims=True), 2.0**-100)
    power = jnp.broadcast_to(jnp.ceil(jnp.log2(top)), (8, kd))
    part = part.reshape(nz, nx, ny, 2, rows, kd)
    z_low = z_me % (nz // 2)
    z_top = z_me - z_low
    z_away = nz // 2 - z_top

    def row(power, factor=1.0):
        return factor * jnp.exp2(power[:1])

    def core_term(first_z, core):
        return pick(part, (0, first_z, nz // 2), (3, core))

    def packed(value):
        return (value * row(TOP - power)).astype(jnp.float16)

    power, shards[1] = together((power, shards[1]))
    power_core = swap(power, "core", 1)
    power_x = top_of(jnp.maximum(power, power_core) + 1.0, "x")
    power_x, shards[nz // 2 :] = together((power_x, shards[nz // 2 :]))
    power_xy = top_of(power_x, "y")
    power_z = top_of(power_xy, "z")

    def chip_sum(own, other):
        total = own + other.astype(jnp.float32) * row(power_core - TOP)
        return (total * row(TOP - power_xy)).astype(jnp.float16)

    upper, lower = (4, 0, half), (4, half, half)

    def near_halves(blocks):
        blocks = jnp.stack(blocks).reshape(-1, 2, half, kd)
        one, two = blocks[:, 0], blocks[:, 1]
        return (one, from_all(one, "x")), (two, from_all(two, "y"))

    def far_halves(one, two):
        one, two = in_order(*one, "x"), in_order(*two, "y")
        return (one, from_all(one, "y")), (two, from_all(two, "x"))

    def joined(one, two):
        one, two = in_order(*one, "y"), in_order(*two, "x")
        both = jnp.stack([one.transpose(2, 1, 0, 3, 4), two.transpose(2, 0, 1, 3, 4)], axis=3)
        return both, from_all(both, "core")

    def whole(both, other):
        weight = in_order(both, other, "core")
        return weight.transpose(1, 2, 3, 0, 4, 5, 6).reshape(-1, nx * ny * 2 * rows, kd)

    def first_sums(total):
        return trade(total, "x", 1, upper), trade(total, "y", 2, lower)

    def second_sums(one, two):
        one = added(*one).astype(jnp.float16)
        two = added(*two).astype(jnp.float16)
        return trade(one, "y", 2), trade(two, "x", 1)

    def last_sums(one, two):
        total = jnp.concatenate([added(*one), added(*two)], axis=4).reshape(-1, rows, kd)
        return (total * row(power_xy - power_z)).astype(jnp.float16)

    away_got = swap(packed(core_term(z_away, 1 - core)), "core", 1)
    near_1 = near_halves(shards[: nz // 2])
    near_2 = far_halves(*near_1)
    away_got, home_sent = together((away_got, packed(core_term(z_top, 1 - core))))
    home_got = swap(home_sent, "core", 1)
    away_total = chip_sum(core_term(z_away, core), away_got)
    away_total, far_shards = together((away_total, shards[nz // 2 :]))
    away_1 = first_sums(away_total)
    far_1 = near_halves(far_shards)
    near_3 = joined(*near_2)
    away_2 = second_sums(*away_1)
    away_2, far_1, home_got = together((away_2, far_1, home_got))
    far_2 = far_halves(*far_1)
    home_1 = first_sums(chip_sum(core_term(z_top, core), home_got))
    begun = products(tokens, cotangent, whole(*near_3), z_me, 0, None, False)
    away_2, begun = together((away_2, begun))
    away_3 = last_sums(*away_2)
    away_sent = [pick(away_3, (0, z_low ^ j)) for j in range(nz // 2)]
    home_1, away_sent = together((home_1, away_sent))
    far_got = [swap(sent, "z", nz // 2 + j) for j, sent in enumerate(away_sent)]
    home_2 = second_sums(*home_1)
    far_3, begun = together((joined(*far_2), begun))
    home_3 = last_sums(*home_2)
    near_got = [swap(pick(home_3, (0, z_low ^ j)), "z", j) for j in range(1, nz // 2)]
    keys, input_grad = products(tokens, cotangent, whole(*far_3), z_me, nz // 2, begun, True)
    total = added(pick(home_3, (0, z_low)), near_got + far_got)[0]
    total_tokens = tokens.shape[0] * wide * node
    weight_grad = total * row(power_z - TOP, 1.0 / jnp.sqrt(jnp.float32(total_tokens)))
    return (keys, input_grad, weight_grad)


def solution(mesh):
    placed = (P(AXES, None), P(("node", "wide"), None), P(AXES, None))
    return jax.shard_map(
        on_device,
        mesh=mesh,
        in_specs=placed,
        out_specs=(P(AXES, None), P(AXES, None), P(("node", "wide"), None)),
        check_vma=False,
    )
```

time: 84.8 us -> 98.8 us (1.17)
  waiting for transfers between devices: 25.8 us -> 36.3 us
  other arithmetic: 8.1 us -> 3.38 us
  starting transfers between devices: 31.2 us -> 35.4 us
  matrix products: 4.7 us -> 7.98 us
    ppermute x26 -> x31, waiting for transfers between devices: 25.8 us -> 36.3 us  [swap(): lax.ppermute(value, AXES, [(i, i ^ j * mask[name]) for i in range(wide *...]
    ppermute x26 -> x31, starting transfers between devices: 31.2 us -> 35.4 us  [swap(): lax.ppermute(value, AXES, [(i, i ^ j * mask[name]) for i in range(wide *...]
    dynamic_slice x9 -> x11, local copies, waits for them, and re-layouts: 0.91 us -> 5.05 us  [pick(): return lax.dynamic_slice(value, start, extent)]
    dot_general x1, matrix products: 4.7 us -> 7.98 us  [on_device(): lax.dot_general(tokens, cotangent, (((0,), (0,)), ((), ())), preferred_el...]
    unnamed x12 -> x6, local copies, waits for them, and re-layouts: 2.99 us -> 0.02 us
    mul x6 -> x2, other arithmetic: 3.14 us -> 0.8 us  [the longest x1 0.78 us: on_device(): total * row(power_z - TOP, 1.0 / jnp.sqrt(jnp.float32(total_tokens)))]
    add x8 -> x7, other arithmetic: 1.69 us -> 0.16 us  [the longest x3 0.14 us: added(): sum((other.astype(jnp.float32) for other in others), own.astype(jnp.float...]
    convert_element_type x8 -> x9, other arithmetic: 2.14 us -> 2.1 us  [the longest x2 0.97 us: chip_sum(): return (total * row(TOP - power_xy)).astype(jnp.float16)]
  transfers between devices with their start and end apart: 26 -> 31, of which waited for: 12 -> 17; matrix products, arithmetic and copies ran while one was open for 17% -> 17% of each run, Pallas kernels for 9% -> 4%
where the time goes in v3:
time: 98.8 us; the launch traced here: 98.6 us
  waiting for transfers between devices  36.3 us (37%)
  starting transfers between devices  35.4 us (36%)
  matrix products  7.98 us (8%)
  Pallas kernels  7.96 us (8%)
  local copies, waits for them, and re-layouts  6.45 us (7%)
  other arithmetic  3.38 us (3%)
  between operations  1.18 us (1%)
    ppermute x31, waiting for transfers between devices, swap(): lax.ppermute(value, AXES, [(i, i ^ j * mask[name]) for i in range(wide *...  36.3 us
    ppermute x31, starting transfers between devices, swap(): lax.ppermute(value, AXES, [(i, i ^ j * mask[name]) for i in range(wide *...  35.4 us
    dot_general x1, matrix products, on_device(): lax.dot_general(tokens, cotangent, (((0,), (0,)), ((), ())), preferred_el...  7.98 us
    pallas_call x2, Pallas kernels, products(): pl.pallas_call(functools.partial(products_kernel, first=before is None, l...  7.96 us
    dynamic_slice x11, local copies, waits for them, and re-layouts, pick(): return lax.dynamic_slice(value, start, extent)  5.05 us
  transfers between devices with their start and end apart: 31, of which 17 were waited for; matrix products, arithmetic and copies ran while one was open for 17% of the time, Pallas kernels for 4%

profile of v3, /device:TPU:0, one launch (start us, length us, event | category | flops | bytes accessed | tf_op | source)
XLA Modules:
  0.0 98.6 jit_solution(4986425452290472825)
XLA Ops:
  0.6 3.1 %collective-permute-start = (bf16[128,512]{1,0:T(8,128)(2,1)}, bf16[128,512]{1,0:T(8,128)(2,1)S(1)}, u32[]{:S(2)}, u32[]{:S(2)}) collective-permute-start(bf16[128,512]{1,0:T(8,128)(2,1)} %param.4), channel_id=1, source_target_pairs={{0,2},{1,3},{2,0},{3,1},{4,6},{5,7},{6,4},{7,5},{8,10},{9,11},{10,... | collective-permute-start | bytes 393224 | tf_op jit(solution)/shard_map/ppermute | solution.py:81
  3.7 2.6 %collective-permute-start.4 = (bf16[128,512]{1,0:T(8,128)(2,1)}, bf16[128,512]{1,0:T(8,128)(2,1)S(1)}, u32[]{:S(2)}, u32[]{:S(2)}) collective-permute-start(bf16[128,512]{1,0:T(8,128)(2,1)} %param.4), channel_id=1, source_target_pairs={{0,4},{1,5},{2,6},{3,7},{4,0},{5,1},{6,2},{7,3},{8,12},{9,13},{10,... | collective-permute-start | bytes 393224 | tf_op jit(solution)/shard_map/ppermute | solution.py:81
  6.3 8.0 %abs_reduce_fusion = (f32[512]{0:T(512)S(1)}, f32[4096,512]{1,0:T(8,128)}) fusion(bf16[512,4096]{1,0:T(8,128)(2,1)} %tok.3, bf16[512,512]{1,0:T(8,128)(2,1)} %cot.3), kind=kOutput, calls=%fused_computation | convolution fusion | flops 2151677440 | bytes 13109248 | tf_op jit(solution)/shard_map/dot_general | solution.py:119
  14.3 4.5 %constant_dynamic-slice_fusion.9 = (f32[2,2,2,1,128,512]{5,4,3,2,1,0:T(8,128)S(1)}, f32[2,2,2,1,128,512]{5,4,3,2,1,0:T(8,128)S(1)}, f32[2,2,2,1,128,512]{5,4,3,2,1,0:T(8,128)S(1)}, f32[2,2,2,1,128,512]{5,4,3,2,1,0:T(8,128)S(1)}) fusion(f32[4,2,2,2,128,512]{5,4,3,2,1,0:T(8,128)} %bitcast.135, s32[]{:T(128)S(6)} %select_n.84, s32[]{:T(128)S(6)} %select_n.82, ...), kind=kLoop, calls=%fused_computation.72 | loop fusion | bytes 16777232 | tf_op jit(solution)/shard_map/dynamic_slice | solution.py:87
  20.1 1.8 %collective-permute-start.3 = (f32[8,512]{1,0:T(8,128)S(1)}, f32[8,512]{1,0:T(8,128)S(1)}, u32[]{:S(2)}, u32[]{:S(2)}) collective-permute-start(f32[8,512]{1,0:T(8,128)S(1)} %maximum_add_fusion.3), channel_id=1, source_target_pairs={{0,1},{1,0},{2,3},{3,2},{4,5},{5,4},{6,7},{7,6},{8,9},{9,8},{10,11... | collective-permute-start | bytes 49160 | tf_op jit(solution)/shard_map/ppermute | solution.py:81
  23.9 1.7 %collective-permute-start.17 = (bf16[2,64,512]{2,1,0:T(8,128)(2,1)S(1)}, bf16[2,64,512]{2,1,0:T(8,128)(2,1)S(1)}, u32[]{:S(2)}, u32[]{:S(2)}) collective-permute-start(bf16[2,64,512]{2,1,0:T(8,128)(2,1)S(1)} %get-tuple-element.93), channel_id=1, source_target_pairs={{0,1},{1,0},{2,3},{3,2},{4,5},{5,4},{6,7},{7,6},{8,9},{9,8},{10,11... | collective-permute-start | bytes 393224 | tf_op jit(solution)/shard_map/ppermute | solution.py:81
  27.3 2.2 %collective-permute-done.6 = f32[8,512]{1,0:T(8,128)S(1)} collective-permute-done((f32[8,512]{1,0:T(8,128)S(1)}, f32[8,512]{1,0:T(8,128)S(1)}, u32[]{:S(2)}, u32[]{:S(2)}) %collective-permute-start.6) | collective-permute-done | bytes 16416 | tf_op jit(solution)/shard_map/ppermute | solution.py:81
  30.2 3.0 %collective-permute-done.24 = f32[8,512]{1,0:T(8,128)S(1)} collective-permute-done((f32[8,512]{1,0:T(8,128)S(1)}, f32[8,512]{1,0:T(8,128)S(1)}, u32[]{:S(2)}, u32[]{:S(2)}) %collective-permute-start.24) | collective-permute-done | bytes 16416 | tf_op jit(solution)/shard_map/ppermute | solution.py:81
  33.2 2.2 %collective-permute-start.25 = (f32[8,512]{1,0:T(8,128)S(1)}, f32[8,512]{1,0:T(8,128)S(1)}, u32[]{:S(2)}, u32[]{:S(2)}) collective-permute-start(f32[8,512]{1,0:T(8,128)S(1)} %maximum_add_fusion), channel_id=1, source_target_pairs={{0,4},{1,5},{2,6},{3,7},{4,0},{5,1},{6,2},{7,3},{8,12},{9,13},{10,... | collective-permute-start | bytes 49160 | tf_op jit(solution)/shard_map/ppermute | solution.py:81
  35.4 2.4 %collective-permute-done.25 = f32[8,512]{1,0:T(8,128)S(1)} collective-permute-done((f32[8,512]{1,0:T(8,128)S(1)}, f32[8,512]{1,0:T(8,128)S(1)}, u32[]{:S(2)}, u32[]{:S(2)}) %collective-permute-start.25) | collective-permute-done | bytes 16416 | tf_op jit(solution)/shard_map/ppermute | solution.py:81
  38.4 1.8 %collective-permute-start.18 = (bf16[2,2,64,512]{3,2,0,1:T(8,128)(2,1)S(1)}, bf16[2,2,64,512]{3,2,0,1:T(8,128)(2,1)S(1)}, u32[]{:S(2)}, u32[]{:S(2)}) collective-permute-start(bf16[2,2,64,512]{3,2,0,1:T(8,128)(2,1)S(1)} %bitcast_dynamic-update-slice_fusion.11), channel_id=1, source_target_pairs={{0,16},{1,17},{2,18},{3,19},{4,20},{5,21},{6,22},{7,23},{8,24},{9,... | collective-permute-start | bytes 786440 | tf_op jit(solution)/shard_map/ppermute | solution.py:81
  40.3 4.1 %collective-permute-done.20 = bf16[2,2,64,512]{3,2,0,1:T(8,128)(2,1)S(1)} collective-permute-done((bf16[2,2,64,512]{3,2,0,1:T(8,128)(2,1)S(1)}, bf16[2,2,64,512]{3,2,0,1:T(8,128)(2,1)S(1)}, u32[]{:S(2)}, u32[]{:S(2)}) %collective-permute-start.20) | collective-permute-done | bytes 262176 | tf_op jit(solution)/shard_map/ppermute | solution.py:81
  45.7 1.8 %collective-permute-start.7 = (f16[2,1,2,1,64,512]{5,4,0,3,2,1:T(8,128)(2,1)S(1)}, f16[2,1,2,1,64,512]{5,4,0,3,2,1:T(8,128)(2,1)S(1)}, u32[]{:S(2)}, u32[]{:S(2)}) collective-permute-start(f16[2,1,2,1,64,512]{5,4,0,3,2,1:T(8,128)(2,1)S(1)} %constant_dynamic-slice_fusion.15), channel_id=1, source_target_pairs={{0,1},{1,0},{2,3},{3,2},{4,5},{5,4},{6,7},{7,6},{8,9},{9,8},{10,11... | collective-permute-start | bytes 786440 | tf_op jit(solution)/shard_map/ppermute | solution.py:81
  47.9 1.6 %collective-permute-start.9 = (f16[2,2,1,1,64,512]{5,4,0,3,2,1:T(8,128)(2,1)S(1)}, f16[2,2,1,1,64,512]{5,4,0,3,2,1:T(8,128)(2,1)S(1)}, u32[]{:S(2)}, u32[]{:S(2)}) collective-permute-start(f16[2,2,1,1,64,512]{5,4,0,3,2,1:T(8,128)(2,1)S(1)} %constant_dynamic-slice_fusion.12), channel_id=1, source_target_pairs={{0,16},{1,17},{2,18},{3,19},{4,20},{5,21},{6,22},{7,23},{8,24},{9,... | collective-permute-start | bytes 786440 | tf_op jit(solution)/shard_map/ppermute | solution.py:81
  50.4 4.5 %collective-permute-done.7 = f16[2,1,2,1,64,512]{5,4,0,3,2,1:T(8,128)(2,1)S(1)} collective-permute-done((f16[2,1,2,1,64,512]{5,4,0,3,2,1:T(8,128)(2,1)S(1)}, f16[2,1,2,1,64,512]{5,4,0,3,2,1:T(8,128)(2,1)S(1)}, u32[]{:S(2)}, u32[]{:S(2)}) %collective-permute-start.7) | collective-permute-done | bytes 262176 | tf_op jit(solution)/shard_map/ppermute | solution.py:81
  55.0 2.1 %collective-permute-done.9 = f16[2,2,1,1,64,512]{5,4,0,3,2,1:T(8,128)(2,1)S(1)} collective-permute-done((f16[2,2,1,1,64,512]{5,4,0,3,2,1:T(8,128)(2,1)S(1)}, f16[2,2,1,1,64,512]{5,4,0,3,2,1:T(8,128)(2,1)S(1)}, u32[]{:S(2)}, u32[]{:S(2)}) %collective-permute-start.9) | collective-permute-done | bytes 262176 | tf_op jit(solution)/shard_map/ppermute | solution.py:81
  59.5 4.0 %shard_map.58 = (f32[512,512]{1,0:T(8,128)S(1)}, bf16[512,4096]{1,0:T(8,128)(2,1)}) custom-call(s32[1]{0:T(128)} %bitcast.place, bf16[512,4096]{1,0:T(8,128)(2,1)S(1)} %copy-done, bf16[512,512]{1,0:T(8,128)(2,1)S(1)} %copy-done.1, bf16[2,1024,512]{2,1,0:T(8,128)(2,1)S(1)} %bitcast.134), custom_call_target="tpu_custom_call" | custom-call | flops 2147483648 | bytes 7864320 | tf_op jit(solution)/shard_map/pallas_call | solution.py:44
  69.3 4.6 %collective-permute-done.15 = bf16[2,2,64,512]{3,2,0,1:T(8,128)(2,1)S(1)} collective-permute-done((bf16[2,2,64,512]{3,2,0,1:T(8,128)(2,1)S(1)}, bf16[2,2,64,512]{3,2,0,1:T(8,128)(2,1)S(1)}, u32[]{:S(2)}, u32[]{:S(2)}) %collective-permute-start.15) | collective-permute-done | bytes 262176 | tf_op jit(solution)/shard_map/ppermute | solution.py:81
  75.2 2.2 %collective-permute-done.22 = f16[2,1,2,1,64,512]{5,4,0,3,2,1:T(8,128)(2,1)S(1)} collective-permute-done((f16[2,1,2,1,64,512]{5,4,0,3,2,1:T(8,128)(2,1)S(1)}, f16[2,1,2,1,64,512]{5,4,0,3,2,1:T(8,128)(2,1)S(1)}, u32[]{:S(2)}, u32[]{:S(2)}) %collective-permute-start.22) | collective-permute-done | bytes 262176 | tf_op jit(solution)/shard_map/ppermute | solution.py:81
  77.8 3.6 %collective-permute-start.30 = (f16[1,128,512]{2,1,0:T(8,128)(2,1)S(1)}, f16[1,128,512]{2,1,0:T(8,128)(2,1)S(1)}, u32[]{:S(2)}, u32[]{:S(2)}) collective-permute-start(f16[1,128,512]{2,1,0:T(8,128)(2,1)S(1)} %get-tuple-element.80), channel_id=1, source_target_pairs={{0,6},{1,7},{2,4},{3,5},{4,2},{5,3},{6,0},{7,1},{8,14},{9,15},{10,... | collective-permute-start | bytes 393224 | tf_op jit(solution)/shard_map/ppermute | solution.py:81
  83.9 2.7 %collective-permute-done.27 = f16[2,1,1,1,64,512]{5,4,0,3,2,1:T(8,128)(2,1)S(1)} collective-permute-done((f16[2,1,1,1,64,512]{5,4,0,3,2,1:T(8,128)(2,1)S(1)}, f16[2,1,1,1,64,512]{5,4,0,3,2,1:T(8,128)(2,1)S(1)}, u32[]{:S(2)}, u32[]{:S(2)}) %collective-permute-start.27) | collective-permute-done | bytes 131104 | tf_op jit(solution)/shard_map/ppermute | solution.py:81
  86.6 1.6 %collective-permute-done.26 = f16[2,1,1,1,64,512]{5,4,0,3,2,1:T(8,128)(2,1)S(1)} collective-permute-done((f16[2,1,1,1,64,512]{5,4,0,3,2,1:T(8,128)(2,1)S(1)}, f16[2,1,1,1,64,512]{5,4,0,3,2,1:T(8,128)(2,1)S(1)}, u32[]{:S(2)}, u32[]{:S(2)}) %collective-permute-start.26) | collective-permute-done | bytes 131104 | tf_op jit(solution)/shard_map/ppermute | solution.py:81
  90.3 3.1 %collective-permute-done.28 = f16[1,128,512]{2,1,0:T(8,128)(2,1)S(1)} collective-permute-done((f16[1,128,512]{2,1,0:T(8,128)(2,1)S(1)}, f16[1,128,512]{2,1,0:T(8,128)(2,1)S(1)}, u32[]{:S(2)}, u32[]{:S(2)}) %collective-permute-start.28) | collective-permute-done | bytes 131104 | tf_op jit(solution)/shard_map/ppermute | solution.py:81
  94.7 4.0 %shard_map.59 = (bf16[512,512]{1,0:T(8,128)(2,1)}, bf16[512,4096]{1,0:T(8,128)(2,1)}) custom-call(s32[1]{0:T(128)} %bitcast.place, bf16[512,4096]{1,0:T(8,128)(2,1)S(1)} %copy-done, bf16[512,512]{1,0:T(8,128)(2,1)S(1)} %copy-done.1, bf16[2,1024,512]{2,1,0:T(8,128)(2,1)S(1)} %bitcast.133, ...), custom_call_target="tpu_custom_call", output_to_operand_aliasing={{1}: (5, {})} | custom-call | flops 2147483648 | bytes 7864320 | tf_op jit(solution)/shard_map/pallas_call | solution.py:44
  (115 shorter events, 24.5 us)
Async XLA Ops:
  0.6 18.1 %collective-permute-start = (bf16[128,512]{1,0:T(8,128)(2,1)}, bf16[128,512]{1,0:T(8,128)(2,1)S(1)}, u32[]{:S(2)}, u32[]{:S(2)}) collective-permute-start(bf16[128,512]{1,0:T(8,128)(2,1)} %param.4), channel_id=1, source_target_pairs={{0,2},{1,3},{2,0},{3,1},{4,6},{5,7},{6,4},{7,5},{8,10},{9,11},{10,... | collective-permute-start | bytes 393224 | tf_op jit(solution)/shard_map/ppermute | solution.py:81
  3.7 21.9 %collective-permute-start.4 = (bf16[128,512]{1,0:T(8,128)(2,1)}, bf16[128,512]{1,0:T(8,128)(2,1)S(1)}, u32[]{:S(2)}, u32[]{:S(2)}) collective-permute-start(bf16[128,512]{1,0:T(8,128)(2,1)} %param.4), channel_id=1, source_target_pairs={{0,4},{1,5},{2,6},{3,7},{4,0},{5,1},{6,2},{7,3},{8,12},{9,13},{10,... | collective-permute-start | bytes 393224 | tf_op jit(solution)/shard_map/ppermute | solution.py:81
  6.3 19.3 %collective-permute-start.5 = (bf16[128,512]{1,0:T(8,128)(2,1)}, bf16[128,512]{1,0:T(8,128)(2,1)S(1)}, u32[]{:S(2)}, u32[]{:S(2)}) collective-permute-start(bf16[128,512]{1,0:T(8,128)(2,1)} %param.4), channel_id=1, source_target_pairs={{0,6},{1,7},{2,4},{3,5},{4,2},{5,3},{6,0},{7,1},{8,14},{9,15},{10,... | collective-permute-start | bytes 393224 | tf_op jit(solution)/shard_map/ppermute | solution.py:81
  19.6 25.5 %collective-permute-start.1 = (f16[2,2,2,1,128,512]{5,4,0,3,2,1:T(8,128)(2,1)S(1)}, f16[2,2,2,1,128,512]{5,4,0,3,2,1:T(8,128)(2,1)S(1)}, u32[]{:S(2)}, u32[]{:S(2)}) collective-permute-start(f16[2,2,2,1,128,512]{5,4,0,3,2,1:T(8,128)(2,1)S(1)} %get-tuple-element.105), channel_id=1, source_target_pairs={{0,8},{1,9},{2,10},{3,11},{4,12},{5,13},{6,14},{7,15},{8,0},{9,1},... | collective-permute-start | bytes 3145736 | tf_op jit(solution)/shard_map/ppermute | solution.py:81
  21.9 16.0 %collective-permute-start.19 = (bf16[2,64,512]{2,1,0:T(8,128)(2,1)S(1)}, bf16[2,64,512]{2,1,0:T(8,128)(2,1)S(1)}, u32[]{:S(2)}, u32[]{:S(2)}) collective-permute-start(bf16[2,64,512]{2,1,0:T(8,128)(2,1)S(1)} %get-tuple-element.94), channel_id=1, source_target_pairs={{0,16},{1,17},{2,18},{3,19},{4,20},{5,21},{6,22},{7,23},{8,24},{9,... | collective-permute-start | bytes 393224 | tf_op jit(solution)/shard_map/ppermute | solution.py:81
  23.9 14.5 %collective-permute-start.17 = (bf16[2,64,512]{2,1,0:T(8,128)(2,1)S(1)}, bf16[2,64,512]{2,1,0:T(8,128)(2,1)S(1)}, u32[]{:S(2)}, u32[]{:S(2)}) collective-permute-start(bf16[2,64,512]{2,1,0:T(8,128)(2,1)S(1)} %get-tuple-element.93), channel_id=1, source_target_pairs={{0,1},{1,0},{2,3},{3,2},{4,5},{5,4},{6,7},{7,6},{8,9},{9,8},{10,11... | collective-permute-start | bytes 393224 | tf_op jit(solution)/shard_map/ppermute | solution.py:81
  37.9 6.4 %collective-permute-start.20 = (bf16[2,2,64,512]{3,2,0,1:T(8,128)(2,1)S(1)}, bf16[2,2,64,512]{3,2,0,1:T(8,128)(2,1)S(1)}, u32[]{:S(2)}, u32[]{:S(2)}) collective-permute-start(bf16[2,2,64,512]{3,2,0,1:T(8,128)(2,1)S(1)} %bitcast_dynamic-update-slice_fusion.16), channel_id=1, source_target_pairs={{0,1},{1,0},{2,3},{3,2},{4,5},{5,4},{6,7},{7,6},{8,9},{9,8},{10,11... | collective-permute-start | bytes 786440 | tf_op jit(solution)/shard_map/ppermute | solution.py:81
  38.4 6.4 %collective-permute-start.18 = (bf16[2,2,64,512]{3,2,0,1:T(8,128)(2,1)S(1)}, bf16[2,2,64,512]{3,2,0,1:T(8,128)(2,1)S(1)}, u32[]{:S(2)}, u32[]{:S(2)}) collective-permute-start(bf16[2,2,64,512]{3,2,0,1:T(8,128)(2,1)S(1)} %bitcast_dynamic-update-slice_fusion.11), channel_id=1, source_target_pairs={{0,16},{1,17},{2,18},{3,19},{4,20},{5,21},{6,22},{7,23},{8,24},{9,... | collective-permute-start | bytes 786440 | tf_op jit(solution)/shard_map/ppermute | solution.py:81
  45.0 13.7 %collective-permute-start.21 = (bf16[2,2,2,2,64,512]{5,4,2,1,0,3:T(8,128)(2,1)S(1)}, bf16[2,2,2,2,64,512]{5,4,2,1,0,3:T(8,128)(2,1)S(1)}, u32[]{:S(2)}, u32[]{:S(2)}) collective-permute-start(bf16[2,2,2,2,64,512]{5,4,2,1,0,3:T(8,128)(2,1)S(1)} %get-tuple-element.89), channel_id=1, source_target_pairs={{0,8},{1,9},{2,10},{3,11},{4,12},{5,13},{6,14},{7,15},{8,0},{9,1},... | collective-permute-start | bytes 3145736 | tf_op jit(solution)/shard_map/ppermute | solution.py:81
  45.7 9.2 %collective-permute-start.7 = (f16[2,1,2,1,64,512]{5,4,0,3,2,1:T(8,128)(2,1)S(1)}, f16[2,1,2,1,64,512]{5,4,0,3,2,1:T(8,128)(2,1)S(1)}, u32[]{:S(2)}, u32[]{:S(2)}) collective-permute-start(f16[2,1,2,1,64,512]{5,4,0,3,2,1:T(8,128)(2,1)S(1)} %constant_dynamic-slice_fusion.15), channel_id=1, source_target_pairs={{0,1},{1,0},{2,3},{3,2},{4,5},{5,4},{6,7},{7,6},{8,9},{9,8},{10,11... | collective-permute-start | bytes 786440 | tf_op jit(solution)/shard_map/ppermute | solution.py:81
  47.9 9.2 %collective-permute-start.9 = (f16[2,2,1,1,64,512]{5,4,0,3,2,1:T(8,128)(2,1)S(1)}, f16[2,2,1,1,64,512]{5,4,0,3,2,1:T(8,128)(2,1)S(1)}, u32[]{:S(2)}, u32[]{:S(2)}) collective-permute-start(f16[2,2,1,1,64,512]{5,4,0,3,2,1:T(8,128)(2,1)S(1)} %constant_dynamic-slice_fusion.12), channel_id=1, source_target_pairs={{0,16},{1,17},{2,18},{3,19},{4,20},{5,21},{6,22},{7,23},{8,24},{9,... | collective-permute-start | bytes 786440 | tf_op jit(solution)/shard_map/ppermute | solution.py:81
  49.5 14.0 %collective-permute-start.11 = (bf16[2,64,512]{2,1,0:T(8,128)(2,1)S(1)}, bf16[2,64,512]{2,1,0:T(8,128)(2,1)S(1)}, u32[]{:S(2)}, u32[]{:S(2)}) collective-permute-start(bf16[2,64,512]{2,1,0:T(8,128)(2,1)S(1)} %get-tuple-element.51), channel_id=1, source_target_pairs={{0,1},{1,0},{2,3},{3,2},{4,5},{5,4},{6,7},{7,6},{8,9},{9,8},{10,11... | collective-permute-start | bytes 393224 | tf_op jit(solution)/shard_map/ppermute | solution.py:81
  50.1 13.4 %collective-permute-start.12 = (bf16[2,64,512]{2,1,0:T(8,128)(2,1)S(1)}, bf16[2,64,512]{2,1,0:T(8,128)(2,1)S(1)}, u32[]{:S(2)}, u32[]{:S(2)}) collective-permute-start(bf16[2,64,512]{2,1,0:T(8,128)(2,1)S(1)} %get-tuple-element.53), channel_id=1, source_target_pairs={{0,16},{1,17},{2,18},{3,19},{4,20},{5,21},{6,22},{7,23},{8,24},{9,... | collective-permute-start | bytes 393224 | tf_op jit(solution)/shard_map/ppermute | solution.py:81
  54.8 9.0 %collective-permute-start.13 = (f16[2,2,2,1,128,512]{5,4,0,3,2,1:T(8,128)(2,1)S(1)}, f16[2,2,2,1,128,512]{5,4,0,3,2,1:T(8,128)(2,1)S(1)}, u32[]{:S(2)}, u32[]{:S(2)}) collective-permute-start(f16[2,2,2,1,128,512]{5,4,0,3,2,1:T(8,128)(2,1)S(1)} %get-tuple-element.50), channel_id=1, source_target_pairs={{0,8},{1,9},{2,10},{3,11},{4,12},{5,13},{6,14},{7,15},{8,0},{9,1},... | collective-permute-start | bytes 3145736 | tf_op jit(solution)/shard_map/ppermute | solution.py:81
  57.1 6.4 %collective-permute-start.8 = (f16[2,1,1,1,64,512]{5,4,0,3,2,1:T(8,128)(2,1)S(1)}, f16[2,1,1,1,64,512]{5,4,0,3,2,1:T(8,128)(2,1)S(1)}, u32[]{:S(2)}, u32[]{:S(2)}) collective-permute-start(f16[2,1,1,1,64,512]{5,4,0,3,2,1:T(8,128)(2,1)S(1)} %get-tuple-element.99), channel_id=1, source_target_pairs={{0,16},{1,17},{2,18},{3,19},{4,20},{5,21},{6,22},{7,23},{8,24},{9,... | collective-permute-start | bytes 393224 | tf_op jit(solution)/shard_map/ppermute | solution.py:81
  58.8 5.0 %collective-permute-start.10 = (f16[2,1,1,1,64,512]{5,4,0,3,2,1:T(8,128)(2,1)S(1)}, f16[2,1,1,1,64,512]{5,4,0,3,2,1:T(8,128)(2,1)S(1)}, u32[]{:S(2)}, u32[]{:S(2)}) collective-permute-start(f16[2,1,1,1,64,512]{5,4,0,3,2,1:T(8,128)(2,1)S(1)} %get-tuple-element.97), channel_id=1, source_target_pairs={{0,1},{1,0},{2,3},{3,2},{4,5},{5,4},{6,7},{7,6},{8,9},{9,8},{10,11... | collective-permute-start | bytes 393224 | tf_op jit(solution)/shard_map/ppermute | solution.py:81
  64.6 9.3 %collective-permute-start.15 = (bf16[2,2,64,512]{3,2,0,1:T(8,128)(2,1)S(1)}, bf16[2,2,64,512]{3,2,0,1:T(8,128)(2,1)S(1)}, u32[]{:S(2)}, u32[]{:S(2)}) collective-permute-start(bf16[2,2,64,512]{3,2,0,1:T(8,128)(2,1)S(1)} %bitcast_dynamic-update-slice_fusion.17), channel_id=1, source_target_pairs={{0,1},{1,0},{2,3},{3,2},{4,5},{5,4},{6,7},{7,6},{8,9},{9,8},{10,11... | collective-permute-start | bytes 786440 | tf_op jit(solution)/shard_map/ppermute | solution.py:81
  66.0 9.0 %collective-permute-start.14 = (bf16[2,2,64,512]{3,2,0,1:T(8,128)(2,1)S(1)}, bf16[2,2,64,512]{3,2,0,1:T(8,128)(2,1)S(1)}, u32[]{:S(2)}, u32[]{:S(2)}) collective-permute-start(bf16[2,2,64,512]{3,2,0,1:T(8,128)(2,1)S(1)} %bitcast_dynamic-update-slice_fusion.14), channel_id=1, source_target_pairs={{0,16},{1,17},{2,18},{3,19},{4,20},{5,21},{6,22},{7,23},{8,24},{9,... | collective-permute-start | bytes 786440 | tf_op jit(solution)/shard_map/ppermute | solution.py:81
  66.7 10.7 %collective-permute-start.22 = (f16[2,1,2,1,64,512]{5,4,0,3,2,1:T(8,128)(2,1)S(1)}, f16[2,1,2,1,64,512]{5,4,0,3,2,1:T(8,128)(2,1)S(1)}, u32[]{:S(2)}, u32[]{:S(2)}) collective-permute-start(f16[2,1,2,1,64,512]{5,4,0,3,2,1:T(8,128)(2,1)S(1)} %get-tuple-element.87), channel_id=1, source_target_pairs={{0,1},{1,0},{2,3},{3,2},{4,5},{5,4},{6,7},{7,6},{8,9},{9,8},{10,11... | collective-permute-start | bytes 786440 | tf_op jit(solution)/shard_map/ppermute | solution.py:81
  67.6 10.3 %collective-permute-start.23 = (f16[2,2,1,1,64,512]{5,4,0,3,2,1:T(8,128)(2,1)S(1)}, f16[2,2,1,1,64,512]{5,4,0,3,2,1:T(8,128)(2,1)S(1)}, u32[]{:S(2)}, u32[]{:S(2)}) collective-permute-start(f16[2,2,1,1,64,512]{5,4,0,3,2,1:T(8,128)(2,1)S(1)} %get-tuple-element.85), channel_id=1, source_target_pairs={{0,16},{1,17},{2,18},{3,19},{4,20},{5,21},{6,22},{7,23},{8,24},{9,... | collective-permute-start | bytes 786440 | tf_op jit(solution)/shard_map/ppermute | solution.py:81
  75.1 19.1 %collective-permute-start.16 = (bf16[2,2,2,2,64,512]{5,4,3,2,1,0:T(8,128)(2,1)S(1)}, bf16[2,2,2,2,64,512]{5,4,3,2,1,0:T(8,128)(2,1)S(1)}, u32[]{:S(2)}, u32[]{:S(2)}) collective-permute-start(bf16[2,2,2,2,64,512]{5,4,3,2,1,0:T(8,128)(2,1)S(1)} %pad_maximum_fusion), channel_id=1, source_target_pairs={{0,8},{1,9},{2,10},{3,11},{4,12},{5,13},{6,14},{7,15},{8,0},{9,1},... | collective-permute-start | bytes 3145736 | tf_op jit(solution)/shard_map/ppermute | solution.py:81
  77.8 11.4 %collective-permute-start.30 = (f16[1,128,512]{2,1,0:T(8,128)(2,1)S(1)}, f16[1,128,512]{2,1,0:T(8,128)(2,1)S(1)}, u32[]{:S(2)}, u32[]{:S(2)}) collective-permute-start(f16[1,128,512]{2,1,0:T(8,128)(2,1)S(1)} %get-tuple-element.80), channel_id=1, source_target_pairs={{0,6},{1,7},{2,4},{3,5},{4,2},{5,3},{6,0},{7,1},{8,14},{9,15},{10,... | collective-permute-start | bytes 393224 | tf_op jit(solution)/shard_map/ppermute | solution.py:81
  81.4 8.9 %collective-permute-start.29 = (f16[1,128,512]{2,1,0:T(8,128)(2,1)S(1)}, f16[1,128,512]{2,1,0:T(8,128)(2,1)S(1)}, u32[]{:S(2)}, u32[]{:S(2)}) collective-permute-start(f16[1,128,512]{2,1,0:T(8,128)(2,1)S(1)} %get-tuple-element.79), channel_id=1, source_target_pairs={{0,4},{1,5},{2,6},{3,7},{4,0},{5,1},{6,2},{7,3},{8,12},{9,13},{10,... | collective-permute-start | bytes 393224 | tf_op jit(solution)/shard_map/ppermute | solution.py:81
  81.6 5.0 %collective-permute-start.27 = (f16[2,1,1,1,64,512]{5,4,0,3,2,1:T(8,128)(2,1)S(1)}, f16[2,1,1,1,64,512]{5,4,0,3,2,1:T(8,128)(2,1)S(1)}, u32[]{:S(2)}, u32[]{:S(2)}) collective-permute-start(f16[2,1,1,1,64,512]{5,4,0,3,2,1:T(8,128)(2,1)S(1)} %constant_dynamic-slice_fusion.1), channel_id=1, source_target_pairs={{0,1},{1,0},{2,3},{3,2},{4,5},{5,4},{6,7},{7,6},{8,9},{9,8},{10,11... | collective-permute-start | bytes 393224 | tf_op jit(solution)/shard_map/ppermute | solution.py:81
  (10 other events, 39.6 us)

commit v4 on v0

v4 whole, which is shorter than its diff:
```python
import jax
import jax.numpy as jnp
from jax import lax
from jax.experimental import pallas as pl
from jax.experimental.pallas import tpu as pltpu
from jax.sharding import PartitionSpec as P

AXES = ("wide", "node")
TOP = 14.0
NOTE = 8


def products_kernel(tok, cot, weight, keys, grad, total):
    step = pl.program_id(0)

    @pl.when(step == 0)
    def _():
        total[...] = jnp.zeros_like(total)

    total[...] += jnp.dot(tok[...], weight[0], preferred_element_type=jnp.float32)
    grad[...] = lax.dot_general(
        cot[...], weight[0], (((1,), (1,)), ((), ())), preferred_element_type=jnp.float32
    ).astype(grad.dtype)

    @pl.when(step == pl.num_programs(0) - 1)
    def _():
        keys[...] = total[...].astype(keys.dtype)


def products(tokens, cotangent, weight):
    steps, depth, kd = weight.shape
    rows = tokens.shape[0]
    whole = pl.BlockSpec((rows, kd), lambda i: (0, 0))
    columns = pl.BlockSpec((rows, depth), lambda i: (0, i))
    return pl.pallas_call(
        products_kernel,
        grid=(steps,),
        in_specs=[columns, whole, pl.BlockSpec((1, depth, kd), lambda i: (i, 0, 0))],
        out_specs=[whole, columns],
        scratch_shapes=[pltpu.VMEM((rows, kd), jnp.float32)],
        out_shape=[
            jax.ShapeDtypeStruct((rows, kd), jnp.bfloat16),
            jax.ShapeDtypeStruct(tokens.shape, jnp.bfloat16),
        ],
        compiler_params=pltpu.CompilerParams(vmem_limit_bytes=24 * 1024 * 1024),
        cost_estimate=pl.CostEstimate(
            flops=4 * rows * steps * depth * kd,
            bytes_accessed=2 * (2 * rows * steps * depth + steps * depth * kd + 3 * rows * kd),
            transcendentals=0,
        ),
    )(tokens, cotangent, weight)


def on_device(tokens, key_weight, cotangent):
    wide, node = lax.axis_size("wide"), lax.axis_size("node")
    w_me, n_me = lax.axis_index("wide"), lax.axis_index("node")
    rows, kd = key_weight.shape
    half = rows // 2
    ny, nx, nz = wide // 2, 2, node // 2
    core, y_me = w_me & 1, w_me >> 1
    x_me, z_me = n_me & 1, n_me >> 1

    size = {"core": 2, "y": ny, "x": nx, "z": nz}
    place = {"core": core, "y": y_me, "x": x_me, "z": z_me}
    mask = {"core": node, "y": 2 * node, "x": 1, "z": 2}

    def swap(value, name, j):
        return lax.ppermute(value, AXES, [(i, i ^ (j * mask[name])) for i in range(wide * node)])

    def pick(value, *places):
        start, extent = [0] * value.ndim, list(value.shape)
        for axis, index, *more in places:
            start[axis], extent[axis] = index, (more[0] if more else 1)
        return lax.dynamic_slice(value, start, extent)

    def in_order(value, others, name):
        out = jnp.zeros((size[name],) + value.shape, value.dtype)
        for j, part in enumerate([value, *others]):
            out = lax.dynamic_update_index_in_dim(out, part, place[name] ^ j, 0)
        return out

    def noted(value, power):
        note = jnp.broadcast_to(power, (NOTE, kd)).astype(value.dtype)
        return jnp.concatenate([value.reshape(-1, kd), note])

    def read(got, shape):
        return got[:-NOTE].reshape(shape), got[-NOTE:][:1].astype(jnp.float32)

    def gathered(value, name, power):
        message = noted(value, power)
        got = [read(swap(message, name, j), value.shape) for j in range(1, size[name])]
        return in_order(value, [one for one, _ in got], name), [other for _, other in got]

    def scale(power):
        return jnp.exp2(power)

    def bound(power, others):
        for other in others:
            power = jnp.maximum(power, other)
        return power + len(others).bit_length()

    def sums(value, name, axis, power, others):
        me = place[name]
        got = [swap(pick(value, (axis, me ^ j)), name, j) for j in range(1, size[name])]
        top = bound(power, others)
        total = pick(value, (axis, me)).astype(jnp.float32) * scale(power - top)
        for one, other in zip(got, others):
            total = total + one.astype(jnp.float32) * scale(other - top)
        return total.astype(jnp.float16), top

    shards = in_order(key_weight, [swap(key_weight, "z", j) for j in range(1, nz)], "z")

    part = lax.dot_general(
        tokens, cotangent, (((0,), (0,)), ((), ())), preferred_element_type=jnp.float32
    )
    top = jnp.maximum(jnp.max(jnp.abs(part), axis=0, keepdims=True), 2.0**-100)
    power = jnp.ceil(jnp.log2(top))
    part = (part * scale(TOP - power)).astype(jnp.float16).reshape(nz * nx * ny, 2, rows, kd)
    power_2 = swap(jnp.broadcast_to(power, (NOTE, kd)), "core", 1)[:1]
    part, power = sums(part, "core", 1, power, [power_2])
    part = part.reshape(nz, nx, ny, 2, half, kd)

    blocks = shards.reshape(nz, 2, half, kd)
    one, power_x = gathered(blocks[:, 0], "x", power)
    two, power_y = gathered(blocks[:, 1], "y", power)
    part, one, two = lax.optimization_barrier((part, one, two))
    sum_one, top_one = sums(part[:, :, :, 0], "x", 1, power, power_x)
    sum_two, top_two = sums(part[:, :, :, 1], "y", 2, power, power_y)
    one, power_xy = gathered(one, "y", top_one)
    two, power_yx = gathered(two, "x", top_two)
    sum_one, top_one = sums(sum_one, "y", 2, top_one, power_xy)
    sum_two, top_two = sums(sum_two, "x", 1, top_two, power_yx)
    both = jnp.stack([one.transpose(2, 1, 0, 3, 4), two.transpose(2, 0, 1, 3, 4)], axis=3)
    weight = in_order(both, [swap(both, "core", 1)], "core")
    weight = weight.transpose(1, 2, 3, 0, 4, 5, 6).reshape(nz, nx * ny * 2 * rows, kd)

    total = jnp.concatenate([sum_one, sum_two], axis=3).reshape(nz, rows, kd)
    got = [
        read(swap(noted(pick(total, (0, z_me ^ j)), top_one), "z", j), (rows, kd))
        for j in range(1, nz)
    ]
    keys, input_grad = products(tokens, cotangent, weight)
    total = pick(total, (0, z_me))[0].astype(jnp.float32) * scale(top_one - TOP)
    for one, other in got:
        total = total + one.astype(jnp.float32) * scale(other - TOP)
    total_tokens = tokens.shape[0] * wide * node
    weight_grad = total * (1.0 / jnp.sqrt(jnp.float32(total_tokens)))
    return (keys, input_grad, weight_grad)


def solution(mesh):
    placed = (P(AXES, None), P(("node", "wide"), None), P(AXES, None))
    return jax.shard_map(
        on_device,
        mesh=mesh,
        in_specs=placed,
        out_specs=(P(AXES, None), P(AXES, None), P(("node", "wide"), None)),
        check_vma=False,
    )
```

time: 277 us -> 95.4 us (0.34)
  waiting for transfers between devices: 233 us -> 43.4 us
  starting transfers between devices: 0.12 us -> 20.7 us
  between operations: 13.8 us -> 1.23 us
  matrix products: 17.7 us -> 7.93 us
  blocking collectives: 9.08 us -> 0 us
  other arithmetic: 1.67 us -> 9.74 us
  Pallas kernels: 0 us -> 6.63 us
  local copies, waits for them, and re-layouts: 1.83 us -> 5.52 us
    reduce_scatter x2 -> x0, waiting for transfers between devices: 158 us -> none  [the longest x1 142 us: on_device(): lax.psum_scatter(lax.dot_general(columns, cotangent, (((0,), (0,)), ((),...]
    all_gather x1 -> x0, waiting for transfers between devices: 74.7 us -> none  [on_device(): lax.all_gather(secondary, 'node', axis=0, tiled=True)]
    ppermute x0 -> x17, waiting for transfers between devices: none -> 43.4 us  [swap(): lax.ppermute(value, AXES, [(i, i ^ j * mask[name]) for i in range(wide *...]
    ppermute x0 -> x17, starting transfers between devices: none -> 20.7 us  [swap(): lax.ppermute(value, AXES, [(i, i ^ j * mask[name]) for i in range(wide *...]
    dot_general x3 -> x1, matrix products: 17.7 us -> 7.93 us  [on_device(): lax.dot_general(tokens, cotangent, (((0,), (0,)), ((), ())), preferred_el...]
    all_gather x1 -> x0, blocking collectives: 9.08 us -> none  [on_device(): secondary = lax.all_gather(key_weight, 'wide', axis=0, tiled=True)]
    convert_element_type x0 -> x10, other arithmetic: none -> 7.99 us  [the longest x1 4.58 us: on_device(): (part * scale(TOP - power)).astype(jnp.float16)]
    pallas_call x0 -> x1, Pallas kernels: none -> 6.63 us  [products(): pl.pallas_call(products_kernel, grid=(steps,), in_specs=[columns, whole,...]
  transfers between devices with their start and end apart: 3 -> 17, of which waited for: 3 -> 8; matrix products, arithmetic and copies ran while one was open for 4% -> 18% of each run, Pallas kernels for 0% -> 0%
where the time goes in v4:
time: 95.4 us; the launch traced here: 95.2 us
  waiting for transfers between devices  43.4 us (45%)
  starting transfers between devices  20.7 us (22%)
  other arithmetic  9.74 us (10%)
  matrix products  7.93 us (8%)
  Pallas kernels  6.63 us (7%)
  local copies, waits for them, and re-layouts  5.52 us (6%)
  between operations  1.23 us (1%)
    ppermute x17, waiting for transfers between devices, swap(): lax.ppermute(value, AXES, [(i, i ^ j * mask[name]) for i in range(wide *...  43.4 us
    ppermute x17, starting transfers between devices, swap(): lax.ppermute(value, AXES, [(i, i ^ j * mask[name]) for i in range(wide *...  20.7 us
    dot_general x1, matrix products, on_device(): lax.dot_general(tokens, cotangent, (((0,), (0,)), ((), ())), preferred_el...  7.93 us
    pallas_call x1, Pallas kernels, products(): pl.pallas_call(products_kernel, grid=(steps,), in_specs=[columns, whole,...  6.63 us
    convert_element_type x1, other arithmetic, on_device(): (part * scale(TOP - power)).astype(jnp.float16)  4.58 us
    convert_element_type x5, other arithmetic, sums(): return (total.astype(jnp.float16), top)  3.32 us
    unnamed x11, local copies, waits for them, and re-layouts  2.55 us
  transfers between devices with their start and end apart: 17, of which 8 were waited for; matrix products, arithmetic and copies ran while one was open for 18% of the time, Pallas kernels for 0%

profile of v4, /device:TPU:0, one launch (start us, length us, event | category | flops | bytes accessed | tf_op | source)
XLA Modules:
  0.0 95.2 jit_solution(8936439642328406747)
XLA Ops:
  0.6 3.1 %collective-permute-start.2 = (bf16[128,512]{1,0:T(8,128)(2,1)}, bf16[128,512]{1,0:T(8,128)(2,1)S(1)}, u32[]{:S(2)}, u32[]{:S(2)}) collective-permute-start(bf16[128,512]{1,0:T(8,128)(2,1)} %param.4), channel_id=1, source_target_pairs={{0,2},{1,3},{2,0},{3,1},{4,6},{5,7},{6,4},{7,5},{8,10},{9,11},{10,... | collective-permute-start | bytes 393224 | tf_op jit(solution)/shard_map/ppermute | solution.py:68
  3.7 2.6 %collective-permute-start.3 = (bf16[128,512]{1,0:T(8,128)(2,1)}, bf16[128,512]{1,0:T(8,128)(2,1)S(1)}, u32[]{:S(2)}, u32[]{:S(2)}) collective-permute-start(bf16[128,512]{1,0:T(8,128)(2,1)} %param.4), channel_id=1, source_target_pairs={{0,4},{1,5},{2,6},{3,7},{4,0},{5,1},{6,2},{7,3},{8,12},{9,13},{10,... | collective-permute-start | bytes 393224 | tf_op jit(solution)/shard_map/ppermute | solution.py:68
  6.3 7.9 %abs_reduce_fusion = (f32[512]{0:T(512)S(1)}, f32[4096,512]{1,0:T(8,128)}) fusion(bf16[512,4096]{1,0:T(8,128)(2,1)} %tok.1, bf16[512,512]{1,0:T(8,128)(2,1)} %cot.1), kind=kOutput, calls=%fused_computation.1 | convolution fusion | flops 2151677440 | bytes 13109248 | tf_op jit(solution)/shard_map/dot_general | solution.py:113
  14.4 4.6 %multiply_convert_fusion = f16[4096,512]{1,0:T(8,128)(2,1)S(1)} fusion(f32[4096,512]{1,0:T(8,128)} %get-tuple-element.44, f32[512]{0:T(512)S(1)} %get-tuple-element.42), kind=kLoop, calls=%fused_computation | loop fusion | flops 4194304 | bytes 12584960 | tf_op jit(solution)/shard_map/convert_element_type | solution.py:118
  19.0 2.0 %copy-done.2 = f16[4096,512]{1,0:T(8,128)(2,1)} copy-done((f16[4096,512]{1,0:T(8,128)(2,1)}, f16[4096,512]{1,0:T(8,128)(2,1)S(1)}, u32[]{:S(2)}) %copy-start.2) | copy-done | bytes 4194328
  22.4 1.8 %collective-permute-start.6 = (bf16[264,512]{1,0:T(8,128)(2,1)S(1)}, bf16[264,512]{1,0:T(8,128)(2,1)S(1)}, u32[]{:S(2)}, u32[]{:S(2)}) collective-permute-start(bf16[264,512]{1,0:T(8,128)(2,1)S(1)} %get-tuple-element.31), channel_id=1, source_target_pairs={{0,16},{1,17},{2,18},{3,19},{4,20},{5,21},{6,22},{7,23},{8,24},{9,... | collective-permute-start | bytes 811016 | tf_op jit(solution)/shard_map/ppermute | solution.py:68
  24.2 1.5 %collective-permute-start.5 = (bf16[264,512]{1,0:T(8,128)(2,1)S(1)}, bf16[264,512]{1,0:T(8,128)(2,1)S(1)}, u32[]{:S(2)}, u32[]{:S(2)}) collective-permute-start(bf16[264,512]{1,0:T(8,128)(2,1)S(1)} %get-tuple-element.32), channel_id=1, source_target_pairs={{0,1},{1,0},{2,3},{3,2},{4,5},{5,4},{6,7},{7,6},{8,9},{9,8},{10,11... | collective-permute-start | bytes 811016 | tf_op jit(solution)/shard_map/ppermute | solution.py:68
  25.9 5.0 %collective-permute-done.6 = bf16[264,512]{1,0:T(8,128)(2,1)S(1)} collective-permute-done((bf16[264,512]{1,0:T(8,128)(2,1)S(1)}, bf16[264,512]{1,0:T(8,128)(2,1)S(1)}, u32[]{:S(2)}, u32[]{:S(2)}) %collective-permute-start.6) | collective-permute-done | bytes 270368 | tf_op jit(solution)/shard_map/ppermute | solution.py:68
  30.9 1.4 %collective-permute-done.5 = bf16[264,512]{1,0:T(8,128)(2,1)S(1)} collective-permute-done((bf16[264,512]{1,0:T(8,128)(2,1)S(1)}, bf16[264,512]{1,0:T(8,128)(2,1)S(1)}, u32[]{:S(2)}, u32[]{:S(2)}) %collective-permute-start.5) | collective-permute-done | bytes 270368 | tf_op jit(solution)/shard_map/ppermute | solution.py:68
  32.5 2.6 %add_convert_fusion = f16[16,1,128,512]{3,2,0,1:T(8,128)(2,1)S(1)} fusion(f16[16,1,128,512]{3,2,0,1:T(8,128)(2,1)} %collective-permute-done.1, f32[512]{0:T(512)S(1)} %bitcast.132, f32[512]{0:T(512)S(1)} %bitcast.133, f16[16,2,128,512]{3,2,1,0:T(8,128)(2,1)S(1)} %bitcast.102, s32[]{:T(128)S(6)} %select_n.52), kind=kLoop, calls=%fused_computation.2 | loop fusion | flops 6291456 | bytes 6295556 | tf_op jit(solution)/shard_map/convert_element_type | solution.py:109
  36.5 1.7 %collective-permute-start.8 = (bf16[520,512]{1,0:T(8,128)(2,1)S(1)}, bf16[520,512]{1,0:T(8,128)(2,1)S(1)}, u32[]{:S(2)}, u32[]{:S(2)}) collective-permute-start(bf16[520,512]{1,0:T(8,128)(2,1)S(1)} %pad_maximum_fusion.2), channel_id=1, source_target_pairs={{0,1},{1,0},{2,3},{3,2},{4,5},{5,4},{6,7},{7,6},{8,9},{9,8},{10,11... | collective-permute-start | bytes 1597448 | tf_op jit(solution)/shard_map/ppermute | solution.py:68
  38.3 1.6 %collective-permute-start.12 = (f16[4,2,1,64,512]{4,3,1,0,2:T(8,128)(2,1)S(1)}, f16[4,2,1,64,512]{4,3,1,0,2:T(8,128)(2,1)S(1)}, u32[]{:S(2)}, u32[]{:S(2)}) collective-permute-start(f16[4,2,1,64,512]{4,3,1,0,2:T(8,128)(2,1)S(1)} %dynamic-slice_bitcast_fusion.1), channel_id=1, source_target_pairs={{0,16},{1,17},{2,18},{3,19},{4,20},{5,21},{6,22},{7,23},{8,24},{9,... | collective-permute-start | bytes 1572872 | tf_op jit(solution)/shard_map/ppermute | solution.py:68
  40.3 0.6 collective-permute-start.10
  41.2 9.9 %collective-permute-done.7 = bf16[520,512]{1,0:T(8,128)(2,1)S(1)} collective-permute-done((bf16[520,512]{1,0:T(8,128)(2,1)S(1)}, bf16[520,512]{1,0:T(8,128)(2,1)S(1)}, u32[]{:S(2)}, u32[]{:S(2)}) %collective-permute-start.7) | collective-permute-done | bytes 532512 | tf_op jit(solution)/shard_map/ppermute | solution.py:68
  51.6 8.5 %collective-permute-done.12 = f16[4,2,1,64,512]{4,3,1,0,2:T(8,128)(2,1)S(1)} collective-permute-done((f16[4,2,1,64,512]{4,3,1,0,2:T(8,128)(2,1)S(1)}, f16[4,2,1,64,512]{4,3,1,0,2:T(8,128)(2,1)S(1)}, u32[]{:S(2)}, u32[]{:S(2)}) %collective-permute-start.12) | collective-permute-done | bytes 524320 | tf_op jit(solution)/shard_map/ppermute | solution.py:68
  60.5 1.6 %collective-permute-start.13 = (f16[4,1,1,64,512]{4,3,1,0,2:T(8,128)(2,1)S(1)}, f16[4,1,1,64,512]{4,3,1,0,2:T(8,128)(2,1)S(1)}, u32[]{:S(2)}, u32[]{:S(2)}) collective-permute-start(f16[4,1,1,64,512]{4,3,1,0,2:T(8,128)(2,1)S(1)} %constant_dynamic-slice_fusion), channel_id=1, source_target_pairs={{0,1},{1,0},{2,3},{3,2},{4,5},{5,4},{6,7},{7,6},{8,9},{9,8},{10,11... | collective-permute-start | bytes 786440 | tf_op jit(solution)/shard_map/ppermute | solution.py:68
  62.8 0.7 collective-permute-start.11
  63.6 3.3 %collective-permute-done.13 = f16[4,1,1,64,512]{4,3,1,0,2:T(8,128)(2,1)S(1)} collective-permute-done((f16[4,1,1,64,512]{4,3,1,0,2:T(8,128)(2,1)S(1)}, f16[4,1,1,64,512]{4,3,1,0,2:T(8,128)(2,1)S(1)}, u32[]{:S(2)}, u32[]{:S(2)}) %collective-permute-start.13) | collective-permute-done | bytes 262176 | tf_op jit(solution)/shard_map/ppermute | solution.py:68
  67.0 4.6 %collective-permute-done.11 = f16[4,1,1,64,512]{4,3,1,0,2:T(8,128)(2,1)S(1)} collective-permute-done((f16[4,1,1,64,512]{4,3,1,0,2:T(8,128)(2,1)S(1)}, f16[4,1,1,64,512]{4,3,1,0,2:T(8,128)(2,1)S(1)}, u32[]{:S(2)}, u32[]{:S(2)}) %collective-permute-start.11) | collective-permute-done | bytes 262176 | tf_op jit(solution)/shard_map/ppermute | solution.py:68
  72.0 0.7 collective-permute-start.14
  73.5 3.6 %collective-permute-start.15 = (f16[136,512]{1,0:T(8,128)(2,1)S(1)}, f16[136,512]{1,0:T(8,128)(2,1)S(1)}, u32[]{:S(2)}, u32[]{:S(2)}) collective-permute-start(f16[136,512]{1,0:T(8,128)(2,1)S(1)} %get-tuple-element.29), channel_id=1, source_target_pairs={{0,4},{1,5},{2,6},{3,7},{4,0},{5,1},{6,2},{7,3},{8,12},{9,13},{10,... | collective-permute-start | bytes 417800 | tf_op jit(solution)/shard_map/ppermute | solution.py:68
  77.3 10.1 %collective-permute-done.15 = f16[136,512]{1,0:T(8,128)(2,1)S(1)} collective-permute-done((f16[136,512]{1,0:T(8,128)(2,1)S(1)}, f16[136,512]{1,0:T(8,128)(2,1)S(1)}, u32[]{:S(2)}, u32[]{:S(2)}) %collective-permute-start.15) | collective-permute-done | bytes 139296 | tf_op jit(solution)/shard_map/ppermute | solution.py:68
  87.4 0.8 fusion.7
  88.6 6.6 %shard_map.58 = (bf16[512,512]{1,0:T(8,128)(2,1)}, bf16[512,4096]{1,0:T(8,128)(2,1)}) custom-call(bf16[512,4096]{1,0:T(8,128)(2,1)S(1)} %copy-done, bf16[512,512]{1,0:T(8,128)(2,1)S(1)} %copy-done.1, bf16[4,1024,512]{2,1,0:T(8,128)(2,1)S(1)} %bitcast.100), custom_call_target="tpu_custom_call" | custom-call | flops 4294967296 | bytes 14155776 | tf_op jit(solution)/shard_map/pallas_call | solution.py:35
  (86 shorter events, 7.2 us)
Async XLA Ops:
  0.6 21.6 %collective-permute-start.2 = (bf16[128,512]{1,0:T(8,128)(2,1)}, bf16[128,512]{1,0:T(8,128)(2,1)S(1)}, u32[]{:S(2)}, u32[]{:S(2)}) collective-permute-start(bf16[128,512]{1,0:T(8,128)(2,1)} %param.4), channel_id=1, source_target_pairs={{0,2},{1,3},{2,0},{3,1},{4,6},{5,7},{6,4},{7,5},{8,10},{9,11},{10,... | collective-permute-start | bytes 393224 | tf_op jit(solution)/shard_map/ppermute | solution.py:68
  3.7 18.5 %collective-permute-start.3 = (bf16[128,512]{1,0:T(8,128)(2,1)}, bf16[128,512]{1,0:T(8,128)(2,1)S(1)}, u32[]{:S(2)}, u32[]{:S(2)}) collective-permute-start(bf16[128,512]{1,0:T(8,128)(2,1)} %param.4), channel_id=1, source_target_pairs={{0,4},{1,5},{2,6},{3,7},{4,0},{5,1},{6,2},{7,3},{8,12},{9,13},{10,... | collective-permute-start | bytes 393224 | tf_op jit(solution)/shard_map/ppermute | solution.py:68
  6.3 16.0 %collective-permute-start.4 = (bf16[128,512]{1,0:T(8,128)(2,1)}, bf16[128,512]{1,0:T(8,128)(2,1)S(1)}, u32[]{:S(2)}, u32[]{:S(2)}) collective-permute-start(bf16[128,512]{1,0:T(8,128)(2,1)} %param.4), channel_id=1, source_target_pairs={{0,6},{1,7},{2,4},{3,5},{4,2},{5,3},{6,0},{7,1},{8,14},{9,15},{10,... | collective-permute-start | bytes 393224 | tf_op jit(solution)/shard_map/ppermute | solution.py:68
  14.3 7.9 %collective-permute-start = (f32[8,512]{1,0:T(8,128)S(1)}, f32[8,512]{1,0:T(8,128)S(1)}, u32[]{:S(2)}, u32[]{:S(2)}) collective-permute-start(f32[8,512]{1,0:T(8,128)S(1)} %broadcast_in_dim.98), channel_id=1, source_target_pairs={{0,8},{1,9},{2,10},{3,11},{4,12},{5,13},{6,14},{7,15},{8,0},{9,1},... | collective-permute-start | bytes 49160 | tf_op jit(solution)/shard_map/ppermute | solution.py:68
  18.9 2.0 %copy-start.2 = (f16[4096,512]{1,0:T(8,128)(2,1)}, f16[4096,512]{1,0:T(8,128)(2,1)S(1)}, u32[]{:S(2)}) copy-start(f16[4096,512]{1,0:T(8,128)(2,1)S(1)} %multiply_convert_fusion) | copy-start | bytes 12582916
  18.9 3.1 %copy-start.4 = (bf16[128,512]{1,0:T(8,128)(2,1)S(1)}, bf16[128,512]{1,0:T(8,128)(2,1)}, u32[]{:S(2)}) copy-start(bf16[128,512]{1,0:T(8,128)(2,1)} %param.4) | copy-start | bytes 393220
  21.5 11.0 %collective-permute-start.1 = (f16[16,1,128,512]{3,2,0,1:T(8,128)(2,1)S(1)}, f16[16,1,128,512]{3,2,0,1:T(8,128)(2,1)}, u32[]{:S(2)}, u32[]{:S(2)}) collective-permute-start(f16[16,1,128,512]{3,2,0,1:T(8,128)(2,1)S(1)} %dynamic-slice_bitcast_fusion), channel_id=1, source_target_pairs={{0,8},{1,9},{2,10},{3,11},{4,12},{5,13},{6,14},{7,15},{8,0},{9,1},... | collective-permute-start | bytes 6291464 | tf_op jit(solution)/shard_map/ppermute | solution.py:68
  22.2 10.4 %copy-start.3 = (f16[4096,512]{1,0:T(8,128)(2,1)S(1)}, f16[4096,512]{1,0:T(8,128)(2,1)}, u32[]{:S(2)}) copy-start(f16[4096,512]{1,0:T(8,128)(2,1)} %copy-done.2) | copy-start | bytes 12582916
  22.4 8.5 %collective-permute-start.6 = (bf16[264,512]{1,0:T(8,128)(2,1)S(1)}, bf16[264,512]{1,0:T(8,128)(2,1)S(1)}, u32[]{:S(2)}, u32[]{:S(2)}) collective-permute-start(bf16[264,512]{1,0:T(8,128)(2,1)S(1)} %get-tuple-element.31), channel_id=1, source_target_pairs={{0,16},{1,17},{2,18},{3,19},{4,20},{5,21},{6,22},{7,23},{8,24},{9,... | collective-permute-start | bytes 811016 | tf_op jit(solution)/shard_map/ppermute | solution.py:68
  24.2 8.1 %collective-permute-start.5 = (bf16[264,512]{1,0:T(8,128)(2,1)S(1)}, bf16[264,512]{1,0:T(8,128)(2,1)S(1)}, u32[]{:S(2)}, u32[]{:S(2)}) collective-permute-start(bf16[264,512]{1,0:T(8,128)(2,1)S(1)} %get-tuple-element.32), channel_id=1, source_target_pairs={{0,1},{1,0},{2,3},{3,2},{4,5},{5,4},{6,7},{7,6},{8,9},{9,8},{10,11... | collective-permute-start | bytes 811016 | tf_op jit(solution)/shard_map/ppermute | solution.py:68
  36.0 15.1 %collective-permute-start.7 = (bf16[520,512]{1,0:T(8,128)(2,1)S(1)}, bf16[520,512]{1,0:T(8,128)(2,1)S(1)}, u32[]{:S(2)}, u32[]{:S(2)}) collective-permute-start(bf16[520,512]{1,0:T(8,128)(2,1)S(1)} %pad_maximum_fusion.1), channel_id=1, source_target_pairs={{0,16},{1,17},{2,18},{3,19},{4,20},{5,21},{6,22},{7,23},{8,24},{9,... | collective-permute-start | bytes 1597448 | tf_op jit(solution)/shard_map/ppermute | solution.py:68
  36.5 15.1 %collective-permute-start.8 = (bf16[520,512]{1,0:T(8,128)(2,1)S(1)}, bf16[520,512]{1,0:T(8,128)(2,1)S(1)}, u32[]{:S(2)}, u32[]{:S(2)}) collective-permute-start(bf16[520,512]{1,0:T(8,128)(2,1)S(1)} %pad_maximum_fusion.2), channel_id=1, source_target_pairs={{0,1},{1,0},{2,3},{3,2},{4,5},{5,4},{6,7},{7,6},{8,9},{9,8},{10,11... | collective-permute-start | bytes 1597448 | tf_op jit(solution)/shard_map/ppermute | solution.py:68
  38.3 21.8 %collective-permute-start.12 = (f16[4,2,1,64,512]{4,3,1,0,2:T(8,128)(2,1)S(1)}, f16[4,2,1,64,512]{4,3,1,0,2:T(8,128)(2,1)S(1)}, u32[]{:S(2)}, u32[]{:S(2)}) collective-permute-start(f16[4,2,1,64,512]{4,3,1,0,2:T(8,128)(2,1)S(1)} %dynamic-slice_bitcast_fusion.1), channel_id=1, source_target_pairs={{0,16},{1,17},{2,18},{3,19},{4,20},{5,21},{6,22},{7,23},{8,24},{9,... | collective-permute-start | bytes 1572872 | tf_op jit(solution)/shard_map/ppermute | solution.py:68
  40.3 22.3 %collective-permute-start.10 = (f16[4,1,2,64,512]{4,3,1,0,2:T(8,128)(2,1)S(1)}, f16[4,1,2,64,512]{4,3,1,0,2:T(8,128)(2,1)S(1)}, u32[]{:S(2)}, u32[]{:S(2)}) collective-permute-start(f16[4,1,2,64,512]{4,3,1,0,2:T(8,128)(2,1)S(1)} %dynamic-slice_bitcast_fusion.2), channel_id=1, source_target_pairs={{0,1},{1,0},{2,3},{3,2},{4,5},{5,4},{6,7},{7,6},{8,9},{9,8},{10,11... | collective-permute-start | bytes 1572872 | tf_op jit(solution)/shard_map/ppermute | solution.py:68
  60.5 6.4 %collective-permute-start.13 = (f16[4,1,1,64,512]{4,3,1,0,2:T(8,128)(2,1)S(1)}, f16[4,1,1,64,512]{4,3,1,0,2:T(8,128)(2,1)S(1)}, u32[]{:S(2)}, u32[]{:S(2)}) collective-permute-start(f16[4,1,1,64,512]{4,3,1,0,2:T(8,128)(2,1)S(1)} %constant_dynamic-slice_fusion), channel_id=1, source_target_pairs={{0,1},{1,0},{2,3},{3,2},{4,5},{5,4},{6,7},{7,6},{8,9},{9,8},{10,11... | collective-permute-start | bytes 786440 | tf_op jit(solution)/shard_map/ppermute | solution.py:68
  62.4 25.9 %collective-permute-start.9 = (bf16[4,2,2,2,64,512]{5,4,3,2,1,0:T(8,128)(2,1)S(1)}, bf16[4,2,2,2,64,512]{5,4,3,2,1,0:T(8,128)(2,1)S(1)}, u32[]{:S(2)}, u32[]{:S(2)}) collective-permute-start(bf16[4,2,2,2,64,512]{5,4,3,2,1,0:T(8,128)(2,1)S(1)} %pad_maximum_fusion), channel_id=1, source_target_pairs={{0,8},{1,9},{2,10},{3,11},{4,12},{5,13},{6,14},{7,15},{8,0},{9,1},... | collective-permute-start | bytes 6291464 | tf_op jit(solution)/shard_map/ppermute | solution.py:68
  62.8 8.8 %collective-permute-start.11 = (f16[4,1,1,64,512]{4,3,1,0,2:T(8,128)(2,1)S(1)}, f16[4,1,1,64,512]{4,3,1,0,2:T(8,128)(2,1)S(1)}, u32[]{:S(2)}, u32[]{:S(2)}) collective-permute-start(f16[4,1,1,64,512]{4,3,1,0,2:T(8,128)(2,1)S(1)} %constant_dynamic-slice_fusion.1), channel_id=1, source_target_pairs={{0,16},{1,17},{2,18},{3,19},{4,20},{5,21},{6,22},{7,23},{8,24},{9,... | collective-permute-start | bytes 786440 | tf_op jit(solution)/shard_map/ppermute | solution.py:68
  72.0 5.4 %collective-permute-start.14 = (f16[136,512]{1,0:T(8,128)(2,1)S(1)}, f16[136,512]{1,0:T(8,128)(2,1)S(1)}, u32[]{:S(2)}, u32[]{:S(2)}) collective-permute-start(f16[136,512]{1,0:T(8,128)(2,1)S(1)} %get-tuple-element.28), channel_id=1, source_target_pairs={{0,2},{1,3},{2,0},{3,1},{4,6},{5,7},{6,4},{7,5},{8,10},{9,11},{10,... | collective-permute-start | bytes 417800 | tf_op jit(solution)/shard_map/ppermute | solution.py:68
  73.2 15.4 %copy-start = (bf16[512,4096]{1,0:T(8,128)(2,1)S(1)}, bf16[512,4096]{1,0:T(8,128)(2,1)}, u32[]{:S(2)}) copy-start(bf16[512,4096]{1,0:T(8,128)(2,1)} %tok.1) | copy-start | bytes 12582916
  73.2 15.3 %copy-start.1 = (bf16[512,512]{1,0:T(8,128)(2,1)S(1)}, bf16[512,512]{1,0:T(8,128)(2,1)}, u32[]{:S(2)}) copy-start(bf16[512,512]{1,0:T(8,128)(2,1)} %cot.1) | copy-start | bytes 1572868
  73.5 13.9 %collective-permute-start.15 = (f16[136,512]{1,0:T(8,128)(2,1)S(1)}, f16[136,512]{1,0:T(8,128)(2,1)S(1)}, u32[]{:S(2)}, u32[]{:S(2)}) collective-permute-start(f16[136,512]{1,0:T(8,128)(2,1)S(1)} %get-tuple-element.29), channel_id=1, source_target_pairs={{0,4},{1,5},{2,6},{3,7},{4,0},{5,1},{6,2},{7,3},{8,12},{9,13},{10,... | collective-permute-start | bytes 417800 | tf_op jit(solution)/shard_map/ppermute | solution.py:68
  77.1 10.3 %collective-permute-start.16 = (f16[136,512]{1,0:T(8,128)(2,1)S(1)}, f16[136,512]{1,0:T(8,128)(2,1)S(1)}, u32[]{:S(2)}, u32[]{:S(2)}) collective-permute-start(f16[136,512]{1,0:T(8,128)(2,1)S(1)} %get-tuple-element.30), channel_id=1, source_target_pairs={{0,6},{1,7},{2,4},{3,5},{4,2},{5,3},{6,0},{7,1},{8,14},{9,15},{10,... | collective-permute-start | bytes 417800 | tf_op jit(solution)/shard_map/ppermute | solution.py:68

commit v5 on v4

--- a/solution.py
+++ b/solution.py
@@ -51,6 +51,44 @@
     )(tokens, cotangent, weight)
 
 
+def bound_kernel(tok, cot, power, total):
+    step = pl.program_id(0)
+
+    @pl.when(step == 0)
+    def _():
+        total[...] = jnp.zeros_like(total)
+
+    reach = jnp.max(jnp.abs(tok[...]).astype(jnp.float32), axis=1, keepdims=True)
+    terms = reach * jnp.abs(cot[...]).astype(jnp.float32)
+    total[...] += jnp.sum(terms.reshape(-1, NOTE, terms.shape[1]), axis=0)
+
+    @pl.when(step == pl.num_programs(0) - 1)
+    def _():
+        top = jnp.maximum(jnp.sum(total[...], axis=0, keepdims=True), 2.0**-100)
+        power[...] = jnp.broadcast_to(jnp.ceil(jnp.log2(top)), power.shape)
+
+
+def bound_of(tokens, cotangent):
+    rows, width = tokens.shape
+    kd = cotangent.shape[1]
+    block = min(rows, 128)
+    return pl.pallas_call(
+        bound_kernel,
+        grid=(rows // block,),
+        in_specs=[
+            pl.BlockSpec((block, width), lambda i: (i, 0)),
+            pl.BlockSpec((block, kd), lambda i: (i, 0)),
+        ],
+        out_specs=pl.BlockSpec((NOTE, kd), lambda i: (0, 0)),
+        scratch_shapes=[pltpu.VMEM((NOTE, kd), jnp.float32)],
+        out_shape=jax.ShapeDtypeStruct((NOTE, kd), jnp.float32),
+        compiler_params=pltpu.CompilerParams(vmem_limit_bytes=40 * 1024 * 1024),
+        cost_estimate=pl.CostEstimate(
+            flops=2 * rows * width, bytes_accessed=2 * rows * (width + kd), transcendentals=0
+        ),
+    )(tokens, cotangent)
+
+
 def on_device(tokens, key_weight, cotangent):
     wide, node = lax.axis_size("wide"), lax.axis_size("node")
     w_me, n_me = lax.axis_index("wide"), lax.axis_index("node")
@@ -108,16 +146,19 @@
             total = total + one.astype(jnp.float32) * scale(other - top)
         return total.astype(jnp.float16), top
 
-    shards = in_order(key_weight, [swap(key_weight, "z", j) for j in range(1, nz)], "z")
-
+    shards = [swap(key_weight, "z", j) for j in range(1, nz)]
+
+    power = bound_of(tokens, cotangent)
+    power = jnp.maximum(power, swap(power, "core", 1))[:1] + 1.0
     part = lax.dot_general(
         tokens, cotangent, (((0,), (0,)), ((), ())), preferred_element_type=jnp.float32
     )
-    top = jnp.maximum(jnp.max(jnp.abs(part), axis=0, keepdims=True), 2.0**-100)
-    power = jnp.ceil(jnp.log2(top))
     part = (part * scale(TOP - power)).astype(jnp.float16).reshape(nz * nx * ny, 2, rows, kd)
-    power_2 = swap(jnp.broadcast_to(power, (NOTE, kd)), "core", 1)[:1]
-    part, power = sums(part, "core", 1, power, [power_2])
+    part, shards = lax.optimization_barrier((part, shards))
+    shards = in_order(key_weight, shards, "z")
+    other = swap(pick(part, (1, 1 - core)), "core", 1)
+    part = pick(part, (1, core)).astype(jnp.float32) + other.astype(jnp.float32)
+    part = part.astype(jnp.float16)
     part = part.reshape(nz, nx, ny, 2, half, kd)
 
     blocks = shards.reshape(nz, 2, half, kd)
@@ -136,10 +177,12 @@
 
     total = jnp.concatenate([sum_one, sum_two], axis=3).reshape(nz, rows, kd)
     got = [
-        read(swap(noted(pick(total, (0, z_me ^ j)), top_one), "z", j), (rows, kd))
+        swap(noted(pick(total, (0, z_me ^ j)), top_one), "z", j)
         for j in range(1, nz)
     ]
     keys, input_grad = products(tokens, cotangent, weight)
+    keys, input_grad, got = lax.optimization_barrier((keys, input_grad, got))
+    got = [read(one, (rows, kd)) for one in got]
     total = pick(total, (0, z_me))[0].astype(jnp.float32) * scale(top_one - TOP)
     for one, other in got:
         total = total + one.astype(jnp.float32) * scale(other - TOP)

time: 95.4 us -> 84.5 us (0.89)
  other arithmetic: 9.74 us -> 3.33 us
  waiting for transfers between devices: 43.4 us -> 38.5 us
  local copies, waits for them, and re-layouts: 5.52 us -> 9.68 us
  matrix products: 7.93 us -> 4.58 us
  starting transfers between devices: 20.7 us -> 19.3 us
  Pallas kernels: 6.63 us -> 7.66 us
    ppermute x17, waiting for transfers between devices: 43.4 us -> 38.5 us  [swap(): lax.ppermute(value, AXES, [(i, i ^ j * mask[name]) for i in range(wide *...]
    convert_element_type x1, other arithmetic: 4.58 us -> 0.78 us  [on_device(): part = part.astype(jnp.float16)]
    dot_general x1, matrix products: 7.93 us -> 4.58 us  [on_device(): lax.dot_general(tokens, cotangent, (((0,), (0,)), ((), ())), preferred_el...]
    convert_element_type x5 -> x4, other arithmetic: 3.32 us -> 0.73 us  [sums(): return (total.astype(jnp.float16), top)]
    dynamic_slice x4 -> x5, local copies, waits for them, and re-layouts: 0.32 us -> 2.16 us  [pick(): return lax.dynamic_slice(value, start, extent)]
    ppermute x17, starting transfers between devices: 20.7 us -> 19.3 us  [swap(): lax.ppermute(value, AXES, [(i, i ^ j * mask[name]) for i in range(wide *...]
    dynamic_update_slice x13 -> x12, local copies, waits for them, and re-layouts: 0.61 us -> 1.67 us  [in_order(): out = lax.dynamic_update_index_in_dim(out, part, place[name] ^ j, 0)]
    pallas_call x0 -> x1, Pallas kernels: none -> 1.03 us  [bound_of(): pl.pallas_call(bound_kernel, grid=(rows // block,), in_specs=[pl.BlockSpe...]
  transfers between devices with their start and end apart: 17 -> 17, of which waited for: 8 -> 10; matrix products, arithmetic and copies ran while one was open for 18% -> 13% of each run, Pallas kernels for 0% -> 8%
where the time goes in v5:
time: 84.5 us; the launch traced here: 84.2 us
  waiting for transfers between devices  38.5 us (46%)
  starting transfers between devices  19.3 us (23%)
  local copies, waits for them, and re-layouts  9.68 us (11%)
  Pallas kernels  7.66 us (9%)
  matrix products  4.58 us (5%)
  other arithmetic  3.33 us (4%)
  between operations  1.17 us (1%)
    ppermute x17, waiting for transfers between devices, swap(): lax.ppermute(value, AXES, [(i, i ^ j * mask[name]) for i in range(wide *...  38.5 us
    ppermute x17, starting transfers between devices, swap(): lax.ppermute(value, AXES, [(i, i ^ j * mask[name]) for i in range(wide *...  19.3 us
    pallas_call x1, Pallas kernels, products(): pl.pallas_call(products_kernel, grid=(steps,), in_specs=[columns, whole,...  6.63 us
    dot_general x1, matrix products, on_device(): lax.dot_general(tokens, cotangent, (((0,), (0,)), ((), ())), preferred_el...  4.58 us
    unnamed x16, local copies, waits for them, and re-layouts  3.25 us
    dynamic_slice x5, local copies, waits for them, and re-layouts, pick(): return lax.dynamic_slice(value, start, extent)  2.16 us
  transfers between devices with their start and end apart: 17, of which 10 were waited for; matrix products, arithmetic and copies ran while one was open for 13% of the time, Pallas kernels for 8%

profile of v5, /device:TPU:0, one launch (start us, length us, event | category | flops | bytes accessed | tf_op | source)
XLA Modules:
  0.0 84.2 jit_solution(3558289350069616191)
XLA Ops:
  0.6 2.2 %copy-done = bf16[512,4096]{1,0:T(8,128)(2,1)S(1)} copy-done((bf16[512,4096]{1,0:T(8,128)(2,1)S(1)}, bf16[512,4096]{1,0:T(8,128)(2,1)}, u32[]{:S(2)}) %copy-start) | copy-done | bytes 4194328
  2.8 1.0 %copy-done.2 = bf16[512,512]{1,0:T(8,128)(2,1)S(1)} copy-done((bf16[512,512]{1,0:T(8,128)(2,1)S(1)}, bf16[512,512]{1,0:T(8,128)(2,1)}, u32[]{:S(2)}) %copy-start.2) | copy-done | bytes 524312
  3.9 1.0 %shard_map.58 = f32[8,512]{1,0:T(8,128)S(1)} custom-call(bf16[512,4096]{1,0:T(8,128)(2,1)S(1)} %copy-done, bf16[512,512]{1,0:T(8,128)(2,1)S(1)} %copy-done.2), custom_call_target="tpu_custom_call" | custom-call | flops 4194304 | bytes 4718592 | tf_op jit(solution)/shard_map/pallas_call | solution.py:75
  5.4 3.7 %collective-permute-start.2 = (bf16[128,512]{1,0:T(8,128)(2,1)S(1)}, bf16[128,512]{1,0:T(8,128)(2,1)S(1)}, u32[]{:S(2)}, u32[]{:S(2)}) collective-permute-start(bf16[128,512]{1,0:T(8,128)(2,1)S(1)} %copy-done.6), channel_id=1, source_target_pairs={{0,4},{1,5},{2,6},{3,7},{4,0},{5,1},{6,2},{7,3},{8,12},{9,13},{10,... | collective-permute-start | bytes 393224 | tf_op jit(solution)/shard_map/ppermute | solution.py:106
  9.1 1.6 %collective-permute-start.1 = (bf16[128,512]{1,0:T(8,128)(2,1)S(1)}, bf16[128,512]{1,0:T(8,128)(2,1)S(1)}, u32[]{:S(2)}, u32[]{:S(2)}) collective-permute-start(bf16[128,512]{1,0:T(8,128)(2,1)S(1)} %copy-done.6), channel_id=1, source_target_pairs={{0,2},{1,3},{2,0},{3,1},{4,6},{5,7},{6,4},{7,5},{8,10},{9,11},{10,... | collective-permute-start | bytes 393224 | tf_op jit(solution)/shard_map/ppermute | solution.py:106
  10.7 4.6 %multiply_convert_fusion = f16[4096,512]{1,0:T(8,128)(2,1)S(1)} fusion(bf16[512,4096]{1,0:T(8,128)(2,1)} %tok.3, bf16[512,512]{1,0:T(8,128)(2,1)S(1)} %copy-done.3, f32[512]{0:T(512)S(1)} %bitcast.124), kind=kOutput, calls=%fused_computation | convolution fusion | flops 2151677952 | bytes 8914944 | tf_op jit(solution)/shard_map/dot_general | solution.py:153
  15.3 1.0 %collective-permute-done.2 = bf16[128,512]{1,0:T(8,128)(2,1)S(1)} collective-permute-done((bf16[128,512]{1,0:T(8,128)(2,1)S(1)}, bf16[128,512]{1,0:T(8,128)(2,1)S(1)}, u32[]{:S(2)}, u32[]{:S(2)}) %collective-permute-start.2) | collective-permute-done | bytes 131104 | tf_op jit(solution)/shard_map/ppermute | solution.py:106
  16.3 3.7 %collective-permute-done.3 = bf16[128,512]{1,0:T(8,128)(2,1)S(1)} collective-permute-done((bf16[128,512]{1,0:T(8,128)(2,1)S(1)}, bf16[128,512]{1,0:T(8,128)(2,1)S(1)}, u32[]{:S(2)}, u32[]{:S(2)}) %collective-permute-start.3) | collective-permute-done | bytes 131104 | tf_op jit(solution)/shard_map/ppermute | solution.py:106
  20.0 1.8 %constant_dynamic-slice_fusion.2 = f16[16,1,128,512]{3,2,0,1:T(8,128)(2,1)} fusion(s32[]{:T(128)S(6)} %select_n.55, f16[16,2,128,512]{3,2,1,0:T(8,128)(2,1)S(1)} %bitcast.102), kind=kLoop, calls=%fused_computation.57 | loop fusion | bytes 4194308 | tf_op jit(solution)/shard_map/dynamic_slice | solution.py:112
  22.0 1.1 %bitcast_dynamic-update-slice_fusion.8 = bf16[4,128,512]{2,1,0:T(8,128)(2,1)S(1)} fusion(bf16[4,128,512]{2,1,0:T(8,128)(2,1)S(1)} %bitcast_dynamic-update-slice_fusion.9, s32[]{:T(128)S(6)} %select_n.57, bf16[128,512]{1,0:T(8,128)(2,1)} %copy-done.7), kind=kLoop, calls=%fused_computation.51 | loop fusion | bytes 262148 | tf_op jit(solution)/shard_map/jit(dynamic_update_index_in_dim)/dynamic_update_slice | solution.py:117
  23.2 1.6 %collective-permute-start.6 = (bf16[264,512]{1,0:T(8,128)(2,1)S(1)}, bf16[264,512]{1,0:T(8,128)(2,1)S(1)}, u32[]{:S(2)}, u32[]{:S(2)}) collective-permute-start(bf16[264,512]{1,0:T(8,128)(2,1)S(1)} %get-tuple-element.49), channel_id=1, source_target_pairs={{0,16},{1,17},{2,18},{3,19},{4,20},{5,21},{6,22},{7,23},{8,24},{9,... | collective-permute-start | bytes 811016 | tf_op jit(solution)/shard_map/ppermute | solution.py:106
  24.8 1.5 %collective-permute-start.5 = (bf16[264,512]{1,0:T(8,128)(2,1)S(1)}, bf16[264,512]{1,0:T(8,128)(2,1)S(1)}, u32[]{:S(2)}, u32[]{:S(2)}) collective-permute-start(bf16[264,512]{1,0:T(8,128)(2,1)S(1)} %get-tuple-element.50), channel_id=1, source_target_pairs={{0,1},{1,0},{2,3},{3,2},{4,5},{5,4},{6,7},{7,6},{8,9},{9,8},{10,11... | collective-permute-start | bytes 811016 | tf_op jit(solution)/shard_map/ppermute | solution.py:106
  26.5 5.7 %collective-permute-done.6 = bf16[264,512]{1,0:T(8,128)(2,1)S(1)} collective-permute-done((bf16[264,512]{1,0:T(8,128)(2,1)S(1)}, bf16[264,512]{1,0:T(8,128)(2,1)S(1)}, u32[]{:S(2)}, u32[]{:S(2)}) %collective-permute-start.6) | collective-permute-done | bytes 270368 | tf_op jit(solution)/shard_map/ppermute | solution.py:106
  32.2 1.2 %collective-permute-done.5 = bf16[264,512]{1,0:T(8,128)(2,1)S(1)} collective-permute-done((bf16[264,512]{1,0:T(8,128)(2,1)S(1)}, bf16[264,512]{1,0:T(8,128)(2,1)S(1)}, u32[]{:S(2)}, u32[]{:S(2)}) %collective-permute-start.5) | collective-permute-done | bytes 270368 | tf_op jit(solution)/shard_map/ppermute | solution.py:106
  34.7 1.6 %collective-permute-start.8 = (bf16[520,512]{1,0:T(8,128)(2,1)S(1)}, bf16[520,512]{1,0:T(8,128)(2,1)S(1)}, u32[]{:S(2)}, u32[]{:S(2)}) collective-permute-start(bf16[520,512]{1,0:T(8,128)(2,1)S(1)} %pad_maximum_fusion.2), channel_id=1, source_target_pairs={{0,1},{1,0},{2,3},{3,2},{4,5},{5,4},{6,7},{7,6},{8,9},{9,8},{10,11... | collective-permute-start | bytes 1597448 | tf_op jit(solution)/shard_map/ppermute | solution.py:106
  38.6 1.6 %collective-permute-start.12 = (f16[4,2,1,64,512]{4,3,2,1,0:T(8,128)(2,1)S(1)}, f16[4,2,1,64,512]{4,3,2,1,0:T(8,128)(2,1)S(1)}, u32[]{:S(2)}, u32[]{:S(2)}) collective-permute-start(f16[4,2,1,64,512]{4,3,2,1,0:T(8,128)(2,1)S(1)} %dynamic-slice_bitcast_fusion), channel_id=1, source_target_pairs={{0,16},{1,17},{2,18},{3,19},{4,20},{5,21},{6,22},{7,23},{8,24},{9,... | collective-permute-start | bytes 1572872 | tf_op jit(solution)/shard_map/ppermute | solution.py:106
  40.9 8.9 %collective-permute-done.8 = bf16[520,512]{1,0:T(8,128)(2,1)S(1)} collective-permute-done((bf16[520,512]{1,0:T(8,128)(2,1)S(1)}, bf16[520,512]{1,0:T(8,128)(2,1)S(1)}, u32[]{:S(2)}, u32[]{:S(2)}) %collective-permute-start.8) | collective-permute-done | bytes 532512 | tf_op jit(solution)/shard_map/ppermute | solution.py:106
  49.9 2.6 %collective-permute-done.7 = bf16[520,512]{1,0:T(8,128)(2,1)S(1)} collective-permute-done((bf16[520,512]{1,0:T(8,128)(2,1)S(1)}, bf16[520,512]{1,0:T(8,128)(2,1)S(1)}, u32[]{:S(2)}, u32[]{:S(2)}) %collective-permute-start.7) | collective-permute-done | bytes 532512 | tf_op jit(solution)/shard_map/ppermute | solution.py:106
  52.9 8.9 %collective-permute-done.12 = f16[4,2,1,64,512]{4,3,2,1,0:T(8,128)(2,1)S(1)} collective-permute-done((f16[4,2,1,64,512]{4,3,2,1,0:T(8,128)(2,1)S(1)}, f16[4,2,1,64,512]{4,3,2,1,0:T(8,128)(2,1)S(1)}, u32[]{:S(2)}, u32[]{:S(2)}) %collective-permute-start.12) | collective-permute-done | bytes 524320 | tf_op jit(solution)/shard_map/ppermute | solution.py:106
  64.6 4.0 %collective-permute-done.13 = f16[4,1,1,64,512]{4,3,2,1,0:T(8,128)(2,1)S(1)} collective-permute-done((f16[4,1,1,64,512]{4,3,2,1,0:T(8,128)(2,1)S(1)}, f16[4,1,1,64,512]{4,3,2,1,0:T(8,128)(2,1)S(1)}, u32[]{:S(2)}, u32[]{:S(2)}) %collective-permute-start.13) | collective-permute-done | bytes 262176 | tf_op jit(solution)/shard_map/ppermute | solution.py:106
  69.9 2.5 %collective-permute-start.16 = (f16[136,512]{1,0:T(8,128)(2,1)S(1)}, f16[136,512]{1,0:T(8,128)(2,1)S(1)}, u32[]{:S(2)}, u32[]{:S(2)}) collective-permute-start(f16[136,512]{1,0:T(8,128)(2,1)S(1)} %get-tuple-element.46), channel_id=1, source_target_pairs={{0,6},{1,7},{2,4},{3,5},{4,2},{5,3},{6,0},{7,1},{8,14},{9,15},{10,... | collective-permute-start | bytes 417800 | tf_op jit(solution)/shard_map/ppermute | solution.py:106
  72.4 1.8 %collective-permute-start.15 = (f16[136,512]{1,0:T(8,128)(2,1)S(1)}, f16[136,512]{1,0:T(8,128)(2,1)S(1)}, u32[]{:S(2)}, u32[]{:S(2)}) collective-permute-start(f16[136,512]{1,0:T(8,128)(2,1)S(1)} %get-tuple-element.47), channel_id=1, source_target_pairs={{0,4},{1,5},{2,6},{3,7},{4,0},{5,1},{6,2},{7,3},{8,12},{9,13},{10,... | collective-permute-start | bytes 417800 | tf_op jit(solution)/shard_map/ppermute | solution.py:106
  75.0 6.6 %shard_map.59 = (bf16[512,512]{1,0:T(8,128)(2,1)}, bf16[512,4096]{1,0:T(8,128)(2,1)}) custom-call(bf16[512,4096]{1,0:T(8,128)(2,1)S(1)} %copy-done.1, bf16[512,512]{1,0:T(8,128)(2,1)S(1)} %copy-done.3, bf16[4,1024,512]{2,1,0:T(8,128)(2,1)S(1)} %bitcast.94), custom_call_target="tpu_custom_call" | custom-call | flops 4294967296 | bytes 14155776 | tf_op jit(solution)/shard_map/pallas_call | solution.py:35
  81.6 1.7 %collective-permute-done.15 = f16[136,512]{1,0:T(8,128)(2,1)S(1)} collective-permute-done((f16[136,512]{1,0:T(8,128)(2,1)S(1)}, f16[136,512]{1,0:T(8,128)(2,1)S(1)}, u32[]{:S(2)}, u32[]{:S(2)}) %collective-permute-start.15) | collective-permute-done | bytes 139296 | tf_op jit(solution)/shard_map/ppermute | solution.py:106
  (91 shorter events, 11.2 us)
Async XLA Ops:
  0.6 2.2 %copy-start = (bf16[512,4096]{1,0:T(8,128)(2,1)S(1)}, bf16[512,4096]{1,0:T(8,128)(2,1)}, u32[]{:S(2)}) copy-start(bf16[512,4096]{1,0:T(8,128)(2,1)} %tok.3) | copy-start | bytes 12582916
  3.9 1.6 %copy-start.6 = (bf16[128,512]{1,0:T(8,128)(2,1)S(1)}, bf16[128,512]{1,0:T(8,128)(2,1)}, u32[]{:S(2)}) copy-start(bf16[128,512]{1,0:T(8,128)(2,1)} %param.4) | copy-start | bytes 393220
  3.9 6.9 %copy-start.3 = (bf16[512,512]{1,0:T(8,128)(2,1)S(1)}, bf16[512,512]{1,0:T(8,128)(2,1)}, u32[]{:S(2)}) copy-start(bf16[512,512]{1,0:T(8,128)(2,1)} %cot.3) | copy-start | bytes 1572868
  4.9 5.8 %collective-permute-start = (f32[8,512]{1,0:T(8,128)S(1)}, f32[8,512]{1,0:T(8,128)S(1)}, u32[]{:S(2)}, u32[]{:S(2)}) collective-permute-start(f32[8,512]{1,0:T(8,128)S(1)} %shard_map.58), channel_id=1, source_target_pairs={{0,8},{1,9},{2,10},{3,11},{4,12},{5,13},{6,14},{7,15},{8,0},{9,1},... | collective-permute-start | bytes 49160 | tf_op jit(solution)/shard_map/ppermute | solution.py:106
  5.4 10.9 %collective-permute-start.2 = (bf16[128,512]{1,0:T(8,128)(2,1)S(1)}, bf16[128,512]{1,0:T(8,128)(2,1)S(1)}, u32[]{:S(2)}, u32[]{:S(2)}) collective-permute-start(bf16[128,512]{1,0:T(8,128)(2,1)S(1)} %copy-done.6), channel_id=1, source_target_pairs={{0,4},{1,5},{2,6},{3,7},{4,0},{5,1},{6,2},{7,3},{8,12},{9,13},{10,... | collective-permute-start | bytes 393224 | tf_op jit(solution)/shard_map/ppermute | solution.py:106
  9.1 7.2 %collective-permute-start.1 = (bf16[128,512]{1,0:T(8,128)(2,1)S(1)}, bf16[128,512]{1,0:T(8,128)(2,1)S(1)}, u32[]{:S(2)}, u32[]{:S(2)}) collective-permute-start(bf16[128,512]{1,0:T(8,128)(2,1)S(1)} %copy-done.6), channel_id=1, source_target_pairs={{0,2},{1,3},{2,0},{3,1},{4,6},{5,7},{6,4},{7,5},{8,10},{9,11},{10,... | collective-permute-start | bytes 393224 | tf_op jit(solution)/shard_map/ppermute | solution.py:106
  10.7 9.4 %collective-permute-start.3 = (bf16[128,512]{1,0:T(8,128)(2,1)S(1)}, bf16[128,512]{1,0:T(8,128)(2,1)S(1)}, u32[]{:S(2)}, u32[]{:S(2)}) collective-permute-start(bf16[128,512]{1,0:T(8,128)(2,1)S(1)} %copy-done.6), channel_id=1, source_target_pairs={{0,6},{1,7},{2,4},{3,5},{4,2},{5,3},{6,0},{7,1},{8,14},{9,15},{10,... | collective-permute-start | bytes 393224 | tf_op jit(solution)/shard_map/ppermute | solution.py:106
  15.3 6.5 %copy-start.4 = (f16[4096,512]{1,0:T(8,128)(2,1)}, f16[4096,512]{1,0:T(8,128)(2,1)S(1)}, u32[]{:S(2)}) copy-start(f16[4096,512]{1,0:T(8,128)(2,1)S(1)} %multiply_convert_fusion) | copy-start | bytes 12582916
  16.3 5.6 %copy-start.7 = (bf16[128,512]{1,0:T(8,128)(2,1)}, bf16[128,512]{1,0:T(8,128)(2,1)S(1)}, u32[]{:S(2)}) copy-start(bf16[128,512]{1,0:T(8,128)(2,1)S(1)} %collective-permute-done.1) | copy-start | bytes 393220
  21.9 11.7 %collective-permute-start.4 = (f16[16,1,128,512]{3,2,0,1:T(8,128)(2,1)}, f16[16,1,128,512]{3,2,0,1:T(8,128)(2,1)S(1)}, u32[]{:S(2)}, u32[]{:S(2)}) collective-permute-start(f16[16,1,128,512]{3,2,0,1:T(8,128)(2,1)} %constant_dynamic-slice_fusion.2), channel_id=1, source_target_pairs={{0,8},{1,9},{2,10},{3,11},{4,12},{5,13},{6,14},{7,15},{8,0},{9,1},... | collective-permute-start | bytes 6291464 | tf_op jit(solution)/shard_map/ppermute | solution.py:106
  22.0 11.6 %copy-start.5 = (f16[4096,512]{1,0:T(8,128)(2,1)S(1)}, f16[4096,512]{1,0:T(8,128)(2,1)}, u32[]{:S(2)}) copy-start(f16[4096,512]{1,0:T(8,128)(2,1)} %copy-done.4) | copy-start | bytes 12582916
  23.2 9.0 %collective-permute-start.6 = (bf16[264,512]{1,0:T(8,128)(2,1)S(1)}, bf16[264,512]{1,0:T(8,128)(2,1)S(1)}, u32[]{:S(2)}, u32[]{:S(2)}) collective-permute-start(bf16[264,512]{1,0:T(8,128)(2,1)S(1)} %get-tuple-element.49), channel_id=1, source_target_pairs={{0,16},{1,17},{2,18},{3,19},{4,20},{5,21},{6,22},{7,23},{8,24},{9,... | collective-permute-start | bytes 811016 | tf_op jit(solution)/shard_map/ppermute | solution.py:106
  24.8 8.6 %collective-permute-start.5 = (bf16[264,512]{1,0:T(8,128)(2,1)S(1)}, bf16[264,512]{1,0:T(8,128)(2,1)S(1)}, u32[]{:S(2)}, u32[]{:S(2)}) collective-permute-start(bf16[264,512]{1,0:T(8,128)(2,1)S(1)} %get-tuple-element.50), channel_id=1, source_target_pairs={{0,1},{1,0},{2,3},{3,2},{4,5},{5,4},{6,7},{7,6},{8,9},{9,8},{10,11... | collective-permute-start | bytes 811016 | tf_op jit(solution)/shard_map/ppermute | solution.py:106
  34.7 15.1 %collective-permute-start.8 = (bf16[520,512]{1,0:T(8,128)(2,1)S(1)}, bf16[520,512]{1,0:T(8,128)(2,1)S(1)}, u32[]{:S(2)}, u32[]{:S(2)}) collective-permute-start(bf16[520,512]{1,0:T(8,128)(2,1)S(1)} %pad_maximum_fusion.2), channel_id=1, source_target_pairs={{0,1},{1,0},{2,3},{3,2},{4,5},{5,4},{6,7},{7,6},{8,9},{9,8},{10,11... | collective-permute-start | bytes 1597448 | tf_op jit(solution)/shard_map/ppermute | solution.py:106
  37.4 15.1 %collective-permute-start.7 = (bf16[520,512]{1,0:T(8,128)(2,1)S(1)}, bf16[520,512]{1,0:T(8,128)(2,1)S(1)}, u32[]{:S(2)}, u32[]{:S(2)}) collective-permute-start(bf16[520,512]{1,0:T(8,128)(2,1)S(1)} %pad_maximum_fusion.1), channel_id=1, source_target_pairs={{0,16},{1,17},{2,18},{3,19},{4,20},{5,21},{6,22},{7,23},{8,24},{9,... | collective-permute-start | bytes 1597448 | tf_op jit(solution)/shard_map/ppermute | solution.py:106
  38.6 23.2 %collective-permute-start.12 = (f16[4,2,1,64,512]{4,3,2,1,0:T(8,128)(2,1)S(1)}, f16[4,2,1,64,512]{4,3,2,1,0:T(8,128)(2,1)S(1)}, u32[]{:S(2)}, u32[]{:S(2)}) collective-permute-start(f16[4,2,1,64,512]{4,3,2,1,0:T(8,128)(2,1)S(1)} %dynamic-slice_bitcast_fusion), channel_id=1, source_target_pairs={{0,16},{1,17},{2,18},{3,19},{4,20},{5,21},{6,22},{7,23},{8,24},{9,... | collective-permute-start | bytes 1572872 | tf_op jit(solution)/shard_map/ppermute | solution.py:106
  40.2 22.5 %collective-permute-start.10 = (f16[4,1,2,64,512]{4,3,2,1,0:T(8,128)(2,1)S(1)}, f16[4,1,2,64,512]{4,3,2,1,0:T(8,128)(2,1)S(1)}, u32[]{:S(2)}, u32[]{:S(2)}) collective-permute-start(f16[4,1,2,64,512]{4,3,2,1,0:T(8,128)(2,1)S(1)} %dynamic-slice_bitcast_fusion.1), channel_id=1, source_target_pairs={{0,1},{1,0},{2,3},{3,2},{4,5},{5,4},{6,7},{7,6},{8,9},{9,8},{10,11... | collective-permute-start | bytes 1572872 | tf_op jit(solution)/shard_map/ppermute | solution.py:106
  52.8 21.9 %collective-permute-start.9 = (bf16[4,2,2,2,64,512]{5,4,3,2,1,0:T(8,128)(2,1)S(1)}, bf16[4,2,2,2,64,512]{5,4,3,2,1,0:T(8,128)(2,1)S(1)}, u32[]{:S(2)}, u32[]{:S(2)}) collective-permute-start(bf16[4,2,2,2,64,512]{5,4,3,2,1,0:T(8,128)(2,1)S(1)} %pad_maximum_fusion), channel_id=1, source_target_pairs={{0,8},{1,9},{2,10},{3,11},{4,12},{5,13},{6,14},{7,15},{8,0},{9,1},... | collective-permute-start | bytes 6291464 | tf_op jit(solution)/shard_map/ppermute | solution.py:106
  62.1 6.5 %collective-permute-start.13 = (f16[4,1,1,64,512]{4,3,2,1,0:T(8,128)(2,1)S(1)}, f16[4,1,1,64,512]{4,3,2,1,0:T(8,128)(2,1)S(1)}, u32[]{:S(2)}, u32[]{:S(2)}) collective-permute-start(f16[4,1,1,64,512]{4,3,2,1,0:T(8,128)(2,1)S(1)} %constant_dynamic-slice_fusion), channel_id=1, source_target_pairs={{0,1},{1,0},{2,3},{3,2},{4,5},{5,4},{6,7},{7,6},{8,9},{9,8},{10,11... | collective-permute-start | bytes 786440 | tf_op jit(solution)/shard_map/ppermute | solution.py:106
  63.1 6.4 %collective-permute-start.11 = (f16[4,1,1,64,512]{4,3,2,1,0:T(8,128)(2,1)S(1)}, f16[4,1,1,64,512]{4,3,2,1,0:T(8,128)(2,1)S(1)}, u32[]{:S(2)}, u32[]{:S(2)}) collective-permute-start(f16[4,1,1,64,512]{4,3,2,1,0:T(8,128)(2,1)S(1)} %constant_dynamic-slice_fusion.1), channel_id=1, source_target_pairs={{0,16},{1,17},{2,18},{3,19},{4,20},{5,21},{6,22},{7,23},{8,24},{9,... | collective-permute-start | bytes 786440 | tf_op jit(solution)/shard_map/ppermute | solution.py:106
  64.6 10.4 %copy-start.1 = (bf16[512,4096]{1,0:T(8,128)(2,1)S(1)}, bf16[512,4096]{1,0:T(8,128)(2,1)}, u32[]{:S(2)}) copy-start(bf16[512,4096]{1,0:T(8,128)(2,1)} %tok.3) | copy-start | bytes 12582916
  69.9 11.7 %collective-permute-start.16 = (f16[136,512]{1,0:T(8,128)(2,1)S(1)}, f16[136,512]{1,0:T(8,128)(2,1)S(1)}, u32[]{:S(2)}, u32[]{:S(2)}) collective-permute-start(f16[136,512]{1,0:T(8,128)(2,1)S(1)} %get-tuple-element.46), channel_id=1, source_target_pairs={{0,6},{1,7},{2,4},{3,5},{4,2},{5,3},{6,0},{7,1},{8,14},{9,15},{10,... | collective-permute-start | bytes 417800 | tf_op jit(solution)/shard_map/ppermute | solution.py:106
  72.4 10.9 %collective-permute-start.15 = (f16[136,512]{1,0:T(8,128)(2,1)S(1)}, f16[136,512]{1,0:T(8,128)(2,1)S(1)}, u32[]{:S(2)}, u32[]{:S(2)}) collective-permute-start(f16[136,512]{1,0:T(8,128)(2,1)S(1)} %get-tuple-element.47), channel_id=1, source_target_pairs={{0,4},{1,5},{2,6},{3,7},{4,0},{5,1},{6,2},{7,3},{8,12},{9,13},{10,... | collective-permute-start | bytes 417800 | tf_op jit(solution)/shard_map/ppermute | solution.py:106
  74.2 9.2 %collective-permute-start.14 = (f16[136,512]{1,0:T(8,128)(2,1)S(1)}, f16[136,512]{1,0:T(8,128)(2,1)S(1)}, u32[]{:S(2)}, u32[]{:S(2)}) collective-permute-start(f16[136,512]{1,0:T(8,128)(2,1)S(1)} %get-tuple-element.48), channel_id=1, source_target_pairs={{0,2},{1,3},{2,0},{3,1},{4,6},{5,7},{6,4},{7,5},{8,10},{9,11},{10,... | collective-permute-start | bytes 417800 | tf_op jit(solution)/shard_map/ppermute | solution.py:106
  (1 other events, 1.0 us)

commit v6 on v5

--- a/solution.py
+++ b/solution.py
@@ -42,12 +42,7 @@
             jax.ShapeDtypeStruct((rows, kd), jnp.bfloat16),
             jax.ShapeDtypeStruct(tokens.shape, jnp.bfloat16),
         ],
-        compiler_params=pltpu.CompilerParams(vmem_limit_bytes=24 * 1024 * 1024),
-        cost_estimate=pl.CostEstimate(
-            flops=4 * rows * steps * depth * kd,
-            bytes_accessed=2 * (2 * rows * steps * depth + steps * depth * kd + 3 * rows * kd),
-            transcendentals=0,
-        ),
+        compiler_params=pltpu.CompilerParams(vmem_limit_bytes=12 * 1024 * 1024),
     )(tokens, cotangent, weight)
 
 
@@ -82,7 +77,7 @@
         out_specs=pl.BlockSpec((NOTE, kd), lambda i: (0, 0)),
         scratch_shapes=[pltpu.VMEM((NOTE, kd), jnp.float32)],
         out_shape=jax.ShapeDtypeStruct((NOTE, kd), jnp.float32),
-        compiler_params=pltpu.CompilerParams(vmem_limit_bytes=40 * 1024 * 1024),
+        compiler_params=pltpu.CompilerParams(vmem_limit_bytes=60 * 1024 * 1024),
         cost_estimate=pl.CostEstimate(
             flops=2 * rows * width, bytes_accessed=2 * rows * (width + kd), transcendentals=0
         ),
@@ -132,45 +127,48 @@
     def scale(power):
         return jnp.exp2(power)
 
-    def bound(power, others):
+    def factors(power, others):
+        top = power
         for other in others:
-            power = jnp.maximum(power, other)
-        return power + len(others).bit_length()
-
-    def sums(value, name, axis, power, others):
+            top = jnp.maximum(top, other)
+        top = top + len(others).bit_length()
+        return top, [scale(one - top) for one in [power, *others]]
+
+    def sums(value, name, axis, factor, *places):
         me = place[name]
-        got = [swap(pick(value, (axis, me ^ j)), name, j) for j in range(1, size[name])]
-        top = bound(power, others)
-        total = pick(value, (axis, me)).astype(jnp.float32) * scale(power - top)
-        for one, other in zip(got, others):
-            total = total + one.astype(jnp.float32) * scale(other - top)
-        return total.astype(jnp.float16), top
+        got = [swap(pick(value, (axis, me ^ j), *places), name, j) for j in range(1, size[name])]
+        total = pick(value, (axis, me), *places).astype(jnp.float32) * factor[0]
+        for one, other in zip(got, factor[1:]):
+            total = total + one.astype(jnp.float32) * other
+        return total.astype(jnp.float16)
 
     shards = [swap(key_weight, "z", j) for j in range(1, nz)]
 
-    power = bound_of(tokens, cotangent)
+    power, shards[0] = lax.optimization_barrier((bound_of(tokens, cotangent), shards[0]))
     power = jnp.maximum(power, swap(power, "core", 1))[:1] + 1.0
     part = lax.dot_general(
         tokens, cotangent, (((0,), (0,)), ((), ())), preferred_element_type=jnp.float32
     )
     part = (part * scale(TOP - power)).astype(jnp.float16).reshape(nz * nx * ny, 2, rows, kd)
+    other = swap(pick(part, (1, 1 - core)), "core", 1)
     part, shards = lax.optimization_barrier((part, shards))
     shards = in_order(key_weight, shards, "z")
-    other = swap(pick(part, (1, 1 - core)), "core", 1)
     part = pick(part, (1, core)).astype(jnp.float32) + other.astype(jnp.float32)
-    part = part.astype(jnp.float16)
-    part = part.reshape(nz, nx, ny, 2, half, kd)
+    part = part.astype(jnp.float16).reshape(nz, nx, ny, rows, kd)
 
     blocks = shards.reshape(nz, 2, half, kd)
     one, power_x = gathered(blocks[:, 0], "x", power)
     two, power_y = gathered(blocks[:, 1], "y", power)
-    part, one, two = lax.optimization_barrier((part, one, two))
-    sum_one, top_one = sums(part[:, :, :, 0], "x", 1, power, power_x)
-    sum_two, top_two = sums(part[:, :, :, 1], "y", 2, power, power_y)
-    one, power_xy = gathered(one, "y", top_one)
-    two, power_yx = gathered(two, "x", top_two)
-    sum_one, top_one = sums(sum_one, "y", 2, top_one, power_xy)
-    sum_two, top_two = sums(sum_two, "x", 1, top_two, power_yx)
+    by_x, by_y = factors(power, power_x), factors(power, power_y)
+    part, one, two, by_x, by_y = lax.optimization_barrier((part, one, two, by_x, by_y))
+    sum_one = sums(part, "x", 1, by_x[1], (3, 0, half))
+    sum_two = sums(part, "y", 2, by_y[1], (3, half, half))
+    one, power_xy = gathered(one, "y", by_x[0])
+    two, power_yx = gathered(two, "x", by_y[0])
+    by_xy, by_yx = factors(by_x[0], power_xy), factors(by_y[0], power_yx)
+    top_one = by_xy[0]
+    sum_one = sums(sum_one, "y", 2, by_xy[1])
+    sum_two = sums(sum_two, "x", 1, by_yx[1])
     both = jnp.stack([one.transpose(2, 1, 0, 3, 4), two.transpose(2, 0, 1, 3, 4)], axis=3)
     weight = in_order(both, [swap(both, "core", 1)], "core")
     weight = weight.transpose(1, 2, 3, 0, 4, 5, 6).reshape(nz, nx * ny * 2 * rows, kd)

time: 84.5 us -> 76.9 us (0.910)
  local copies, waits for them, and re-layouts: 9.68 us -> 2.49 us
  waiting for transfers between devices: 38.5 us -> 33.8 us
  Pallas kernels: 7.66 us -> 10.7 us
    ppermute x17, waiting for transfers between devices: 38.5 us -> 33.8 us  [swap(): lax.ppermute(value, AXES, [(i, i ^ j * mask[name]) for i in range(wide *...]
    pallas_call x1, Pallas kernels: 1.03 us -> 4.02 us  [bound_of(): pl.pallas_call(bound_kernel, grid=(rows // block,), in_specs=[pl.BlockSpe...]
    unnamed x16 -> x7, local copies, waits for them, and re-layouts: 3.25 us -> 0.51 us
    dynamic_slice x5 -> x4, local copies, waits for them, and re-layouts: 2.16 us -> 0.32 us  [pick(): return lax.dynamic_slice(value, start, extent)]
    optimization_barrier x4 -> x2, local copies, waits for them, and re-layouts: 1.17 us -> 0.07 us  [on_device(): lax.optimization_barrier((part, one, two, by_x, by_y))]
    dynamic_update_slice x12 -> x13, local copies, waits for them, and re-layouts: 1.67 us -> 0.61 us  [in_order(): out = lax.dynamic_update_index_in_dim(out, part, place[name] ^ j, 0)]
  transfers between devices with their start and end apart: 17 -> 17, of which waited for: 10 -> 9; matrix products, arithmetic and copies ran while one was open for 13% -> 11% of each run, Pallas kernels for 8% -> 14%
where the time goes in v6:
time: 76.9 us; the launch traced here: 76.6 us
  waiting for transfers between devices  33.8 us (44%)
  starting transfers between devices  19.9 us (26%)
  Pallas kernels  10.7 us (14%)
  matrix products  4.58 us (6%)
  other arithmetic  4.07 us (5%)
  local copies, waits for them, and re-layouts  2.49 us (3%)
  between operations  1.15 us (1%)
    ppermute x17, waiting for transfers between devices, swap(): lax.ppermute(value, AXES, [(i, i ^ j * mask[name]) for i in range(wide *...  33.8 us
    ppermute x17, starting transfers between devices, swap(): lax.ppermute(value, AXES, [(i, i ^ j * mask[name]) for i in range(wide *...  19.9 us
    pallas_call x1, Pallas kernels, products(): pl.pallas_call(products_kernel, grid=(steps,), in_specs=[columns, whole,...  6.63 us
    dot_general x1, matrix products, on_device(): lax.dot_general(tokens, cotangent, (((0,), (0,)), ((), ())), preferred_el...  4.58 us
    pallas_call x1, Pallas kernels, bound_of(): pl.pallas_call(bound_kernel, grid=(rows // block,), in_specs=[pl.BlockSpe...  4.02 us
  transfers between devices with their start and end apart: 17, of which 9 were waited for; matrix products, arithmetic and copies ran while one was open for 11% of the time, Pallas kernels for 14%

profile of v6, /device:TPU:0, one launch (start us, length us, event | category | flops | bytes accessed | tf_op | source)
XLA Modules:
  0.0 76.6 jit_solution(8679905260983181318)
XLA Ops:
  0.7 3.1 %collective-permute-start = (bf16[128,512]{1,0:T(8,128)(2,1)}, bf16[128,512]{1,0:T(8,128)(2,1)S(1)}, u32[]{:S(2)}, u32[]{:S(2)}) collective-permute-start(bf16[128,512]{1,0:T(8,128)(2,1)} %param.4), channel_id=1, source_target_pairs={{0,2},{1,3},{2,0},{3,1},{4,6},{5,7},{6,4},{7,5},{8,10},{9,11},{10,... | collective-permute-start | bytes 393224 | tf_op jit(solution)/shard_map/ppermute | solution.py:101
  3.7 2.6 %collective-permute-start.2 = (bf16[128,512]{1,0:T(8,128)(2,1)}, bf16[128,512]{1,0:T(8,128)(2,1)S(1)}, u32[]{:S(2)}, u32[]{:S(2)}) collective-permute-start(bf16[128,512]{1,0:T(8,128)(2,1)} %param.4), channel_id=1, source_target_pairs={{0,4},{1,5},{2,6},{3,7},{4,0},{5,1},{6,2},{7,3},{8,12},{9,13},{10,... | collective-permute-start | bytes 393224 | tf_op jit(solution)/shard_map/ppermute | solution.py:101
  6.3 4.0 %shard_map.58 = f32[8,512]{1,0:T(8,128)} custom-call(bf16[512,4096]{1,0:T(8,128)(2,1)} %tok.3, bf16[512,512]{1,0:T(8,128)(2,1)} %cot.3), custom_call_target="tpu_custom_call" | custom-call | flops 4194304 | bytes 4718592 | tf_op jit(solution)/shard_map/pallas_call | solution.py:70
  10.5 1.3 %collective-permute-done.1 = f32[8,512]{1,0:T(8,128)S(1)} collective-permute-done((f32[8,512]{1,0:T(8,128)}, f32[8,512]{1,0:T(8,128)S(1)}, u32[]{:S(2)}, u32[]{:S(2)}) %collective-permute-start.1) | collective-permute-done | bytes 16416 | tf_op jit(solution)/shard_map/ppermute | solution.py:101
  11.8 0.7 convert_reduce_fusion.3
  12.5 4.6 %multiply_convert_fusion = f16[4096,512]{1,0:T(8,128)(2,1)S(1)} fusion(bf16[512,4096]{1,0:T(8,128)(2,1)} %tok.3, bf16[512,512]{1,0:T(8,128)(2,1)S(1)} %copy-done.1, f32[512]{0:T(512)S(1)} %bitcast.118), kind=kOutput, calls=%fused_computation | convolution fusion | flops 2151677952 | bytes 8914944 | tf_op jit(solution)/shard_map/dot_general | solution.py:149
  18.0 1.8 %collective-permute-start.6 = (bf16[264,512]{1,0:T(8,128)(2,1)S(1)}, bf16[264,512]{1,0:T(8,128)(2,1)S(1)}, u32[]{:S(2)}, u32[]{:S(2)}) collective-permute-start(bf16[264,512]{1,0:T(8,128)(2,1)S(1)} %get-tuple-element.65), channel_id=1, source_target_pairs={{0,16},{1,17},{2,18},{3,19},{4,20},{5,21},{6,22},{7,23},{8,24},{9,... | collective-permute-start | bytes 811016 | tf_op jit(solution)/shard_map/ppermute | solution.py:101
  19.8 1.5 %collective-permute-start.5 = (bf16[264,512]{1,0:T(8,128)(2,1)S(1)}, bf16[264,512]{1,0:T(8,128)(2,1)S(1)}, u32[]{:S(2)}, u32[]{:S(2)}) collective-permute-start(bf16[264,512]{1,0:T(8,128)(2,1)S(1)} %get-tuple-element.66), channel_id=1, source_target_pairs={{0,1},{1,0},{2,3},{3,2},{4,5},{5,4},{6,7},{7,6},{8,9},{9,8},{10,11... | collective-permute-start | bytes 811016 | tf_op jit(solution)/shard_map/ppermute | solution.py:101
  21.5 5.3 %collective-permute-done.6 = bf16[264,512]{1,0:T(8,128)(2,1)S(1)} collective-permute-done((bf16[264,512]{1,0:T(8,128)(2,1)S(1)}, bf16[264,512]{1,0:T(8,128)(2,1)S(1)}, u32[]{:S(2)}, u32[]{:S(2)}) %collective-permute-start.6) | collective-permute-done | bytes 270368 | tf_op jit(solution)/shard_map/ppermute | solution.py:101
  26.9 1.4 %collective-permute-done.5 = bf16[264,512]{1,0:T(8,128)(2,1)S(1)} collective-permute-done((bf16[264,512]{1,0:T(8,128)(2,1)S(1)}, bf16[264,512]{1,0:T(8,128)(2,1)S(1)}, u32[]{:S(2)}, u32[]{:S(2)}) %collective-permute-start.5) | collective-permute-done | bytes 270368 | tf_op jit(solution)/shard_map/ppermute | solution.py:101
  28.4 0.8 %add_convert_fusion = f16[16,1,128,512]{3,2,0,1:T(8,128)(2,1)S(1)} fusion(f16[16,1,128,512]{3,2,0,1:T(8,128)(2,1)S(1)} %collective-permute-done.4, s32[]{:T(128)S(6)} %select_n.54, f16[16,2,128,512]{3,2,1,0:T(8,128)(2,1)S(1)} %bitcast.97), kind=kLoop, calls=%fused_computation.1 | loop fusion | flops 4194304 | bytes 6291460 | tf_op jit(solution)/shard_map/convert_element_type | solution.py:157
  29.6 1.6 %collective-permute-start.8 = (bf16[520,512]{1,0:T(8,128)(2,1)S(1)}, bf16[520,512]{1,0:T(8,128)(2,1)S(1)}, u32[]{:S(2)}, u32[]{:S(2)}) collective-permute-start(bf16[520,512]{1,0:T(8,128)(2,1)S(1)} %pad_maximum_fusion.2), channel_id=1, source_target_pairs={{0,1},{1,0},{2,3},{3,2},{4,5},{5,4},{6,7},{7,6},{8,9},{9,8},{10,11... | collective-permute-start | bytes 1597448 | tf_op jit(solution)/shard_map/ppermute | solution.py:101
  32.4 1.7 %collective-permute-start.12 = (f16[4,2,1,64,512]{4,3,2,1,0:T(8,128)(2,1)S(1)}, f16[4,2,1,64,512]{4,3,2,1,0:T(8,128)(2,1)S(1)}, u32[]{:S(2)}, u32[]{:S(2)}) collective-permute-start(f16[4,2,1,64,512]{4,3,2,1,0:T(8,128)(2,1)S(1)} %constant_dynamic-slice_fusion.1), channel_id=1, source_target_pairs={{0,16},{1,17},{2,18},{3,19},{4,20},{5,21},{6,22},{7,23},{8,24},{9,... | collective-permute-start | bytes 1572872 | tf_op jit(solution)/shard_map/ppermute | solution.py:101
  34.3 10.4 %collective-permute-done.8 = bf16[520,512]{1,0:T(8,128)(2,1)S(1)} collective-permute-done((bf16[520,512]{1,0:T(8,128)(2,1)S(1)}, bf16[520,512]{1,0:T(8,128)(2,1)S(1)}, u32[]{:S(2)}, u32[]{:S(2)}) %collective-permute-start.8) | collective-permute-done | bytes 532512 | tf_op jit(solution)/shard_map/ppermute | solution.py:101
  44.8 1.5 %collective-permute-done.7 = bf16[520,512]{1,0:T(8,128)(2,1)S(1)} collective-permute-done((bf16[520,512]{1,0:T(8,128)(2,1)S(1)}, bf16[520,512]{1,0:T(8,128)(2,1)S(1)}, u32[]{:S(2)}, u32[]{:S(2)}) %collective-permute-start.7) | collective-permute-done | bytes 532512 | tf_op jit(solution)/shard_map/ppermute | solution.py:101
  46.7 7.4 %collective-permute-done.10 = f16[4,1,2,64,512]{4,3,2,1,0:T(8,128)(2,1)S(1)} collective-permute-done((f16[4,1,2,64,512]{4,3,2,1,0:T(8,128)(2,1)S(1)}, f16[4,1,2,64,512]{4,3,2,1,0:T(8,128)(2,1)S(1)}, u32[]{:S(2)}, u32[]{:S(2)}) %collective-permute-start.10) | collective-permute-done | bytes 524320 | tf_op jit(solution)/shard_map/ppermute | solution.py:101
  54.4 0.7 collective-permute-start.11
  55.7 1.2 %collective-permute-start.13 = (f16[4,1,1,64,512]{4,3,2,1,0:T(8,128)(2,1)S(1)}, f16[4,1,1,64,512]{4,3,2,1,0:T(8,128)(2,1)S(1)}, u32[]{:S(2)}, u32[]{:S(2)}) collective-permute-start(f16[4,1,1,64,512]{4,3,2,1,0:T(8,128)(2,1)S(1)} %constant_dynamic-slice_fusion), channel_id=1, source_target_pairs={{0,1},{1,0},{2,3},{3,2},{4,5},{5,4},{6,7},{7,6},{8,9},{9,8},{10,11... | collective-permute-start | bytes 786440 | tf_op jit(solution)/shard_map/ppermute | solution.py:101
  57.8 4.3 %collective-permute-done.13 = f16[4,1,1,64,512]{4,3,2,1,0:T(8,128)(2,1)S(1)} collective-permute-done((f16[4,1,1,64,512]{4,3,2,1,0:T(8,128)(2,1)S(1)}, f16[4,1,1,64,512]{4,3,2,1,0:T(8,128)(2,1)S(1)}, u32[]{:S(2)}, u32[]{:S(2)}) %collective-permute-start.13) | collective-permute-done | bytes 262176 | tf_op jit(solution)/shard_map/ppermute | solution.py:101
  62.7 3.7 %collective-permute-start.16 = (f16[136,512]{1,0:T(8,128)(2,1)S(1)}, f16[136,512]{1,0:T(8,128)(2,1)S(1)}, u32[]{:S(2)}, u32[]{:S(2)}) collective-permute-start(f16[136,512]{1,0:T(8,128)(2,1)S(1)} %get-tuple-element.62), channel_id=1, source_target_pairs={{0,6},{1,7},{2,4},{3,5},{4,2},{5,3},{6,0},{7,1},{8,14},{9,15},{10,... | collective-permute-start | bytes 417800 | tf_op jit(solution)/shard_map/ppermute | solution.py:101
  66.4 0.8 %collective-permute-start.14 = (f16[136,512]{1,0:T(8,128)(2,1)S(1)}, f16[136,512]{1,0:T(8,128)(2,1)S(1)}, u32[]{:S(2)}, u32[]{:S(2)}) collective-permute-start(f16[136,512]{1,0:T(8,128)(2,1)S(1)} %get-tuple-element.64), channel_id=1, source_target_pairs={{0,2},{1,3},{2,0},{3,1},{4,6},{5,7},{6,4},{7,5},{8,10},{9,11},{10,... | collective-permute-start | bytes 417800 | tf_op jit(solution)/shard_map/ppermute | solution.py:101
  67.4 6.6 %shard_map.59 = (bf16[512,512]{1,0:T(8,128)(2,1)}, bf16[512,4096]{1,0:T(8,128)(2,1)}) custom-call(bf16[512,4096]{1,0:T(8,128)(2,1)S(1)} %copy-done, bf16[512,512]{1,0:T(8,128)(2,1)S(1)} %copy-done.1, bf16[4,1024,512]{2,1,0:T(8,128)(2,1)S(1)} %bitcast.86), custom_call_target="tpu_custom_call" | custom-call | tf_op jit(solution)/shard_map/pallas_call | solution.py:35
  74.1 1.7 %collective-permute-done.15 = f16[136,512]{1,0:T(8,128)(2,1)S(1)} collective-permute-done((f16[136,512]{1,0:T(8,128)(2,1)S(1)}, f16[136,512]{1,0:T(8,128)(2,1)S(1)}, u32[]{:S(2)}, u32[]{:S(2)}) %collective-permute-start.15) | collective-permute-done | bytes 139296 | tf_op jit(solution)/shard_map/ppermute | solution.py:101
  75.8 0.8 %fusion.3 = f32[128,512]{1,0:T(8,128)} fusion(s32[]{:T(128)S(6)} %select_n.56, f16[4,1,1,64,512]{4,3,2,1,0:T(8,128)(2,1)S(1)} %add_convert_fusion.4, f16[4,1,1,64,512]{4,3,2,1,0:T(8,128)(2,1)S(1)} %add_convert_fusion.3, f32[512]{0:T(512)S(1)} %bitcast.114, f16[136,512]{1,0:T(8,128)(2,1)S(1)} %collective-permute-done.16, f32[512]{0:T(512)S(1)} %bitcast.113, ...), kind=kLoop, calls=%fused_computation.30 | loop fusion | flops 851968 | bytes 1187844 | tf_op jit(solution)/shard_map/mul | solution.py:188
  (79 shorter events, 5.8 us)
Async XLA Ops:
  0.6 9.8 %copy-start.2 = (bf16[128,512]{1,0:T(8,128)(2,1)S(1)}, bf16[128,512]{1,0:T(8,128)(2,1)}, u32[]{:S(2)}) copy-start(bf16[128,512]{1,0:T(8,128)(2,1)} %param.4) | copy-start | bytes 393220
  0.6 11.9 %copy-start.1 = (bf16[512,512]{1,0:T(8,128)(2,1)S(1)}, bf16[512,512]{1,0:T(8,128)(2,1)}, u32[]{:S(2)}) copy-start(bf16[512,512]{1,0:T(8,128)(2,1)} %cot.3) | copy-start | bytes 1572868
  0.7 9.7 %collective-permute-start = (bf16[128,512]{1,0:T(8,128)(2,1)}, bf16[128,512]{1,0:T(8,128)(2,1)S(1)}, u32[]{:S(2)}, u32[]{:S(2)}) collective-permute-start(bf16[128,512]{1,0:T(8,128)(2,1)} %param.4), channel_id=1, source_target_pairs={{0,2},{1,3},{2,0},{3,1},{4,6},{5,7},{6,4},{7,5},{8,10},{9,11},{10,... | collective-permute-start | bytes 393224 | tf_op jit(solution)/shard_map/ppermute | solution.py:101
  3.7 13.4 %collective-permute-start.2 = (bf16[128,512]{1,0:T(8,128)(2,1)}, bf16[128,512]{1,0:T(8,128)(2,1)S(1)}, u32[]{:S(2)}, u32[]{:S(2)}) collective-permute-start(bf16[128,512]{1,0:T(8,128)(2,1)} %param.4), channel_id=1, source_target_pairs={{0,4},{1,5},{2,6},{3,7},{4,0},{5,1},{6,2},{7,3},{8,12},{9,13},{10,... | collective-permute-start | bytes 393224 | tf_op jit(solution)/shard_map/ppermute | solution.py:101
  6.3 10.8 %collective-permute-start.3 = (bf16[128,512]{1,0:T(8,128)(2,1)}, bf16[128,512]{1,0:T(8,128)(2,1)S(1)}, u32[]{:S(2)}, u32[]{:S(2)}) collective-permute-start(bf16[128,512]{1,0:T(8,128)(2,1)} %param.4), channel_id=1, source_target_pairs={{0,6},{1,7},{2,4},{3,5},{4,2},{5,3},{6,0},{7,1},{8,14},{9,15},{10,... | collective-permute-start | bytes 393224 | tf_op jit(solution)/shard_map/ppermute | solution.py:101
  10.4 1.4 %collective-permute-start.1 = (f32[8,512]{1,0:T(8,128)}, f32[8,512]{1,0:T(8,128)S(1)}, u32[]{:S(2)}, u32[]{:S(2)}) collective-permute-start(f32[8,512]{1,0:T(8,128)} %shard_map.58), channel_id=1, source_target_pairs={{0,8},{1,9},{2,10},{3,11},{4,12},{5,13},{6,14},{7,15},{8,0},{9,1},... | collective-permute-start | bytes 49160 | tf_op jit(solution)/shard_map/ppermute | solution.py:101
  17.6 10.8 %collective-permute-start.4 = (f16[16,1,128,512]{3,2,0,1:T(8,128)(2,1)S(1)}, f16[16,1,128,512]{3,2,0,1:T(8,128)(2,1)S(1)}, u32[]{:S(2)}, u32[]{:S(2)}) collective-permute-start(f16[16,1,128,512]{3,2,0,1:T(8,128)(2,1)S(1)} %dynamic-slice_bitcast_fusion), channel_id=1, source_target_pairs={{0,8},{1,9},{2,10},{3,11},{4,12},{5,13},{6,14},{7,15},{8,0},{9,1},... | collective-permute-start | bytes 6291464 | tf_op jit(solution)/shard_map/ppermute | solution.py:101
  18.0 8.8 %collective-permute-start.6 = (bf16[264,512]{1,0:T(8,128)(2,1)S(1)}, bf16[264,512]{1,0:T(8,128)(2,1)S(1)}, u32[]{:S(2)}, u32[]{:S(2)}) collective-permute-start(bf16[264,512]{1,0:T(8,128)(2,1)S(1)} %get-tuple-element.65), channel_id=1, source_target_pairs={{0,16},{1,17},{2,18},{3,19},{4,20},{5,21},{6,22},{7,23},{8,24},{9,... | collective-permute-start | bytes 811016 | tf_op jit(solution)/shard_map/ppermute | solution.py:101
  19.8 8.5 %collective-permute-start.5 = (bf16[264,512]{1,0:T(8,128)(2,1)S(1)}, bf16[264,512]{1,0:T(8,128)(2,1)S(1)}, u32[]{:S(2)}, u32[]{:S(2)}) collective-permute-start(bf16[264,512]{1,0:T(8,128)(2,1)S(1)} %get-tuple-element.66), channel_id=1, source_target_pairs={{0,1},{1,0},{2,3},{3,2},{4,5},{5,4},{6,7},{7,6},{8,9},{9,8},{10,11... | collective-permute-start | bytes 811016 | tf_op jit(solution)/shard_map/ppermute | solution.py:101
  29.6 15.1 %collective-permute-start.8 = (bf16[520,512]{1,0:T(8,128)(2,1)S(1)}, bf16[520,512]{1,0:T(8,128)(2,1)S(1)}, u32[]{:S(2)}, u32[]{:S(2)}) collective-permute-start(bf16[520,512]{1,0:T(8,128)(2,1)S(1)} %pad_maximum_fusion.2), channel_id=1, source_target_pairs={{0,1},{1,0},{2,3},{3,2},{4,5},{5,4},{6,7},{7,6},{8,9},{9,8},{10,11... | collective-permute-start | bytes 1597448 | tf_op jit(solution)/shard_map/ppermute | solution.py:101
  31.2 15.1 %collective-permute-start.7 = (bf16[520,512]{1,0:T(8,128)(2,1)S(1)}, bf16[520,512]{1,0:T(8,128)(2,1)S(1)}, u32[]{:S(2)}, u32[]{:S(2)}) collective-permute-start(bf16[520,512]{1,0:T(8,128)(2,1)S(1)} %pad_maximum_fusion.1), channel_id=1, source_target_pairs={{0,16},{1,17},{2,18},{3,19},{4,20},{5,21},{6,22},{7,23},{8,24},{9,... | collective-permute-start | bytes 1597448 | tf_op jit(solution)/shard_map/ppermute | solution.py:101
  32.0 22.1 %collective-permute-start.10 = (f16[4,1,2,64,512]{4,3,2,1,0:T(8,128)(2,1)S(1)}, f16[4,1,2,64,512]{4,3,2,1,0:T(8,128)(2,1)S(1)}, u32[]{:S(2)}, u32[]{:S(2)}) collective-permute-start(f16[4,1,2,64,512]{4,3,2,1,0:T(8,128)(2,1)S(1)} %constant_dynamic-slice_fusion.3), channel_id=1, source_target_pairs={{0,1},{1,0},{2,3},{3,2},{4,5},{5,4},{6,7},{7,6},{8,9},{9,8},{10,11... | collective-permute-start | bytes 1572872 | tf_op jit(solution)/shard_map/ppermute | solution.py:101
  32.4 23.0 %collective-permute-start.12 = (f16[4,2,1,64,512]{4,3,2,1,0:T(8,128)(2,1)S(1)}, f16[4,2,1,64,512]{4,3,2,1,0:T(8,128)(2,1)S(1)}, u32[]{:S(2)}, u32[]{:S(2)}) collective-permute-start(f16[4,2,1,64,512]{4,3,2,1,0:T(8,128)(2,1)S(1)} %constant_dynamic-slice_fusion.1), channel_id=1, source_target_pairs={{0,16},{1,17},{2,18},{3,19},{4,20},{5,21},{6,22},{7,23},{8,24},{9,... | collective-permute-start | bytes 1572872 | tf_op jit(solution)/shard_map/ppermute | solution.py:101
  46.6 20.5 %collective-permute-start.9 = (bf16[4,2,2,2,64,512]{5,4,3,2,1,0:T(8,128)(2,1)S(1)}, bf16[4,2,2,2,64,512]{5,4,3,2,1,0:T(8,128)(2,1)S(1)}, u32[]{:S(2)}, u32[]{:S(2)}) collective-permute-start(bf16[4,2,2,2,64,512]{5,4,3,2,1,0:T(8,128)(2,1)S(1)} %pad_maximum_fusion), channel_id=1, source_target_pairs={{0,8},{1,9},{2,10},{3,11},{4,12},{5,13},{6,14},{7,15},{8,0},{9,1},... | collective-permute-start | bytes 6291464 | tf_op jit(solution)/shard_map/ppermute | solution.py:101
  54.4 7.9 %collective-permute-start.11 = (f16[4,1,1,64,512]{4,3,2,1,0:T(8,128)(2,1)S(1)}, f16[4,1,1,64,512]{4,3,2,1,0:T(8,128)(2,1)S(1)}, u32[]{:S(2)}, u32[]{:S(2)}) collective-permute-start(f16[4,1,1,64,512]{4,3,2,1,0:T(8,128)(2,1)S(1)} %constant_dynamic-slice_fusion.2), channel_id=1, source_target_pairs={{0,16},{1,17},{2,18},{3,19},{4,20},{5,21},{6,22},{7,23},{8,24},{9,... | collective-permute-start | bytes 786440 | tf_op jit(solution)/shard_map/ppermute | solution.py:101
  55.7 6.4 %collective-permute-start.13 = (f16[4,1,1,64,512]{4,3,2,1,0:T(8,128)(2,1)S(1)}, f16[4,1,1,64,512]{4,3,2,1,0:T(8,128)(2,1)S(1)}, u32[]{:S(2)}, u32[]{:S(2)}) collective-permute-start(f16[4,1,1,64,512]{4,3,2,1,0:T(8,128)(2,1)S(1)} %constant_dynamic-slice_fusion), channel_id=1, source_target_pairs={{0,1},{1,0},{2,3},{3,2},{4,5},{5,4},{6,7},{7,6},{8,9},{9,8},{10,11... | collective-permute-start | bytes 786440 | tf_op jit(solution)/shard_map/ppermute | solution.py:101
  57.8 9.6 %copy-start = (bf16[512,4096]{1,0:T(8,128)(2,1)S(1)}, bf16[512,4096]{1,0:T(8,128)(2,1)}, u32[]{:S(2)}) copy-start(bf16[512,4096]{1,0:T(8,128)(2,1)} %tok.3) | copy-start | bytes 12582916
  62.7 11.4 %collective-permute-start.16 = (f16[136,512]{1,0:T(8,128)(2,1)S(1)}, f16[136,512]{1,0:T(8,128)(2,1)S(1)}, u32[]{:S(2)}, u32[]{:S(2)}) collective-permute-start(f16[136,512]{1,0:T(8,128)(2,1)S(1)} %get-tuple-element.62), channel_id=1, source_target_pairs={{0,6},{1,7},{2,4},{3,5},{4,2},{5,3},{6,0},{7,1},{8,14},{9,15},{10,... | collective-permute-start | bytes 417800 | tf_op jit(solution)/shard_map/ppermute | solution.py:101
  66.4 9.4 %collective-permute-start.15 = (f16[136,512]{1,0:T(8,128)(2,1)S(1)}, f16[136,512]{1,0:T(8,128)(2,1)S(1)}, u32[]{:S(2)}, u32[]{:S(2)}) collective-permute-start(f16[136,512]{1,0:T(8,128)(2,1)S(1)} %get-tuple-element.63), channel_id=1, source_target_pairs={{0,4},{1,5},{2,6},{3,7},{4,0},{5,1},{6,2},{7,3},{8,12},{9,13},{10,... | collective-permute-start | bytes 417800 | tf_op jit(solution)/shard_map/ppermute | solution.py:101
  66.4 9.4 %collective-permute-start.14 = (f16[136,512]{1,0:T(8,128)(2,1)S(1)}, f16[136,512]{1,0:T(8,128)(2,1)S(1)}, u32[]{:S(2)}, u32[]{:S(2)}) collective-permute-start(f16[136,512]{1,0:T(8,128)(2,1)S(1)} %get-tuple-element.64), channel_id=1, source_target_pairs={{0,2},{1,3},{2,0},{3,1},{4,6},{5,7},{6,4},{7,5},{8,10},{9,11},{10,... | collective-permute-start | bytes 417800 | tf_op jit(solution)/shard_map/ppermute | solution.py:101

commit v7 on v6

--- a/solution.py
+++ b/solution.py
@@ -48,12 +48,16 @@
 
 def bound_kernel(tok, cot, power, total):
     step = pl.program_id(0)
+    lanes = 128
 
     @pl.when(step == 0)
     def _():
         total[...] = jnp.zeros_like(total)
 
-    reach = jnp.max(jnp.abs(tok[...]).astype(jnp.float32), axis=1, keepdims=True)
+    reach = jnp.abs(tok[:, :lanes])
+    for first in range(lanes, tok.shape[1], lanes):
+        reach = jnp.maximum(reach, jnp.abs(tok[:, first : first + lanes]))
+    reach = jnp.max(reach.astype(jnp.float32), axis=1, keepdims=True)
     terms = reach * jnp.abs(cot[...]).astype(jnp.float32)
     total[...] += jnp.sum(terms.reshape(-1, NOTE, terms.shape[1]), axis=0)
 
@@ -66,7 +70,7 @@
 def bound_of(tokens, cotangent):
     rows, width = tokens.shape
     kd = cotangent.shape[1]
-    block = min(rows, 128)
+    block = min(rows, 64)
     return pl.pallas_call(
         bound_kernel,
         grid=(rows // block,),
@@ -134,55 +138,83 @@
         top = top + len(others).bit_length()
         return top, [scale(one - top) for one in [power, *others]]
 
-    def sums(value, name, axis, factor, *places):
+    def given(value, name, axis, *places):
         me = place[name]
-        got = [swap(pick(value, (axis, me ^ j), *places), name, j) for j in range(1, size[name])]
-        total = pick(value, (axis, me), *places).astype(jnp.float32) * factor[0]
+        return [swap(pick(value, (axis, me ^ j), *places), name, j) for j in range(1, size[name])]
+
+    def taken(value, got, name, axis, factor, *places):
+        total = pick(value, (axis, place[name]), *places).astype(jnp.float32) * factor[0]
         for one, other in zip(got, factor[1:]):
             total = total + one.astype(jnp.float32) * other
         return total.astype(jnp.float16)
 
+    held = lax.optimization_barrier
+
     shards = [swap(key_weight, "z", j) for j in range(1, nz)]
 
-    power, shards[0] = lax.optimization_barrier((bound_of(tokens, cotangent), shards[0]))
+    power, shards[0] = held((bound_of(tokens, cotangent), shards[0]))
     power = jnp.maximum(power, swap(power, "core", 1))[:1] + 1.0
     part = lax.dot_general(
         tokens, cotangent, (((0,), (0,)), ((), ())), preferred_element_type=jnp.float32
     )
-    part = (part * scale(TOP - power)).astype(jnp.float16).reshape(nz * nx * ny, 2, rows, kd)
-    other = swap(pick(part, (1, 1 - core)), "core", 1)
-    part, shards = lax.optimization_barrier((part, shards))
+    part = (part * scale(TOP - power)).astype(jnp.float16).reshape(nz, nx, ny, 2, rows, kd)
+    z_low = z_me % (nz // 2)
+    z_top = z_me - z_low
+    far, near = (0, nz // 2 - z_top, nz // 2), (0, z_top, nz // 2)
+    far_got = swap(pick(part, far, (3, 1 - core)), "core", 1)
+    near_got = swap(pick(part, near, (3, 1 - core)), "core", 1)
+    part, shards = held((part, shards))
     shards = in_order(key_weight, shards, "z")
-    part = pick(part, (1, core)).astype(jnp.float32) + other.astype(jnp.float32)
-    part = part.astype(jnp.float16).reshape(nz, nx, ny, rows, kd)
+
+    def pair_sum(where, got):
+        total = pick(part, where, (3, core)).astype(jnp.float32) + got.astype(jnp.float32)
+        return total.astype(jnp.float16).reshape(nz // 2, nx, ny, rows, kd)
+
+    upper, lower = (3, 0, half), (3, half, half)
 
     blocks = shards.reshape(nz, 2, half, kd)
     one, power_x = gathered(blocks[:, 0], "x", power)
     two, power_y = gathered(blocks[:, 1], "y", power)
     by_x, by_y = factors(power, power_x), factors(power, power_y)
-    part, one, two, by_x, by_y = lax.optimization_barrier((part, one, two, by_x, by_y))
-    sum_one = sums(part, "x", 1, by_x[1], (3, 0, half))
-    sum_two = sums(part, "y", 2, by_y[1], (3, half, half))
+    far_sum = pair_sum(far, far_got)
+    far_one, far_two = given(far_sum, "x", 1, upper), given(far_sum, "y", 2, lower)
+    far_sum, one, two, by_x, by_y = held((far_sum, one, two, by_x, by_y))
     one, power_xy = gathered(one, "y", by_x[0])
     two, power_yx = gathered(two, "x", by_y[0])
     by_xy, by_yx = factors(by_x[0], power_xy), factors(by_y[0], power_yx)
-    top_one = by_xy[0]
-    sum_one = sums(sum_one, "y", 2, by_xy[1])
-    sum_two = sums(sum_two, "x", 1, by_yx[1])
+    top = by_xy[0]
+
+    far_one = taken(far_sum, far_one, "x", 1, by_x[1], upper)
+    far_two = taken(far_sum, far_two, "y", 2, by_y[1], lower)
+    far_one_got, far_two_got = given(far_one, "y", 2), given(far_two, "x", 1)
+    near_got, far_one, far_two = held((near_got, far_one, far_two))
+    near_sum = pair_sum(near, near_got)
+    near_one, near_two = given(near_sum, "x", 1, upper), given(near_sum, "y", 2, lower)
+
     both = jnp.stack([one.transpose(2, 1, 0, 3, 4), two.transpose(2, 0, 1, 3, 4)], axis=3)
     weight = in_order(both, [swap(both, "core", 1)], "core")
     weight = weight.transpose(1, 2, 3, 0, 4, 5, 6).reshape(nz, nx * ny * 2 * rows, kd)
 
-    total = jnp.concatenate([sum_one, sum_two], axis=3).reshape(nz, rows, kd)
-    got = [
-        swap(noted(pick(total, (0, z_me ^ j)), top_one), "z", j)
-        for j in range(1, nz)
-    ]
+    def last_sum(one, one_got, two, two_got):
+        one = taken(one, one_got, "y", 2, by_xy[1])
+        two = taken(two, two_got, "x", 1, by_yx[1])
+        return jnp.concatenate([one, two], axis=3).reshape(nz // 2, rows, kd)
+
+    far_sum = last_sum(far_one, far_one_got, far_two, far_two_got)
+    packets = [noted(pick(far_sum, (0, z_low ^ j)), top) for j in range(nz // 2)]
+    near_one = taken(near_sum, near_one, "x", 1, by_x[1], upper)
+    near_two = taken(near_sum, near_two, "y", 2, by_y[1], lower)
+    later, near_one, near_two = held((packets[nz // 4 :], near_one, near_two))
+    packets[nz // 4 :] = later
+    got = [swap(packet, "z", nz // 2 + j) for j, packet in enumerate(packets)]
+    near_one_got, near_two_got = given(near_one, "y", 2), given(near_two, "x", 1)
+    near_sum = last_sum(near_one, near_one_got, near_two, near_two_got)
+    got += [swap(noted(pick(near_sum, (0, z_low ^ j)), top), "z", j) for j in range(1, nz // 2)]
+
     keys, input_grad = products(tokens, cotangent, weight)
-    keys, input_grad, got = lax.optimization_barrier((keys, input_grad, got))
-    got = [read(one, (rows, kd)) for one in got]
-    total = pick(total, (0, z_me))[0].astype(jnp.float32) * scale(top_one - TOP)
-    for one, other in got:
+    keys, input_grad, got = held((keys, input_grad, got))
+    total = pick(near_sum, (0, z_low))[0].astype(jnp.float32) * scale(top - TOP)
+    for one, other in [read(one, (rows, kd)) for one in got]:
         total = total + one.astype(jnp.float32) * scale(other - TOP)
     total_tokens = tokens.shape[0] * wide * node
     weight_grad = total * (1.0 / jnp.sqrt(jnp.float32(total_tokens)))

time: 76.9 us -> 80.6 us (1.048)
  starting transfers between devices: 19.9 us -> 26.1 us
  waiting for transfers between devices: 33.8 us -> 28.8 us
  Pallas kernels: 10.7 us -> 12.4 us
    ppermute x17 -> x22, starting transfers between devices: 19.9 us -> 26.1 us  [swap(): lax.ppermute(value, AXES, [(i, i ^ j * mask[name]) for i in range(wide *...]
    ppermute x17 -> x22, waiting for transfers between devices: 33.8 us -> 28.8 us  [swap(): lax.ppermute(value, AXES, [(i, i ^ j * mask[name]) for i in range(wide *...]
    pallas_call x1, Pallas kernels: 4.02 us -> 5.78 us  [bound_of(): pl.pallas_call(bound_kernel, grid=(rows // block,), in_specs=[pl.BlockSpe...]
    convert_element_type x5 -> x10, other arithmetic: 1.53 us -> 1.63 us  [the longest x2 0.91 us: pair_sum(): return total.astype(jnp.float16).reshape(nz // 2, nx, ny, rows, kd)]
  transfers between devices with their start and end apart: 17 -> 22, of which waited for: 9 -> 7; matrix products, arithmetic and copies ran while one was open for 11% -> 13% of each run, Pallas kernels for 14% -> 15%
where the time goes in v7:
time: 80.6 us; the launch traced here: 80.3 us
  waiting for transfers between devices  28.8 us (36%)
  starting transfers between devices  26.1 us (32%)
  Pallas kernels  12.4 us (15%)
  matrix products  4.58 us (6%)
  other arithmetic  4.3 us (5%)
  local copies, waits for them, and re-layouts  2.79 us (3%)
  between operations  1.31 us (2%)
    ppermute x22, waiting for transfers between devices, swap(): lax.ppermute(value, AXES, [(i, i ^ j * mask[name]) for i in range(wide *...  28.8 us
    ppermute x22, starting transfers between devices, swap(): lax.ppermute(value, AXES, [(i, i ^ j * mask[name]) for i in range(wide *...  26.1 us
    pallas_call x1, Pallas kernels, products(): pl.pallas_call(products_kernel, grid=(steps,), in_specs=[columns, whole,...  6.63 us
    pallas_call x1, Pallas kernels, bound_of(): pl.pallas_call(bound_kernel, grid=(rows // block,), in_specs=[pl.BlockSpe...  5.78 us
    dot_general x1, matrix products, on_device(): lax.dot_general(tokens, cotangent, (((0,), (0,)), ((), ())), preferred_el...  4.58 us
  transfers between devices with their start and end apart: 22, of which 7 were waited for; matrix products, arithmetic and copies ran while one was open for 13% of the time, Pallas kernels for 15%

profile of v7, /device:TPU:0, one launch (start us, length us, event | category | flops | bytes accessed | tf_op | source)
XLA Modules:
  0.0 80.3 jit_solution(2252086813756205123)
XLA Ops:
  0.7 3.1 %collective-permute-start = (bf16[128,512]{1,0:T(8,128)(2,1)}, bf16[128,512]{1,0:T(8,128)(2,1)S(1)}, u32[]{:S(2)}, u32[]{:S(2)}) collective-permute-start(bf16[128,512]{1,0:T(8,128)(2,1)} %param.4), channel_id=1, source_target_pairs={{0,2},{1,3},{2,0},{3,1},{4,6},{5,7},{6,4},{7,5},{8,10},{9,11},{10,... | collective-permute-start | bytes 393224 | tf_op jit(solution)/shard_map/ppermute | solution.py:105
  3.7 2.6 %collective-permute-start.2 = (bf16[128,512]{1,0:T(8,128)(2,1)}, bf16[128,512]{1,0:T(8,128)(2,1)S(1)}, u32[]{:S(2)}, u32[]{:S(2)}) collective-permute-start(bf16[128,512]{1,0:T(8,128)(2,1)} %param.4), channel_id=1, source_target_pairs={{0,4},{1,5},{2,6},{3,7},{4,0},{5,1},{6,2},{7,3},{8,12},{9,13},{10,... | collective-permute-start | bytes 393224 | tf_op jit(solution)/shard_map/ppermute | solution.py:105
  6.3 5.8 %shard_map.58 = f32[8,512]{1,0:T(8,128)} custom-call(bf16[512,4096]{1,0:T(8,128)(2,1)} %tok.3, bf16[512,512]{1,0:T(8,128)(2,1)} %cot.3), custom_call_target="tpu_custom_call" | custom-call | flops 4194304 | bytes 4718592 | tf_op jit(solution)/shard_map/pallas_call | solution.py:74
  12.3 1.2 %collective-permute-done.1 = f32[8,512]{1,0:T(8,128)S(1)} collective-permute-done((f32[8,512]{1,0:T(8,128)}, f32[8,512]{1,0:T(8,128)S(1)}, u32[]{:S(2)}, u32[]{:S(2)}) %collective-permute-start.1) | collective-permute-done | bytes 16416 | tf_op jit(solution)/shard_map/ppermute | solution.py:105
  13.5 0.7 convert_reduce_fusion.3
  14.3 4.6 %multiply_convert_fusion = f16[4096,512]{1,0:T(8,128)(2,1)S(1)} fusion(bf16[512,4096]{1,0:T(8,128)(2,1)} %tok.3, bf16[512,512]{1,0:T(8,128)(2,1)S(1)} %copy-done.1, f32[512]{0:T(512)S(1)} %bitcast.141), kind=kOutput, calls=%fused_computation | convolution fusion | flops 2151677952 | bytes 8914944 | tf_op jit(solution)/shard_map/dot_general | solution.py:157
  19.1 1.8 %collective-permute-start.6 = (bf16[264,512]{1,0:T(8,128)(2,1)S(1)}, bf16[264,512]{1,0:T(8,128)(2,1)S(1)}, u32[]{:S(2)}, u32[]{:S(2)}) collective-permute-start(bf16[264,512]{1,0:T(8,128)(2,1)S(1)} %get-tuple-element.79), channel_id=1, source_target_pairs={{0,16},{1,17},{2,18},{3,19},{4,20},{5,21},{6,22},{7,23},{8,24},{9,... | collective-permute-start | bytes 811016 | tf_op jit(solution)/shard_map/ppermute | solution.py:105
  20.9 1.5 %collective-permute-start.5 = (bf16[264,512]{1,0:T(8,128)(2,1)S(1)}, bf16[264,512]{1,0:T(8,128)(2,1)S(1)}, u32[]{:S(2)}, u32[]{:S(2)}) collective-permute-start(bf16[264,512]{1,0:T(8,128)(2,1)S(1)} %get-tuple-element.80), channel_id=1, source_target_pairs={{0,1},{1,0},{2,3},{3,2},{4,5},{5,4},{6,7},{7,6},{8,9},{9,8},{10,11... | collective-permute-start | bytes 811016 | tf_op jit(solution)/shard_map/ppermute | solution.py:105
  23.9 3.8 %collective-permute-done.6 = bf16[264,512]{1,0:T(8,128)(2,1)S(1)} collective-permute-done((bf16[264,512]{1,0:T(8,128)(2,1)S(1)}, bf16[264,512]{1,0:T(8,128)(2,1)S(1)}, u32[]{:S(2)}, u32[]{:S(2)}) %collective-permute-start.6) | collective-permute-done | bytes 270368 | tf_op jit(solution)/shard_map/ppermute | solution.py:105
  27.7 1.4 %collective-permute-done.5 = bf16[264,512]{1,0:T(8,128)(2,1)S(1)} collective-permute-done((bf16[264,512]{1,0:T(8,128)(2,1)S(1)}, bf16[264,512]{1,0:T(8,128)(2,1)S(1)}, u32[]{:S(2)}, u32[]{:S(2)}) %collective-permute-start.5) | collective-permute-done | bytes 270368 | tf_op jit(solution)/shard_map/ppermute | solution.py:105
  30.1 1.6 %collective-permute-start.11 = (f16[2,1,2,64,512]{4,3,2,1,0:T(8,128)(2,1)S(1)}, f16[2,1,2,64,512]{4,3,2,1,0:T(8,128)(2,1)S(1)}, u32[]{:S(2)}, u32[]{:S(2)}) collective-permute-start(f16[2,1,2,64,512]{4,3,2,1,0:T(8,128)(2,1)S(1)} %dynamic-slice_bitcast_fusion.4), channel_id=1, source_target_pairs={{0,1},{1,0},{2,3},{3,2},{4,5},{5,4},{6,7},{7,6},{8,9},{9,8},{10,11... | collective-permute-start | bytes 786440 | tf_op jit(solution)/shard_map/ppermute | solution.py:105
  32.9 1.7 %collective-permute-start.7 = (bf16[520,512]{1,0:T(8,128)(2,1)S(1)}, bf16[520,512]{1,0:T(8,128)(2,1)S(1)}, u32[]{:S(2)}, u32[]{:S(2)}) collective-permute-start(bf16[520,512]{1,0:T(8,128)(2,1)S(1)} %pad_maximum_fusion.1), channel_id=1, source_target_pairs={{0,16},{1,17},{2,18},{3,19},{4,20},{5,21},{6,22},{7,23},{8,24},{9,... | collective-permute-start | bytes 1597448 | tf_op jit(solution)/shard_map/ppermute | solution.py:105
  34.7 4.7 %collective-permute-done.11 = f16[2,1,2,64,512]{4,3,2,1,0:T(8,128)(2,1)S(1)} collective-permute-done((f16[2,1,2,64,512]{4,3,2,1,0:T(8,128)(2,1)S(1)}, f16[2,1,2,64,512]{4,3,2,1,0:T(8,128)(2,1)S(1)}, u32[]{:S(2)}, u32[]{:S(2)}) %collective-permute-start.11) | collective-permute-done | bytes 262176 | tf_op jit(solution)/shard_map/ppermute | solution.py:105
  39.5 1.4 %collective-permute-done.12 = f16[2,2,1,64,512]{4,3,2,1,0:T(8,128)(2,1)S(1)} collective-permute-done((f16[2,2,1,64,512]{4,3,2,1,0:T(8,128)(2,1)S(1)}, f16[2,2,1,64,512]{4,3,2,1,0:T(8,128)(2,1)S(1)}, u32[]{:S(2)}, u32[]{:S(2)}) %collective-permute-start.12) | collective-permute-done | bytes 262176 | tf_op jit(solution)/shard_map/ppermute | solution.py:105
  41.5 0.6 collective-permute-start.17
  42.8 1.7 %collective-permute-start.13 = (f16[2,1,1,64,512]{4,3,2,1,0:T(8,128)(2,1)S(1)}, f16[2,1,1,64,512]{4,3,2,1,0:T(8,128)(2,1)S(1)}, u32[]{:S(2)}, u32[]{:S(2)}) collective-permute-start(f16[2,1,1,64,512]{4,3,2,1,0:T(8,128)(2,1)S(1)} %constant_dynamic-slice_fusion.3), channel_id=1, source_target_pairs={{0,16},{1,17},{2,18},{3,19},{4,20},{5,21},{6,22},{7,23},{8,24},{9,... | collective-permute-start | bytes 393224 | tf_op jit(solution)/shard_map/ppermute | solution.py:105
  44.5 12.5 %collective-permute-done.17 = f16[2,2,1,64,512]{4,3,2,1,0:T(8,128)(2,1)S(1)} collective-permute-done((f16[2,2,1,64,512]{4,3,2,1,0:T(8,128)(2,1)S(1)}, f16[2,2,1,64,512]{4,3,2,1,0:T(8,128)(2,1)S(1)}, u32[]{:S(2)}, u32[]{:S(2)}) %collective-permute-start.17) | collective-permute-done | bytes 262176 | tf_op jit(solution)/shard_map/ppermute | solution.py:105
  58.3 3.7 %collective-permute-done.14 = f16[2,1,1,64,512]{4,3,2,1,0:T(8,128)(2,1)S(1)} collective-permute-done((f16[2,1,1,64,512]{4,3,2,1,0:T(8,128)(2,1)S(1)}, f16[2,1,1,64,512]{4,3,2,1,0:T(8,128)(2,1)S(1)}, u32[]{:S(2)}, u32[]{:S(2)}) %collective-permute-start.14) | collective-permute-done | bytes 131104 | tf_op jit(solution)/shard_map/ppermute | solution.py:105
  63.0 0.7 collective-permute-start.19
  63.7 3.6 %collective-permute-start.18 = (f16[136,512]{1,0:T(8,128)(2,1)S(1)}, f16[136,512]{1,0:T(8,128)(2,1)S(1)}, u32[]{:S(2)}, u32[]{:S(2)}) collective-permute-start(f16[136,512]{1,0:T(8,128)(2,1)S(1)} %pad_maximum_fusion.6), channel_id=1, source_target_pairs={{0,6},{1,7},{2,4},{3,5},{4,2},{5,3},{6,0},{7,1},{8,14},{9,15},{10,... | collective-permute-start | bytes 417800 | tf_op jit(solution)/shard_map/ppermute | solution.py:105
  68.4 0.6 collective-permute-start.21
  69.0 3.5 %collective-permute-start.15 = (f16[136,512]{1,0:T(8,128)(2,1)S(1)}, f16[136,512]{1,0:T(8,128)(2,1)S(1)}, u32[]{:S(2)}, u32[]{:S(2)}) collective-permute-start(f16[136,512]{1,0:T(8,128)(2,1)S(1)} %get-tuple-element.78), channel_id=1, source_target_pairs={{0,4},{1,5},{2,6},{3,7},{4,0},{5,1},{6,2},{7,3},{8,12},{9,13},{10,... | collective-permute-start | bytes 417800 | tf_op jit(solution)/shard_map/ppermute | solution.py:105
  72.7 6.6 %shard_map.59 = (bf16[512,512]{1,0:T(8,128)(2,1)}, bf16[512,4096]{1,0:T(8,128)(2,1)}) custom-call(bf16[512,4096]{1,0:T(8,128)(2,1)S(1)} %copy-done, bf16[512,512]{1,0:T(8,128)(2,1)S(1)} %copy-done.1, bf16[4,1024,512]{2,1,0:T(8,128)(2,1)S(1)} %bitcast.102), custom_call_target="tpu_custom_call" | custom-call | tf_op jit(solution)/shard_map/pallas_call | solution.py:35
  79.4 0.8 %fusion.7 = f32[128,512]{1,0:T(8,128)} fusion(s32[]{:T(128)S(6)} %select_n.97, f16[2,1,1,64,512]{4,3,2,1,0:T(8,128)(2,1)S(1)} %add_convert_fusion.5, f16[2,1,1,64,512]{4,3,2,1,0:T(8,128)(2,1)S(1)} %add_convert_fusion.4, f32[512]{0:T(512)S(1)} %bitcast.139, f16[136,512]{1,0:T(8,128)(2,1)S(1)} %collective-permute-done.21, f32[512]{0:T(512)S(1)} %bitcast.138, ...), kind=kLoop, calls=%fused_computation.35 | loop fusion | flops 851968 | bytes 925700 | tf_op jit(solution)/shard_map/mul | solution.py:220
  (102 shorter events, 8.7 us)
Async XLA Ops:
  0.6 11.5 %copy-start.2 = (bf16[128,512]{1,0:T(8,128)(2,1)S(1)}, bf16[128,512]{1,0:T(8,128)(2,1)}, u32[]{:S(2)}) copy-start(bf16[128,512]{1,0:T(8,128)(2,1)} %param.4) | copy-start | bytes 393220
  0.6 13.6 %copy-start.1 = (bf16[512,512]{1,0:T(8,128)(2,1)S(1)}, bf16[512,512]{1,0:T(8,128)(2,1)}, u32[]{:S(2)}) copy-start(bf16[512,512]{1,0:T(8,128)(2,1)} %cot.3) | copy-start | bytes 1572868
  0.7 11.5 %collective-permute-start = (bf16[128,512]{1,0:T(8,128)(2,1)}, bf16[128,512]{1,0:T(8,128)(2,1)S(1)}, u32[]{:S(2)}, u32[]{:S(2)}) collective-permute-start(bf16[128,512]{1,0:T(8,128)(2,1)} %param.4), channel_id=1, source_target_pairs={{0,2},{1,3},{2,0},{3,1},{4,6},{5,7},{6,4},{7,5},{8,10},{9,11},{10,... | collective-permute-start | bytes 393224 | tf_op jit(solution)/shard_map/ppermute | solution.py:105
  3.7 15.1 %collective-permute-start.2 = (bf16[128,512]{1,0:T(8,128)(2,1)}, bf16[128,512]{1,0:T(8,128)(2,1)S(1)}, u32[]{:S(2)}, u32[]{:S(2)}) collective-permute-start(bf16[128,512]{1,0:T(8,128)(2,1)} %param.4), channel_id=1, source_target_pairs={{0,4},{1,5},{2,6},{3,7},{4,0},{5,1},{6,2},{7,3},{8,12},{9,13},{10,... | collective-permute-start | bytes 393224 | tf_op jit(solution)/shard_map/ppermute | solution.py:105
  6.3 12.5 %collective-permute-start.3 = (bf16[128,512]{1,0:T(8,128)(2,1)}, bf16[128,512]{1,0:T(8,128)(2,1)S(1)}, u32[]{:S(2)}, u32[]{:S(2)}) collective-permute-start(bf16[128,512]{1,0:T(8,128)(2,1)} %param.4), channel_id=1, source_target_pairs={{0,6},{1,7},{2,4},{3,5},{4,2},{5,3},{6,0},{7,1},{8,14},{9,15},{10,... | collective-permute-start | bytes 393224 | tf_op jit(solution)/shard_map/ppermute | solution.py:105
  12.1 1.4 %collective-permute-start.1 = (f32[8,512]{1,0:T(8,128)}, f32[8,512]{1,0:T(8,128)S(1)}, u32[]{:S(2)}, u32[]{:S(2)}) collective-permute-start(f32[8,512]{1,0:T(8,128)} %shard_map.58), channel_id=1, source_target_pairs={{0,8},{1,9},{2,10},{3,11},{4,12},{5,13},{6,14},{7,15},{8,0},{9,1},... | collective-permute-start | bytes 49160 | tf_op jit(solution)/shard_map/ppermute | solution.py:105
  19.1 8.6 %collective-permute-start.6 = (bf16[264,512]{1,0:T(8,128)(2,1)S(1)}, bf16[264,512]{1,0:T(8,128)(2,1)S(1)}, u32[]{:S(2)}, u32[]{:S(2)}) collective-permute-start(bf16[264,512]{1,0:T(8,128)(2,1)S(1)} %get-tuple-element.79), channel_id=1, source_target_pairs={{0,16},{1,17},{2,18},{3,19},{4,20},{5,21},{6,22},{7,23},{8,24},{9,... | collective-permute-start | bytes 811016 | tf_op jit(solution)/shard_map/ppermute | solution.py:105
  20.9 8.3 %collective-permute-start.5 = (bf16[264,512]{1,0:T(8,128)(2,1)S(1)}, bf16[264,512]{1,0:T(8,128)(2,1)S(1)}, u32[]{:S(2)}, u32[]{:S(2)}) collective-permute-start(bf16[264,512]{1,0:T(8,128)(2,1)S(1)} %get-tuple-element.80), channel_id=1, source_target_pairs={{0,1},{1,0},{2,3},{3,2},{4,5},{5,4},{6,7},{7,6},{8,9},{9,8},{10,11... | collective-permute-start | bytes 811016 | tf_op jit(solution)/shard_map/ppermute | solution.py:105
  23.2 17.8 %collective-permute-start.10 = (f16[2,2,2,1,128,512]{5,4,1,0,3,2:T(8,128)(2,1)S(1)}, f16[2,2,2,1,128,512]{5,4,1,0,3,2:T(8,128)(2,1)S(1)}, u32[]{:S(2)}, u32[]{:S(2)}) collective-permute-start(f16[2,2,2,1,128,512]{5,4,1,0,3,2:T(8,128)(2,1)S(1)} %copy.40), channel_id=1, source_target_pairs={{0,8},{1,9},{2,10},{3,11},{4,12},{5,13},{6,14},{7,15},{8,0},{9,1},... | collective-permute-start | bytes 3145736 | tf_op jit(solution)/shard_map/ppermute | solution.py:105
  23.3 6.0 %collective-permute-start.4 = (f16[2,2,2,1,128,512]{5,4,2,1,0,3:T(8,128)(2,1)S(1)}, f16[2,2,2,1,128,512]{5,4,2,1,0,3:T(8,128)(2,1)S(1)}, u32[]{:S(2)}, u32[]{:S(2)}) collective-permute-start(f16[2,2,2,1,128,512]{5,4,2,1,0,3:T(8,128)(2,1)S(1)} %get-tuple-element.68), channel_id=1, source_target_pairs={{0,8},{1,9},{2,10},{3,11},{4,12},{5,13},{6,14},{7,15},{8,0},{9,1},... | collective-permute-start | bytes 3145736 | tf_op jit(solution)/shard_map/ppermute | solution.py:105
  30.1 9.3 %collective-permute-start.11 = (f16[2,1,2,64,512]{4,3,2,1,0:T(8,128)(2,1)S(1)}, f16[2,1,2,64,512]{4,3,2,1,0:T(8,128)(2,1)S(1)}, u32[]{:S(2)}, u32[]{:S(2)}) collective-permute-start(f16[2,1,2,64,512]{4,3,2,1,0:T(8,128)(2,1)S(1)} %dynamic-slice_bitcast_fusion.4), channel_id=1, source_target_pairs={{0,1},{1,0},{2,3},{3,2},{4,5},{5,4},{6,7},{7,6},{8,9},{9,8},{10,11... | collective-permute-start | bytes 786440 | tf_op jit(solution)/shard_map/ppermute | solution.py:105
  31.6 9.2 %collective-permute-start.12 = (f16[2,2,1,64,512]{4,3,2,1,0:T(8,128)(2,1)S(1)}, f16[2,2,1,64,512]{4,3,2,1,0:T(8,128)(2,1)S(1)}, u32[]{:S(2)}, u32[]{:S(2)}) collective-permute-start(f16[2,2,1,64,512]{4,3,2,1,0:T(8,128)(2,1)S(1)} %dynamic-slice_bitcast_fusion.3), channel_id=1, source_target_pairs={{0,16},{1,17},{2,18},{3,19},{4,20},{5,21},{6,22},{7,23},{8,24},{9,... | collective-permute-start | bytes 786440 | tf_op jit(solution)/shard_map/ppermute | solution.py:105
  32.4 25.4 %collective-permute-start.8 = (bf16[520,512]{1,0:T(8,128)(2,1)S(1)}, bf16[520,512]{1,0:T(8,128)(2,1)S(1)}, u32[]{:S(2)}, u32[]{:S(2)}) collective-permute-start(bf16[520,512]{1,0:T(8,128)(2,1)S(1)} %pad_maximum_fusion.2), channel_id=1, source_target_pairs={{0,1},{1,0},{2,3},{3,2},{4,5},{5,4},{6,7},{7,6},{8,9},{9,8},{10,11... | collective-permute-start | bytes 1597448 | tf_op jit(solution)/shard_map/ppermute | solution.py:105
  32.9 25.0 %collective-permute-start.7 = (bf16[520,512]{1,0:T(8,128)(2,1)S(1)}, bf16[520,512]{1,0:T(8,128)(2,1)S(1)}, u32[]{:S(2)}, u32[]{:S(2)}) collective-permute-start(bf16[520,512]{1,0:T(8,128)(2,1)S(1)} %pad_maximum_fusion.1), channel_id=1, source_target_pairs={{0,16},{1,17},{2,18},{3,19},{4,20},{5,21},{6,22},{7,23},{8,24},{9,... | collective-permute-start | bytes 1597448 | tf_op jit(solution)/shard_map/ppermute | solution.py:105
  41.5 15.5 %collective-permute-start.17 = (f16[2,2,1,64,512]{4,3,2,1,0:T(8,128)(2,1)S(1)}, f16[2,2,1,64,512]{4,3,2,1,0:T(8,128)(2,1)S(1)}, u32[]{:S(2)}, u32[]{:S(2)}) collective-permute-start(f16[2,2,1,64,512]{4,3,2,1,0:T(8,128)(2,1)S(1)} %dynamic-slice_bitcast_fusion.1), channel_id=1, source_target_pairs={{0,16},{1,17},{2,18},{3,19},{4,20},{5,21},{6,22},{7,23},{8,24},{9,... | collective-permute-start | bytes 786440 | tf_op jit(solution)/shard_map/ppermute | solution.py:105
  42.2 15.4 %collective-permute-start.16 = (f16[2,1,2,64,512]{4,3,2,1,0:T(8,128)(2,1)S(1)}, f16[2,1,2,64,512]{4,3,2,1,0:T(8,128)(2,1)S(1)}, u32[]{:S(2)}, u32[]{:S(2)}) collective-permute-start(f16[2,1,2,64,512]{4,3,2,1,0:T(8,128)(2,1)S(1)} %copy.36), channel_id=1, source_target_pairs={{0,1},{1,0},{2,3},{3,2},{4,5},{5,4},{6,7},{7,6},{8,9},{9,8},{10,11... | collective-permute-start | bytes 786440 | tf_op jit(solution)/shard_map/ppermute | solution.py:105
  42.8 19.4 %collective-permute-start.13 = (f16[2,1,1,64,512]{4,3,2,1,0:T(8,128)(2,1)S(1)}, f16[2,1,1,64,512]{4,3,2,1,0:T(8,128)(2,1)S(1)}, u32[]{:S(2)}, u32[]{:S(2)}) collective-permute-start(f16[2,1,1,64,512]{4,3,2,1,0:T(8,128)(2,1)S(1)} %constant_dynamic-slice_fusion.3), channel_id=1, source_target_pairs={{0,16},{1,17},{2,18},{3,19},{4,20},{5,21},{6,22},{7,23},{8,24},{9,... | collective-permute-start | bytes 393224 | tf_op jit(solution)/shard_map/ppermute | solution.py:105
  57.0 5.0 %collective-permute-start.14 = (f16[2,1,1,64,512]{4,3,2,1,0:T(8,128)(2,1)S(1)}, f16[2,1,1,64,512]{4,3,2,1,0:T(8,128)(2,1)S(1)}, u32[]{:S(2)}, u32[]{:S(2)}) collective-permute-start(f16[2,1,1,64,512]{4,3,2,1,0:T(8,128)(2,1)S(1)} %constant_dynamic-slice_fusion.2), channel_id=1, source_target_pairs={{0,1},{1,0},{2,3},{3,2},{4,5},{5,4},{6,7},{7,6},{8,9},{9,8},{10,11... | collective-permute-start | bytes 393224 | tf_op jit(solution)/shard_map/ppermute | solution.py:105
  58.2 14.2 %collective-permute-start.9 = (bf16[4,2,2,2,64,512]{5,4,3,2,1,0:T(8,128)(2,1)S(1)}, bf16[4,2,2,2,64,512]{5,4,3,2,1,0:T(8,128)(2,1)S(1)}, u32[]{:S(2)}, u32[]{:S(2)}) collective-permute-start(bf16[4,2,2,2,64,512]{5,4,3,2,1,0:T(8,128)(2,1)S(1)} %pad_maximum_fusion), channel_id=1, source_target_pairs={{0,8},{1,9},{2,10},{3,11},{4,12},{5,13},{6,14},{7,15},{8,0},{9,1},... | collective-permute-start | bytes 6291464 | tf_op jit(solution)/shard_map/ppermute | solution.py:105
  62.4 5.7 %collective-permute-start.20 = (f16[2,1,1,64,512]{4,3,2,1,0:T(8,128)(2,1)S(1)}, f16[2,1,1,64,512]{4,3,2,1,0:T(8,128)(2,1)S(1)}, u32[]{:S(2)}, u32[]{:S(2)}) collective-permute-start(f16[2,1,1,64,512]{4,3,2,1,0:T(8,128)(2,1)S(1)} %constant_dynamic-slice_fusion), channel_id=1, source_target_pairs={{0,1},{1,0},{2,3},{3,2},{4,5},{5,4},{6,7},{7,6},{8,9},{9,8},{10,11... | collective-permute-start | bytes 393224 | tf_op jit(solution)/shard_map/ppermute | solution.py:105
  63.0 5.2 %collective-permute-start.19 = (f16[2,1,1,64,512]{4,3,2,1,0:T(8,128)(2,1)S(1)}, f16[2,1,1,64,512]{4,3,2,1,0:T(8,128)(2,1)S(1)}, u32[]{:S(2)}, u32[]{:S(2)}) collective-permute-start(f16[2,1,1,64,512]{4,3,2,1,0:T(8,128)(2,1)S(1)} %constant_dynamic-slice_fusion.1), channel_id=1, source_target_pairs={{0,16},{1,17},{2,18},{3,19},{4,20},{5,21},{6,22},{7,23},{8,24},{9,... | collective-permute-start | bytes 393224 | tf_op jit(solution)/shard_map/ppermute | solution.py:105
  63.7 15.7 %collective-permute-start.18 = (f16[136,512]{1,0:T(8,128)(2,1)S(1)}, f16[136,512]{1,0:T(8,128)(2,1)S(1)}, u32[]{:S(2)}, u32[]{:S(2)}) collective-permute-start(f16[136,512]{1,0:T(8,128)(2,1)S(1)} %pad_maximum_fusion.6), channel_id=1, source_target_pairs={{0,6},{1,7},{2,4},{3,5},{4,2},{5,3},{6,0},{7,1},{8,14},{9,15},{10,... | collective-permute-start | bytes 417800 | tf_op jit(solution)/shard_map/ppermute | solution.py:105
  68.4 11.0 %collective-permute-start.21 = (f16[136,512]{1,0:T(8,128)(2,1)S(1)}, f16[136,512]{1,0:T(8,128)(2,1)S(1)}, u32[]{:S(2)}, u32[]{:S(2)}) collective-permute-start(f16[136,512]{1,0:T(8,128)(2,1)S(1)} %get-tuple-element.77), channel_id=1, source_target_pairs={{0,2},{1,3},{2,0},{3,1},{4,6},{5,7},{6,4},{7,5},{8,10},{9,11},{10,... | collective-permute-start | bytes 417800 | tf_op jit(solution)/shard_map/ppermute | solution.py:105
  69.0 10.4 %collective-permute-start.15 = (f16[136,512]{1,0:T(8,128)(2,1)S(1)}, f16[136,512]{1,0:T(8,128)(2,1)S(1)}, u32[]{:S(2)}, u32[]{:S(2)}) collective-permute-start(f16[136,512]{1,0:T(8,128)(2,1)S(1)} %get-tuple-element.78), channel_id=1, source_target_pairs={{0,4},{1,5},{2,6},{3,7},{4,0},{5,1},{6,2},{7,3},{8,12},{9,13},{10,... | collective-permute-start | bytes 417800 | tf_op jit(solution)/shard_map/ppermute | solution.py:105
  (1 other events, 4.9 us)

commit v8 on v7

--- a/solution.py
+++ b/solution.py
@@ -46,40 +46,39 @@
     )(tokens, cotangent, weight)
 
 
-def bound_kernel(tok, cot, power, total):
-    step = pl.program_id(0)
-    lanes = 128
-
-    @pl.when(step == 0)
-    def _():
-        total[...] = jnp.zeros_like(total)
-
-    reach = jnp.abs(tok[:, :lanes])
-    for first in range(lanes, tok.shape[1], lanes):
-        reach = jnp.maximum(reach, jnp.abs(tok[:, first : first + lanes]))
-    reach = jnp.max(reach.astype(jnp.float32), axis=1, keepdims=True)
-    terms = reach * jnp.abs(cot[...]).astype(jnp.float32)
-    total[...] += jnp.sum(terms.reshape(-1, NOTE, terms.shape[1]), axis=0)
-
-    @pl.when(step == pl.num_programs(0) - 1)
-    def _():
-        top = jnp.maximum(jnp.sum(total[...], axis=0, keepdims=True), 2.0**-100)
-        power[...] = jnp.broadcast_to(jnp.ceil(jnp.log2(top)), power.shape)
+def bound_kernel(tok, cot, power, tok_here, cot_here, arrived):
+    parts = arrived.shape[0] - 1
+    block = tok.shape[0] // parts
+    copies = [pltpu.make_async_copy(cot, cot_here, arrived.at[parts])]
+    for i in range(parts):
+        some = pl.ds(i * block, block)
+        copies.append(pltpu.make_async_copy(tok.at[some], tok_here.at[some], arrived.at[i]))
+    for copy in copies:
+        copy.start()
+    copies[0].wait()
+    total = jnp.zeros(power.shape, jnp.float32)
+    for i in range(parts):
+        copies[1 + i].wait()
+        some = pl.ds(i * block, block)
+        reach = jnp.max(jnp.abs(tok_here[some]).astype(jnp.float32), axis=1, keepdims=True)
+        terms = reach * jnp.abs(cot_here[some]).astype(jnp.float32)
+        total += jnp.sum(terms.reshape(-1, NOTE, terms.shape[1]), axis=0)
+    top = jnp.maximum(jnp.sum(total, axis=0, keepdims=True), 2.0**-100)
+    power[...] = jnp.broadcast_to(jnp.ceil(jnp.log2(top)), power.shape)
 
 
 def bound_of(tokens, cotangent):
     rows, width = tokens.shape
     kd = cotangent.shape[1]
-    block = min(rows, 64)
     return pl.pallas_call(
         bound_kernel,
-        grid=(rows // block,),
-        in_specs=[
-            pl.BlockSpec((block, width), lambda i: (i, 0)),
-            pl.BlockSpec((block, kd), lambda i: (i, 0)),
+        in_specs=[pl.BlockSpec(memory_space=pl.ANY)] * 2,
+        out_specs=pl.BlockSpec(memory_space=pltpu.VMEM),
+        scratch_shapes=[
+            pltpu.VMEM(tokens.shape, tokens.dtype),
+            pltpu.VMEM(cotangent.shape, cotangent.dtype),
+            pltpu.SemaphoreType.DMA((max(rows // 128, 1) + 1,)),
         ],
-        out_specs=pl.BlockSpec((NOTE, kd), lambda i: (0, 0)),
-        scratch_shapes=[pltpu.VMEM((NOTE, kd), jnp.float32)],
         out_shape=jax.ShapeDtypeStruct((NOTE, kd), jnp.float32),
         compiler_params=pltpu.CompilerParams(vmem_limit_bytes=60 * 1024 * 1024),
         cost_estimate=pl.CostEstimate(
@@ -161,36 +160,29 @@
     z_low = z_me % (nz // 2)
     z_top = z_me - z_low
     far, near = (0, nz // 2 - z_top, nz // 2), (0, z_top, nz // 2)
-    far_got = swap(pick(part, far, (3, 1 - core)), "core", 1)
-    near_got = swap(pick(part, near, (3, 1 - core)), "core", 1)
-    part, shards = held((part, shards))
-    shards = in_order(key_weight, shards, "z")
-
-    def pair_sum(where, got):
-        total = pick(part, where, (3, core)).astype(jnp.float32) + got.astype(jnp.float32)
-        return total.astype(jnp.float16).reshape(nz // 2, nx, ny, rows, kd)
-
     upper, lower = (3, 0, half), (3, half, half)
-
-    blocks = shards.reshape(nz, 2, half, kd)
+    other = swap(pick(part, (3, 1 - core)), "core", 1)
+    part = pick(part, (3, core)).astype(jnp.float32) + other.astype(jnp.float32)
+    part = part.astype(jnp.float16).reshape(nz, nx, ny, rows, kd)
+
+    part, power, shards = held((part, power, shards))
+    far_one, far_two = given(part, "x", 1, far, upper), given(part, "y", 2, far, lower)
+    blocks = in_order(key_weight, shards, "z").reshape(nz, 2, half, kd)
     one, power_x = gathered(blocks[:, 0], "x", power)
     two, power_y = gathered(blocks[:, 1], "y", power)
     by_x, by_y = factors(power, power_x), factors(power, power_y)
-    far_sum = pair_sum(far, far_got)
-    far_one, far_two = given(far_sum, "x", 1, upper), given(far_sum, "y", 2, lower)
-    far_sum, one, two, by_x, by_y = held((far_sum, one, two, by_x, by_y))
+    by_x, by_y = held((by_x, by_y))
     one, power_xy = gathered(one, "y", by_x[0])
     two, power_yx = gathered(two, "x", by_y[0])
+
+    far_one = taken(part, far_one, "x", 1, by_x[1], far, upper)
+    far_two = taken(part, far_two, "y", 2, by_y[1], far, lower)
+    far_one_got, far_two_got = given(far_one, "y", 2), given(far_two, "x", 1)
+    part, far_one_got, far_two_got = held((part, far_one_got, far_two_got))
+    near_one, near_two = given(part, "x", 1, near, upper), given(part, "y", 2, near, lower)
+
     by_xy, by_yx = factors(by_x[0], power_xy), factors(by_y[0], power_yx)
     top = by_xy[0]
-
-    far_one = taken(far_sum, far_one, "x", 1, by_x[1], upper)
-    far_two = taken(far_sum, far_two, "y", 2, by_y[1], lower)
-    far_one_got, far_two_got = given(far_one, "y", 2), given(far_two, "x", 1)
-    near_got, far_one, far_two = held((near_got, far_one, far_two))
-    near_sum = pair_sum(near, near_got)
-    near_one, near_two = given(near_sum, "x", 1, upper), given(near_sum, "y", 2, lower)
-
     both = jnp.stack([one.transpose(2, 1, 0, 3, 4), two.transpose(2, 0, 1, 3, 4)], axis=3)
     weight = in_order(both, [swap(both, "core", 1)], "core")
     weight = weight.transpose(1, 2, 3, 0, 4, 5, 6).reshape(nz, nx * ny * 2 * rows, kd)
@@ -202,10 +194,9 @@
 
     far_sum = last_sum(far_one, far_one_got, far_two, far_two_got)
     packets = [noted(pick(far_sum, (0, z_low ^ j)), top) for j in range(nz // 2)]
-    near_one = taken(near_sum, near_one, "x", 1, by_x[1], upper)
-    near_two = taken(near_sum, near_two, "y", 2, by_y[1], lower)
-    later, near_one, near_two = held((packets[nz // 4 :], near_one, near_two))
-    packets[nz // 4 :] = later
+    near_one = taken(part, near_one, "x", 1, by_x[1], near, upper)
+    near_two = taken(part, near_two, "y", 2, by_y[1], near, lower)
+    packets, near_one, near_two = held((packets, near_one, near_two))
     got = [swap(packet, "z", nz // 2 + j) for j, packet in enumerate(packets)]
     near_one_got, near_two_got = given(near_one, "y", 2), given(near_two, "x", 1)
     near_sum = last_sum(near_one, near_one_got, near_two, near_two_got)

time: 80.6 us -> 89.5 us (1.11)
  waiting for transfers between devices: 28.8 us -> 38.4 us
  local copies, waits for them, and re-layouts: 2.79 us -> 6.41 us
  starting transfers between devices: 26.1 us -> 23.2 us
  Pallas kernels: 12.4 us -> 9.86 us
  other arithmetic: 4.3 us -> 5.66 us
    ppermute x22 -> x21, waiting for transfers between devices: 28.8 us -> 38.4 us  [swap(): lax.ppermute(value, AXES, [(i, i ^ j * mask[name]) for i in range(wide *...]
    unnamed x7 -> x9, local copies, waits for them, and re-layouts: 0.25 us -> 4.46 us
    ppermute x22 -> x21, starting transfers between devices: 26.1 us -> 23.2 us  [swap(): lax.ppermute(value, AXES, [(i, i ^ j * mask[name]) for i in range(wide *...]
    pallas_call x1, Pallas kernels: 5.78 us -> 3.25 us  [bound_of(): pl.pallas_call(bound_kernel, in_specs=[pl.BlockSpec(memory_space=pl.ANY)]...]
    reshape x0 -> x1, other arithmetic: none -> 2.37 us  [on_device(): part = part.astype(jnp.float16).reshape(nz, nx, ny, rows, kd)]
    convert_element_type x2 -> x0, other arithmetic: 0.91 us -> none  [pair_sum(): return total.astype(jnp.float16).reshape(nz // 2, nx, ny, rows, kd)]
  transfers between devices with their start and end apart: 22 -> 21, of which waited for: 7 -> 14; matrix products, arithmetic and copies ran while one was open for 13% -> 6% of each run, Pallas kernels for 15% -> 11%
where the time goes in v8:
time: 89.5 us; the launch traced here: 89.3 us
  waiting for transfers between devices  38.4 us (43%)
  starting transfers between devices  23.2 us (26%)
  Pallas kernels  9.86 us (11%)
  local copies, waits for them, and re-layouts  6.41 us (7%)
  other arithmetic  5.66 us (6%)
  matrix products  4.58 us (5%)
  between operations  1.17 us (1%)
    ppermute x21, waiting for transfers between devices, swap(): lax.ppermute(value, AXES, [(i, i ^ j * mask[name]) for i in range(wide *...  38.4 us
    ppermute x21, starting transfers between devices, swap(): lax.ppermute(value, AXES, [(i, i ^ j * mask[name]) for i in range(wide *...  23.2 us
    pallas_call x1, Pallas kernels, products(): pl.pallas_call(products_kernel, grid=(steps,), in_specs=[columns, whole,...  6.62 us
    dot_general x1, matrix products, on_device(): lax.dot_general(tokens, cotangent, (((0,), (0,)), ((), ())), preferred_el...  4.58 us
    unnamed x9, local copies, waits for them, and re-layouts  4.46 us
    pallas_call x1, Pallas kernels, bound_of(): pl.pallas_call(bound_kernel, in_specs=[pl.BlockSpec(memory_space=pl.ANY)]...  3.25 us
    reshape x1, other arithmetic, on_device(): part = part.astype(jnp.float16).reshape(nz, nx, ny, rows, kd)  2.37 us
  transfers between devices with their start and end apart: 21, of which 14 were waited for; matrix products, arithmetic and copies ran while one was open for 6% of the time, Pallas kernels for 11%

profile of v8, /device:TPU:0, one launch (start us, length us, event | category | flops | bytes accessed | tf_op | source)
XLA Modules:
  0.0 89.3 jit_solution(7496335348736183477)
XLA Ops:
  0.6 3.1 %collective-permute-start = (bf16[128,512]{1,0:T(8,128)(2,1)}, bf16[128,512]{1,0:T(8,128)(2,1)S(1)}, u32[]{:S(2)}, u32[]{:S(2)}) collective-permute-start(bf16[128,512]{1,0:T(8,128)(2,1)} %param.4), channel_id=1, source_target_pairs={{0,2},{1,3},{2,0},{3,1},{4,6},{5,7},{6,4},{7,5},{8,10},{9,11},{10,... | collective-permute-start | bytes 393224 | tf_op jit(solution)/shard_map/ppermute | solution.py:104
  3.7 3.2 %shard_map.58 = f32[8,512]{1,0:T(8,128)} custom-call(bf16[512,4096]{1,0:T(8,128)(2,1)} %tok.3, bf16[512,512]{1,0:T(8,128)(2,1)} %cot.3), custom_call_target="tpu_custom_call" | custom-call | flops 4194304 | bytes 4718592 | tf_op jit(solution)/shard_map/pallas_call | solution.py:73
  7.4 1.4 %collective-permute-done.1 = f32[8,512]{1,0:T(8,128)S(1)} collective-permute-done((f32[8,512]{1,0:T(8,128)}, f32[8,512]{1,0:T(8,128)S(1)}, u32[]{:S(2)}, u32[]{:S(2)}) %collective-permute-start.1) | collective-permute-done | bytes 16416 | tf_op jit(solution)/shard_map/ppermute | solution.py:104
  9.6 4.6 %multiply_convert_fusion = f16[4096,512]{1,0:T(8,128)(2,1)S(1)} fusion(bf16[512,4096]{1,0:T(8,128)(2,1)} %tok.3, bf16[512,512]{1,0:T(8,128)(2,1)S(1)} %copy-done.1, f32[512]{0:T(512)S(1)} %bitcast.125), kind=kOutput, calls=%fused_computation | convolution fusion | flops 2151677952 | bytes 8914944 | tf_op jit(solution)/shard_map/dot_general | solution.py:156
  14.2 2.2 %dynamic-slice_bitcast_fusion = f16[4,2,2,1,128,512]{5,4,2,1,0,3:T(8,128)(2,1)} fusion(f16[4,2,2,2,128,512]{5,4,3,2,1,0:T(8,128)(2,1)S(1)} %bitcast.95, s32[]{:T(128)S(6)} %select_n.87), kind=kLoop, calls=%fused_computation.6 | loop fusion | bytes 4194308
  17.0 3.8 %collective-permute-start.4 = (bf16[128,512]{1,0:T(8,128)(2,1)S(1)}, bf16[128,512]{1,0:T(8,128)(2,1)S(1)}, u32[]{:S(2)}, u32[]{:S(2)}) collective-permute-start(bf16[128,512]{1,0:T(8,128)(2,1)S(1)} %copy-done.3), channel_id=1, source_target_pairs={{0,6},{1,7},{2,4},{3,5},{4,2},{5,3},{6,0},{7,1},{8,14},{9,15},{10,... | collective-permute-start | bytes 393224 | tf_op jit(solution)/shard_map/ppermute | solution.py:104
  21.2 2.4 %fusion = f16[4,2,2,128,512]{4,3,2,1,0:T(8,128)(2,1)S(1)} fusion(f16[4,2,2,1,128,512]{5,4,2,1,0,3:T(8,128)(2,1)S(1)} %collective-permute-done.2, f16[4,2,2,2,128,512]{5,4,3,2,1,0:T(8,128)(2,1)} %bitcast.96, s32[]{:T(128)S(6)} %select_n.86), kind=kLoop, calls=%fused_computation.2 | loop fusion | flops 4194304 | bytes 6291460 | tf_op jit(solution)/shard_map/reshape | solution.py:166
  23.6 1.6 %collective-permute-done.4 = bf16[128,512]{1,0:T(8,128)(2,1)S(1)} collective-permute-done((bf16[128,512]{1,0:T(8,128)(2,1)S(1)}, bf16[128,512]{1,0:T(8,128)(2,1)S(1)}, u32[]{:S(2)}, u32[]{:S(2)}) %collective-permute-start.4) | collective-permute-done | bytes 131104 | tf_op jit(solution)/shard_map/ppermute | solution.py:104
  25.2 7.2 %collective-permute-done.3 = bf16[128,512]{1,0:T(8,128)(2,1)S(1)} collective-permute-done((bf16[128,512]{1,0:T(8,128)(2,1)S(1)}, bf16[128,512]{1,0:T(8,128)(2,1)S(1)}, u32[]{:S(2)}, u32[]{:S(2)}) %collective-permute-start.3) | collective-permute-done | bytes 131104 | tf_op jit(solution)/shard_map/ppermute | solution.py:104
  32.6 1.6 %collective-permute-start.10 = (f16[2,1,2,64,512]{4,3,2,1,0:T(8,128)(2,1)S(1)}, f16[2,1,2,64,512]{4,3,2,1,0:T(8,128)(2,1)S(1)}, u32[]{:S(2)}, u32[]{:S(2)}) collective-permute-start(f16[2,1,2,64,512]{4,3,2,1,0:T(8,128)(2,1)S(1)} %constant_dynamic-slice_fusion.7), channel_id=1, source_target_pairs={{0,1},{1,0},{2,3},{3,2},{4,5},{5,4},{6,7},{7,6},{8,9},{9,8},{10,11... | collective-permute-start | bytes 786440 | tf_op jit(solution)/shard_map/ppermute | solution.py:104
  34.1 1.5 %collective-permute-start.12 = (f16[2,2,1,64,512]{4,3,2,1,0:T(8,128)(2,1)S(1)}, f16[2,2,1,64,512]{4,3,2,1,0:T(8,128)(2,1)S(1)}, u32[]{:S(2)}, u32[]{:S(2)}) collective-permute-start(f16[2,2,1,64,512]{4,3,2,1,0:T(8,128)(2,1)S(1)} %constant_dynamic-slice_fusion.5), channel_id=1, source_target_pairs={{0,16},{1,17},{2,18},{3,19},{4,20},{5,21},{6,22},{7,23},{8,24},{9,... | collective-permute-start | bytes 786440 | tf_op jit(solution)/shard_map/ppermute | solution.py:104
  37.0 9.2 %collective-permute-done.5 = bf16[264,512]{1,0:T(8,128)(2,1)S(1)} collective-permute-done((bf16[264,512]{1,0:T(8,128)(2,1)S(1)}, bf16[264,512]{1,0:T(8,128)(2,1)S(1)}, u32[]{:S(2)}, u32[]{:S(2)}) %collective-permute-start.5) | collective-permute-done | bytes 270368 | tf_op jit(solution)/shard_map/ppermute | solution.py:104
  46.2 1.2 %collective-permute-done.6 = bf16[264,512]{1,0:T(8,128)(2,1)S(1)} collective-permute-done((bf16[264,512]{1,0:T(8,128)(2,1)S(1)}, bf16[264,512]{1,0:T(8,128)(2,1)S(1)}, u32[]{:S(2)}, u32[]{:S(2)}) %collective-permute-start.6) | collective-permute-done | bytes 270368 | tf_op jit(solution)/shard_map/ppermute | solution.py:104
  48.6 1.5 %collective-permute-start.11 = (f16[2,1,1,64,512]{4,3,2,1,0:T(8,128)(2,1)S(1)}, f16[2,1,1,64,512]{4,3,2,1,0:T(8,128)(2,1)S(1)}, u32[]{:S(2)}, u32[]{:S(2)}) collective-permute-start(f16[2,1,1,64,512]{4,3,2,1,0:T(8,128)(2,1)S(1)} %constant_dynamic-slice_fusion.6), channel_id=1, source_target_pairs={{0,16},{1,17},{2,18},{3,19},{4,20},{5,21},{6,22},{7,23},{8,24},{9,... | collective-permute-start | bytes 393224 | tf_op jit(solution)/shard_map/ppermute | solution.py:104
  50.2 1.6 %collective-permute-start.8 = (bf16[520,512]{1,0:T(8,128)(2,1)S(1)}, bf16[520,512]{1,0:T(8,128)(2,1)S(1)}, u32[]{:S(2)}, u32[]{:S(2)}) collective-permute-start(bf16[520,512]{1,0:T(8,128)(2,1)S(1)} %pad_maximum_fusion.2), channel_id=1, source_target_pairs={{0,1},{1,0},{2,3},{3,2},{4,5},{5,4},{6,7},{7,6},{8,9},{9,8},{10,11... | collective-permute-start | bytes 1597448 | tf_op jit(solution)/shard_map/ppermute | solution.py:104
  52.5 1.9 %collective-permute-done.13 = f16[2,1,1,64,512]{4,3,2,1,0:T(8,128)(2,1)S(1)} collective-permute-done((f16[2,1,1,64,512]{4,3,2,1,0:T(8,128)(2,1)S(1)}, f16[2,1,1,64,512]{4,3,2,1,0:T(8,128)(2,1)S(1)}, u32[]{:S(2)}, u32[]{:S(2)}) %collective-permute-start.13) | collective-permute-done | bytes 131104 | tf_op jit(solution)/shard_map/ppermute | solution.py:104
  55.1 1.6 %collective-permute-start.14 = (f16[2,1,2,64,512]{4,3,2,1,0:T(8,128)(2,1)S(1)}, f16[2,1,2,64,512]{4,3,2,1,0:T(8,128)(2,1)S(1)}, u32[]{:S(2)}, u32[]{:S(2)}) collective-permute-start(f16[2,1,2,64,512]{4,3,2,1,0:T(8,128)(2,1)S(1)} %constant_dynamic-slice_fusion.3), channel_id=1, source_target_pairs={{0,1},{1,0},{2,3},{3,2},{4,5},{5,4},{6,7},{7,6},{8,9},{9,8},{10,11... | collective-permute-start | bytes 786440 | tf_op jit(solution)/shard_map/ppermute | solution.py:104
  56.7 1.6 %collective-permute-start.15 = (f16[2,2,1,64,512]{4,3,2,1,0:T(8,128)(2,1)S(1)}, f16[2,2,1,64,512]{4,3,2,1,0:T(8,128)(2,1)S(1)}, u32[]{:S(2)}, u32[]{:S(2)}) collective-permute-start(f16[2,2,1,64,512]{4,3,2,1,0:T(8,128)(2,1)S(1)} %constant_dynamic-slice_fusion.2), channel_id=1, source_target_pairs={{0,16},{1,17},{2,18},{3,19},{4,20},{5,21},{6,22},{7,23},{8,24},{9,... | collective-permute-start | bytes 786440 | tf_op jit(solution)/shard_map/ppermute | solution.py:104
  58.5 10.6 %collective-permute-done.14 = f16[2,1,2,64,512]{4,3,2,1,0:T(8,128)(2,1)S(1)} collective-permute-done((f16[2,1,2,64,512]{4,3,2,1,0:T(8,128)(2,1)S(1)}, f16[2,1,2,64,512]{4,3,2,1,0:T(8,128)(2,1)S(1)}, u32[]{:S(2)}, u32[]{:S(2)}) %collective-permute-start.14) | collective-permute-done | bytes 262176 | tf_op jit(solution)/shard_map/ppermute | solution.py:104
  72.1 1.2 %collective-permute-start.18 = (f16[2,1,1,64,512]{4,3,2,1,0:T(8,128)(2,1)S(1)}, f16[2,1,1,64,512]{4,3,2,1,0:T(8,128)(2,1)S(1)}, u32[]{:S(2)}, u32[]{:S(2)}) collective-permute-start(f16[2,1,1,64,512]{4,3,2,1,0:T(8,128)(2,1)S(1)} %constant_dynamic-slice_fusion.1), channel_id=1, source_target_pairs={{0,16},{1,17},{2,18},{3,19},{4,20},{5,21},{6,22},{7,23},{8,24},{9,... | collective-permute-start | bytes 393224 | tf_op jit(solution)/shard_map/ppermute | solution.py:104
  73.4 2.5 %collective-permute-start.17 = (f16[136,512]{1,0:T(8,128)(2,1)S(1)}, f16[136,512]{1,0:T(8,128)(2,1)S(1)}, u32[]{:S(2)}, u32[]{:S(2)}) collective-permute-start(f16[136,512]{1,0:T(8,128)(2,1)S(1)} %get-tuple-element.49), channel_id=1, source_target_pairs={{0,6},{1,7},{2,4},{3,5},{4,2},{5,3},{6,0},{7,1},{8,14},{9,15},{10,... | collective-permute-start | bytes 417800 | tf_op jit(solution)/shard_map/ppermute | solution.py:104
  78.3 1.8 %copy-done = bf16[512,4096]{1,0:T(8,128)(2,1)S(1)} copy-done((bf16[512,4096]{1,0:T(8,128)(2,1)S(1)}, bf16[512,4096]{1,0:T(8,128)(2,1)}, u32[]{:S(2)}) %copy-start) | copy-done | bytes 4194328
  80.2 6.6 %shard_map.59 = (bf16[512,512]{1,0:T(8,128)(2,1)}, bf16[512,4096]{1,0:T(8,128)(2,1)}) custom-call(bf16[512,4096]{1,0:T(8,128)(2,1)S(1)} %copy-done, bf16[512,512]{1,0:T(8,128)(2,1)S(1)} %copy-done.1, bf16[4,1024,512]{2,1,0:T(8,128)(2,1)S(1)} %bitcast.89), custom_call_target="tpu_custom_call" | custom-call | tf_op jit(solution)/shard_map/pallas_call | solution.py:35
  86.8 1.6 %collective-permute-done.20 = f16[136,512]{1,0:T(8,128)(2,1)S(1)} collective-permute-done((f16[136,512]{1,0:T(8,128)(2,1)S(1)}, f16[136,512]{1,0:T(8,128)(2,1)S(1)}, u32[]{:S(2)}, u32[]{:S(2)}) %collective-permute-start.20) | collective-permute-done | bytes 139296 | tf_op jit(solution)/shard_map/ppermute | solution.py:104
  (99 shorter events, 12.6 us)
Async XLA Ops:
  0.6 8.9 %copy-start.1 = (bf16[512,512]{1,0:T(8,128)(2,1)S(1)}, bf16[512,512]{1,0:T(8,128)(2,1)}, u32[]{:S(2)}) copy-start(bf16[512,512]{1,0:T(8,128)(2,1)} %cot.3) | copy-start | bytes 1572868
  0.6 6.8 %collective-permute-start = (bf16[128,512]{1,0:T(8,128)(2,1)}, bf16[128,512]{1,0:T(8,128)(2,1)S(1)}, u32[]{:S(2)}, u32[]{:S(2)}) collective-permute-start(bf16[128,512]{1,0:T(8,128)(2,1)} %param.4), channel_id=1, source_target_pairs={{0,2},{1,3},{2,0},{3,1},{4,6},{5,7},{6,4},{7,5},{8,10},{9,11},{10,... | collective-permute-start | bytes 393224 | tf_op jit(solution)/shard_map/ppermute | solution.py:104
  7.4 1.4 %collective-permute-start.1 = (f32[8,512]{1,0:T(8,128)}, f32[8,512]{1,0:T(8,128)S(1)}, u32[]{:S(2)}, u32[]{:S(2)}) collective-permute-start(f32[8,512]{1,0:T(8,128)} %shard_map.58), channel_id=1, source_target_pairs={{0,8},{1,9},{2,10},{3,11},{4,12},{5,13},{6,14},{7,15},{8,0},{9,1},... | collective-permute-start | bytes 49160 | tf_op jit(solution)/shard_map/ppermute | solution.py:104
  14.2 2.6 %copy-start.2 = (f16[4096,512]{1,0:T(8,128)(2,1)}, f16[4096,512]{1,0:T(8,128)(2,1)S(1)}, u32[]{:S(2)}) copy-start(f16[4096,512]{1,0:T(8,128)(2,1)S(1)} %multiply_convert_fusion) | copy-start | bytes 12582916
  14.2 2.8 %copy-start.3 = (bf16[128,512]{1,0:T(8,128)(2,1)S(1)}, bf16[128,512]{1,0:T(8,128)(2,1)}, u32[]{:S(2)}) copy-start(bf16[128,512]{1,0:T(8,128)(2,1)} %param.4) | copy-start | bytes 393220
  16.8 4.4 %collective-permute-start.2 = (f16[4,2,2,1,128,512]{5,4,2,1,0,3:T(8,128)(2,1)}, f16[4,2,2,1,128,512]{5,4,2,1,0,3:T(8,128)(2,1)S(1)}, u32[]{:S(2)}, u32[]{:S(2)}) collective-permute-start(f16[4,2,2,1,128,512]{5,4,2,1,0,3:T(8,128)(2,1)} %dynamic-slice_bitcast_fusion), channel_id=1, source_target_pairs={{0,8},{1,9},{2,10},{3,11},{4,12},{5,13},{6,14},{7,15},{8,0},{9,1},... | collective-permute-start | bytes 6291464 | tf_op jit(solution)/shard_map/ppermute | solution.py:104
  17.0 8.2 %collective-permute-start.4 = (bf16[128,512]{1,0:T(8,128)(2,1)S(1)}, bf16[128,512]{1,0:T(8,128)(2,1)S(1)}, u32[]{:S(2)}, u32[]{:S(2)}) collective-permute-start(bf16[128,512]{1,0:T(8,128)(2,1)S(1)} %copy-done.3), channel_id=1, source_target_pairs={{0,6},{1,7},{2,4},{3,5},{4,2},{5,3},{6,0},{7,1},{8,14},{9,15},{10,... | collective-permute-start | bytes 393224 | tf_op jit(solution)/shard_map/ppermute | solution.py:104
  20.7 11.6 %collective-permute-start.3 = (bf16[128,512]{1,0:T(8,128)(2,1)S(1)}, bf16[128,512]{1,0:T(8,128)(2,1)S(1)}, u32[]{:S(2)}, u32[]{:S(2)}) collective-permute-start(bf16[128,512]{1,0:T(8,128)(2,1)S(1)} %copy-done.3), channel_id=1, source_target_pairs={{0,4},{1,5},{2,6},{3,7},{4,0},{5,1},{6,2},{7,3},{8,12},{9,13},{10,... | collective-permute-start | bytes 393224 | tf_op jit(solution)/shard_map/ppermute | solution.py:104
  32.6 15.0 %collective-permute-start.10 = (f16[2,1,2,64,512]{4,3,2,1,0:T(8,128)(2,1)S(1)}, f16[2,1,2,64,512]{4,3,2,1,0:T(8,128)(2,1)S(1)}, u32[]{:S(2)}, u32[]{:S(2)}) collective-permute-start(f16[2,1,2,64,512]{4,3,2,1,0:T(8,128)(2,1)S(1)} %constant_dynamic-slice_fusion.7), channel_id=1, source_target_pairs={{0,1},{1,0},{2,3},{3,2},{4,5},{5,4},{6,7},{7,6},{8,9},{9,8},{10,11... | collective-permute-start | bytes 786440 | tf_op jit(solution)/shard_map/ppermute | solution.py:104
  34.1 13.7 %collective-permute-start.12 = (f16[2,2,1,64,512]{4,3,2,1,0:T(8,128)(2,1)S(1)}, f16[2,2,1,64,512]{4,3,2,1,0:T(8,128)(2,1)S(1)}, u32[]{:S(2)}, u32[]{:S(2)}) collective-permute-start(f16[2,2,1,64,512]{4,3,2,1,0:T(8,128)(2,1)S(1)} %constant_dynamic-slice_fusion.5), channel_id=1, source_target_pairs={{0,16},{1,17},{2,18},{3,19},{4,20},{5,21},{6,22},{7,23},{8,24},{9,... | collective-permute-start | bytes 786440 | tf_op jit(solution)/shard_map/ppermute | solution.py:104
  35.7 10.5 %collective-permute-start.5 = (bf16[264,512]{1,0:T(8,128)(2,1)S(1)}, bf16[264,512]{1,0:T(8,128)(2,1)S(1)}, u32[]{:S(2)}, u32[]{:S(2)}) collective-permute-start(bf16[264,512]{1,0:T(8,128)(2,1)S(1)} %get-tuple-element.73), channel_id=1, source_target_pairs={{0,1},{1,0},{2,3},{3,2},{4,5},{5,4},{6,7},{7,6},{8,9},{9,8},{10,11... | collective-permute-start | bytes 811016 | tf_op jit(solution)/shard_map/ppermute | solution.py:104
  36.3 11.1 %collective-permute-start.6 = (bf16[264,512]{1,0:T(8,128)(2,1)S(1)}, bf16[264,512]{1,0:T(8,128)(2,1)S(1)}, u32[]{:S(2)}, u32[]{:S(2)}) collective-permute-start(bf16[264,512]{1,0:T(8,128)(2,1)S(1)} %get-tuple-element.74), channel_id=1, source_target_pairs={{0,16},{1,17},{2,18},{3,19},{4,20},{5,21},{6,22},{7,23},{8,24},{9,... | collective-permute-start | bytes 811016 | tf_op jit(solution)/shard_map/ppermute | solution.py:104
  48.0 6.4 %collective-permute-start.13 = (f16[2,1,1,64,512]{4,3,2,1,0:T(8,128)(2,1)S(1)}, f16[2,1,1,64,512]{4,3,2,1,0:T(8,128)(2,1)S(1)}, u32[]{:S(2)}, u32[]{:S(2)}) collective-permute-start(f16[2,1,1,64,512]{4,3,2,1,0:T(8,128)(2,1)S(1)} %constant_dynamic-slice_fusion.4), channel_id=1, source_target_pairs={{0,1},{1,0},{2,3},{3,2},{4,5},{5,4},{6,7},{7,6},{8,9},{9,8},{10,11... | collective-permute-start | bytes 393224 | tf_op jit(solution)/shard_map/ppermute | solution.py:104
  48.6 6.4 %collective-permute-start.11 = (f16[2,1,1,64,512]{4,3,2,1,0:T(8,128)(2,1)S(1)}, f16[2,1,1,64,512]{4,3,2,1,0:T(8,128)(2,1)S(1)}, u32[]{:S(2)}, u32[]{:S(2)}) collective-permute-start(f16[2,1,1,64,512]{4,3,2,1,0:T(8,128)(2,1)S(1)} %constant_dynamic-slice_fusion.6), channel_id=1, source_target_pairs={{0,16},{1,17},{2,18},{3,19},{4,20},{5,21},{6,22},{7,23},{8,24},{9,... | collective-permute-start | bytes 393224 | tf_op jit(solution)/shard_map/ppermute | solution.py:104
  50.2 20.3 %collective-permute-start.8 = (bf16[520,512]{1,0:T(8,128)(2,1)S(1)}, bf16[520,512]{1,0:T(8,128)(2,1)S(1)}, u32[]{:S(2)}, u32[]{:S(2)}) collective-permute-start(bf16[520,512]{1,0:T(8,128)(2,1)S(1)} %pad_maximum_fusion.2), channel_id=1, source_target_pairs={{0,1},{1,0},{2,3},{3,2},{4,5},{5,4},{6,7},{7,6},{8,9},{9,8},{10,11... | collective-permute-start | bytes 1597448 | tf_op jit(solution)/shard_map/ppermute | solution.py:104
  51.8 18.7 %collective-permute-start.7 = (bf16[520,512]{1,0:T(8,128)(2,1)S(1)}, bf16[520,512]{1,0:T(8,128)(2,1)S(1)}, u32[]{:S(2)}, u32[]{:S(2)}) collective-permute-start(bf16[520,512]{1,0:T(8,128)(2,1)S(1)} %pad_maximum_fusion.1), channel_id=1, source_target_pairs={{0,16},{1,17},{2,18},{3,19},{4,20},{5,21},{6,22},{7,23},{8,24},{9,... | collective-permute-start | bytes 1597448 | tf_op jit(solution)/shard_map/ppermute | solution.py:104
  55.1 14.1 %collective-permute-start.14 = (f16[2,1,2,64,512]{4,3,2,1,0:T(8,128)(2,1)S(1)}, f16[2,1,2,64,512]{4,3,2,1,0:T(8,128)(2,1)S(1)}, u32[]{:S(2)}, u32[]{:S(2)}) collective-permute-start(f16[2,1,2,64,512]{4,3,2,1,0:T(8,128)(2,1)S(1)} %constant_dynamic-slice_fusion.3), channel_id=1, source_target_pairs={{0,1},{1,0},{2,3},{3,2},{4,5},{5,4},{6,7},{7,6},{8,9},{9,8},{10,11... | collective-permute-start | bytes 786440 | tf_op jit(solution)/shard_map/ppermute | solution.py:104
  56.7 13.7 %collective-permute-start.15 = (f16[2,2,1,64,512]{4,3,2,1,0:T(8,128)(2,1)S(1)}, f16[2,2,1,64,512]{4,3,2,1,0:T(8,128)(2,1)S(1)}, u32[]{:S(2)}, u32[]{:S(2)}) collective-permute-start(f16[2,2,1,64,512]{4,3,2,1,0:T(8,128)(2,1)S(1)} %constant_dynamic-slice_fusion.2), channel_id=1, source_target_pairs={{0,16},{1,17},{2,18},{3,19},{4,20},{5,21},{6,22},{7,23},{8,24},{9,... | collective-permute-start | bytes 786440 | tf_op jit(solution)/shard_map/ppermute | solution.py:104
  71.0 7.1 %collective-permute-start.9 = (bf16[4,2,2,2,64,512]{5,4,3,2,1,0:T(8,128)(2,1)S(1)}, bf16[4,2,2,2,64,512]{5,4,3,2,1,0:T(8,128)(2,1)S(1)}, u32[]{:S(2)}, u32[]{:S(2)}) collective-permute-start(bf16[4,2,2,2,64,512]{5,4,3,2,1,0:T(8,128)(2,1)S(1)} %pad_maximum_fusion), channel_id=1, source_target_pairs={{0,8},{1,9},{2,10},{3,11},{4,12},{5,13},{6,14},{7,15},{8,0},{9,1},... | collective-permute-start | bytes 6291464 | tf_op jit(solution)/shard_map/ppermute | solution.py:104
  71.5 6.0 %collective-permute-start.19 = (f16[2,1,1,64,512]{4,3,2,1,0:T(8,128)(2,1)S(1)}, f16[2,1,1,64,512]{4,3,2,1,0:T(8,128)(2,1)S(1)}, u32[]{:S(2)}, u32[]{:S(2)}) collective-permute-start(f16[2,1,1,64,512]{4,3,2,1,0:T(8,128)(2,1)S(1)} %constant_dynamic-slice_fusion), channel_id=1, source_target_pairs={{0,1},{1,0},{2,3},{3,2},{4,5},{5,4},{6,7},{7,6},{8,9},{9,8},{10,11... | collective-permute-start | bytes 393224 | tf_op jit(solution)/shard_map/ppermute | solution.py:104
  72.1 5.7 %collective-permute-start.18 = (f16[2,1,1,64,512]{4,3,2,1,0:T(8,128)(2,1)S(1)}, f16[2,1,1,64,512]{4,3,2,1,0:T(8,128)(2,1)S(1)}, u32[]{:S(2)}, u32[]{:S(2)}) collective-permute-start(f16[2,1,1,64,512]{4,3,2,1,0:T(8,128)(2,1)S(1)} %constant_dynamic-slice_fusion.1), channel_id=1, source_target_pairs={{0,16},{1,17},{2,18},{3,19},{4,20},{5,21},{6,22},{7,23},{8,24},{9,... | collective-permute-start | bytes 393224 | tf_op jit(solution)/shard_map/ppermute | solution.py:104
  73.4 13.4 %collective-permute-start.16 = (f16[136,512]{1,0:T(8,128)(2,1)S(1)}, f16[136,512]{1,0:T(8,128)(2,1)S(1)}, u32[]{:S(2)}, u32[]{:S(2)}) collective-permute-start(f16[136,512]{1,0:T(8,128)(2,1)S(1)} %get-tuple-element.48), channel_id=1, source_target_pairs={{0,4},{1,5},{2,6},{3,7},{4,0},{5,1},{6,2},{7,3},{8,12},{9,13},{10,... | collective-permute-start | bytes 417800 | tf_op jit(solution)/shard_map/ppermute | solution.py:104
  73.4 13.4 %collective-permute-start.17 = (f16[136,512]{1,0:T(8,128)(2,1)S(1)}, f16[136,512]{1,0:T(8,128)(2,1)S(1)}, u32[]{:S(2)}, u32[]{:S(2)}) collective-permute-start(f16[136,512]{1,0:T(8,128)(2,1)S(1)} %get-tuple-element.49), channel_id=1, source_target_pairs={{0,6},{1,7},{2,4},{3,5},{4,2},{5,3},{6,0},{7,1},{8,14},{9,15},{10,... | collective-permute-start | bytes 417800 | tf_op jit(solution)/shard_map/ppermute | solution.py:104
  78.0 10.4 %collective-permute-start.20 = (f16[136,512]{1,0:T(8,128)(2,1)S(1)}, f16[136,512]{1,0:T(8,128)(2,1)S(1)}, u32[]{:S(2)}, u32[]{:S(2)}) collective-permute-start(f16[136,512]{1,0:T(8,128)(2,1)S(1)} %pad_maximum_fusion.5), channel_id=1, source_target_pairs={{0,2},{1,3},{2,0},{3,1},{4,6},{5,7},{6,4},{7,5},{8,10},{9,11},{10,... | collective-permute-start | bytes 417800 | tf_op jit(solution)/shard_map/ppermute | solution.py:104
  (1 other events, 2.2 us)

commit v9 on v8

--- a/solution.py
+++ b/solution.py
@@ -91,17 +91,28 @@
     wide, node = lax.axis_size("wide"), lax.axis_size("node")
     w_me, n_me = lax.axis_index("wide"), lax.axis_index("node")
     rows, kd = key_weight.shape
-    half = rows // 2
-    ny, nx, nz = wide // 2, 2, node // 2
+    n = wide // 2
+    nz = node // n
     core, y_me = w_me & 1, w_me >> 1
-    x_me, z_me = n_me & 1, n_me >> 1
-
-    size = {"core": 2, "y": ny, "x": nx, "z": nz}
-    place = {"core": core, "y": y_me, "x": x_me, "z": z_me}
-    mask = {"core": node, "y": 2 * node, "x": 1, "z": 2}
+    x_me, z_me = n_me % n, n_me // n
+    size = {"core": 2, "first": n, "second": n, "z": nz}
+    place = {
+        "core": core,
+        "first": jnp.where(core == 0, x_me, y_me),
+        "second": jnp.where(core == 0, y_me, x_me),
+        "z": z_me,
+    }
 
     def swap(value, name, j):
-        return lax.ppermute(value, AXES, [(i, i ^ (j * mask[name])) for i in range(wide * node)])
+        over_x, over_y = 1, 2 * node
+        mask = {
+            "core": (node, node),
+            "first": (over_x, over_y),
+            "second": (over_y, over_x),
+            "z": (n, n),
+        }[name]
+        pairs = [(i, i ^ (j * mask[i // node % 2])) for i in range(wide * node)]
+        return lax.ppermute(value, AXES, pairs)
 
     def pick(value, *places):
         start, extent = [0] * value.ndim, list(value.shape)
@@ -156,55 +167,33 @@
     part = lax.dot_general(
         tokens, cotangent, (((0,), (0,)), ((), ())), preferred_element_type=jnp.float32
     )
-    part = (part * scale(TOP - power)).astype(jnp.float16).reshape(nz, nx, ny, 2, rows, kd)
-    z_low = z_me % (nz // 2)
-    z_top = z_me - z_low
-    far, near = (0, nz // 2 - z_top, nz // 2), (0, z_top, nz // 2)
-    upper, lower = (3, 0, half), (3, half, half)
-    other = swap(pick(part, (3, 1 - core)), "core", 1)
-    part = pick(part, (3, core)).astype(jnp.float32) + other.astype(jnp.float32)
-    part = part.astype(jnp.float16).reshape(nz, nx, ny, rows, kd)
-
-    part, power, shards = held((part, power, shards))
-    far_one, far_two = given(part, "x", 1, far, upper), given(part, "y", 2, far, lower)
-    blocks = in_order(key_weight, shards, "z").reshape(nz, 2, half, kd)
-    one, power_x = gathered(blocks[:, 0], "x", power)
-    two, power_y = gathered(blocks[:, 1], "y", power)
-    by_x, by_y = factors(power, power_x), factors(power, power_y)
-    by_x, by_y = held((by_x, by_y))
-    one, power_xy = gathered(one, "y", by_x[0])
-    two, power_yx = gathered(two, "x", by_y[0])
-
-    far_one = taken(part, far_one, "x", 1, by_x[1], far, upper)
-    far_two = taken(part, far_two, "y", 2, by_y[1], far, lower)
-    far_one_got, far_two_got = given(far_one, "y", 2), given(far_two, "x", 1)
-    part, far_one_got, far_two_got = held((part, far_one_got, far_two_got))
-    near_one, near_two = given(part, "x", 1, near, upper), given(part, "y", 2, near, lower)
-
-    by_xy, by_yx = factors(by_x[0], power_xy), factors(by_y[0], power_yx)
-    top = by_xy[0]
-    both = jnp.stack([one.transpose(2, 1, 0, 3, 4), two.transpose(2, 0, 1, 3, 4)], axis=3)
-    weight = in_order(both, [swap(both, "core", 1)], "core")
-    weight = weight.transpose(1, 2, 3, 0, 4, 5, 6).reshape(nz, nx * ny * 2 * rows, kd)
-
-    def last_sum(one, one_got, two, two_got):
-        one = taken(one, one_got, "y", 2, by_xy[1])
-        two = taken(two, two_got, "x", 1, by_yx[1])
-        return jnp.concatenate([one, two], axis=3).reshape(nz // 2, rows, kd)
-
-    far_sum = last_sum(far_one, far_one_got, far_two, far_two_got)
-    packets = [noted(pick(far_sum, (0, z_low ^ j)), top) for j in range(nz // 2)]
-    near_one = taken(part, near_one, "x", 1, by_x[1], near, upper)
-    near_two = taken(part, near_two, "y", 2, by_y[1], near, lower)
-    packets, near_one, near_two = held((packets, near_one, near_two))
-    got = [swap(packet, "z", nz // 2 + j) for j, packet in enumerate(packets)]
-    near_one_got, near_two_got = given(near_one, "y", 2), given(near_two, "x", 1)
-    near_sum = last_sum(near_one, near_one_got, near_two, near_two_got)
-    got += [swap(noted(pick(near_sum, (0, z_low ^ j)), top), "z", j) for j in range(1, nz // 2)]
-
+    part = (part * scale(TOP - power)).astype(jnp.float16).reshape(nz * n * n, 2, rows, kd)
+    other = swap(pick(part, (1, 1 - core)), "core", 1)
+    part, shards = held((part, shards))
+    blocks = in_order(key_weight, shards, "z")
+    part = pick(part, (1, core)).astype(jnp.float32) + other.astype(jnp.float32)
+    part = part.astype(jnp.float16).reshape(nz, n, n, rows, kd)
+    part = jnp.where(core == 0, part, part.transpose(0, 2, 1, 3, 4))
+
+    blocks, power_first = gathered(blocks, "first", power)
+    by_first = factors(power, power_first)
+    part, blocks, by_first = held((part, blocks, by_first))
+    sums = taken(part, given(part, "first", 1), "first", 1, by_first[1])
+    blocks, power_second = gathered(blocks, "second", by_first[0])
+    by_second = factors(by_first[0], power_second)
+    sums = taken(sums, given(sums, "second", 2), "second", 2, by_second[1])
+    sums = sums.reshape(nz, rows, kd)
+
+    other = swap(blocks, "core", 1)
+    x_first = jnp.where(core == 0, blocks, other).transpose(2, 1, 0, 3, 4)
+    y_first = jnp.where(core == 0, other, blocks).transpose(2, 0, 1, 3, 4)
+    weight = jnp.stack([x_first, y_first], axis=3).reshape(nz, n * n * 2 * rows, kd)
+
+    top = by_second[0]
+    got = [swap(noted(pick(sums, (0, z_me ^ j)), top), "z", j) for j in range(1, nz)]
     keys, input_grad = products(tokens, cotangent, weight)
     keys, input_grad, got = held((keys, input_grad, got))
-    total = pick(near_sum, (0, z_low))[0].astype(jnp.float32) * scale(top - TOP)
+    total = pick(sums, (0, z_me))[0].astype(jnp.float32) * scale(top - TOP)
     for one, other in [read(one, (rows, kd)) for one in got]:
         total = total + one.astype(jnp.float32) * scale(other - TOP)
     total_tokens = tokens.shape[0] * wide * node

time: 89.5 us -> 90.1 us (level); the launches traced: 89.3 us -> 88.9 us
  other arithmetic: 5.66 us -> 8.77 us
  waiting for transfers between devices: 38.4 us -> 35.7 us
  starting transfers between devices: 23.2 us -> 20.8 us
  local copies, waits for them, and re-layouts: 6.41 us -> 8.25 us
    ppermute x21 -> x13, waiting for transfers between devices: 38.4 us -> 35.7 us  [swap(): return lax.ppermute(value, AXES, pairs)]
    reshape x3 -> x0, other arithmetic: 2.48 us -> none  [the longest x1 2.37 us: on_device(): part = part.astype(jnp.float16).reshape(nz, nx, ny, rows, kd)]
    convert_element_type x0 -> x1, other arithmetic: none -> 2.37 us  [on_device(): part = part.astype(jnp.float16).reshape(nz, n, n, rows, kd)]
    ppermute x21 -> x13, starting transfers between devices: 23.2 us -> 20.8 us  [swap(): return lax.ppermute(value, AXES, pairs)]
    select_n x0 -> x1, other arithmetic: none -> 1.84 us  [on_device(): part = jnp.where(core == 0, part, part.transpose(0, 2, 1, 3, 4))]
    dynamic_slice x8 -> x2, local copies, waits for them, and re-layouts: 0.32 us -> 1.55 us  [pick(): return lax.dynamic_slice(value, start, extent)]
    slice x4 -> x2, local copies, waits for them, and re-layouts: 0.11 us -> 1.33 us  [read(): return (got[:-NOTE].reshape(shape), got[-NOTE:][:1].astype(jnp.float32))]
    unnamed x9 -> x13, local copies, waits for them, and re-layouts: 4.46 us -> 4.56 us
  transfers between devices with their start and end apart: 21 -> 13, of which waited for: 14 -> 6; matrix products, arithmetic and copies ran while one was open for 6% -> 16% of each run, Pallas kernels for 11% -> 11%
where the time goes in v9:
time: 90.1 us; the launch traced here: 88.9 us
  waiting for transfers between devices  35.7 us (40%)
  starting transfers between devices  20.8 us (23%)
  Pallas kernels  9.87 us (11%)
  other arithmetic  8.77 us (10%)
  local copies, waits for them, and re-layouts  8.25 us (9%)
  matrix products  4.58 us (5%)
  between operations  0.95 us (1%)
    ppermute x13, waiting for transfers between devices, swap(): return lax.ppermute(value, AXES, pairs)  35.7 us
    ppermute x13, starting transfers between devices, swap(): return lax.ppermute(value, AXES, pairs)  20.8 us
    pallas_call x1, Pallas kernels, products(): pl.pallas_call(products_kernel, grid=(steps,), in_specs=[columns, whole,...  6.62 us
    dot_general x1, matrix products, on_device(): lax.dot_general(tokens, cotangent, (((0,), (0,)), ((), ())), preferred_el...  4.58 us
    unnamed x13, local copies, waits for them, and re-layouts  4.56 us
    pallas_call x1, Pallas kernels, bound_of(): pl.pallas_call(bound_kernel, in_specs=[pl.BlockSpec(memory_space=pl.ANY)]...  3.25 us
    convert_element_type x1, other arithmetic, on_device(): part = part.astype(jnp.float16).reshape(nz, n, n, rows, kd)  2.37 us
    select_n x1, other arithmetic, on_device(): part = jnp.where(core == 0, part, part.transpose(0, 2, 1, 3, 4))  1.84 us
  transfers between devices with their start and end apart: 13, of which 6 were waited for; matrix products, arithmetic and copies ran while one was open for 16% of the time, Pallas kernels for 11%

profile of v9, /device:TPU:0, one launch (start us, length us, event | category | flops | bytes accessed | tf_op | source)
XLA Modules:
  0.0 88.9 jit_solution(1357082969571858142)
XLA Ops:
  0.7 3.1 %collective-permute-start = (bf16[128,512]{1,0:T(8,128)(2,1)}, bf16[128,512]{1,0:T(8,128)(2,1)S(1)}, u32[]{:S(2)}, u32[]{:S(2)}) collective-permute-start(bf16[128,512]{1,0:T(8,128)(2,1)} %param.4), channel_id=1, source_target_pairs={{0,2},{1,3},{2,0},{3,1},{4,6},{5,7},{6,4},{7,5},{8,10},{9,11},{10,... | collective-permute-start | bytes 393224 | tf_op jit(solution)/shard_map/ppermute | solution.py:115
  3.7 3.2 %shard_map.58 = f32[8,512]{1,0:T(8,128)} custom-call(bf16[512,4096]{1,0:T(8,128)(2,1)} %tok.3, bf16[512,512]{1,0:T(8,128)(2,1)} %cot.3), custom_call_target="tpu_custom_call" | custom-call | flops 4194304 | bytes 4718592 | tf_op jit(solution)/shard_map/pallas_call | solution.py:73
  7.5 2.8 %collective-permute-start.2 = (bf16[128,512]{1,0:T(8,128)(2,1)S(1)}, bf16[128,512]{1,0:T(8,128)(2,1)S(1)}, u32[]{:S(2)}, u32[]{:S(2)}) collective-permute-start(bf16[128,512]{1,0:T(8,128)(2,1)S(1)} %copy-done.5), channel_id=1, source_target_pairs={{0,4},{1,5},{2,6},{3,7},{4,0},{5,1},{6,2},{7,3},{8,12},{9,13},{10,... | collective-permute-start | bytes 393224 | tf_op jit(solution)/shard_map/ppermute | solution.py:115
  10.2 1.3 %collective-permute-start.3 = (bf16[128,512]{1,0:T(8,128)(2,1)S(1)}, bf16[128,512]{1,0:T(8,128)(2,1)S(1)}, u32[]{:S(2)}, u32[]{:S(2)}) collective-permute-start(bf16[128,512]{1,0:T(8,128)(2,1)S(1)} %copy-done.5), channel_id=1, source_target_pairs={{0,6},{1,7},{2,4},{3,5},{4,2},{5,3},{6,0},{7,1},{8,14},{9,15},{10,... | collective-permute-start | bytes 393224 | tf_op jit(solution)/shard_map/ppermute | solution.py:115
  12.3 4.6 %multiply_convert_fusion = f16[4096,512]{1,0:T(8,128)(2,1)S(1)} fusion(bf16[512,4096]{1,0:T(8,128)(2,1)} %tok.3, bf16[512,512]{1,0:T(8,128)(2,1)S(1)} %copy-done.1, f32[512]{0:T(512)S(1)} %bitcast.69), kind=kOutput, calls=%fused_computation | convolution fusion | flops 2151677952 | bytes 8914944 | tf_op jit(solution)/shard_map/dot_general | solution.py:167
  16.9 2.1 %dynamic-slice_bitcast_fusion = f16[16,1,128,512]{3,2,0,1:T(8,128)(2,1)} fusion(f16[16,2,128,512]{3,2,1,0:T(8,128)(2,1)S(1)} %bitcast.56, s32[]{:T(128)S(6)} %select_n.81), kind=kLoop, calls=%fused_computation.7 | loop fusion | bytes 4194308
  20.4 1.7 %collective-permute-start.5 = (bf16[520,512]{1,0:T(8,128)(2,1)S(1)}, bf16[520,512]{1,0:T(8,128)(2,1)S(1)}, u32[]{:S(2)}, u32[]{:S(2)}) collective-permute-start(bf16[520,512]{1,0:T(8,128)(2,1)S(1)} %pad_maximum_fusion.2), channel_id=1, source_target_pairs={{0,1},{1,0},{2,3},{3,2},{4,5},{5,4},{6,7},{7,6},{8,24},{9,25},{10,... | collective-permute-start | bytes 1597448 | tf_op jit(solution)/shard_map/ppermute | solution.py:115
  22.3 7.5 %collective-permute-done.5 = bf16[520,512]{1,0:T(8,128)(2,1)S(1)} collective-permute-done((bf16[520,512]{1,0:T(8,128)(2,1)S(1)}, bf16[520,512]{1,0:T(8,128)(2,1)S(1)}, u32[]{:S(2)}, u32[]{:S(2)}) %collective-permute-start.5) | collective-permute-done | bytes 532512 | tf_op jit(solution)/shard_map/ppermute | solution.py:115
  29.9 2.4 %add_convert_fusion = f16[16,1,128,512]{3,2,0,1:T(8,128)(2,1)S(1)} fusion(f16[16,1,128,512]{3,2,0,1:T(8,128)(2,1)} %collective-permute-done.4, s32[]{:T(128)S(6)} %select_n.80, f16[16,2,128,512]{3,2,1,0:T(8,128)(2,1)S(1)} %bitcast.57), kind=kLoop, calls=%fused_computation.2 | loop fusion | flops 4194304 | bytes 6291460 | tf_op jit(solution)/shard_map/convert_element_type | solution.py:175
  32.2 1.8 %bitcast_select_fusion = f16[4,2,2,128,512]{4,3,2,1,0:T(8,128)(2,1)} fusion(f16[4,2,2,128,512]{4,3,2,1,0:T(8,128)(2,1)S(1)} %bitcast.54, pred[]{:T(512)S(6)} %eq.4), kind=kLoop, calls=%fused_computation.3 | loop fusion | flops 1048576 | bytes 4194305 | tf_op jit(solution)/shard_map/jit(_where)/select_n | solution.py:176
  34.2 1.8 %collective-permute-start.6 = (bf16[1032,512]{1,0:T(8,128)(2,1)S(1)}, bf16[1032,512]{1,0:T(8,128)(2,1)}, u32[]{:S(2)}, u32[]{:S(2)}) collective-permute-start(bf16[1032,512]{1,0:T(8,128)(2,1)S(1)} %pad_maximum_fusion.1), channel_id=1, source_target_pairs={{0,16},{1,17},{2,18},{3,19},{4,20},{5,21},{6,22},{7,23},{8,9},{9,8... | collective-permute-start | bytes 3170312 | tf_op jit(solution)/shard_map/ppermute | solution.py:115
  36.0 1.4 %constant_dynamic-slice_fusion.1 = f16[4,1,2,128,512]{4,3,2,1,0:T(8,128)(2,1)S(1)} fusion(f16[4,2,2,128,512]{4,3,2,1,0:T(8,128)(2,1)} %bitcast_select_fusion, s32[]{:T(128)S(6)} %select_n.91), kind=kLoop, calls=%fused_computation.30 | loop fusion | bytes 2097156 | tf_op jit(solution)/shard_map/dynamic_slice | solution.py:121
  37.5 1.6 %collective-permute-start.8 = (f16[4,1,2,128,512]{4,3,2,1,0:T(8,128)(2,1)S(1)}, f16[4,1,2,128,512]{4,3,2,1,0:T(8,128)(2,1)S(1)}, u32[]{:S(2)}, u32[]{:S(2)}) collective-permute-start(f16[4,1,2,128,512]{4,3,2,1,0:T(8,128)(2,1)S(1)} %constant_dynamic-slice_fusion.1), channel_id=1, source_target_pairs={{0,1},{1,0},{2,3},{3,2},{4,5},{5,4},{6,7},{7,6},{8,24},{9,25},{10,... | collective-permute-start | bytes 3145736 | tf_op jit(solution)/shard_map/ppermute | solution.py:115
  39.3 20.5 %collective-permute-done.6 = bf16[1032,512]{1,0:T(8,128)(2,1)} collective-permute-done((bf16[1032,512]{1,0:T(8,128)(2,1)S(1)}, bf16[1032,512]{1,0:T(8,128)(2,1)}, u32[]{:S(2)}, u32[]{:S(2)}) %collective-permute-start.6) | collective-permute-done | bytes 1056800 | tf_op jit(solution)/shard_map/ppermute | solution.py:115
  59.8 1.3 %slice.58 = bf16[1024,512]{1,0:T(8,128)(2,1)S(1)} slice(bf16[1032,512]{1,0:T(8,128)(2,1)} %collective-permute-done.6), slice={[0:1024], [0:512]} | slice | bytes 2097152 | tf_op jit(solution)/shard_map/slice | solution.py:134
  61.9 2.0 %collective-permute-start.9 = (f16[4,1,1,128,512]{4,3,2,1,0:T(8,128)(2,1)S(1)}, f16[4,1,1,128,512]{4,3,2,1,0:T(8,128)(2,1)S(1)}, u32[]{:S(2)}, u32[]{:S(2)}) collective-permute-start(f16[4,1,1,128,512]{4,3,2,1,0:T(8,128)(2,1)S(1)} %constant_dynamic-slice_fusion), channel_id=1, source_target_pairs={{0,16},{1,17},{2,18},{3,19},{4,20},{5,21},{6,22},{7,23},{8,9},{9,8... | collective-permute-start | bytes 1572872 | tf_op jit(solution)/shard_map/ppermute | solution.py:115
  65.4 5.8 %collective-permute-done.9 = f16[4,1,1,128,512]{4,3,2,1,0:T(8,128)(2,1)S(1)} collective-permute-done((f16[4,1,1,128,512]{4,3,2,1,0:T(8,128)(2,1)S(1)}, f16[4,1,1,128,512]{4,3,2,1,0:T(8,128)(2,1)S(1)}, u32[]{:S(2)}, u32[]{:S(2)}) %collective-permute-start.9) | collective-permute-done | bytes 524320 | tf_op jit(solution)/shard_map/ppermute | solution.py:115
  71.6 3.2 %collective-permute-start.10 = (f16[136,512]{1,0:T(8,128)(2,1)S(1)}, f16[136,512]{1,0:T(8,128)(2,1)S(1)}, u32[]{:S(2)}, u32[]{:S(2)}) collective-permute-start(f16[136,512]{1,0:T(8,128)(2,1)S(1)} %get-tuple-element.52), channel_id=1, source_target_pairs={{0,2},{1,3},{2,0},{3,1},{4,6},{5,7},{6,4},{7,5},{8,10},{9,11},{10,... | collective-permute-start | bytes 417800 | tf_op jit(solution)/shard_map/ppermute | solution.py:115
  74.8 1.9 %collective-permute-start.11 = (f16[136,512]{1,0:T(8,128)(2,1)S(1)}, f16[136,512]{1,0:T(8,128)(2,1)S(1)}, u32[]{:S(2)}, u32[]{:S(2)}) collective-permute-start(f16[136,512]{1,0:T(8,128)(2,1)S(1)} %get-tuple-element.51), channel_id=1, source_target_pairs={{0,4},{1,5},{2,6},{3,7},{4,0},{5,1},{6,2},{7,3},{8,12},{9,13},{10,... | collective-permute-start | bytes 417800 | tf_op jit(solution)/shard_map/ppermute | solution.py:115
  76.8 1.4 %collective-permute-start.12 = (f16[136,512]{1,0:T(8,128)(2,1)S(1)}, f16[136,512]{1,0:T(8,128)(2,1)S(1)}, u32[]{:S(2)}, u32[]{:S(2)}) collective-permute-start(f16[136,512]{1,0:T(8,128)(2,1)S(1)} %get-tuple-element.50), channel_id=1, source_target_pairs={{0,6},{1,7},{2,4},{3,5},{4,2},{5,3},{6,0},{7,1},{8,14},{9,15},{10,... | collective-permute-start | bytes 417800 | tf_op jit(solution)/shard_map/ppermute | solution.py:115
  78.7 1.9 %copy-done = bf16[512,4096]{1,0:T(8,128)(2,1)S(1)} copy-done((bf16[512,4096]{1,0:T(8,128)(2,1)S(1)}, bf16[512,4096]{1,0:T(8,128)(2,1)}, u32[]{:S(2)}) %copy-start) | copy-done | bytes 4194328
  80.6 6.6 %shard_map.59 = (bf16[512,512]{1,0:T(8,128)(2,1)}, bf16[512,4096]{1,0:T(8,128)(2,1)}) custom-call(bf16[512,4096]{1,0:T(8,128)(2,1)S(1)} %copy-done, bf16[512,512]{1,0:T(8,128)(2,1)S(1)} %copy-done.1, bf16[4,1024,512]{2,1,0:T(8,128)(2,1)S(1)} %bitcast.53), custom_call_target="tpu_custom_call" | custom-call | tf_op jit(solution)/shard_map/pallas_call | solution.py:35
  87.3 0.8 collective-permute-done.11
  88.1 0.8 fusion.3
  (58 shorter events, 6.4 us)
Async XLA Ops:
  0.6 6.8 %copy-start.5 = (bf16[128,512]{1,0:T(8,128)(2,1)S(1)}, bf16[128,512]{1,0:T(8,128)(2,1)}, u32[]{:S(2)}) copy-start(bf16[128,512]{1,0:T(8,128)(2,1)} %param.4) | copy-start | bytes 393220
  0.6 11.7 %copy-start.1 = (bf16[512,512]{1,0:T(8,128)(2,1)S(1)}, bf16[512,512]{1,0:T(8,128)(2,1)}, u32[]{:S(2)}) copy-start(bf16[512,512]{1,0:T(8,128)(2,1)} %cot.3) | copy-start | bytes 1572868
  0.7 6.8 %collective-permute-start = (bf16[128,512]{1,0:T(8,128)(2,1)}, bf16[128,512]{1,0:T(8,128)(2,1)S(1)}, u32[]{:S(2)}, u32[]{:S(2)}) collective-permute-start(bf16[128,512]{1,0:T(8,128)(2,1)} %param.4), channel_id=1, source_target_pairs={{0,2},{1,3},{2,0},{3,1},{4,6},{5,7},{6,4},{7,5},{8,10},{9,11},{10,... | collective-permute-start | bytes 393224 | tf_op jit(solution)/shard_map/ppermute | solution.py:115
  7.4 4.1 %collective-permute-start.1 = (f32[8,512]{1,0:T(8,128)}, f32[8,512]{1,0:T(8,128)S(1)}, u32[]{:S(2)}, u32[]{:S(2)}) collective-permute-start(f32[8,512]{1,0:T(8,128)} %shard_map.58), channel_id=1, source_target_pairs={{0,8},{1,9},{2,10},{3,11},{4,12},{5,13},{6,14},{7,15},{8,0},{9,1},... | collective-permute-start | bytes 49160 | tf_op jit(solution)/shard_map/ppermute | solution.py:115
  7.5 12.8 %collective-permute-start.2 = (bf16[128,512]{1,0:T(8,128)(2,1)S(1)}, bf16[128,512]{1,0:T(8,128)(2,1)S(1)}, u32[]{:S(2)}, u32[]{:S(2)}) collective-permute-start(bf16[128,512]{1,0:T(8,128)(2,1)S(1)} %copy-done.5), channel_id=1, source_target_pairs={{0,4},{1,5},{2,6},{3,7},{4,0},{5,1},{6,2},{7,3},{8,12},{9,13},{10,... | collective-permute-start | bytes 393224 | tf_op jit(solution)/shard_map/ppermute | solution.py:115
  10.2 10.0 %collective-permute-start.3 = (bf16[128,512]{1,0:T(8,128)(2,1)S(1)}, bf16[128,512]{1,0:T(8,128)(2,1)S(1)}, u32[]{:S(2)}, u32[]{:S(2)}) collective-permute-start(bf16[128,512]{1,0:T(8,128)(2,1)S(1)} %copy-done.5), channel_id=1, source_target_pairs={{0,6},{1,7},{2,4},{3,5},{4,2},{5,3},{6,0},{7,1},{8,14},{9,15},{10,... | collective-permute-start | bytes 393224 | tf_op jit(solution)/shard_map/ppermute | solution.py:115
  16.9 2.6 %copy-start.3 = (f16[4096,512]{1,0:T(8,128)(2,1)}, f16[4096,512]{1,0:T(8,128)(2,1)S(1)}, u32[]{:S(2)}) copy-start(f16[4096,512]{1,0:T(8,128)(2,1)S(1)} %multiply_convert_fusion) | copy-start | bytes 12582916
  19.6 10.3 %collective-permute-start.4 = (f16[16,1,128,512]{3,2,0,1:T(8,128)(2,1)}, f16[16,1,128,512]{3,2,0,1:T(8,128)(2,1)}, u32[]{:S(2)}, u32[]{:S(2)}) collective-permute-start(f16[16,1,128,512]{3,2,0,1:T(8,128)(2,1)} %dynamic-slice_bitcast_fusion), channel_id=1, source_target_pairs={{0,8},{1,9},{2,10},{3,11},{4,12},{5,13},{6,14},{7,15},{8,0},{9,1},... | collective-permute-start | bytes 6291464 | tf_op jit(solution)/shard_map/ppermute | solution.py:115
  20.4 9.3 %collective-permute-start.5 = (bf16[520,512]{1,0:T(8,128)(2,1)S(1)}, bf16[520,512]{1,0:T(8,128)(2,1)S(1)}, u32[]{:S(2)}, u32[]{:S(2)}) collective-permute-start(bf16[520,512]{1,0:T(8,128)(2,1)S(1)} %pad_maximum_fusion.2), channel_id=1, source_target_pairs={{0,1},{1,0},{2,3},{3,2},{4,5},{5,4},{6,7},{7,6},{8,24},{9,25},{10,... | collective-permute-start | bytes 1597448 | tf_op jit(solution)/shard_map/ppermute | solution.py:115
  22.1 7.7 %copy-start.4 = (f16[4096,512]{1,0:T(8,128)(2,1)S(1)}, f16[4096,512]{1,0:T(8,128)(2,1)}, u32[]{:S(2)}) copy-start(f16[4096,512]{1,0:T(8,128)(2,1)} %copy-done.3) | copy-start | bytes 12582916
  34.2 25.6 %collective-permute-start.6 = (bf16[1032,512]{1,0:T(8,128)(2,1)S(1)}, bf16[1032,512]{1,0:T(8,128)(2,1)}, u32[]{:S(2)}, u32[]{:S(2)}) collective-permute-start(bf16[1032,512]{1,0:T(8,128)(2,1)S(1)} %pad_maximum_fusion.1), channel_id=1, source_target_pairs={{0,16},{1,17},{2,18},{3,19},{4,20},{5,21},{6,22},{7,23},{8,9},{9,8... | collective-permute-start | bytes 3170312 | tf_op jit(solution)/shard_map/ppermute | solution.py:115
  37.5 23.9 %collective-permute-start.8 = (f16[4,1,2,128,512]{4,3,2,1,0:T(8,128)(2,1)S(1)}, f16[4,1,2,128,512]{4,3,2,1,0:T(8,128)(2,1)S(1)}, u32[]{:S(2)}, u32[]{:S(2)}) collective-permute-start(f16[4,1,2,128,512]{4,3,2,1,0:T(8,128)(2,1)S(1)} %constant_dynamic-slice_fusion.1), channel_id=1, source_target_pairs={{0,1},{1,0},{2,3},{3,2},{4,5},{5,4},{6,7},{7,6},{8,24},{9,25},{10,... | collective-permute-start | bytes 3145736 | tf_op jit(solution)/shard_map/ppermute | solution.py:115
  39.3 22.0 %copy-start.2 = (f16[4,2,2,128,512]{4,3,2,1,0:T(8,128)(2,1)S(1)}, f16[4,2,2,128,512]{4,3,2,1,0:T(8,128)(2,1)}, u32[]{:S(2)}) copy-start(f16[4,2,2,128,512]{4,3,2,1,0:T(8,128)(2,1)} %bitcast_select_fusion) | copy-start | bytes 6291460
  61.2 16.9 %collective-permute-start.7 = (bf16[2,2,4,128,512]{4,3,1,0,2:T(8,128)(2,1)S(1)}, bf16[2,2,4,128,512]{4,3,1,0,2:T(8,128)(2,1)S(1)}, u32[]{:S(2)}, u32[]{:S(2)}) collective-permute-start(bf16[2,2,4,128,512]{4,3,1,0,2:T(8,128)(2,1)S(1)} %copy_dynamic-update-slice_fusion), channel_id=1, source_target_pairs={{0,8},{1,9},{2,10},{3,11},{4,12},{5,13},{6,14},{7,15},{8,0},{9,1},... | collective-permute-start | bytes 6291464 | tf_op jit(solution)/shard_map/ppermute | solution.py:115
  61.9 9.2 %collective-permute-start.9 = (f16[4,1,1,128,512]{4,3,2,1,0:T(8,128)(2,1)S(1)}, f16[4,1,1,128,512]{4,3,2,1,0:T(8,128)(2,1)S(1)}, u32[]{:S(2)}, u32[]{:S(2)}) collective-permute-start(f16[4,1,1,128,512]{4,3,2,1,0:T(8,128)(2,1)S(1)} %constant_dynamic-slice_fusion), channel_id=1, source_target_pairs={{0,16},{1,17},{2,18},{3,19},{4,20},{5,21},{6,22},{7,23},{8,9},{9,8... | collective-permute-start | bytes 1572872 | tf_op jit(solution)/shard_map/ppermute | solution.py:115
  71.6 15.6 %collective-permute-start.10 = (f16[136,512]{1,0:T(8,128)(2,1)S(1)}, f16[136,512]{1,0:T(8,128)(2,1)S(1)}, u32[]{:S(2)}, u32[]{:S(2)}) collective-permute-start(f16[136,512]{1,0:T(8,128)(2,1)S(1)} %get-tuple-element.52), channel_id=1, source_target_pairs={{0,2},{1,3},{2,0},{3,1},{4,6},{5,7},{6,4},{7,5},{8,10},{9,11},{10,... | collective-permute-start | bytes 417800 | tf_op jit(solution)/shard_map/ppermute | solution.py:115
  74.8 13.2 %collective-permute-start.11 = (f16[136,512]{1,0:T(8,128)(2,1)S(1)}, f16[136,512]{1,0:T(8,128)(2,1)S(1)}, u32[]{:S(2)}, u32[]{:S(2)}) collective-permute-start(f16[136,512]{1,0:T(8,128)(2,1)S(1)} %get-tuple-element.51), channel_id=1, source_target_pairs={{0,4},{1,5},{2,6},{3,7},{4,0},{5,1},{6,2},{7,3},{8,12},{9,13},{10,... | collective-permute-start | bytes 417800 | tf_op jit(solution)/shard_map/ppermute | solution.py:115
  76.8 11.3 %collective-permute-start.12 = (f16[136,512]{1,0:T(8,128)(2,1)S(1)}, f16[136,512]{1,0:T(8,128)(2,1)S(1)}, u32[]{:S(2)}, u32[]{:S(2)}) collective-permute-start(f16[136,512]{1,0:T(8,128)(2,1)S(1)} %get-tuple-element.50), channel_id=1, source_target_pairs={{0,6},{1,7},{2,4},{3,5},{4,2},{5,3},{6,0},{7,1},{8,14},{9,15},{10,... | collective-permute-start | bytes 417800 | tf_op jit(solution)/shard_map/ppermute | solution.py:115
  78.4 2.2 %copy-start = (bf16[512,4096]{1,0:T(8,128)(2,1)S(1)}, bf16[512,4096]{1,0:T(8,128)(2,1)}, u32[]{:S(2)}) copy-start(bf16[512,4096]{1,0:T(8,128)(2,1)} %tok.3) | copy-start | bytes 12582916

commit v10 on v9

--- a/solution.py
+++ b/solution.py
@@ -46,39 +46,36 @@
     )(tokens, cotangent, weight)
 
 
-def bound_kernel(tok, cot, power, tok_here, cot_here, arrived):
-    parts = arrived.shape[0] - 1
-    block = tok.shape[0] // parts
-    copies = [pltpu.make_async_copy(cot, cot_here, arrived.at[parts])]
-    for i in range(parts):
-        some = pl.ds(i * block, block)
-        copies.append(pltpu.make_async_copy(tok.at[some], tok_here.at[some], arrived.at[i]))
-    for copy in copies:
-        copy.start()
-    copies[0].wait()
-    total = jnp.zeros(power.shape, jnp.float32)
-    for i in range(parts):
-        copies[1 + i].wait()
-        some = pl.ds(i * block, block)
-        reach = jnp.max(jnp.abs(tok_here[some]).astype(jnp.float32), axis=1, keepdims=True)
-        terms = reach * jnp.abs(cot_here[some]).astype(jnp.float32)
-        total += jnp.sum(terms.reshape(-1, NOTE, terms.shape[1]), axis=0)
-    top = jnp.maximum(jnp.sum(total, axis=0, keepdims=True), 2.0**-100)
-    power[...] = jnp.broadcast_to(jnp.ceil(jnp.log2(top)), power.shape)
+def bound_kernel(tok, cot, power, total):
+    step = pl.program_id(0)
+
+    @pl.when(step == 0)
+    def _():
+        total[...] = jnp.zeros_like(total)
+
+    reach = jnp.max(jnp.abs(tok[...]).astype(jnp.float32), axis=1, keepdims=True)
+    terms = reach * jnp.abs(cot[...]).astype(jnp.float32)
+    total[...] += jnp.sum(terms.reshape(-1, NOTE, terms.shape[1]), axis=0)
+
+    @pl.when(step == pl.num_programs(0) - 1)
+    def _():
+        top = jnp.maximum(jnp.sum(total[...], axis=0, keepdims=True), 2.0**-100)
+        power[...] = jnp.broadcast_to(jnp.ceil(jnp.log2(top)), power.shape)
 
 
 def bound_of(tokens, cotangent):
     rows, width = tokens.shape
     kd = cotangent.shape[1]
+    block = min(rows, 128)
     return pl.pallas_call(
         bound_kernel,
-        in_specs=[pl.BlockSpec(memory_space=pl.ANY)] * 2,
-        out_specs=pl.BlockSpec(memory_space=pltpu.VMEM),
-        scratch_shapes=[
-            pltpu.VMEM(tokens.shape, tokens.dtype),
-            pltpu.VMEM(cotangent.shape, cotangent.dtype),
-            pltpu.SemaphoreType.DMA((max(rows // 128, 1) + 1,)),
+        grid=(rows // block,),
+        in_specs=[
+            pl.BlockSpec((block, width), lambda i: (i, 0)),
+            pl.BlockSpec((block, kd), lambda i: (i, 0)),
         ],
+        out_specs=pl.BlockSpec((NOTE, kd), lambda i: (0, 0)),
+        scratch_shapes=[pltpu.VMEM((NOTE, kd), jnp.float32)],
         out_shape=jax.ShapeDtypeStruct((NOTE, kd), jnp.float32),
         compiler_params=pltpu.CompilerParams(vmem_limit_bytes=60 * 1024 * 1024),
         cost_estimate=pl.CostEstimate(
@@ -167,18 +164,23 @@
     part = lax.dot_general(
         tokens, cotangent, (((0,), (0,)), ((), ())), preferred_element_type=jnp.float32
     )
-    part = (part * scale(TOP - power)).astype(jnp.float16).reshape(nz * n * n, 2, rows, kd)
-    other = swap(pick(part, (1, 1 - core)), "core", 1)
+    part = (part * scale(TOP - power)).astype(jnp.float16).reshape(nz, n * n, 2, rows, kd)
+    others = [swap(pick(part, (0, z), (2, 1 - core)), "core", 1) for z in range(nz)]
     part, shards = held((part, shards))
     blocks = in_order(key_weight, shards, "z")
-    part = pick(part, (1, core)).astype(jnp.float32) + other.astype(jnp.float32)
-    part = part.astype(jnp.float16).reshape(nz, n, n, rows, kd)
-    part = jnp.where(core == 0, part, part.transpose(0, 2, 1, 3, 4))
-
+
+    def pair_sum(z, other):
+        total = pick(part, (0, z), (2, core)).astype(jnp.float32) + other.astype(jnp.float32)
+        total = total.astype(jnp.float16).reshape(n, n, rows, kd)
+        return jnp.where(core == 0, total, total.transpose(1, 0, 2, 3))
+
+    part = jnp.stack([pair_sum(z, other) for z, other in enumerate(others)])
+
+    given_first = given(part, "first", 1)
     blocks, power_first = gathered(blocks, "first", power)
     by_first = factors(power, power_first)
-    part, blocks, by_first = held((part, blocks, by_first))
-    sums = taken(part, given(part, "first", 1), "first", 1, by_first[1])
+    part, given_first, blocks, by_first = held((part, given_first, blocks, by_first))
+    sums = taken(part, given_first, "first", 1, by_first[1])
     blocks, power_second = gathered(blocks, "second", by_first[0])
     by_second = factors(by_first[0], power_second)
     sums = taken(sums, given(sums, "second", 2), "second", 2, by_second[1])

time: 90.1 us -> 85.2 us (0.946)
  starting transfers between devices: 20.8 us -> 18.4 us
  waiting for transfers between devices: 35.7 us -> 33.5 us
  local copies, waits for them, and re-layouts: 8.25 us -> 7.24 us
    ppermute x13 -> x16, starting transfers between devices: 20.8 us -> 18.4 us  [swap(): return lax.ppermute(value, AXES, pairs)]
    ppermute x13 -> x16, waiting for transfers between devices: 35.7 us -> 33.5 us  [swap(): return lax.ppermute(value, AXES, pairs)]
    select_n x1 -> x0, other arithmetic: 1.84 us -> none  [on_device(): part = jnp.where(core == 0, part, part.transpose(0, 2, 1, 3, 4))]
    convert_element_type x1, other arithmetic: 2.37 us -> 0.81 us  [pair_sum(): total = total.astype(jnp.float16).reshape(n, n, rows, kd)]
    convert_element_type x2, other arithmetic: 0.71 us -> 1.92 us  [taken(): return total.astype(jnp.float16)]
    dynamic_slice x2, local copies, waits for them, and re-layouts: 1.55 us -> 0.34 us  [pick(): return lax.dynamic_slice(value, start, extent)]
    another operation x0 -> x3, other arithmetic: none -> 1.16 us  [on_device(): part = jnp.stack([pair_sum(z, other) for z, other in enumerate(others)])]
    slice x2, local copies, waits for them, and re-layouts: 1.33 us -> 2.37 us  [read(): return (got[:-NOTE].reshape(shape), got[-NOTE:][:1].astype(jnp.float32))]
  transfers between devices with their start and end apart: 13 -> 16, of which waited for: 6 -> 7; matrix products, arithmetic and copies ran while one was open for 16% -> 18% of each run, Pallas kernels for 11% -> 13%
where the time goes in v10:
time: 85.2 us; the launch traced here: 84.7 us
  waiting for transfers between devices  33.5 us (39%)
  starting transfers between devices  18.4 us (22%)
  Pallas kernels  10.7 us (13%)
  other arithmetic  9.24 us (11%)
  local copies, waits for them, and re-layouts  7.24 us (8%)
  matrix products  4.58 us (5%)
  between operations  1.01 us (1%)
    ppermute x16, waiting for transfers between devices, swap(): return lax.ppermute(value, AXES, pairs)  33.5 us
    ppermute x16, starting transfers between devices, swap(): return lax.ppermute(value, AXES, pairs)  18.4 us
    pallas_call x1, Pallas kernels, products(): pl.pallas_call(products_kernel, grid=(steps,), in_specs=[columns, whole,...  6.62 us
    dot_general x1, matrix products, on_device(): lax.dot_general(tokens, cotangent, (((0,), (0,)), ((), ())), preferred_el...  4.58 us
    pallas_call x1, Pallas kernels, bound_of(): pl.pallas_call(bound_kernel, grid=(rows // block,), in_specs=[pl.BlockSpe...  4.09 us
    unnamed x11, local copies, waits for them, and re-layouts  3.72 us
    slice x2, local copies, waits for them, and re-layouts, read(): return (got[:-NOTE].reshape(shape), got[-NOTE:][:1].astype(jnp.float32))  2.37 us
    exp2 x8, other arithmetic, scale(): return jnp.exp2(power)  2.18 us
  transfers between devices with their start and end apart: 16, of which 7 were waited for; matrix products, arithmetic and copies ran while one was open for 18% of the time, Pallas kernels for 13%

profile of v10, /device:TPU:0, one launch (start us, length us, event | category | flops | bytes accessed | tf_op | source)
XLA Modules:
  0.0 84.7 jit_solution(3934285013365533220)
XLA Ops:
  0.6 3.1 %collective-permute-start = (bf16[128,512]{1,0:T(8,128)(2,1)}, bf16[128,512]{1,0:T(8,128)(2,1)S(1)}, u32[]{:S(2)}, u32[]{:S(2)}) collective-permute-start(bf16[128,512]{1,0:T(8,128)(2,1)} %param.4), channel_id=1, source_target_pairs={{0,2},{1,3},{2,0},{3,1},{4,6},{5,7},{6,4},{7,5},{8,10},{9,11},{10,... | collective-permute-start | bytes 393224 | tf_op jit(solution)/shard_map/ppermute | solution.py:112
  3.7 2.6 %collective-permute-start.2 = (bf16[128,512]{1,0:T(8,128)(2,1)}, bf16[128,512]{1,0:T(8,128)(2,1)S(1)}, u32[]{:S(2)}, u32[]{:S(2)}) collective-permute-start(bf16[128,512]{1,0:T(8,128)(2,1)} %param.4), channel_id=1, source_target_pairs={{0,4},{1,5},{2,6},{3,7},{4,0},{5,1},{6,2},{7,3},{8,12},{9,13},{10,... | collective-permute-start | bytes 393224 | tf_op jit(solution)/shard_map/ppermute | solution.py:112
  6.3 4.1 %shard_map.58 = f32[8,512]{1,0:T(8,128)} custom-call(bf16[512,4096]{1,0:T(8,128)(2,1)} %tok.3, bf16[512,512]{1,0:T(8,128)(2,1)} %cot.3), custom_call_target="tpu_custom_call" | custom-call | flops 4194304 | bytes 4718592 | tf_op jit(solution)/shard_map/pallas_call | solution.py:70
  10.5 1.3 %collective-permute-done.1 = f32[8,512]{1,0:T(8,128)S(1)} collective-permute-done((f32[8,512]{1,0:T(8,128)}, f32[8,512]{1,0:T(8,128)S(1)}, u32[]{:S(2)}, u32[]{:S(2)}) %collective-permute-start.1) | collective-permute-done | bytes 16416 | tf_op jit(solution)/shard_map/ppermute | solution.py:112
  12.6 4.6 %multiply_convert_fusion = f16[4096,512]{1,0:T(8,128)(2,1)S(1)} fusion(bf16[512,4096]{1,0:T(8,128)(2,1)} %tok.3, bf16[512,512]{1,0:T(8,128)(2,1)S(1)} %copy-done.1, f32[512]{0:T(512)S(1)} %bitcast.103), kind=kOutput, calls=%fused_computation | convolution fusion | flops 2151677952 | bytes 8914944 | tf_op jit(solution)/shard_map/dot_general | solution.py:164
  18.8 0.8 pad_maximum_fusion.3
  19.7 1.7 %collective-permute-start.9 = (bf16[520,512]{1,0:T(8,128)(2,1)}, bf16[520,512]{1,0:T(8,128)(2,1)}, u32[]{:S(2)}, u32[]{:S(2)}) collective-permute-start(bf16[520,512]{1,0:T(8,128)(2,1)} %pad_maximum_fusion.3), channel_id=1, source_target_pairs={{0,1},{1,0},{2,3},{3,2},{4,5},{5,4},{6,7},{7,6},{8,24},{9,25},{10,... | collective-permute-start | bytes 1597448 | tf_op jit(solution)/shard_map/ppermute | solution.py:112
  23.9 1.3 %copy-done.2 = f16[4,2,2,128,512]{4,3,2,1,0:T(8,128)(2,1)} copy-done((f16[4,2,2,128,512]{4,3,2,1,0:T(8,128)(2,1)}, f16[4,2,2,128,512]{4,3,2,1,0:T(8,128)(2,1)S(1)}, u32[]{:S(2)}) %copy-start.2) | copy-done | bytes 2097176
  25.5 1.8 %collective-permute-start.8 = (f16[4,1,2,128,512]{4,3,2,1,0:T(8,128)(2,1)S(1)}, f16[4,1,2,128,512]{4,3,2,1,0:T(8,128)(2,1)}, u32[]{:S(2)}, u32[]{:S(2)}) collective-permute-start(f16[4,1,2,128,512]{4,3,2,1,0:T(8,128)(2,1)S(1)} %constant_dynamic-slice_fusion.1), channel_id=1, source_target_pairs={{0,1},{1,0},{2,3},{3,2},{4,5},{5,4},{6,7},{7,6},{8,24},{9,25},{10,... | collective-permute-start | bytes 3145736 | tf_op jit(solution)/shard_map/ppermute | solution.py:112
  27.4 1.9 %collective-permute-done.9 = bf16[520,512]{1,0:T(8,128)(2,1)} collective-permute-done((bf16[520,512]{1,0:T(8,128)(2,1)}, bf16[520,512]{1,0:T(8,128)(2,1)}, u32[]{:S(2)}, u32[]{:S(2)}) %collective-permute-start.9) | collective-permute-done | bytes 532512 | tf_op jit(solution)/shard_map/ppermute | solution.py:112
  29.2 1.1 %slice.56 = bf16[512,512]{1,0:T(8,128)(2,1)S(1)} slice(bf16[520,512]{1,0:T(8,128)(2,1)} %collective-permute-done.9), slice={[0:512], [0:512]} | slice | bytes 1048576 | tf_op jit(solution)/shard_map/slice | solution.py:131
  31.1 9.4 %collective-permute-done.8 = f16[4,1,2,128,512]{4,3,2,1,0:T(8,128)(2,1)} collective-permute-done((f16[4,1,2,128,512]{4,3,2,1,0:T(8,128)(2,1)S(1)}, f16[4,1,2,128,512]{4,3,2,1,0:T(8,128)(2,1)}, u32[]{:S(2)}, u32[]{:S(2)}) %collective-permute-start.8) | collective-permute-done | bytes 1048608 | tf_op jit(solution)/shard_map/ppermute | solution.py:112
  40.7 1.8 %collective-permute-start.10 = (bf16[1032,512]{1,0:T(8,128)(2,1)S(1)}, bf16[1032,512]{1,0:T(8,128)(2,1)}, u32[]{:S(2)}, u32[]{:S(2)}) collective-permute-start(bf16[1032,512]{1,0:T(8,128)(2,1)S(1)} %pad_maximum_fusion.2), channel_id=1, source_target_pairs={{0,16},{1,17},{2,18},{3,19},{4,20},{5,21},{6,22},{7,23},{8,9},{9,8... | collective-permute-start | bytes 3170312 | tf_op jit(solution)/shard_map/ppermute | solution.py:112
  42.8 12.9 %collective-permute-done.10 = bf16[1032,512]{1,0:T(8,128)(2,1)} collective-permute-done((bf16[1032,512]{1,0:T(8,128)(2,1)S(1)}, bf16[1032,512]{1,0:T(8,128)(2,1)}, u32[]{:S(2)}, u32[]{:S(2)}) %collective-permute-start.10) | collective-permute-done | bytes 1056800 | tf_op jit(solution)/shard_map/ppermute | solution.py:112
  55.7 1.3 %slice.58 = bf16[1024,512]{1,0:T(8,128)(2,1)S(1)} slice(bf16[1032,512]{1,0:T(8,128)(2,1)} %collective-permute-done.10), slice={[0:1024], [0:512]} | slice | bytes 2097152 | tf_op jit(solution)/shard_map/slice | solution.py:131
  57.2 1.7 %add_convert_fusion = f16[4,1,2,128,512]{4,3,2,1,0:T(8,128)(2,1)S(1)} fusion(f16[4,1,2,128,512]{4,3,2,1,0:T(8,128)(2,1)} %collective-permute-done.8, f32[512]{0:T(512)S(1)} %bitcast.102, f32[512]{0:T(512)S(1)} %bitcast.101, f16[4,2,2,128,512]{4,3,2,1,0:T(8,128)(2,1)S(1)} %copy-done.3, s32[]{:T(128)S(6)} %select_n.112), kind=kLoop, calls=%fused_computation.3 | loop fusion | flops 3145728 | bytes 3149828 | tf_op jit(solution)/shard_map/convert_element_type | solution.py:156
  59.0 1.8 %collective-permute-start.12 = (f16[4,1,1,128,512]{4,3,2,1,0:T(8,128)(2,1)S(1)}, f16[4,1,1,128,512]{4,3,2,1,0:T(8,128)(2,1)S(1)}, u32[]{:S(2)}, u32[]{:S(2)}) collective-permute-start(f16[4,1,1,128,512]{4,3,2,1,0:T(8,128)(2,1)S(1)} %constant_dynamic-slice_fusion), channel_id=1, source_target_pairs={{0,16},{1,17},{2,18},{3,19},{4,20},{5,21},{6,22},{7,23},{8,9},{9,8... | collective-permute-start | bytes 1572872 | tf_op jit(solution)/shard_map/ppermute | solution.py:112
  62.3 6.0 %collective-permute-done.12 = f16[4,1,1,128,512]{4,3,2,1,0:T(8,128)(2,1)S(1)} collective-permute-done((f16[4,1,1,128,512]{4,3,2,1,0:T(8,128)(2,1)S(1)}, f16[4,1,1,128,512]{4,3,2,1,0:T(8,128)(2,1)S(1)}, u32[]{:S(2)}, u32[]{:S(2)}) %collective-permute-start.12) | collective-permute-done | bytes 524320 | tf_op jit(solution)/shard_map/ppermute | solution.py:112
  68.7 1.7 %collective-permute-start.13 = (f16[136,512]{1,0:T(8,128)(2,1)S(1)}, f16[136,512]{1,0:T(8,128)(2,1)S(1)}, u32[]{:S(2)}, u32[]{:S(2)}) collective-permute-start(f16[136,512]{1,0:T(8,128)(2,1)S(1)} %get-tuple-element.62), channel_id=1, source_target_pairs={{0,2},{1,3},{2,0},{3,1},{4,6},{5,7},{6,4},{7,5},{8,10},{9,11},{10,... | collective-permute-start | bytes 417800 | tf_op jit(solution)/shard_map/ppermute | solution.py:112
  70.4 2.7 %collective-permute-start.14 = (f16[136,512]{1,0:T(8,128)(2,1)S(1)}, f16[136,512]{1,0:T(8,128)(2,1)S(1)}, u32[]{:S(2)}, u32[]{:S(2)}) collective-permute-start(f16[136,512]{1,0:T(8,128)(2,1)S(1)} %get-tuple-element.61), channel_id=1, source_target_pairs={{0,4},{1,5},{2,6},{3,7},{4,0},{5,1},{6,2},{7,3},{8,12},{9,13},{10,... | collective-permute-start | bytes 417800 | tf_op jit(solution)/shard_map/ppermute | solution.py:112
  73.7 1.9 %copy-done = bf16[512,4096]{1,0:T(8,128)(2,1)S(1)} copy-done((bf16[512,4096]{1,0:T(8,128)(2,1)S(1)}, bf16[512,4096]{1,0:T(8,128)(2,1)}, u32[]{:S(2)}) %copy-start) | copy-done | bytes 4194328
  75.6 6.6 %shard_map.59 = (bf16[512,512]{1,0:T(8,128)(2,1)}, bf16[512,4096]{1,0:T(8,128)(2,1)}) custom-call(bf16[512,4096]{1,0:T(8,128)(2,1)S(1)} %copy-done, bf16[512,512]{1,0:T(8,128)(2,1)S(1)} %copy-done.1, bf16[4,1024,512]{2,1,0:T(8,128)(2,1)S(1)} %bitcast.84), custom_call_target="tpu_custom_call" | custom-call | tf_op jit(solution)/shard_map/pallas_call | solution.py:35
  82.3 1.5 %collective-permute-done.14 = f16[136,512]{1,0:T(8,128)(2,1)S(1)} collective-permute-done((f16[136,512]{1,0:T(8,128)(2,1)S(1)}, f16[136,512]{1,0:T(8,128)(2,1)S(1)}, u32[]{:S(2)}, u32[]{:S(2)}) %collective-permute-start.14) | collective-permute-done | bytes 139296 | tf_op jit(solution)/shard_map/ppermute | solution.py:112
  83.8 0.8 fusion.7
  (65 shorter events, 9.3 us)
Async XLA Ops:
  0.6 9.8 %collective-permute-start = (bf16[128,512]{1,0:T(8,128)(2,1)}, bf16[128,512]{1,0:T(8,128)(2,1)S(1)}, u32[]{:S(2)}, u32[]{:S(2)}) collective-permute-start(bf16[128,512]{1,0:T(8,128)(2,1)} %param.4), channel_id=1, source_target_pairs={{0,2},{1,3},{2,0},{3,1},{4,6},{5,7},{6,4},{7,5},{8,10},{9,11},{10,... | collective-permute-start | bytes 393224 | tf_op jit(solution)/shard_map/ppermute | solution.py:112
  3.7 13.4 %collective-permute-start.2 = (bf16[128,512]{1,0:T(8,128)(2,1)}, bf16[128,512]{1,0:T(8,128)(2,1)S(1)}, u32[]{:S(2)}, u32[]{:S(2)}) collective-permute-start(bf16[128,512]{1,0:T(8,128)(2,1)} %param.4), channel_id=1, source_target_pairs={{0,4},{1,5},{2,6},{3,7},{4,0},{5,1},{6,2},{7,3},{8,12},{9,13},{10,... | collective-permute-start | bytes 393224 | tf_op jit(solution)/shard_map/ppermute | solution.py:112
  6.3 10.9 %collective-permute-start.3 = (bf16[128,512]{1,0:T(8,128)(2,1)}, bf16[128,512]{1,0:T(8,128)(2,1)S(1)}, u32[]{:S(2)}, u32[]{:S(2)}) collective-permute-start(bf16[128,512]{1,0:T(8,128)(2,1)} %param.4), channel_id=1, source_target_pairs={{0,6},{1,7},{2,4},{3,5},{4,2},{5,3},{6,0},{7,1},{8,14},{9,15},{10,... | collective-permute-start | bytes 393224 | tf_op jit(solution)/shard_map/ppermute | solution.py:112
  6.3 4.2 %copy-start.4 = (bf16[128,512]{1,0:T(8,128)(2,1)S(1)}, bf16[128,512]{1,0:T(8,128)(2,1)}, u32[]{:S(2)}) copy-start(bf16[128,512]{1,0:T(8,128)(2,1)} %param.4) | copy-start | bytes 393220
  6.3 6.2 %copy-start.1 = (bf16[512,512]{1,0:T(8,128)(2,1)S(1)}, bf16[512,512]{1,0:T(8,128)(2,1)}, u32[]{:S(2)}) copy-start(bf16[512,512]{1,0:T(8,128)(2,1)} %cot.3) | copy-start | bytes 1572868
  10.4 1.4 %collective-permute-start.1 = (f32[8,512]{1,0:T(8,128)}, f32[8,512]{1,0:T(8,128)S(1)}, u32[]{:S(2)}, u32[]{:S(2)}) collective-permute-start(f32[8,512]{1,0:T(8,128)} %shard_map.58), channel_id=1, source_target_pairs={{0,8},{1,9},{2,10},{3,11},{4,12},{5,13},{6,14},{7,15},{8,0},{9,1},... | collective-permute-start | bytes 49160 | tf_op jit(solution)/shard_map/ppermute | solution.py:112
  17.7 3.7 %collective-permute-start.4 = (f16[1,4,1,128,512]{4,3,1,2,0:T(8,128)(2,1)S(1)}, f16[1,4,1,128,512]{4,3,1,2,0:T(8,128)(2,1)S(1)}, u32[]{:S(2)}, u32[]{:S(2)}) collective-permute-start(f16[1,4,1,128,512]{4,3,1,2,0:T(8,128)(2,1)S(1)} %get-tuple-element.53), channel_id=1, source_target_pairs={{0,8},{1,9},{2,10},{3,11},{4,12},{5,13},{6,14},{7,15},{8,0},{9,1},... | collective-permute-start | bytes 1572872 | tf_op jit(solution)/shard_map/ppermute | solution.py:112
  17.9 3.5 %collective-permute-start.5 = (f16[1,4,1,128,512]{4,3,1,2,0:T(8,128)(2,1)S(1)}, f16[1,4,1,128,512]{4,3,1,2,0:T(8,128)(2,1)S(1)}, u32[]{:S(2)}, u32[]{:S(2)}) collective-permute-start(f16[1,4,1,128,512]{4,3,1,2,0:T(8,128)(2,1)S(1)} %get-tuple-element.55), channel_id=1, source_target_pairs={{0,8},{1,9},{2,10},{3,11},{4,12},{5,13},{6,14},{7,15},{8,0},{9,1},... | collective-permute-start | bytes 1572872 | tf_op jit(solution)/shard_map/ppermute | solution.py:112
  18.3 3.1 %collective-permute-start.6 = (f16[1,4,1,128,512]{4,3,1,2,0:T(8,128)(2,1)S(1)}, f16[1,4,1,128,512]{4,3,1,2,0:T(8,128)(2,1)S(1)}, u32[]{:S(2)}, u32[]{:S(2)}) collective-permute-start(f16[1,4,1,128,512]{4,3,1,2,0:T(8,128)(2,1)S(1)} %get-tuple-element.54), channel_id=1, source_target_pairs={{0,8},{1,9},{2,10},{3,11},{4,12},{5,13},{6,14},{7,15},{8,0},{9,1},... | collective-permute-start | bytes 1572872 | tf_op jit(solution)/shard_map/ppermute | solution.py:112
  18.4 3.5 %collective-permute-start.7 = (f16[1,4,1,128,512]{4,3,1,2,0:T(8,128)(2,1)S(1)}, f16[1,4,1,128,512]{4,3,1,2,0:T(8,128)(2,1)S(1)}, u32[]{:S(2)}, u32[]{:S(2)}) collective-permute-start(f16[1,4,1,128,512]{4,3,1,2,0:T(8,128)(2,1)S(1)} %get-tuple-element.56), channel_id=1, source_target_pairs={{0,8},{1,9},{2,10},{3,11},{4,12},{5,13},{6,14},{7,15},{8,0},{9,1},... | collective-permute-start | bytes 1572872 | tf_op jit(solution)/shard_map/ppermute | solution.py:112
  19.7 9.6 %collective-permute-start.9 = (bf16[520,512]{1,0:T(8,128)(2,1)}, bf16[520,512]{1,0:T(8,128)(2,1)}, u32[]{:S(2)}, u32[]{:S(2)}) collective-permute-start(bf16[520,512]{1,0:T(8,128)(2,1)} %pad_maximum_fusion.3), channel_id=1, source_target_pairs={{0,1},{1,0},{2,3},{3,2},{4,5},{5,4},{6,7},{7,6},{8,24},{9,25},{10,... | collective-permute-start | bytes 1597448 | tf_op jit(solution)/shard_map/ppermute | solution.py:112
  23.9 1.3 %copy-start.2 = (f16[4,2,2,128,512]{4,3,2,1,0:T(8,128)(2,1)}, f16[4,2,2,128,512]{4,3,2,1,0:T(8,128)(2,1)S(1)}, u32[]{:S(2)}) copy-start(f16[4,2,2,128,512]{4,3,2,1,0:T(8,128)(2,1)S(1)} %pad_maximum_fusion.1) | copy-start | bytes 6291460
  25.5 15.0 %collective-permute-start.8 = (f16[4,1,2,128,512]{4,3,2,1,0:T(8,128)(2,1)S(1)}, f16[4,1,2,128,512]{4,3,2,1,0:T(8,128)(2,1)}, u32[]{:S(2)}, u32[]{:S(2)}) collective-permute-start(f16[4,1,2,128,512]{4,3,2,1,0:T(8,128)(2,1)S(1)} %constant_dynamic-slice_fusion.1), channel_id=1, source_target_pairs={{0,1},{1,0},{2,3},{3,2},{4,5},{5,4},{6,7},{7,6},{8,24},{9,25},{10,... | collective-permute-start | bytes 3145736 | tf_op jit(solution)/shard_map/ppermute | solution.py:112
  40.7 15.1 %collective-permute-start.10 = (bf16[1032,512]{1,0:T(8,128)(2,1)S(1)}, bf16[1032,512]{1,0:T(8,128)(2,1)}, u32[]{:S(2)}, u32[]{:S(2)}) collective-permute-start(bf16[1032,512]{1,0:T(8,128)(2,1)S(1)} %pad_maximum_fusion.2), channel_id=1, source_target_pairs={{0,16},{1,17},{2,18},{3,19},{4,20},{5,21},{6,22},{7,23},{8,9},{9,8... | collective-permute-start | bytes 3170312 | tf_op jit(solution)/shard_map/ppermute | solution.py:112
  42.8 14.4 %copy-start.3 = (f16[4,2,2,128,512]{4,3,2,1,0:T(8,128)(2,1)S(1)}, f16[4,2,2,128,512]{4,3,2,1,0:T(8,128)(2,1)}, u32[]{:S(2)}) copy-start(f16[4,2,2,128,512]{4,3,2,1,0:T(8,128)(2,1)} %copy-done.2) | copy-start | bytes 6291460
  57.1 16.0 %collective-permute-start.11 = (bf16[2,2,4,128,512]{4,3,1,0,2:T(8,128)(2,1)S(1)}, bf16[2,2,4,128,512]{4,3,1,0,2:T(8,128)(2,1)S(1)}, u32[]{:S(2)}, u32[]{:S(2)}) collective-permute-start(bf16[2,2,4,128,512]{4,3,1,0,2:T(8,128)(2,1)S(1)} %copy_dynamic-update-slice_fusion), channel_id=1, source_target_pairs={{0,8},{1,9},{2,10},{3,11},{4,12},{5,13},{6,14},{7,15},{8,0},{9,1},... | collective-permute-start | bytes 6291464 | tf_op jit(solution)/shard_map/ppermute | solution.py:112
  59.0 9.2 %collective-permute-start.12 = (f16[4,1,1,128,512]{4,3,2,1,0:T(8,128)(2,1)S(1)}, f16[4,1,1,128,512]{4,3,2,1,0:T(8,128)(2,1)S(1)}, u32[]{:S(2)}, u32[]{:S(2)}) collective-permute-start(f16[4,1,1,128,512]{4,3,2,1,0:T(8,128)(2,1)S(1)} %constant_dynamic-slice_fusion), channel_id=1, source_target_pairs={{0,16},{1,17},{2,18},{3,19},{4,20},{5,21},{6,22},{7,23},{8,9},{9,8... | collective-permute-start | bytes 1572872 | tf_op jit(solution)/shard_map/ppermute | solution.py:112
  68.7 13.6 %collective-permute-start.13 = (f16[136,512]{1,0:T(8,128)(2,1)S(1)}, f16[136,512]{1,0:T(8,128)(2,1)S(1)}, u32[]{:S(2)}, u32[]{:S(2)}) collective-permute-start(f16[136,512]{1,0:T(8,128)(2,1)S(1)} %get-tuple-element.62), channel_id=1, source_target_pairs={{0,2},{1,3},{2,0},{3,1},{4,6},{5,7},{6,4},{7,5},{8,10},{9,11},{10,... | collective-permute-start | bytes 417800 | tf_op jit(solution)/shard_map/ppermute | solution.py:112
  70.4 13.4 %collective-permute-start.14 = (f16[136,512]{1,0:T(8,128)(2,1)S(1)}, f16[136,512]{1,0:T(8,128)(2,1)S(1)}, u32[]{:S(2)}, u32[]{:S(2)}) collective-permute-start(f16[136,512]{1,0:T(8,128)(2,1)S(1)} %get-tuple-element.61), channel_id=1, source_target_pairs={{0,4},{1,5},{2,6},{3,7},{4,0},{5,1},{6,2},{7,3},{8,12},{9,13},{10,... | collective-permute-start | bytes 417800 | tf_op jit(solution)/shard_map/ppermute | solution.py:112
  73.2 10.6 %collective-permute-start.15 = (f16[136,512]{1,0:T(8,128)(2,1)S(1)}, f16[136,512]{1,0:T(8,128)(2,1)S(1)}, u32[]{:S(2)}, u32[]{:S(2)}) collective-permute-start(f16[136,512]{1,0:T(8,128)(2,1)S(1)} %get-tuple-element.60), channel_id=1, source_target_pairs={{0,6},{1,7},{2,4},{3,5},{4,2},{5,3},{6,0},{7,1},{8,14},{9,15},{10,... | collective-permute-start | bytes 417800 | tf_op jit(solution)/shard_map/ppermute | solution.py:112
  73.4 2.2 %copy-start = (bf16[512,4096]{1,0:T(8,128)(2,1)S(1)}, bf16[512,4096]{1,0:T(8,128)(2,1)}, u32[]{:S(2)}) copy-start(bf16[512,4096]{1,0:T(8,128)(2,1)} %tok.3) | copy-start | bytes 12582916

commit v11 on v6

--- a/solution.py
+++ b/solution.py
@@ -66,7 +66,7 @@
 def bound_of(tokens, cotangent):
     rows, width = tokens.shape
     kd = cotangent.shape[1]
-    block = min(rows, 128)
+    block = min(rows, 256)
     return pl.pallas_call(
         bound_kernel,
         grid=(rows // block,),
@@ -134,52 +134,72 @@
         top = top + len(others).bit_length()
         return top, [scale(one - top) for one in [power, *others]]
 
-    def sums(value, name, axis, factor, *places):
+    def given(value, name, axis, *places):
         me = place[name]
-        got = [swap(pick(value, (axis, me ^ j), *places), name, j) for j in range(1, size[name])]
-        total = pick(value, (axis, me), *places).astype(jnp.float32) * factor[0]
+        return [swap(pick(value, (axis, me ^ j), *places), name, j) for j in range(1, size[name])]
+
+    def given_noted(value, name, axis, power):
+        me = place[name]
+        shape = value.shape[:axis] + (1,) + value.shape[axis + 1 :]
+        got = [
+            read(swap(noted(pick(value, (axis, me ^ j)), power), name, j), shape)
+            for j in range(1, size[name])
+        ]
+        return [one for one, _ in got], [other for _, other in got]
+
+    def taken(value, got, name, axis, factor, *places):
+        total = pick(value, (axis, place[name]), *places).astype(jnp.float32) * factor[0]
         for one, other in zip(got, factor[1:]):
             total = total + one.astype(jnp.float32) * other
         return total.astype(jnp.float16)
 
+    held = lax.optimization_barrier
+
     shards = [swap(key_weight, "z", j) for j in range(1, nz)]
 
-    power, shards[0] = lax.optimization_barrier((bound_of(tokens, cotangent), shards[0]))
+    early = nz // 2
+    power, shards[:early] = held((bound_of(tokens, cotangent), shards[:early]))
     power = jnp.maximum(power, swap(power, "core", 1))[:1] + 1.0
     part = lax.dot_general(
         tokens, cotangent, (((0,), (0,)), ((), ())), preferred_element_type=jnp.float32
     )
     part = (part * scale(TOP - power)).astype(jnp.float16).reshape(nz * nx * ny, 2, rows, kd)
-    other = swap(pick(part, (1, 1 - core)), "core", 1)
-    part, shards = lax.optimization_barrier((part, shards))
-    shards = in_order(key_weight, shards, "z")
+    sent, shards[early:] = held((pick(part, (1, 1 - core)), shards[early:]))
+    other = swap(sent, "core", 1)
+    part, shards = held((part, shards))
+    blocks = in_order(key_weight, shards, "z").reshape(nz, 2, half, kd)
     part = pick(part, (1, core)).astype(jnp.float32) + other.astype(jnp.float32)
     part = part.astype(jnp.float16).reshape(nz, nx, ny, rows, kd)
 
-    blocks = shards.reshape(nz, 2, half, kd)
+    upper, lower = (3, 0, half), (3, half, half)
+    got_one, got_two = given(part, "x", 1, upper), given(part, "y", 2, lower)
     one, power_x = gathered(blocks[:, 0], "x", power)
     two, power_y = gathered(blocks[:, 1], "y", power)
     by_x, by_y = factors(power, power_x), factors(power, power_y)
-    part, one, two, by_x, by_y = lax.optimization_barrier((part, one, two, by_x, by_y))
-    sum_one = sums(part, "x", 1, by_x[1], (3, 0, half))
-    sum_two = sums(part, "y", 2, by_y[1], (3, half, half))
-    one, power_xy = gathered(one, "y", by_x[0])
-    two, power_yx = gathered(two, "x", by_y[0])
+    part, got_one, got_two, one, two, by_x, by_y = held(
+        (part, got_one, got_two, one, two, by_x, by_y)
+    )
+    sum_one = taken(part, got_one, "x", 1, by_x[1], upper)
+    sum_two = taken(part, got_two, "y", 2, by_y[1], lower)
+    got_one, power_xy = given_noted(sum_one, "y", 2, by_x[0])
+    got_two, power_yx = given_noted(sum_two, "x", 1, by_y[0])
+    one = in_order(one, [swap(one, "y", j) for j in range(1, ny)], "y")
+    two = in_order(two, [swap(two, "x", j) for j in range(1, nx)], "x")
     by_xy, by_yx = factors(by_x[0], power_xy), factors(by_y[0], power_yx)
     top_one = by_xy[0]
-    sum_one = sums(sum_one, "y", 2, by_xy[1])
-    sum_two = sums(sum_two, "x", 1, by_yx[1])
-    both = jnp.stack([one.transpose(2, 1, 0, 3, 4), two.transpose(2, 0, 1, 3, 4)], axis=3)
-    weight = in_order(both, [swap(both, "core", 1)], "core")
-    weight = weight.transpose(1, 2, 3, 0, 4, 5, 6).reshape(nz, nx * ny * 2 * rows, kd)
-
+    sum_one = taken(sum_one, got_one, "y", 2, by_xy[1])
+    sum_two = taken(sum_two, got_two, "x", 1, by_yx[1])
     total = jnp.concatenate([sum_one, sum_two], axis=3).reshape(nz, rows, kd)
     got = [
         swap(noted(pick(total, (0, z_me ^ j)), top_one), "z", j)
         for j in range(1, nz)
     ]
+    total, one, two, got[:early] = held((total, one, two, got[:early]))
+    both = jnp.stack([one.transpose(2, 1, 0, 3, 4), two.transpose(2, 0, 1, 3, 4)], axis=3)
+    weight = in_order(both, [swap(both, "core", 1)], "core")
+    weight = weight.transpose(1, 2, 3, 0, 4, 5, 6).reshape(nz, nx * ny * 2 * rows, kd)
     keys, input_grad = products(tokens, cotangent, weight)
-    keys, input_grad, got = lax.optimization_barrier((keys, input_grad, got))
+    keys, input_grad, got = held((keys, input_grad, got))
     got = [read(one, (rows, kd)) for one in got]
     total = pick(total, (0, z_me))[0].astype(jnp.float32) * scale(top_one - TOP)
     for one, other in got:

time: 76.9 us -> 85.9 us (1.12)
  local copies, waits for them, and re-layouts: 2.49 us -> 8.23 us
  other arithmetic: 4.07 us -> 5.51 us
  starting transfers between devices: 19.9 us -> 21.3 us
  waiting for transfers between devices: 33.8 us -> 34.9 us
    unnamed x7 -> x16, local copies, waits for them, and re-layouts: 0.51 us -> 2.89 us
    optimization_barrier x2 -> x1, local copies, waits for them, and re-layouts: 0.07 us -> 1.82 us  [on_device(): sent, shards[early:] = held((pick(part, (1, 1 - core)), shards[early:]))]
    dynamic_update_slice x13, local copies, waits for them, and re-layouts: 0.61 us -> 2.2 us  [in_order(): out = lax.dynamic_update_index_in_dim(out, part, place[name] ^ j, 0)]
    ppermute x17, starting transfers between devices: 19.9 us -> 21.3 us  [swap(): lax.ppermute(value, AXES, [(i, i ^ j * mask[name]) for i in range(wide *...]
    another operation x1, other arithmetic: 0.21 us -> 1.48 us  [on_device(): jnp.stack([one.transpose(2, 1, 0, 3, 4), two.transpose(2, 0, 1, 3, 4)], a...]
    ppermute x17, waiting for transfers between devices: 33.8 us -> 34.9 us  [swap(): lax.ppermute(value, AXES, [(i, i ^ j * mask[name]) for i in range(wide *...]
  transfers between devices with their start and end apart: 17 -> 17, of which waited for: 9 -> 10; matrix products, arithmetic and copies ran while one was open for 11% -> 14% of each run, Pallas kernels for 14% -> 12%
where the time goes in v11:
time: 85.9 us; the launch traced here: 85.6 us
  waiting for transfers between devices  34.9 us (41%)
  starting transfers between devices  21.3 us (25%)
  Pallas kernels  9.98 us (12%)
  local copies, waits for them, and re-layouts  8.23 us (10%)
  other arithmetic  5.51 us (6%)
  matrix products  4.58 us (5%)
  between operations  1.12 us (1%)
    ppermute x17, waiting for transfers between devices, swap(): lax.ppermute(value, AXES, [(i, i ^ j * mask[name]) for i in range(wide *...  34.9 us
    ppermute x17, starting transfers between devices, swap(): lax.ppermute(value, AXES, [(i, i ^ j * mask[name]) for i in range(wide *...  21.3 us
    pallas_call x1, Pallas kernels, products(): pl.pallas_call(products_kernel, grid=(steps,), in_specs=[columns, whole,...  6.63 us
    dot_general x1, matrix products, on_device(): lax.dot_general(tokens, cotangent, (((0,), (0,)), ((), ())), preferred_el...  4.58 us
    pallas_call x1, Pallas kernels, bound_of(): pl.pallas_call(bound_kernel, grid=(rows // block,), in_specs=[pl.BlockSpe...  3.35 us
    unnamed x16, local copies, waits for them, and re-layouts  2.89 us
    dynamic_update_slice x13, local copies, waits for them, and re-layouts, in_order(): out = lax.dynamic_update_index_in_dim(out, part, place[name] ^ j, 0)  2.2 us
    optimization_barrier x1, local copies, waits for them, and re-layouts, on_device(): sent, shards[early:] = held((pick(part, (1, 1 - core)), shards[early:]))  1.82 us
  transfers between devices with their start and end apart: 17, of which 10 were waited for; matrix products, arithmetic and copies ran while one was open for 14% of the time, Pallas kernels for 12%

profile of v11, /device:TPU:0, one launch (start us, length us, event | category | flops | bytes accessed | tf_op | source)
XLA Modules:
  0.0 85.6 jit_solution(7523209629689452672)
XLA Ops:
  0.7 3.1 %collective-permute-start = (bf16[128,512]{1,0:T(8,128)(2,1)}, bf16[128,512]{1,0:T(8,128)(2,1)S(1)}, u32[]{:S(2)}, u32[]{:S(2)}) collective-permute-start(bf16[128,512]{1,0:T(8,128)(2,1)} %param.4), channel_id=1, source_target_pairs={{0,2},{1,3},{2,0},{3,1},{4,6},{5,7},{6,4},{7,5},{8,10},{9,11},{10,... | collective-permute-start | bytes 393224 | tf_op jit(solution)/shard_map/ppermute | solution.py:101
  3.7 2.6 %collective-permute-start.1 = (bf16[128,512]{1,0:T(8,128)(2,1)}, bf16[128,512]{1,0:T(8,128)(2,1)S(1)}, u32[]{:S(2)}, u32[]{:S(2)}) collective-permute-start(bf16[128,512]{1,0:T(8,128)(2,1)} %param.4), channel_id=1, source_target_pairs={{0,4},{1,5},{2,6},{3,7},{4,0},{5,1},{6,2},{7,3},{8,12},{9,13},{10,... | collective-permute-start | bytes 393224 | tf_op jit(solution)/shard_map/ppermute | solution.py:101
  6.3 3.3 %shard_map.58 = f32[8,512]{1,0:T(8,128)} custom-call(bf16[512,4096]{1,0:T(8,128)(2,1)} %tok.3, bf16[512,512]{1,0:T(8,128)(2,1)} %cot.3), custom_call_target="tpu_custom_call" | custom-call | flops 4194304 | bytes 4718592 | tf_op jit(solution)/shard_map/pallas_call | solution.py:70
  9.7 3.0 %collective-permute-done.1 = bf16[128,512]{1,0:T(8,128)(2,1)S(1)} collective-permute-done((bf16[128,512]{1,0:T(8,128)(2,1)}, bf16[128,512]{1,0:T(8,128)(2,1)S(1)}, u32[]{:S(2)}, u32[]{:S(2)}) %collective-permute-start.1) | collective-permute-done | bytes 131104 | tf_op jit(solution)/shard_map/ppermute | solution.py:101
  12.7 2.5 %collective-permute-start.3 = (bf16[128,512]{1,0:T(8,128)(2,1)S(1)}, bf16[128,512]{1,0:T(8,128)(2,1)S(1)}, u32[]{:S(2)}, u32[]{:S(2)}) collective-permute-start(bf16[128,512]{1,0:T(8,128)(2,1)S(1)} %copy-done.4), channel_id=1, source_target_pairs={{0,6},{1,7},{2,4},{3,5},{4,2},{5,3},{6,0},{7,1},{8,14},{9,15},{10,... | collective-permute-start | bytes 393224 | tf_op jit(solution)/shard_map/ppermute | solution.py:101
  15.9 4.6 %multiply_convert_fusion = f16[4096,512]{1,0:T(8,128)(2,1)S(1)} fusion(bf16[512,4096]{1,0:T(8,128)(2,1)} %tok.3, bf16[512,512]{1,0:T(8,128)(2,1)S(1)} %copy-done.1, f32[512]{0:T(512)S(1)} %bitcast.128), kind=kOutput, calls=%fused_computation | convolution fusion | flops 2151677952 | bytes 8914944 | tf_op jit(solution)/shard_map/dot_general | solution.py:163
  20.5 2.0 %copy-done.2 = f16[4096,512]{1,0:T(8,128)(2,1)} copy-done((f16[4096,512]{1,0:T(8,128)(2,1)}, f16[4096,512]{1,0:T(8,128)(2,1)S(1)}, u32[]{:S(2)}) %copy-start.2) | copy-done | bytes 4194328
  22.5 1.8 %dynamic-slice_bitcast_fusion = f16[16,1,128,512]{3,2,0,1:T(8,128)(2,1)} fusion(f16[16,2,128,512]{3,2,1,0:T(8,128)(2,1)S(1)} %bitcast.106, s32[]{:T(128)S(6)} %select_n.54), kind=kLoop, calls=%fused_computation.5 | loop fusion | bytes 4194308 | tf_op jit(solution)/shard_map/optimization_barrier | solution.py:167
  24.8 1.6 %collective-permute-start.7 = (bf16[264,512]{1,0:T(8,128)(2,1)S(1)}, bf16[264,512]{1,0:T(8,128)(2,1)S(1)}, u32[]{:S(2)}, u32[]{:S(2)}) collective-permute-start(bf16[264,512]{1,0:T(8,128)(2,1)S(1)} %get-tuple-element.86), channel_id=1, source_target_pairs={{0,1},{1,0},{2,3},{3,2},{4,5},{5,4},{6,7},{7,6},{8,9},{9,8},{10,11... | collective-permute-start | bytes 811016 | tf_op jit(solution)/shard_map/ppermute | solution.py:101
  26.4 1.5 %collective-permute-start.8 = (bf16[264,512]{1,0:T(8,128)(2,1)S(1)}, bf16[264,512]{1,0:T(8,128)(2,1)S(1)}, u32[]{:S(2)}, u32[]{:S(2)}) collective-permute-start(bf16[264,512]{1,0:T(8,128)(2,1)S(1)} %get-tuple-element.85), channel_id=1, source_target_pairs={{0,16},{1,17},{2,18},{3,19},{4,20},{5,21},{6,22},{7,23},{8,24},{9,... | collective-permute-start | bytes 811016 | tf_op jit(solution)/shard_map/ppermute | solution.py:101
  28.0 5.5 %collective-permute-done.7 = bf16[264,512]{1,0:T(8,128)(2,1)S(1)} collective-permute-done((bf16[264,512]{1,0:T(8,128)(2,1)S(1)}, bf16[264,512]{1,0:T(8,128)(2,1)S(1)}, u32[]{:S(2)}, u32[]{:S(2)}) %collective-permute-start.7) | collective-permute-done | bytes 270368 | tf_op jit(solution)/shard_map/ppermute | solution.py:101
  36.7 1.6 %collective-permute-start.6 = (f16[4,2,1,64,512]{4,3,0,2,1:T(8,128)(2,1)S(1)}, f16[4,2,1,64,512]{4,3,0,2,1:T(8,128)(2,1)S(1)}, u32[]{:S(2)}, u32[]{:S(2)}) collective-permute-start(f16[4,2,1,64,512]{4,3,0,2,1:T(8,128)(2,1)S(1)} %copy.31), channel_id=1, source_target_pairs={{0,16},{1,17},{2,18},{3,19},{4,20},{5,21},{6,22},{7,23},{8,24},{9,... | collective-permute-start | bytes 1572872 | tf_op jit(solution)/shard_map/ppermute | solution.py:101
  38.3 10.6 %collective-permute-done.5 = f16[4,1,2,64,512]{4,3,0,2,1:T(8,128)(2,1)S(1)} collective-permute-done((f16[4,1,2,64,512]{4,3,0,2,1:T(8,128)(2,1)S(1)}, f16[4,1,2,64,512]{4,3,0,2,1:T(8,128)(2,1)S(1)}, u32[]{:S(2)}, u32[]{:S(2)}) %collective-permute-start.5) | collective-permute-done | bytes 524320 | tf_op jit(solution)/shard_map/ppermute | solution.py:101
  50.0 1.5 %collective-permute-start.10 = (f16[264,512]{1,0:T(8,128)(2,1)S(1)}, f16[264,512]{1,0:T(8,128)(2,1)S(1)}, u32[]{:S(2)}, u32[]{:S(2)}) collective-permute-start(f16[264,512]{1,0:T(8,128)(2,1)S(1)} %pad_maximum_fusion.5), channel_id=1, source_target_pairs={{0,1},{1,0},{2,3},{3,2},{4,5},{5,4},{6,7},{7,6},{8,9},{9,8},{10,11... | collective-permute-start | bytes 811016 | tf_op jit(solution)/shard_map/ppermute | solution.py:101
  51.8 1.6 %collective-permute-start.9 = (f16[264,512]{1,0:T(8,128)(2,1)S(1)}, f16[264,512]{1,0:T(8,128)(2,1)S(1)}, u32[]{:S(2)}, u32[]{:S(2)}) collective-permute-start(f16[264,512]{1,0:T(8,128)(2,1)S(1)} %pad_maximum_fusion.4), channel_id=1, source_target_pairs={{0,16},{1,17},{2,18},{3,19},{4,20},{5,21},{6,22},{7,23},{8,24},{9,... | collective-permute-start | bytes 811016 | tf_op jit(solution)/shard_map/ppermute | solution.py:101
  54.9 4.2 %collective-permute-done.10 = f16[264,512]{1,0:T(8,128)(2,1)S(1)} collective-permute-done((f16[264,512]{1,0:T(8,128)(2,1)S(1)}, f16[264,512]{1,0:T(8,128)(2,1)S(1)}, u32[]{:S(2)}, u32[]{:S(2)}) %collective-permute-start.10) | collective-permute-done | bytes 270368 | tf_op jit(solution)/shard_map/ppermute | solution.py:101
  59.2 2.1 %collective-permute-done.9 = f16[264,512]{1,0:T(8,128)(2,1)S(1)} collective-permute-done((f16[264,512]{1,0:T(8,128)(2,1)S(1)}, f16[264,512]{1,0:T(8,128)(2,1)S(1)}, u32[]{:S(2)}, u32[]{:S(2)}) %collective-permute-start.9) | collective-permute-done | bytes 270368 | tf_op jit(solution)/shard_map/ppermute | solution.py:101
  62.0 1.9 %collective-permute-start.14 = (f16[136,512]{1,0:T(8,128)(2,1)S(1)}, f16[136,512]{1,0:T(8,128)(2,1)S(1)}, u32[]{:S(2)}, u32[]{:S(2)}) collective-permute-start(f16[136,512]{1,0:T(8,128)(2,1)S(1)} %get-tuple-element.83), channel_id=1, source_target_pairs={{0,4},{1,5},{2,6},{3,7},{4,0},{5,1},{6,2},{7,3},{8,12},{9,13},{10,... | collective-permute-start | bytes 417800 | tf_op jit(solution)/shard_map/ppermute | solution.py:101
  64.1 5.1 %collective-permute-done.11 = bf16[2,4,64,512]{3,2,0,1:T(8,128)(2,1)S(1)} collective-permute-done((bf16[2,4,64,512]{3,2,0,1:T(8,128)(2,1)S(1)}, bf16[2,4,64,512]{3,2,0,1:T(8,128)(2,1)S(1)}, u32[]{:S(2)}, u32[]{:S(2)}) %collective-permute-start.11) | collective-permute-done | bytes 524320 | tf_op jit(solution)/shard_map/ppermute | solution.py:101
  70.2 1.5 %pad_maximum_fusion = bf16[4,2,2,2,64,512]{5,4,3,2,1,0:T(8,128)(2,1)} fusion(bf16[4,2,2,1,64,512]{5,4,3,2,1,0:T(8,128)(2,1)S(1)} %bitcast.97, bf16[2,2,4,64,512]{4,3,1,0,2:T(8,128)(2,1)S(1)} %bitcast_dynamic-update-slice_fusion.3), kind=kLoop, calls=%fused_computation.2 | loop fusion | flops 4194304 | bytes 4194304 | tf_op jit(solution)/shard_map/stack | solution.py:198
  71.7 1.4 %collective-permute-start.16 = (f16[136,512]{1,0:T(8,128)(2,1)S(1)}, f16[136,512]{1,0:T(8,128)(2,1)S(1)}, u32[]{:S(2)}, u32[]{:S(2)}) collective-permute-start(f16[136,512]{1,0:T(8,128)(2,1)S(1)} %get-tuple-element.82), channel_id=1, source_target_pairs={{0,6},{1,7},{2,4},{3,5},{4,2},{5,3},{6,0},{7,1},{8,14},{9,15},{10,... | collective-permute-start | bytes 417800 | tf_op jit(solution)/shard_map/ppermute | solution.py:101
  73.9 2.3 %collective-permute-done.15 = bf16[4,2,2,2,64,512]{5,4,3,2,1,0:T(8,128)(2,1)} collective-permute-done((bf16[4,2,2,2,64,512]{5,4,3,2,1,0:T(8,128)(2,1)}, bf16[4,2,2,2,64,512]{5,4,3,2,1,0:T(8,128)(2,1)}, u32[]{:S(2)}, u32[]{:S(2)}) %collective-permute-start.15) | collective-permute-done | bytes 2097184 | tf_op jit(solution)/shard_map/ppermute | solution.py:101
  76.2 1.9 %bitcast_dynamic-update-slice_fusion.1 = bf16[2,4,2,2,2,64,512]{6,5,4,0,3,2,1:T(8,128)(2,1)S(1)} fusion(bf16[2,4,2,2,2,64,512]{6,5,4,0,3,2,1:T(8,128)(2,1)S(1)} %bitcast_dynamic-update-slice_fusion, s32[]{:T(128)S(6)} %select_n.64, bf16[4,2,2,2,64,512]{5,4,3,2,1,0:T(8,128)(2,1)} %collective-permute-done.15), kind=kLoop, calls=%fused_computation.4 | loop fusion | bytes 4194308 | tf_op jit(solution)/shard_map/jit(dynamic_update_index_in_dim)/dynamic_update_slice | solution.py:112
  78.1 6.6 %shard_map.59 = (bf16[512,512]{1,0:T(8,128)(2,1)}, bf16[512,4096]{1,0:T(8,128)(2,1)}) custom-call(bf16[512,4096]{1,0:T(8,128)(2,1)S(1)} %copy-done, bf16[512,512]{1,0:T(8,128)(2,1)S(1)} %copy-done.1, bf16[4,1024,512]{2,1,0:T(8,128)(2,1)S(1)} %bitcast.96), custom_call_target="tpu_custom_call" | custom-call | tf_op jit(solution)/shard_map/pallas_call | solution.py:35
  (88 shorter events, 10.8 us)
Async XLA Ops:
  0.6 12.1 %copy-start.4 = (bf16[128,512]{1,0:T(8,128)(2,1)S(1)}, bf16[128,512]{1,0:T(8,128)(2,1)}, u32[]{:S(2)}) copy-start(bf16[128,512]{1,0:T(8,128)(2,1)} %param.4) | copy-start | bytes 393220
  0.6 15.3 %copy-start.1 = (bf16[512,512]{1,0:T(8,128)(2,1)S(1)}, bf16[512,512]{1,0:T(8,128)(2,1)}, u32[]{:S(2)}) copy-start(bf16[512,512]{1,0:T(8,128)(2,1)} %cot.3) | copy-start | bytes 1572868
  0.7 9.0 %collective-permute-start = (bf16[128,512]{1,0:T(8,128)(2,1)}, bf16[128,512]{1,0:T(8,128)(2,1)S(1)}, u32[]{:S(2)}, u32[]{:S(2)}) collective-permute-start(bf16[128,512]{1,0:T(8,128)(2,1)} %param.4), channel_id=1, source_target_pairs={{0,2},{1,3},{2,0},{3,1},{4,6},{5,7},{6,4},{7,5},{8,10},{9,11},{10,... | collective-permute-start | bytes 393224 | tf_op jit(solution)/shard_map/ppermute | solution.py:101
  3.7 8.9 %collective-permute-start.1 = (bf16[128,512]{1,0:T(8,128)(2,1)}, bf16[128,512]{1,0:T(8,128)(2,1)S(1)}, u32[]{:S(2)}, u32[]{:S(2)}) collective-permute-start(bf16[128,512]{1,0:T(8,128)(2,1)} %param.4), channel_id=1, source_target_pairs={{0,4},{1,5},{2,6},{3,7},{4,0},{5,1},{6,2},{7,3},{8,12},{9,13},{10,... | collective-permute-start | bytes 393224 | tf_op jit(solution)/shard_map/ppermute | solution.py:101
  12.7 2.5 %collective-permute-start.2 = (f32[8,512]{1,0:T(8,128)}, f32[8,512]{1,0:T(8,128)S(1)}, u32[]{:S(2)}, u32[]{:S(2)}) collective-permute-start(f32[8,512]{1,0:T(8,128)} %shard_map.58), channel_id=1, source_target_pairs={{0,8},{1,9},{2,10},{3,11},{4,12},{5,13},{6,14},{7,15},{8,0},{9,1},... | collective-permute-start | bytes 49160 | tf_op jit(solution)/shard_map/ppermute | solution.py:101
  12.7 11.6 %collective-permute-start.3 = (bf16[128,512]{1,0:T(8,128)(2,1)S(1)}, bf16[128,512]{1,0:T(8,128)(2,1)S(1)}, u32[]{:S(2)}, u32[]{:S(2)}) collective-permute-start(bf16[128,512]{1,0:T(8,128)(2,1)S(1)} %copy-done.4), channel_id=1, source_target_pairs={{0,6},{1,7},{2,4},{3,5},{4,2},{5,3},{6,0},{7,1},{8,14},{9,15},{10,... | collective-permute-start | bytes 393224 | tf_op jit(solution)/shard_map/ppermute | solution.py:101
  20.5 2.0 %copy-start.2 = (f16[4096,512]{1,0:T(8,128)(2,1)}, f16[4096,512]{1,0:T(8,128)(2,1)S(1)}, u32[]{:S(2)}) copy-start(f16[4096,512]{1,0:T(8,128)(2,1)S(1)} %multiply_convert_fusion) | copy-start | bytes 12582916
  24.3 10.5 %collective-permute-start.4 = (f16[16,1,128,512]{3,2,0,1:T(8,128)(2,1)}, f16[16,1,128,512]{3,2,0,1:T(8,128)(2,1)S(1)}, u32[]{:S(2)}, u32[]{:S(2)}) collective-permute-start(f16[16,1,128,512]{3,2,0,1:T(8,128)(2,1)} %dynamic-slice_bitcast_fusion), channel_id=1, source_target_pairs={{0,8},{1,9},{2,10},{3,11},{4,12},{5,13},{6,14},{7,15},{8,0},{9,1},... | collective-permute-start | bytes 6291464 | tf_op jit(solution)/shard_map/ppermute | solution.py:101
  24.6 10.3 %copy-start.3 = (f16[4096,512]{1,0:T(8,128)(2,1)S(1)}, f16[4096,512]{1,0:T(8,128)(2,1)}, u32[]{:S(2)}) copy-start(f16[4096,512]{1,0:T(8,128)(2,1)} %copy-done.2) | copy-start | bytes 12582916
  24.8 8.7 %collective-permute-start.7 = (bf16[264,512]{1,0:T(8,128)(2,1)S(1)}, bf16[264,512]{1,0:T(8,128)(2,1)S(1)}, u32[]{:S(2)}, u32[]{:S(2)}) collective-permute-start(bf16[264,512]{1,0:T(8,128)(2,1)S(1)} %get-tuple-element.86), channel_id=1, source_target_pairs={{0,1},{1,0},{2,3},{3,2},{4,5},{5,4},{6,7},{7,6},{8,9},{9,8},{10,11... | collective-permute-start | bytes 811016 | tf_op jit(solution)/shard_map/ppermute | solution.py:101
  26.4 8.4 %collective-permute-start.8 = (bf16[264,512]{1,0:T(8,128)(2,1)S(1)}, bf16[264,512]{1,0:T(8,128)(2,1)S(1)}, u32[]{:S(2)}, u32[]{:S(2)}) collective-permute-start(bf16[264,512]{1,0:T(8,128)(2,1)S(1)} %get-tuple-element.85), channel_id=1, source_target_pairs={{0,16},{1,17},{2,18},{3,19},{4,20},{5,21},{6,22},{7,23},{8,24},{9,... | collective-permute-start | bytes 811016 | tf_op jit(solution)/shard_map/ppermute | solution.py:101
  35.9 13.0 %collective-permute-start.5 = (f16[4,1,2,64,512]{4,3,0,2,1:T(8,128)(2,1)S(1)}, f16[4,1,2,64,512]{4,3,0,2,1:T(8,128)(2,1)S(1)}, u32[]{:S(2)}, u32[]{:S(2)}) collective-permute-start(f16[4,1,2,64,512]{4,3,0,2,1:T(8,128)(2,1)S(1)} %copy.30), channel_id=1, source_target_pairs={{0,1},{1,0},{2,3},{3,2},{4,5},{5,4},{6,7},{7,6},{8,9},{9,8},{10,11... | collective-permute-start | bytes 1572872 | tf_op jit(solution)/shard_map/ppermute | solution.py:101
  36.7 12.9 %collective-permute-start.6 = (f16[4,2,1,64,512]{4,3,0,2,1:T(8,128)(2,1)S(1)}, f16[4,2,1,64,512]{4,3,0,2,1:T(8,128)(2,1)S(1)}, u32[]{:S(2)}, u32[]{:S(2)}) collective-permute-start(f16[4,2,1,64,512]{4,3,0,2,1:T(8,128)(2,1)S(1)} %copy.31), channel_id=1, source_target_pairs={{0,16},{1,17},{2,18},{3,19},{4,20},{5,21},{6,22},{7,23},{8,24},{9,... | collective-permute-start | bytes 1572872 | tf_op jit(solution)/shard_map/ppermute | solution.py:101
  50.0 9.2 %collective-permute-start.10 = (f16[264,512]{1,0:T(8,128)(2,1)S(1)}, f16[264,512]{1,0:T(8,128)(2,1)S(1)}, u32[]{:S(2)}, u32[]{:S(2)}) collective-permute-start(f16[264,512]{1,0:T(8,128)(2,1)S(1)} %pad_maximum_fusion.5), channel_id=1, source_target_pairs={{0,1},{1,0},{2,3},{3,2},{4,5},{5,4},{6,7},{7,6},{8,9},{9,8},{10,11... | collective-permute-start | bytes 811016 | tf_op jit(solution)/shard_map/ppermute | solution.py:101
  51.8 9.5 %collective-permute-start.9 = (f16[264,512]{1,0:T(8,128)(2,1)S(1)}, f16[264,512]{1,0:T(8,128)(2,1)S(1)}, u32[]{:S(2)}, u32[]{:S(2)}) collective-permute-start(f16[264,512]{1,0:T(8,128)(2,1)S(1)} %pad_maximum_fusion.4), channel_id=1, source_target_pairs={{0,16},{1,17},{2,18},{3,19},{4,20},{5,21},{6,22},{7,23},{8,24},{9,... | collective-permute-start | bytes 811016 | tf_op jit(solution)/shard_map/ppermute | solution.py:101
  53.4 15.8 %collective-permute-start.11 = (bf16[2,4,64,512]{3,2,0,1:T(8,128)(2,1)S(1)}, bf16[2,4,64,512]{3,2,0,1:T(8,128)(2,1)S(1)}, u32[]{:S(2)}, u32[]{:S(2)}) collective-permute-start(bf16[2,4,64,512]{3,2,0,1:T(8,128)(2,1)S(1)} %constant_dynamic-update-slice_fusion.1), channel_id=1, source_target_pairs={{0,16},{1,17},{2,18},{3,19},{4,20},{5,21},{6,22},{7,23},{8,24},{9,... | collective-permute-start | bytes 1572872 | tf_op jit(solution)/shard_map/ppermute | solution.py:101
  54.1 15.2 %collective-permute-start.12 = (bf16[2,4,64,512]{3,2,0,1:T(8,128)(2,1)S(1)}, bf16[2,4,64,512]{3,2,0,1:T(8,128)(2,1)S(1)}, u32[]{:S(2)}, u32[]{:S(2)}) collective-permute-start(bf16[2,4,64,512]{3,2,0,1:T(8,128)(2,1)S(1)} %constant_dynamic-update-slice_fusion), channel_id=1, source_target_pairs={{0,1},{1,0},{2,3},{3,2},{4,5},{5,4},{6,7},{7,6},{8,9},{9,8},{10,11... | collective-permute-start | bytes 1572872 | tf_op jit(solution)/shard_map/ppermute | solution.py:101
  61.9 7.4 %collective-permute-start.13 = (f16[136,512]{1,0:T(8,128)(2,1)S(1)}, f16[136,512]{1,0:T(8,128)(2,1)S(1)}, u32[]{:S(2)}, u32[]{:S(2)}) collective-permute-start(f16[136,512]{1,0:T(8,128)(2,1)S(1)} %get-tuple-element.84), channel_id=1, source_target_pairs={{0,2},{1,3},{2,0},{3,1},{4,6},{5,7},{6,4},{7,5},{8,10},{9,11},{10,... | collective-permute-start | bytes 417800 | tf_op jit(solution)/shard_map/ppermute | solution.py:101
  62.0 7.6 %collective-permute-start.14 = (f16[136,512]{1,0:T(8,128)(2,1)S(1)}, f16[136,512]{1,0:T(8,128)(2,1)S(1)}, u32[]{:S(2)}, u32[]{:S(2)}) collective-permute-start(f16[136,512]{1,0:T(8,128)(2,1)S(1)} %get-tuple-element.83), channel_id=1, source_target_pairs={{0,4},{1,5},{2,6},{3,7},{4,0},{5,1},{6,2},{7,3},{8,12},{9,13},{10,... | collective-permute-start | bytes 417800 | tf_op jit(solution)/shard_map/ppermute | solution.py:101
  69.5 0.7 copy-start.5
  71.7 4.5 %collective-permute-start.15 = (bf16[4,2,2,2,64,512]{5,4,3,2,1,0:T(8,128)(2,1)}, bf16[4,2,2,2,64,512]{5,4,3,2,1,0:T(8,128)(2,1)}, u32[]{:S(2)}, u32[]{:S(2)}) collective-permute-start(bf16[4,2,2,2,64,512]{5,4,3,2,1,0:T(8,128)(2,1)} %pad_maximum_fusion), channel_id=1, source_target_pairs={{0,8},{1,9},{2,10},{3,11},{4,12},{5,13},{6,14},{7,15},{8,0},{9,1},... | collective-permute-start | bytes 6291464 | tf_op jit(solution)/shard_map/ppermute | solution.py:101
  71.7 13.0 %collective-permute-start.16 = (f16[136,512]{1,0:T(8,128)(2,1)S(1)}, f16[136,512]{1,0:T(8,128)(2,1)S(1)}, u32[]{:S(2)}, u32[]{:S(2)}) collective-permute-start(f16[136,512]{1,0:T(8,128)(2,1)S(1)} %get-tuple-element.82), channel_id=1, source_target_pairs={{0,6},{1,7},{2,4},{3,5},{4,2},{5,3},{6,0},{7,1},{8,14},{9,15},{10,... | collective-permute-start | bytes 417800 | tf_op jit(solution)/shard_map/ppermute | solution.py:101
  73.6 4.5 %copy-start = (bf16[512,4096]{1,0:T(8,128)(2,1)S(1)}, bf16[512,4096]{1,0:T(8,128)(2,1)}, u32[]{:S(2)}) copy-start(bf16[512,4096]{1,0:T(8,128)(2,1)} %tok.3) | copy-start | bytes 12582916
  78.1 6.7 %copy-start.6 = (f16[136,512]{1,0:T(8,128)(2,1)S(1)}, f16[136,512]{1,0:T(8,128)(2,1)}, u32[]{:S(2)}) copy-start(f16[136,512]{1,0:T(8,128)(2,1)} %copy-done.5) | copy-start | bytes 417796

commit v12 on v6

--- a/solution.py
+++ b/solution.py
@@ -46,7 +46,7 @@
     )(tokens, cotangent, weight)
 
 
-def bound_kernel(tok, cot, power, total):
+def bound_kernel(tok, cot, power, scale, total):
     step = pl.program_id(0)
 
     @pl.when(step == 0)
@@ -60,13 +60,15 @@
     @pl.when(step == pl.num_programs(0) - 1)
     def _():
         top = jnp.maximum(jnp.sum(total[...], axis=0, keepdims=True), 2.0**-100)
-        power[...] = jnp.broadcast_to(jnp.ceil(jnp.log2(top)), power.shape)
+        least = jnp.ceil(jnp.log2(top))
+        power[...] = jnp.broadcast_to(least, power.shape)
+        scale[...] = jnp.exp2(TOP - least)
 
 
 def bound_of(tokens, cotangent):
     rows, width = tokens.shape
     kd = cotangent.shape[1]
-    block = min(rows, 128)
+    block = min(rows, 256)
     return pl.pallas_call(
         bound_kernel,
         grid=(rows // block,),
@@ -74,9 +76,9 @@
             pl.BlockSpec((block, width), lambda i: (i, 0)),
             pl.BlockSpec((block, kd), lambda i: (i, 0)),
         ],
-        out_specs=pl.BlockSpec((NOTE, kd), lambda i: (0, 0)),
+        out_specs=[pl.BlockSpec((size, kd), lambda i: (0, 0)) for size in (NOTE, 1)],
         scratch_shapes=[pltpu.VMEM((NOTE, kd), jnp.float32)],
-        out_shape=jax.ShapeDtypeStruct((NOTE, kd), jnp.float32),
+        out_shape=[jax.ShapeDtypeStruct((size, kd), jnp.float32) for size in (NOTE, 1)],
         compiler_params=pltpu.CompilerParams(vmem_limit_bytes=60 * 1024 * 1024),
         cost_estimate=pl.CostEstimate(
             flops=2 * rows * width, bytes_accessed=2 * rows * (width + kd), transcendentals=0
@@ -144,16 +146,18 @@
 
     shards = [swap(key_weight, "z", j) for j in range(1, nz)]
 
-    power, shards[0] = lax.optimization_barrier((bound_of(tokens, cotangent), shards[0]))
-    power = jnp.maximum(power, swap(power, "core", 1))[:1] + 1.0
+    power, to_top = bound_of(tokens, cotangent)
+    power, shards[0] = lax.optimization_barrier((power, shards[0]))
+    power, by_core = factors(power[:1], [swap(power, "core", 1)[:1]])
     part = lax.dot_general(
         tokens, cotangent, (((0,), (0,)), ((), ())), preferred_element_type=jnp.float32
     )
-    part = (part * scale(TOP - power)).astype(jnp.float16).reshape(nz * nx * ny, 2, rows, kd)
+    part = (part * to_top).astype(jnp.float16).reshape(nz * nx * ny, 2, rows, kd)
     other = swap(pick(part, (1, 1 - core)), "core", 1)
     part, shards = lax.optimization_barrier((part, shards))
     shards = in_order(key_weight, shards, "z")
-    part = pick(part, (1, core)).astype(jnp.float32) + other.astype(jnp.float32)
+    part = pick(part, (1, core)).astype(jnp.float32) * by_core[0]
+    part = part + other.astype(jnp.float32) * by_core[1]
     part = part.astype(jnp.float16).reshape(nz, nx, ny, rows, kd)
 
     blocks = shards.reshape(nz, 2, half, kd)

time: 76.9 us -> 82.1 us (1.068)
  matrix products: 4.58 us -> 6.6 us
  local copies, waits for them, and re-layouts: 2.49 us -> 4.14 us
  other arithmetic: 4.07 us -> 5.11 us
  waiting for transfers between devices: 33.8 us -> 34.7 us
    dot_general x1, matrix products: 4.58 us -> 6.6 us  [on_device(): lax.dot_general(tokens, cotangent, (((0,), (0,)), ((), ())), preferred_el...]
    convert_element_type x1, other arithmetic: 0.81 us -> 2.58 us  [on_device(): part = part.astype(jnp.float16).reshape(nz, nx, ny, rows, kd)]
    unnamed x7 -> x11, local copies, waits for them, and re-layouts: 0.51 us -> 2.15 us
    ppermute x17, waiting for transfers between devices: 33.8 us -> 34.7 us  [swap(): lax.ppermute(value, AXES, [(i, i ^ j * mask[name]) for i in range(wide *...]
  transfers between devices with their start and end apart: 17 -> 17, of which waited for: 9 -> 9; matrix products, arithmetic and copies ran while one was open for 11% -> 15% of each run, Pallas kernels for 14% -> 12%
where the time goes in v12:
time: 82.1 us; the launch traced here: 81.9 us
  waiting for transfers between devices  34.7 us (42%)
  starting transfers between devices  20.3 us (25%)
  Pallas kernels  9.99 us (12%)
  matrix products  6.6 us (8%)
  other arithmetic  5.11 us (6%)
  local copies, waits for them, and re-layouts  4.14 us (5%)
  between operations  1.14 us (1%)
    ppermute x17, waiting for transfers between devices, swap(): lax.ppermute(value, AXES, [(i, i ^ j * mask[name]) for i in range(wide *...  34.7 us
    ppermute x17, starting transfers between devices, swap(): lax.ppermute(value, AXES, [(i, i ^ j * mask[name]) for i in range(wide *...  20.3 us
    pallas_call x1, Pallas kernels, products(): pl.pallas_call(products_kernel, grid=(steps,), in_specs=[columns, whole,...  6.63 us
    dot_general x1, matrix products, on_device(): lax.dot_general(tokens, cotangent, (((0,), (0,)), ((), ())), preferred_el...  6.6 us
    pallas_call x1, Pallas kernels, bound_of(): pl.pallas_call(bound_kernel, grid=(rows // block,), in_specs=[pl.BlockSpe...  3.36 us
    convert_element_type x1, other arithmetic, on_device(): part = part.astype(jnp.float16).reshape(nz, nx, ny, rows, kd)  2.58 us
    unnamed x11, local copies, waits for them, and re-layouts  2.15 us
  transfers between devices with their start and end apart: 17, of which 9 were waited for; matrix products, arithmetic and copies ran while one was open for 15% of the time, Pallas kernels for 12%

profile of v12, /device:TPU:0, one launch (start us, length us, event | category | flops | bytes accessed | tf_op | source)
XLA Modules:
  0.0 81.9 jit_solution(10764935004571211858)
XLA Ops:
  0.6 4.1 %collective-permute-start.1 = (bf16[128,512]{1,0:T(8,128)(2,1)}, bf16[128,512]{1,0:T(8,128)(2,1)S(1)}, u32[]{:S(2)}, u32[]{:S(2)}) collective-permute-start(bf16[128,512]{1,0:T(8,128)(2,1)} %param.4), channel_id=1, source_target_pairs={{0,4},{1,5},{2,6},{3,7},{4,0},{5,1},{6,2},{7,3},{8,12},{9,13},{10,... | collective-permute-start | bytes 393224 | tf_op jit(solution)/shard_map/ppermute | solution.py:103
  4.7 1.6 %collective-permute-start = (bf16[128,512]{1,0:T(8,128)(2,1)}, bf16[128,512]{1,0:T(8,128)(2,1)S(1)}, u32[]{:S(2)}, u32[]{:S(2)}) collective-permute-start(bf16[128,512]{1,0:T(8,128)(2,1)} %param.4), channel_id=1, source_target_pairs={{0,2},{1,3},{2,0},{3,1},{4,6},{5,7},{6,4},{7,5},{8,10},{9,11},{10,... | collective-permute-start | bytes 393224 | tf_op jit(solution)/shard_map/ppermute | solution.py:103
  6.3 3.4 %shard_map.58 = (f32[8,512]{1,0:T(8,128)}, f32[1,512]{1,0:T(1,128)}) custom-call(bf16[512,4096]{1,0:T(8,128)(2,1)} %tok.3, bf16[512,512]{1,0:T(8,128)(2,1)} %cot.3), custom_call_target="tpu_custom_call" | custom-call | flops 4194304 | bytes 4718592 | tf_op jit(solution)/shard_map/pallas_call | solution.py:72
  9.7 6.6 %multiply_convert_fusion = f16[4096,512]{1,0:T(8,128)(2,1)} fusion(bf16[512,4096]{1,0:T(8,128)(2,1)} %tok.3, bf16[512,512]{1,0:T(8,128)(2,1)S(1)} %copy-done.1, f32[512]{0:T(512)} %bitcast.122), kind=kOutput, calls=%fused_computation | convolution fusion | flops 2151677952 | bytes 8914944 | tf_op jit(solution)/shard_map/dot_general | solution.py:152
  16.3 2.1 %dynamic-slice_bitcast_fusion = f16[16,1,128,512]{3,2,0,1:T(8,128)(2,1)S(1)} fusion(f16[16,2,128,512]{3,2,1,0:T(8,128)(2,1)} %bitcast.98, s32[]{:T(128)S(6)} %select_n.55), kind=kLoop, calls=%fused_computation.5 | loop fusion | bytes 4194308
  19.3 3.0 %collective-permute-done.3 = f32[8,512]{1,0:T(8,128)S(1)} collective-permute-done((f32[8,512]{1,0:T(8,128)S(1)}, f32[8,512]{1,0:T(8,128)S(1)}, u32[]{:S(2)}, u32[]{:S(2)}) %collective-permute-start.3) | collective-permute-done | bytes 16416 | tf_op jit(solution)/shard_map/ppermute | solution.py:103
  22.4 1.8 %collective-permute-start.6 = (bf16[264,512]{1,0:T(8,128)(2,1)S(1)}, bf16[264,512]{1,0:T(8,128)(2,1)S(1)}, u32[]{:S(2)}, u32[]{:S(2)}) collective-permute-start(bf16[264,512]{1,0:T(8,128)(2,1)S(1)} %get-tuple-element.69), channel_id=1, source_target_pairs={{0,16},{1,17},{2,18},{3,19},{4,20},{5,21},{6,22},{7,23},{8,24},{9,... | collective-permute-start | bytes 811016 | tf_op jit(solution)/shard_map/ppermute | solution.py:103
  24.2 1.5 %collective-permute-start.5 = (bf16[264,512]{1,0:T(8,128)(2,1)S(1)}, bf16[264,512]{1,0:T(8,128)(2,1)S(1)}, u32[]{:S(2)}, u32[]{:S(2)}) collective-permute-start(bf16[264,512]{1,0:T(8,128)(2,1)S(1)} %get-tuple-element.70), channel_id=1, source_target_pairs={{0,1},{1,0},{2,3},{3,2},{4,5},{5,4},{6,7},{7,6},{8,9},{9,8},{10,11... | collective-permute-start | bytes 811016 | tf_op jit(solution)/shard_map/ppermute | solution.py:103
  25.8 5.4 %collective-permute-done.6 = bf16[264,512]{1,0:T(8,128)(2,1)S(1)} collective-permute-done((bf16[264,512]{1,0:T(8,128)(2,1)S(1)}, bf16[264,512]{1,0:T(8,128)(2,1)S(1)}, u32[]{:S(2)}, u32[]{:S(2)}) %collective-permute-start.6) | collective-permute-done | bytes 270368 | tf_op jit(solution)/shard_map/ppermute | solution.py:103
  31.2 1.4 %collective-permute-done.5 = bf16[264,512]{1,0:T(8,128)(2,1)S(1)} collective-permute-done((bf16[264,512]{1,0:T(8,128)(2,1)S(1)}, bf16[264,512]{1,0:T(8,128)(2,1)S(1)}, u32[]{:S(2)}, u32[]{:S(2)}) %collective-permute-start.5) | collective-permute-done | bytes 270368 | tf_op jit(solution)/shard_map/ppermute | solution.py:103
  32.8 2.6 %add_convert_fusion = f16[16,1,128,512]{3,2,0,1:T(8,128)(2,1)S(1)} fusion(f16[16,1,128,512]{3,2,0,1:T(8,128)(2,1)} %collective-permute-done.4, f32[512]{0:T(512)S(1)} %bitcast.114, f32[512]{0:T(512)S(1)} %bitcast.115, s32[]{:T(128)S(6)} %select_n.54, f16[16,2,128,512]{3,2,1,0:T(8,128)(2,1)S(1)} %bitcast.99), kind=kLoop, calls=%fused_computation.1 | loop fusion | flops 6291456 | bytes 6295556 | tf_op jit(solution)/shard_map/convert_element_type | solution.py:161
  35.8 1.6 %collective-permute-start.8 = (bf16[520,512]{1,0:T(8,128)(2,1)S(1)}, bf16[520,512]{1,0:T(8,128)(2,1)S(1)}, u32[]{:S(2)}, u32[]{:S(2)}) collective-permute-start(bf16[520,512]{1,0:T(8,128)(2,1)S(1)} %pad_maximum_fusion.2), channel_id=1, source_target_pairs={{0,1},{1,0},{2,3},{3,2},{4,5},{5,4},{6,7},{7,6},{8,9},{9,8},{10,11... | collective-permute-start | bytes 1597448 | tf_op jit(solution)/shard_map/ppermute | solution.py:103
  38.6 1.7 %collective-permute-start.12 = (f16[4,2,1,64,512]{4,3,2,1,0:T(8,128)(2,1)S(1)}, f16[4,2,1,64,512]{4,3,2,1,0:T(8,128)(2,1)S(1)}, u32[]{:S(2)}, u32[]{:S(2)}) collective-permute-start(f16[4,2,1,64,512]{4,3,2,1,0:T(8,128)(2,1)S(1)} %constant_dynamic-slice_fusion.1), channel_id=1, source_target_pairs={{0,16},{1,17},{2,18},{3,19},{4,20},{5,21},{6,22},{7,23},{8,24},{9,... | collective-permute-start | bytes 1572872 | tf_op jit(solution)/shard_map/ppermute | solution.py:103
  40.5 10.4 %collective-permute-done.8 = bf16[520,512]{1,0:T(8,128)(2,1)S(1)} collective-permute-done((bf16[520,512]{1,0:T(8,128)(2,1)S(1)}, bf16[520,512]{1,0:T(8,128)(2,1)S(1)}, u32[]{:S(2)}, u32[]{:S(2)}) %collective-permute-start.8) | collective-permute-done | bytes 532512 | tf_op jit(solution)/shard_map/ppermute | solution.py:103
  51.0 1.5 %collective-permute-done.7 = bf16[520,512]{1,0:T(8,128)(2,1)S(1)} collective-permute-done((bf16[520,512]{1,0:T(8,128)(2,1)S(1)}, bf16[520,512]{1,0:T(8,128)(2,1)S(1)}, u32[]{:S(2)}, u32[]{:S(2)}) %collective-permute-start.7) | collective-permute-done | bytes 532512 | tf_op jit(solution)/shard_map/ppermute | solution.py:103
  52.9 7.4 %collective-permute-done.10 = f16[4,1,2,64,512]{4,3,2,1,0:T(8,128)(2,1)S(1)} collective-permute-done((f16[4,1,2,64,512]{4,3,2,1,0:T(8,128)(2,1)S(1)}, f16[4,1,2,64,512]{4,3,2,1,0:T(8,128)(2,1)S(1)}, u32[]{:S(2)}, u32[]{:S(2)}) %collective-permute-start.10) | collective-permute-done | bytes 524320 | tf_op jit(solution)/shard_map/ppermute | solution.py:103
  60.6 0.7 collective-permute-start.11
  61.9 1.2 %collective-permute-start.13 = (f16[4,1,1,64,512]{4,3,2,1,0:T(8,128)(2,1)S(1)}, f16[4,1,1,64,512]{4,3,2,1,0:T(8,128)(2,1)S(1)}, u32[]{:S(2)}, u32[]{:S(2)}) collective-permute-start(f16[4,1,1,64,512]{4,3,2,1,0:T(8,128)(2,1)S(1)} %constant_dynamic-slice_fusion), channel_id=1, source_target_pairs={{0,1},{1,0},{2,3},{3,2},{4,5},{5,4},{6,7},{7,6},{8,9},{9,8},{10,11... | collective-permute-start | bytes 786440 | tf_op jit(solution)/shard_map/ppermute | solution.py:103
  64.0 4.3 %collective-permute-done.13 = f16[4,1,1,64,512]{4,3,2,1,0:T(8,128)(2,1)S(1)} collective-permute-done((f16[4,1,1,64,512]{4,3,2,1,0:T(8,128)(2,1)S(1)}, f16[4,1,1,64,512]{4,3,2,1,0:T(8,128)(2,1)S(1)}, u32[]{:S(2)}, u32[]{:S(2)}) %collective-permute-start.13) | collective-permute-done | bytes 262176 | tf_op jit(solution)/shard_map/ppermute | solution.py:103
  68.9 3.7 %collective-permute-start.16 = (f16[136,512]{1,0:T(8,128)(2,1)S(1)}, f16[136,512]{1,0:T(8,128)(2,1)S(1)}, u32[]{:S(2)}, u32[]{:S(2)}) collective-permute-start(f16[136,512]{1,0:T(8,128)(2,1)S(1)} %get-tuple-element.66), channel_id=1, source_target_pairs={{0,6},{1,7},{2,4},{3,5},{4,2},{5,3},{6,0},{7,1},{8,14},{9,15},{10,... | collective-permute-start | bytes 417800 | tf_op jit(solution)/shard_map/ppermute | solution.py:103
  72.5 0.8 collective-permute-start.14
  73.6 6.6 %shard_map.59 = (bf16[512,512]{1,0:T(8,128)(2,1)}, bf16[512,4096]{1,0:T(8,128)(2,1)}) custom-call(bf16[512,4096]{1,0:T(8,128)(2,1)S(1)} %copy-done, bf16[512,512]{1,0:T(8,128)(2,1)S(1)} %copy-done.1, bf16[4,1024,512]{2,1,0:T(8,128)(2,1)S(1)} %bitcast.88), custom_call_target="tpu_custom_call" | custom-call | tf_op jit(solution)/shard_map/pallas_call | solution.py:35
  80.2 0.8 collective-permute-done.15
  81.1 0.8 %fusion.3 = f32[128,512]{1,0:T(8,128)} fusion(s32[]{:T(128)S(6)} %select_n.56, f16[4,1,1,64,512]{4,3,2,1,0:T(8,128)(2,1)S(1)} %add_convert_fusion.4, f16[4,1,1,64,512]{4,3,2,1,0:T(8,128)(2,1)S(1)} %add_convert_fusion.3, f32[512]{0:T(512)S(1)} %bitcast.118, f16[136,512]{1,0:T(8,128)(2,1)S(1)} %collective-permute-done.16, f32[512]{0:T(512)S(1)} %bitcast.117, ...), kind=kLoop, calls=%fused_computation.30 | loop fusion | flops 851968 | bytes 1187844 | tf_op jit(solution)/shard_map/mul | solution.py:192
  (82 shorter events, 5.7 us)
Async XLA Ops:
  0.6 9.1 %copy-start.1 = (bf16[512,512]{1,0:T(8,128)(2,1)S(1)}, bf16[512,512]{1,0:T(8,128)(2,1)}, u32[]{:S(2)}) copy-start(bf16[512,512]{1,0:T(8,128)(2,1)} %cot.3) | copy-start | bytes 1572868
  0.6 18.5 %collective-permute-start.1 = (bf16[128,512]{1,0:T(8,128)(2,1)}, bf16[128,512]{1,0:T(8,128)(2,1)S(1)}, u32[]{:S(2)}, u32[]{:S(2)}) collective-permute-start(bf16[128,512]{1,0:T(8,128)(2,1)} %param.4), channel_id=1, source_target_pairs={{0,4},{1,5},{2,6},{3,7},{4,0},{5,1},{6,2},{7,3},{8,12},{9,13},{10,... | collective-permute-start | bytes 393224 | tf_op jit(solution)/shard_map/ppermute | solution.py:103
  4.7 13.9 %collective-permute-start = (bf16[128,512]{1,0:T(8,128)(2,1)}, bf16[128,512]{1,0:T(8,128)(2,1)S(1)}, u32[]{:S(2)}, u32[]{:S(2)}) collective-permute-start(bf16[128,512]{1,0:T(8,128)(2,1)} %param.4), channel_id=1, source_target_pairs={{0,2},{1,3},{2,0},{3,1},{4,6},{5,7},{6,4},{7,5},{8,10},{9,11},{10,... | collective-permute-start | bytes 393224 | tf_op jit(solution)/shard_map/ppermute | solution.py:103
  6.3 12.8 %collective-permute-start.2 = (bf16[128,512]{1,0:T(8,128)(2,1)}, bf16[128,512]{1,0:T(8,128)(2,1)S(1)}, u32[]{:S(2)}, u32[]{:S(2)}) collective-permute-start(bf16[128,512]{1,0:T(8,128)(2,1)} %param.4), channel_id=1, source_target_pairs={{0,6},{1,7},{2,4},{3,5},{4,2},{5,3},{6,0},{7,1},{8,14},{9,15},{10,... | collective-permute-start | bytes 393224 | tf_op jit(solution)/shard_map/ppermute | solution.py:103
  16.3 2.3 %copy-start.3 = (bf16[128,512]{1,0:T(8,128)(2,1)S(1)}, bf16[128,512]{1,0:T(8,128)(2,1)}, u32[]{:S(2)}) copy-start(bf16[128,512]{1,0:T(8,128)(2,1)} %param.4) | copy-start | bytes 393220
  16.3 2.4 %copy-start.4 = (f32[8,512]{1,0:T(8,128)S(1)}, f32[8,512]{1,0:T(8,128)}, u32[]{:S(2)}) copy-start(f32[8,512]{1,0:T(8,128)} %get-tuple-element.31) | copy-start | bytes 49156
  18.4 14.4 %collective-permute-start.4 = (f16[16,1,128,512]{3,2,0,1:T(8,128)(2,1)S(1)}, f16[16,1,128,512]{3,2,0,1:T(8,128)(2,1)}, u32[]{:S(2)}, u32[]{:S(2)}) collective-permute-start(f16[16,1,128,512]{3,2,0,1:T(8,128)(2,1)S(1)} %dynamic-slice_bitcast_fusion), channel_id=1, source_target_pairs={{0,8},{1,9},{2,10},{3,11},{4,12},{5,13},{6,14},{7,15},{8,0},{9,1},... | collective-permute-start | bytes 6291464 | tf_op jit(solution)/shard_map/ppermute | solution.py:103
  18.5 14.3 %copy-start.2 = (f16[4096,512]{1,0:T(8,128)(2,1)S(1)}, f16[4096,512]{1,0:T(8,128)(2,1)}, u32[]{:S(2)}) copy-start(f16[4096,512]{1,0:T(8,128)(2,1)} %multiply_convert_fusion) | copy-start | bytes 12582916
  18.7 3.6 %collective-permute-start.3 = (f32[8,512]{1,0:T(8,128)S(1)}, f32[8,512]{1,0:T(8,128)S(1)}, u32[]{:S(2)}, u32[]{:S(2)}) collective-permute-start(f32[8,512]{1,0:T(8,128)S(1)} %copy-done.4), channel_id=1, source_target_pairs={{0,8},{1,9},{2,10},{3,11},{4,12},{5,13},{6,14},{7,15},{8,0},{9,1},... | collective-permute-start | bytes 49160 | tf_op jit(solution)/shard_map/ppermute | solution.py:103
  22.4 8.8 %collective-permute-start.6 = (bf16[264,512]{1,0:T(8,128)(2,1)S(1)}, bf16[264,512]{1,0:T(8,128)(2,1)S(1)}, u32[]{:S(2)}, u32[]{:S(2)}) collective-permute-start(bf16[264,512]{1,0:T(8,128)(2,1)S(1)} %get-tuple-element.69), channel_id=1, source_target_pairs={{0,16},{1,17},{2,18},{3,19},{4,20},{5,21},{6,22},{7,23},{8,24},{9,... | collective-permute-start | bytes 811016 | tf_op jit(solution)/shard_map/ppermute | solution.py:103
  24.2 8.5 %collective-permute-start.5 = (bf16[264,512]{1,0:T(8,128)(2,1)S(1)}, bf16[264,512]{1,0:T(8,128)(2,1)S(1)}, u32[]{:S(2)}, u32[]{:S(2)}) collective-permute-start(bf16[264,512]{1,0:T(8,128)(2,1)S(1)} %get-tuple-element.70), channel_id=1, source_target_pairs={{0,1},{1,0},{2,3},{3,2},{4,5},{5,4},{6,7},{7,6},{8,9},{9,8},{10,11... | collective-permute-start | bytes 811016 | tf_op jit(solution)/shard_map/ppermute | solution.py:103
  35.8 15.1 %collective-permute-start.8 = (bf16[520,512]{1,0:T(8,128)(2,1)S(1)}, bf16[520,512]{1,0:T(8,128)(2,1)S(1)}, u32[]{:S(2)}, u32[]{:S(2)}) collective-permute-start(bf16[520,512]{1,0:T(8,128)(2,1)S(1)} %pad_maximum_fusion.2), channel_id=1, source_target_pairs={{0,1},{1,0},{2,3},{3,2},{4,5},{5,4},{6,7},{7,6},{8,9},{9,8},{10,11... | collective-permute-start | bytes 1597448 | tf_op jit(solution)/shard_map/ppermute | solution.py:103
  37.4 15.1 %collective-permute-start.7 = (bf16[520,512]{1,0:T(8,128)(2,1)S(1)}, bf16[520,512]{1,0:T(8,128)(2,1)S(1)}, u32[]{:S(2)}, u32[]{:S(2)}) collective-permute-start(bf16[520,512]{1,0:T(8,128)(2,1)S(1)} %pad_maximum_fusion.1), channel_id=1, source_target_pairs={{0,16},{1,17},{2,18},{3,19},{4,20},{5,21},{6,22},{7,23},{8,24},{9,... | collective-permute-start | bytes 1597448 | tf_op jit(solution)/shard_map/ppermute | solution.py:103
  38.2 22.2 %collective-permute-start.10 = (f16[4,1,2,64,512]{4,3,2,1,0:T(8,128)(2,1)S(1)}, f16[4,1,2,64,512]{4,3,2,1,0:T(8,128)(2,1)S(1)}, u32[]{:S(2)}, u32[]{:S(2)}) collective-permute-start(f16[4,1,2,64,512]{4,3,2,1,0:T(8,128)(2,1)S(1)} %constant_dynamic-slice_fusion.3), channel_id=1, source_target_pairs={{0,1},{1,0},{2,3},{3,2},{4,5},{5,4},{6,7},{7,6},{8,9},{9,8},{10,11... | collective-permute-start | bytes 1572872 | tf_op jit(solution)/shard_map/ppermute | solution.py:103
  38.6 23.0 %collective-permute-start.12 = (f16[4,2,1,64,512]{4,3,2,1,0:T(8,128)(2,1)S(1)}, f16[4,2,1,64,512]{4,3,2,1,0:T(8,128)(2,1)S(1)}, u32[]{:S(2)}, u32[]{:S(2)}) collective-permute-start(f16[4,2,1,64,512]{4,3,2,1,0:T(8,128)(2,1)S(1)} %constant_dynamic-slice_fusion.1), channel_id=1, source_target_pairs={{0,16},{1,17},{2,18},{3,19},{4,20},{5,21},{6,22},{7,23},{8,24},{9,... | collective-permute-start | bytes 1572872 | tf_op jit(solution)/shard_map/ppermute | solution.py:103
  52.8 20.5 %collective-permute-start.9 = (bf16[4,2,2,2,64,512]{5,4,3,2,1,0:T(8,128)(2,1)S(1)}, bf16[4,2,2,2,64,512]{5,4,3,2,1,0:T(8,128)(2,1)S(1)}, u32[]{:S(2)}, u32[]{:S(2)}) collective-permute-start(bf16[4,2,2,2,64,512]{5,4,3,2,1,0:T(8,128)(2,1)S(1)} %pad_maximum_fusion), channel_id=1, source_target_pairs={{0,8},{1,9},{2,10},{3,11},{4,12},{5,13},{6,14},{7,15},{8,0},{9,1},... | collective-permute-start | bytes 6291464 | tf_op jit(solution)/shard_map/ppermute | solution.py:103
  60.6 7.9 %collective-permute-start.11 = (f16[4,1,1,64,512]{4,3,2,1,0:T(8,128)(2,1)S(1)}, f16[4,1,1,64,512]{4,3,2,1,0:T(8,128)(2,1)S(1)}, u32[]{:S(2)}, u32[]{:S(2)}) collective-permute-start(f16[4,1,1,64,512]{4,3,2,1,0:T(8,128)(2,1)S(1)} %constant_dynamic-slice_fusion.2), channel_id=1, source_target_pairs={{0,16},{1,17},{2,18},{3,19},{4,20},{5,21},{6,22},{7,23},{8,24},{9,... | collective-permute-start | bytes 786440 | tf_op jit(solution)/shard_map/ppermute | solution.py:103
  61.9 6.4 %collective-permute-start.13 = (f16[4,1,1,64,512]{4,3,2,1,0:T(8,128)(2,1)S(1)}, f16[4,1,1,64,512]{4,3,2,1,0:T(8,128)(2,1)S(1)}, u32[]{:S(2)}, u32[]{:S(2)}) collective-permute-start(f16[4,1,1,64,512]{4,3,2,1,0:T(8,128)(2,1)S(1)} %constant_dynamic-slice_fusion), channel_id=1, source_target_pairs={{0,1},{1,0},{2,3},{3,2},{4,5},{5,4},{6,7},{7,6},{8,9},{9,8},{10,11... | collective-permute-start | bytes 786440 | tf_op jit(solution)/shard_map/ppermute | solution.py:103
  64.0 9.6 %copy-start = (bf16[512,4096]{1,0:T(8,128)(2,1)S(1)}, bf16[512,4096]{1,0:T(8,128)(2,1)}, u32[]{:S(2)}) copy-start(bf16[512,4096]{1,0:T(8,128)(2,1)} %tok.3) | copy-start | bytes 12582916
  68.9 11.4 %collective-permute-start.16 = (f16[136,512]{1,0:T(8,128)(2,1)S(1)}, f16[136,512]{1,0:T(8,128)(2,1)S(1)}, u32[]{:S(2)}, u32[]{:S(2)}) collective-permute-start(f16[136,512]{1,0:T(8,128)(2,1)S(1)} %get-tuple-element.66), channel_id=1, source_target_pairs={{0,6},{1,7},{2,4},{3,5},{4,2},{5,3},{6,0},{7,1},{8,14},{9,15},{10,... | collective-permute-start | bytes 417800 | tf_op jit(solution)/shard_map/ppermute | solution.py:103
  72.5 8.5 %collective-permute-start.15 = (f16[136,512]{1,0:T(8,128)(2,1)S(1)}, f16[136,512]{1,0:T(8,128)(2,1)S(1)}, u32[]{:S(2)}, u32[]{:S(2)}) collective-permute-start(f16[136,512]{1,0:T(8,128)(2,1)S(1)} %get-tuple-element.67), channel_id=1, source_target_pairs={{0,4},{1,5},{2,6},{3,7},{4,0},{5,1},{6,2},{7,3},{8,12},{9,13},{10,... | collective-permute-start | bytes 417800 | tf_op jit(solution)/shard_map/ppermute | solution.py:103
  72.5 8.5 %collective-permute-start.14 = (f16[136,512]{1,0:T(8,128)(2,1)S(1)}, f16[136,512]{1,0:T(8,128)(2,1)S(1)}, u32[]{:S(2)}, u32[]{:S(2)}) collective-permute-start(f16[136,512]{1,0:T(8,128)(2,1)S(1)} %get-tuple-element.68), channel_id=1, source_target_pairs={{0,2},{1,3},{2,0},{3,1},{4,6},{5,7},{6,4},{7,5},{8,10},{9,11},{10,... | collective-permute-start | bytes 417800 | tf_op jit(solution)/shard_map/ppermute | solution.py:103

commit v13 on v12

--- a/solution.py
+++ b/solution.py
@@ -147,13 +147,15 @@
     shards = [swap(key_weight, "z", j) for j in range(1, nz)]
 
     power, to_top = bound_of(tokens, cotangent)
-    power, shards[0] = lax.optimization_barrier((power, shards[0]))
-    power, by_core = factors(power[:1], [swap(power, "core", 1)[:1]])
+    power, to_top, shards[0] = lax.optimization_barrier((power, to_top, shards[0]))
+    power_core = swap(power, "core", 1)
     part = lax.dot_general(
         tokens, cotangent, (((0,), (0,)), ((), ())), preferred_element_type=jnp.float32
     )
     part = (part * to_top).astype(jnp.float16).reshape(nz * nx * ny, 2, rows, kd)
-    other = swap(pick(part, (1, 1 - core)), "core", 1)
+    sent, power_core = lax.optimization_barrier((pick(part, (1, 1 - core)), power_core))
+    other = swap(sent, "core", 1)
+    power, by_core = factors(power[:1], [power_core[:1]])
     part, shards = lax.optimization_barrier((part, shards))
     shards = in_order(key_weight, shards, "z")
     part = pick(part, (1, core)).astype(jnp.float32) * by_core[0]

time: 82.1 us -> 77.6 us (0.945)
  matrix products: 6.6 us -> 4.58 us
  local copies, waits for them, and re-layouts: 4.14 us -> 2.56 us
    unnamed x11 -> x6, local copies, waits for them, and re-layouts: 2.15 us -> 0.01 us
    dot_general x1, matrix products: 6.6 us -> 4.58 us  [on_device(): lax.dot_general(tokens, cotangent, (((0,), (0,)), ((), ())), preferred_el...]
    convert_element_type x1, other arithmetic: 2.58 us -> 0.99 us  [on_device(): part = part.astype(jnp.float16).reshape(nz, nx, ny, rows, kd)]
  transfers between devices with their start and end apart: 17 -> 17, of which waited for: 9 -> 9; matrix products, arithmetic and copies ran while one was open for 15% -> 13% of each run, Pallas kernels for 12% -> 13%
where the time goes in v13:
time: 77.6 us; the launch traced here: 77.2 us
  waiting for transfers between devices  34.4 us (44%)
  starting transfers between devices  19.7 us (25%)
  Pallas kernels  10 us (13%)
  other arithmetic  4.96 us (6%)
  matrix products  4.58 us (6%)
  local copies, waits for them, and re-layouts  2.56 us (3%)
  between operations  1.09 us (1%)
    ppermute x17, waiting for transfers between devices, swap(): lax.ppermute(value, AXES, [(i, i ^ j * mask[name]) for i in range(wide *...  34.4 us
    ppermute x17, starting transfers between devices, swap(): lax.ppermute(value, AXES, [(i, i ^ j * mask[name]) for i in range(wide *...  19.7 us
    pallas_call x1, Pallas kernels, products(): pl.pallas_call(products_kernel, grid=(steps,), in_specs=[columns, whole,...  6.63 us
    dot_general x1, matrix products, on_device(): lax.dot_general(tokens, cotangent, (((0,), (0,)), ((), ())), preferred_el...  4.58 us
    pallas_call x1, Pallas kernels, bound_of(): pl.pallas_call(bound_kernel, grid=(rows // block,), in_specs=[pl.BlockSpe...  3.36 us
  transfers between devices with their start and end apart: 17, of which 9 were waited for; matrix products, arithmetic and copies ran while one was open for 13% of the time, Pallas kernels for 13%

profile of v13, /device:TPU:0, one launch (start us, length us, event | category | flops | bytes accessed | tf_op | source)
XLA Modules:
  0.0 77.2 jit_solution(3286618755249372513)
XLA Ops:
  0.7 4.1 %collective-permute-start.1 = (bf16[128,512]{1,0:T(8,128)(2,1)}, bf16[128,512]{1,0:T(8,128)(2,1)S(1)}, u32[]{:S(2)}, u32[]{:S(2)}) collective-permute-start(bf16[128,512]{1,0:T(8,128)(2,1)} %param.4), channel_id=1, source_target_pairs={{0,4},{1,5},{2,6},{3,7},{4,0},{5,1},{6,2},{7,3},{8,12},{9,13},{10,... | collective-permute-start | bytes 393224 | tf_op jit(solution)/shard_map/ppermute | solution.py:103
  4.8 1.6 %collective-permute-start = (bf16[128,512]{1,0:T(8,128)(2,1)}, bf16[128,512]{1,0:T(8,128)(2,1)S(1)}, u32[]{:S(2)}, u32[]{:S(2)}) collective-permute-start(bf16[128,512]{1,0:T(8,128)(2,1)} %param.4), channel_id=1, source_target_pairs={{0,2},{1,3},{2,0},{3,1},{4,6},{5,7},{6,4},{7,5},{8,10},{9,11},{10,... | collective-permute-start | bytes 393224 | tf_op jit(solution)/shard_map/ppermute | solution.py:103
  6.3 3.4 %shard_map.58 = (f32[8,512]{1,0:T(8,128)}, f32[1,512]{1,0:T(1,128)}) custom-call(bf16[512,4096]{1,0:T(8,128)(2,1)} %tok.3, bf16[512,512]{1,0:T(8,128)(2,1)} %cot.3), custom_call_target="tpu_custom_call" | custom-call | flops 4194304 | bytes 4718592 | tf_op jit(solution)/shard_map/pallas_call | solution.py:72
  9.8 2.0 %collective-permute-done = bf16[128,512]{1,0:T(8,128)(2,1)S(1)} collective-permute-done((bf16[128,512]{1,0:T(8,128)(2,1)}, bf16[128,512]{1,0:T(8,128)(2,1)S(1)}, u32[]{:S(2)}, u32[]{:S(2)}) %collective-permute-start) | collective-permute-done | bytes 131104 | tf_op jit(solution)/shard_map/ppermute | solution.py:103
  11.8 4.6 %multiply_convert_fusion = f16[4096,512]{1,0:T(8,128)(2,1)S(1)} fusion(f32[512]{0:T(512)} %bitcast.122, bf16[512,4096]{1,0:T(8,128)(2,1)} %tok.3, bf16[512,512]{1,0:T(8,128)(2,1)S(1)} %copy-done.1), kind=kOutput, calls=%fused_computation | convolution fusion | flops 2151677952 | bytes 8914944 | tf_op jit(solution)/shard_map/dot_general | solution.py:152
  17.7 0.7 convert_reduce_fusion.3
  18.5 1.6 %collective-permute-start.6 = (bf16[264,512]{1,0:T(8,128)(2,1)S(1)}, bf16[264,512]{1,0:T(8,128)(2,1)S(1)}, u32[]{:S(2)}, u32[]{:S(2)}) collective-permute-start(bf16[264,512]{1,0:T(8,128)(2,1)S(1)} %get-tuple-element.75), channel_id=1, source_target_pairs={{0,16},{1,17},{2,18},{3,19},{4,20},{5,21},{6,22},{7,23},{8,24},{9,... | collective-permute-start | bytes 811016 | tf_op jit(solution)/shard_map/ppermute | solution.py:103
  20.1 1.5 %collective-permute-start.5 = (bf16[264,512]{1,0:T(8,128)(2,1)S(1)}, bf16[264,512]{1,0:T(8,128)(2,1)S(1)}, u32[]{:S(2)}, u32[]{:S(2)}) collective-permute-start(bf16[264,512]{1,0:T(8,128)(2,1)S(1)} %get-tuple-element.76), channel_id=1, source_target_pairs={{0,1},{1,0},{2,3},{3,2},{4,5},{5,4},{6,7},{7,6},{8,9},{9,8},{10,11... | collective-permute-start | bytes 811016 | tf_op jit(solution)/shard_map/ppermute | solution.py:103
  21.7 5.2 %collective-permute-done.6 = bf16[264,512]{1,0:T(8,128)(2,1)S(1)} collective-permute-done((bf16[264,512]{1,0:T(8,128)(2,1)S(1)}, bf16[264,512]{1,0:T(8,128)(2,1)S(1)}, u32[]{:S(2)}, u32[]{:S(2)}) %collective-permute-start.6) | collective-permute-done | bytes 270368 | tf_op jit(solution)/shard_map/ppermute | solution.py:103
  27.0 1.2 %collective-permute-done.5 = bf16[264,512]{1,0:T(8,128)(2,1)S(1)} collective-permute-done((bf16[264,512]{1,0:T(8,128)(2,1)S(1)}, bf16[264,512]{1,0:T(8,128)(2,1)S(1)}, u32[]{:S(2)}, u32[]{:S(2)}) %collective-permute-start.5) | collective-permute-done | bytes 270368 | tf_op jit(solution)/shard_map/ppermute | solution.py:103
  28.3 0.7 multiply_exponential_fusion.9
  29.0 1.0 %add_convert_fusion = f16[16,1,128,512]{3,2,0,1:T(8,128)(2,1)S(1)} fusion(f16[16,1,128,512]{3,2,0,1:T(8,128)(2,1)S(1)} %collective-permute-done.4, f32[512]{0:T(512)S(1)} %bitcast.114, f32[512]{0:T(512)S(1)} %bitcast.115, s32[]{:T(128)S(6)} %select_n.54, f16[16,2,128,512]{3,2,1,0:T(8,128)(2,1)S(1)} %bitcast.99), kind=kLoop, calls=%fused_computation.1 | loop fusion | flops 6291456 | bytes 6295556 | tf_op jit(solution)/shard_map/convert_element_type | solution.py:163
  30.4 1.6 %collective-permute-start.8 = (bf16[520,512]{1,0:T(8,128)(2,1)S(1)}, bf16[520,512]{1,0:T(8,128)(2,1)S(1)}, u32[]{:S(2)}, u32[]{:S(2)}) collective-permute-start(bf16[520,512]{1,0:T(8,128)(2,1)S(1)} %pad_maximum_fusion.2), channel_id=1, source_target_pairs={{0,1},{1,0},{2,3},{3,2},{4,5},{5,4},{6,7},{7,6},{8,9},{9,8},{10,11... | collective-permute-start | bytes 1597448 | tf_op jit(solution)/shard_map/ppermute | solution.py:103
  33.4 1.5 %collective-permute-start.12 = (f16[4,2,1,64,512]{4,3,2,1,0:T(8,128)(2,1)S(1)}, f16[4,2,1,64,512]{4,3,2,1,0:T(8,128)(2,1)S(1)}, u32[]{:S(2)}, u32[]{:S(2)}) collective-permute-start(f16[4,2,1,64,512]{4,3,2,1,0:T(8,128)(2,1)S(1)} %constant_dynamic-slice_fusion.1), channel_id=1, source_target_pairs={{0,16},{1,17},{2,18},{3,19},{4,20},{5,21},{6,22},{7,23},{8,24},{9,... | collective-permute-start | bytes 1572872 | tf_op jit(solution)/shard_map/ppermute | solution.py:103
  35.1 10.4 %collective-permute-done.8 = bf16[520,512]{1,0:T(8,128)(2,1)S(1)} collective-permute-done((bf16[520,512]{1,0:T(8,128)(2,1)S(1)}, bf16[520,512]{1,0:T(8,128)(2,1)S(1)}, u32[]{:S(2)}, u32[]{:S(2)}) %collective-permute-start.8) | collective-permute-done | bytes 532512 | tf_op jit(solution)/shard_map/ppermute | solution.py:103
  45.6 1.5 %collective-permute-done.7 = bf16[520,512]{1,0:T(8,128)(2,1)S(1)} collective-permute-done((bf16[520,512]{1,0:T(8,128)(2,1)S(1)}, bf16[520,512]{1,0:T(8,128)(2,1)S(1)}, u32[]{:S(2)}, u32[]{:S(2)}) %collective-permute-start.7) | collective-permute-done | bytes 532512 | tf_op jit(solution)/shard_map/ppermute | solution.py:103
  47.5 7.1 %collective-permute-done.10 = f16[4,1,2,64,512]{4,3,2,1,0:T(8,128)(2,1)S(1)} collective-permute-done((f16[4,1,2,64,512]{4,3,2,1,0:T(8,128)(2,1)S(1)}, f16[4,1,2,64,512]{4,3,2,1,0:T(8,128)(2,1)S(1)}, u32[]{:S(2)}, u32[]{:S(2)}) %collective-permute-start.10) | collective-permute-done | bytes 524320 | tf_op jit(solution)/shard_map/ppermute | solution.py:103
  56.5 0.9 %collective-permute-start.13 = (f16[4,1,1,64,512]{4,3,2,1,0:T(8,128)(2,1)S(1)}, f16[4,1,1,64,512]{4,3,2,1,0:T(8,128)(2,1)S(1)}, u32[]{:S(2)}, u32[]{:S(2)}) collective-permute-start(f16[4,1,1,64,512]{4,3,2,1,0:T(8,128)(2,1)S(1)} %constant_dynamic-slice_fusion), channel_id=1, source_target_pairs={{0,1},{1,0},{2,3},{3,2},{4,5},{5,4},{6,7},{7,6},{8,9},{9,8},{10,11... | collective-permute-start | bytes 786440 | tf_op jit(solution)/shard_map/ppermute | solution.py:103
  58.3 4.7 %collective-permute-done.13 = f16[4,1,1,64,512]{4,3,2,1,0:T(8,128)(2,1)S(1)} collective-permute-done((f16[4,1,1,64,512]{4,3,2,1,0:T(8,128)(2,1)S(1)}, f16[4,1,1,64,512]{4,3,2,1,0:T(8,128)(2,1)S(1)}, u32[]{:S(2)}, u32[]{:S(2)}) %collective-permute-start.13) | collective-permute-done | bytes 262176 | tf_op jit(solution)/shard_map/ppermute | solution.py:103
  63.5 1.9 %collective-permute-start.16 = (f16[136,512]{1,0:T(8,128)(2,1)S(1)}, f16[136,512]{1,0:T(8,128)(2,1)S(1)}, u32[]{:S(2)}, u32[]{:S(2)}) collective-permute-start(f16[136,512]{1,0:T(8,128)(2,1)S(1)} %get-tuple-element.72), channel_id=1, source_target_pairs={{0,6},{1,7},{2,4},{3,5},{4,2},{5,3},{6,0},{7,1},{8,14},{9,15},{10,... | collective-permute-start | bytes 417800 | tf_op jit(solution)/shard_map/ppermute | solution.py:103
  65.4 2.0 %collective-permute-start.15 = (f16[136,512]{1,0:T(8,128)(2,1)S(1)}, f16[136,512]{1,0:T(8,128)(2,1)S(1)}, u32[]{:S(2)}, u32[]{:S(2)}) collective-permute-start(f16[136,512]{1,0:T(8,128)(2,1)S(1)} %get-tuple-element.73), channel_id=1, source_target_pairs={{0,4},{1,5},{2,6},{3,7},{4,0},{5,1},{6,2},{7,3},{8,12},{9,13},{10,... | collective-permute-start | bytes 417800 | tf_op jit(solution)/shard_map/ppermute | solution.py:103
  68.2 6.6 %shard_map.59 = (bf16[512,512]{1,0:T(8,128)(2,1)}, bf16[512,4096]{1,0:T(8,128)(2,1)}) custom-call(bf16[512,4096]{1,0:T(8,128)(2,1)S(1)} %copy-done, bf16[512,512]{1,0:T(8,128)(2,1)S(1)} %copy-done.1, bf16[4,1024,512]{2,1,0:T(8,128)(2,1)S(1)} %bitcast.88), custom_call_target="tpu_custom_call" | custom-call | tf_op jit(solution)/shard_map/pallas_call | solution.py:35
  74.9 1.5 %collective-permute-done.15 = f16[136,512]{1,0:T(8,128)(2,1)S(1)} collective-permute-done((f16[136,512]{1,0:T(8,128)(2,1)S(1)}, f16[136,512]{1,0:T(8,128)(2,1)S(1)}, u32[]{:S(2)}, u32[]{:S(2)}) %collective-permute-start.15) | collective-permute-done | bytes 139296 | tf_op jit(solution)/shard_map/ppermute | solution.py:103
  76.4 0.8 %fusion.3 = f32[128,512]{1,0:T(8,128)} fusion(s32[]{:T(128)S(6)} %select_n.56, f16[4,1,1,64,512]{4,3,2,1,0:T(8,128)(2,1)S(1)} %add_convert_fusion.4, f16[4,1,1,64,512]{4,3,2,1,0:T(8,128)(2,1)S(1)} %add_convert_fusion.3, f32[512]{0:T(512)S(1)} %bitcast.118, f16[136,512]{1,0:T(8,128)(2,1)S(1)} %collective-permute-done.16, f32[512]{0:T(512)S(1)} %bitcast.117, ...), kind=kLoop, calls=%fused_computation.30 | loop fusion | flops 851968 | bytes 1187844 | tf_op jit(solution)/shard_map/mul | solution.py:194
  (78 shorter events, 8.0 us)
Async XLA Ops:
  0.6 9.1 %copy-start.2 = (bf16[128,512]{1,0:T(8,128)(2,1)S(1)}, bf16[128,512]{1,0:T(8,128)(2,1)}, u32[]{:S(2)}) copy-start(bf16[128,512]{1,0:T(8,128)(2,1)} %param.4) | copy-start | bytes 393220
  0.6 11.1 %copy-start.1 = (bf16[512,512]{1,0:T(8,128)(2,1)S(1)}, bf16[512,512]{1,0:T(8,128)(2,1)}, u32[]{:S(2)}) copy-start(bf16[512,512]{1,0:T(8,128)(2,1)} %cot.3) | copy-start | bytes 1572868
  0.7 15.7 %collective-permute-start.1 = (bf16[128,512]{1,0:T(8,128)(2,1)}, bf16[128,512]{1,0:T(8,128)(2,1)S(1)}, u32[]{:S(2)}, u32[]{:S(2)}) collective-permute-start(bf16[128,512]{1,0:T(8,128)(2,1)} %param.4), channel_id=1, source_target_pairs={{0,4},{1,5},{2,6},{3,7},{4,0},{5,1},{6,2},{7,3},{8,12},{9,13},{10,... | collective-permute-start | bytes 393224 | tf_op jit(solution)/shard_map/ppermute | solution.py:103
  4.8 7.0 %collective-permute-start = (bf16[128,512]{1,0:T(8,128)(2,1)}, bf16[128,512]{1,0:T(8,128)(2,1)S(1)}, u32[]{:S(2)}, u32[]{:S(2)}) collective-permute-start(bf16[128,512]{1,0:T(8,128)(2,1)} %param.4), channel_id=1, source_target_pairs={{0,2},{1,3},{2,0},{3,1},{4,6},{5,7},{6,4},{7,5},{8,10},{9,11},{10,... | collective-permute-start | bytes 393224 | tf_op jit(solution)/shard_map/ppermute | solution.py:103
  6.3 10.1 %collective-permute-start.2 = (bf16[128,512]{1,0:T(8,128)(2,1)}, bf16[128,512]{1,0:T(8,128)(2,1)S(1)}, u32[]{:S(2)}, u32[]{:S(2)}) collective-permute-start(bf16[128,512]{1,0:T(8,128)(2,1)} %param.4), channel_id=1, source_target_pairs={{0,6},{1,7},{2,4},{3,5},{4,2},{5,3},{6,0},{7,1},{8,14},{9,15},{10,... | collective-permute-start | bytes 393224 | tf_op jit(solution)/shard_map/ppermute | solution.py:103
  11.8 5.2 %collective-permute-start.3 = (f32[8,512]{1,0:T(8,128)}, f32[8,512]{1,0:T(8,128)S(1)}, u32[]{:S(2)}, u32[]{:S(2)}) collective-permute-start(f32[8,512]{1,0:T(8,128)} %get-tuple-element.35), channel_id=1, source_target_pairs={{0,8},{1,9},{2,10},{3,11},{4,12},{5,13},{6,14},{7,15},{8,0},{9,1},... | collective-permute-start | bytes 49160 | tf_op jit(solution)/shard_map/ppermute | solution.py:103
  17.0 12.0 %collective-permute-start.4 = (f16[16,1,128,512]{3,2,0,1:T(8,128)(2,1)S(1)}, f16[16,1,128,512]{3,2,0,1:T(8,128)(2,1)S(1)}, u32[]{:S(2)}, u32[]{:S(2)}) collective-permute-start(f16[16,1,128,512]{3,2,0,1:T(8,128)(2,1)S(1)} %dynamic-slice_bitcast_fusion), channel_id=1, source_target_pairs={{0,8},{1,9},{2,10},{3,11},{4,12},{5,13},{6,14},{7,15},{8,0},{9,1},... | collective-permute-start | bytes 6291464 | tf_op jit(solution)/shard_map/ppermute | solution.py:103
  18.5 8.5 %collective-permute-start.6 = (bf16[264,512]{1,0:T(8,128)(2,1)S(1)}, bf16[264,512]{1,0:T(8,128)(2,1)S(1)}, u32[]{:S(2)}, u32[]{:S(2)}) collective-permute-start(bf16[264,512]{1,0:T(8,128)(2,1)S(1)} %get-tuple-element.75), channel_id=1, source_target_pairs={{0,16},{1,17},{2,18},{3,19},{4,20},{5,21},{6,22},{7,23},{8,24},{9,... | collective-permute-start | bytes 811016 | tf_op jit(solution)/shard_map/ppermute | solution.py:103
  20.1 8.1 %collective-permute-start.5 = (bf16[264,512]{1,0:T(8,128)(2,1)S(1)}, bf16[264,512]{1,0:T(8,128)(2,1)S(1)}, u32[]{:S(2)}, u32[]{:S(2)}) collective-permute-start(bf16[264,512]{1,0:T(8,128)(2,1)S(1)} %get-tuple-element.76), channel_id=1, source_target_pairs={{0,1},{1,0},{2,3},{3,2},{4,5},{5,4},{6,7},{7,6},{8,9},{9,8},{10,11... | collective-permute-start | bytes 811016 | tf_op jit(solution)/shard_map/ppermute | solution.py:103
  30.4 15.1 %collective-permute-start.8 = (bf16[520,512]{1,0:T(8,128)(2,1)S(1)}, bf16[520,512]{1,0:T(8,128)(2,1)S(1)}, u32[]{:S(2)}, u32[]{:S(2)}) collective-permute-start(bf16[520,512]{1,0:T(8,128)(2,1)S(1)} %pad_maximum_fusion.2), channel_id=1, source_target_pairs={{0,1},{1,0},{2,3},{3,2},{4,5},{5,4},{6,7},{7,6},{8,9},{9,8},{10,11... | collective-permute-start | bytes 1597448 | tf_op jit(solution)/shard_map/ppermute | solution.py:103
  32.0 15.1 %collective-permute-start.7 = (bf16[520,512]{1,0:T(8,128)(2,1)S(1)}, bf16[520,512]{1,0:T(8,128)(2,1)S(1)}, u32[]{:S(2)}, u32[]{:S(2)}) collective-permute-start(bf16[520,512]{1,0:T(8,128)(2,1)S(1)} %pad_maximum_fusion.1), channel_id=1, source_target_pairs={{0,16},{1,17},{2,18},{3,19},{4,20},{5,21},{6,22},{7,23},{8,24},{9,... | collective-permute-start | bytes 1597448 | tf_op jit(solution)/shard_map/ppermute | solution.py:103
  32.8 21.8 %collective-permute-start.10 = (f16[4,1,2,64,512]{4,3,2,1,0:T(8,128)(2,1)S(1)}, f16[4,1,2,64,512]{4,3,2,1,0:T(8,128)(2,1)S(1)}, u32[]{:S(2)}, u32[]{:S(2)}) collective-permute-start(f16[4,1,2,64,512]{4,3,2,1,0:T(8,128)(2,1)S(1)} %constant_dynamic-slice_fusion.3), channel_id=1, source_target_pairs={{0,1},{1,0},{2,3},{3,2},{4,5},{5,4},{6,7},{7,6},{8,9},{9,8},{10,11... | collective-permute-start | bytes 1572872 | tf_op jit(solution)/shard_map/ppermute | solution.py:103
  33.4 22.9 %collective-permute-start.12 = (f16[4,2,1,64,512]{4,3,2,1,0:T(8,128)(2,1)S(1)}, f16[4,2,1,64,512]{4,3,2,1,0:T(8,128)(2,1)S(1)}, u32[]{:S(2)}, u32[]{:S(2)}) collective-permute-start(f16[4,2,1,64,512]{4,3,2,1,0:T(8,128)(2,1)S(1)} %constant_dynamic-slice_fusion.1), channel_id=1, source_target_pairs={{0,16},{1,17},{2,18},{3,19},{4,20},{5,21},{6,22},{7,23},{8,24},{9,... | collective-permute-start | bytes 1572872 | tf_op jit(solution)/shard_map/ppermute | solution.py:103
  47.4 20.5 %collective-permute-start.9 = (bf16[4,2,2,2,64,512]{5,4,3,2,1,0:T(8,128)(2,1)S(1)}, bf16[4,2,2,2,64,512]{5,4,3,2,1,0:T(8,128)(2,1)S(1)}, u32[]{:S(2)}, u32[]{:S(2)}) collective-permute-start(bf16[4,2,2,2,64,512]{5,4,3,2,1,0:T(8,128)(2,1)S(1)} %pad_maximum_fusion), channel_id=1, source_target_pairs={{0,8},{1,9},{2,10},{3,11},{4,12},{5,13},{6,14},{7,15},{8,0},{9,1},... | collective-permute-start | bytes 6291464 | tf_op jit(solution)/shard_map/ppermute | solution.py:103
  54.8 8.3 %collective-permute-start.11 = (f16[4,1,1,64,512]{4,3,2,1,0:T(8,128)(2,1)S(1)}, f16[4,1,1,64,512]{4,3,2,1,0:T(8,128)(2,1)S(1)}, u32[]{:S(2)}, u32[]{:S(2)}) collective-permute-start(f16[4,1,1,64,512]{4,3,2,1,0:T(8,128)(2,1)S(1)} %constant_dynamic-slice_fusion.2), channel_id=1, source_target_pairs={{0,16},{1,17},{2,18},{3,19},{4,20},{5,21},{6,22},{7,23},{8,24},{9,... | collective-permute-start | bytes 786440 | tf_op jit(solution)/shard_map/ppermute | solution.py:103
  56.5 6.4 %collective-permute-start.13 = (f16[4,1,1,64,512]{4,3,2,1,0:T(8,128)(2,1)S(1)}, f16[4,1,1,64,512]{4,3,2,1,0:T(8,128)(2,1)S(1)}, u32[]{:S(2)}, u32[]{:S(2)}) collective-permute-start(f16[4,1,1,64,512]{4,3,2,1,0:T(8,128)(2,1)S(1)} %constant_dynamic-slice_fusion), channel_id=1, source_target_pairs={{0,1},{1,0},{2,3},{3,2},{4,5},{5,4},{6,7},{7,6},{8,9},{9,8},{10,11... | collective-permute-start | bytes 786440 | tf_op jit(solution)/shard_map/ppermute | solution.py:103
  58.2 10.0 %copy-start = (bf16[512,4096]{1,0:T(8,128)(2,1)S(1)}, bf16[512,4096]{1,0:T(8,128)(2,1)}, u32[]{:S(2)}) copy-start(bf16[512,4096]{1,0:T(8,128)(2,1)} %tok.3) | copy-start | bytes 12582916
  63.5 11.4 %collective-permute-start.16 = (f16[136,512]{1,0:T(8,128)(2,1)S(1)}, f16[136,512]{1,0:T(8,128)(2,1)S(1)}, u32[]{:S(2)}, u32[]{:S(2)}) collective-permute-start(f16[136,512]{1,0:T(8,128)(2,1)S(1)} %get-tuple-element.72), channel_id=1, source_target_pairs={{0,6},{1,7},{2,4},{3,5},{4,2},{5,3},{6,0},{7,1},{8,14},{9,15},{10,... | collective-permute-start | bytes 417800 | tf_op jit(solution)/shard_map/ppermute | solution.py:103
  65.4 10.9 %collective-permute-start.15 = (f16[136,512]{1,0:T(8,128)(2,1)S(1)}, f16[136,512]{1,0:T(8,128)(2,1)S(1)}, u32[]{:S(2)}, u32[]{:S(2)}) collective-permute-start(f16[136,512]{1,0:T(8,128)(2,1)S(1)} %get-tuple-element.73), channel_id=1, source_target_pairs={{0,4},{1,5},{2,6},{3,7},{4,0},{5,1},{6,2},{7,3},{8,12},{9,13},{10,... | collective-permute-start | bytes 417800 | tf_op jit(solution)/shard_map/ppermute | solution.py:103
  67.4 8.9 %collective-permute-start.14 = (f16[136,512]{1,0:T(8,128)(2,1)S(1)}, f16[136,512]{1,0:T(8,128)(2,1)S(1)}, u32[]{:S(2)}, u32[]{:S(2)}) collective-permute-start(f16[136,512]{1,0:T(8,128)(2,1)S(1)} %get-tuple-element.74), channel_id=1, source_target_pairs={{0,2},{1,3},{2,0},{3,1},{4,6},{5,7},{6,4},{7,5},{8,10},{9,11},{10,... | collective-permute-start | bytes 417800 | tf_op jit(solution)/shard_map/ppermute | solution.py:103

commit v14 on v6

--- a/solution.py
+++ b/solution.py
@@ -66,7 +66,7 @@
 def bound_of(tokens, cotangent):
     rows, width = tokens.shape
     kd = cotangent.shape[1]
-    block = min(rows, 128)
+    block = min(rows, 256)
     return pl.pallas_call(
         bound_kernel,
         grid=(rows // block,),
@@ -134,9 +134,11 @@
         top = top + len(others).bit_length()
         return top, [scale(one - top) for one in [power, *others]]
 
-    def sums(value, name, axis, factor, *places):
+    def sums(value, name, axis, factor, *places, sent=None):
         me = place[name]
-        got = [swap(pick(value, (axis, me ^ j), *places), name, j) for j in range(1, size[name])]
+        if sent is None:
+            sent = [pick(value, (axis, me ^ j), *places) for j in range(1, size[name])]
+        got = [swap(one, name, j) for j, one in enumerate(sent, 1)]
         total = pick(value, (axis, me), *places).astype(jnp.float32) * factor[0]
         for one, other in zip(got, factor[1:]):
             total = total + one.astype(jnp.float32) * other
@@ -160,9 +162,14 @@
     one, power_x = gathered(blocks[:, 0], "x", power)
     two, power_y = gathered(blocks[:, 1], "y", power)
     by_x, by_y = factors(power, power_x), factors(power, power_y)
-    part, one, two, by_x, by_y = lax.optimization_barrier((part, one, two, by_x, by_y))
-    sum_one = sums(part, "x", 1, by_x[1], (3, 0, half))
-    sum_two = sums(part, "y", 2, by_y[1], (3, half, half))
+    upper, lower = (3, 0, half), (3, half, half)
+    to_x = [pick(part, (1, x_me ^ j), upper) for j in range(1, nx)]
+    to_y = [pick(part, (2, y_me ^ j), lower) for j in range(1, ny)]
+    part, to_x, to_y, one, two, by_x, by_y = lax.optimization_barrier(
+        (part, to_x, to_y, one, two, by_x, by_y)
+    )
+    sum_one = sums(part, "x", 1, by_x[1], upper, sent=to_x)
+    sum_two = sums(part, "y", 2, by_y[1], lower, sent=to_y)
     one, power_xy = gathered(one, "y", by_x[0])
     two, power_yx = gathered(two, "x", by_y[0])
     by_xy, by_yx = factors(by_x[0], power_xy), factors(by_y[0], power_yx)

time: 76.9 us -> 77 us (level)
  waiting for transfers between devices: 33.8 us -> 34.9 us
    ppermute x17, waiting for transfers between devices: 33.8 us -> 34.9 us  [swap(): lax.ppermute(value, AXES, [(i, i ^ j * mask[name]) for i in range(wide *...]
  transfers between devices with their start and end apart: 17 -> 17, of which waited for: 9 -> 10; matrix products, arithmetic and copies ran while one was open for 11% -> 11% of each run, Pallas kernels for 14% -> 13%
where the time goes in v14:
time: 77 us; the launch traced here: 76.7 us
  waiting for transfers between devices  34.9 us (45%)
  starting transfers between devices  19.5 us (25%)
  Pallas kernels  9.98 us (13%)
  matrix products  4.58 us (6%)
  other arithmetic  4.09 us (5%)
  local copies, waits for them, and re-layouts  2.51 us (3%)
  between operations  1.15 us (1%)
    ppermute x17, waiting for transfers between devices, swap(): lax.ppermute(value, AXES, [(i, i ^ j * mask[name]) for i in range(wide *...  34.9 us
    ppermute x17, starting transfers between devices, swap(): lax.ppermute(value, AXES, [(i, i ^ j * mask[name]) for i in range(wide *...  19.5 us
    pallas_call x1, Pallas kernels, products(): pl.pallas_call(products_kernel, grid=(steps,), in_specs=[columns, whole,...  6.63 us
    dot_general x1, matrix products, on_device(): lax.dot_general(tokens, cotangent, (((0,), (0,)), ((), ())), preferred_el...  4.58 us
    pallas_call x1, Pallas kernels, bound_of(): pl.pallas_call(bound_kernel, grid=(rows // block,), in_specs=[pl.BlockSpe...  3.35 us
  transfers between devices with their start and end apart: 17, of which 10 were waited for; matrix products, arithmetic and copies ran while one was open for 11% of the time, Pallas kernels for 13%

profile of v14, /device:TPU:0, one launch (start us, length us, event | category | flops | bytes accessed | tf_op | source)
XLA Modules:
  0.0 76.7 jit_solution(5217159141040931439)
XLA Ops:
  0.7 3.1 %collective-permute-start = (bf16[128,512]{1,0:T(8,128)(2,1)}, bf16[128,512]{1,0:T(8,128)(2,1)S(1)}, u32[]{:S(2)}, u32[]{:S(2)}) collective-permute-start(bf16[128,512]{1,0:T(8,128)(2,1)} %param.4), channel_id=1, source_target_pairs={{0,2},{1,3},{2,0},{3,1},{4,6},{5,7},{6,4},{7,5},{8,10},{9,11},{10,... | collective-permute-start | bytes 393224 | tf_op jit(solution)/shard_map/ppermute | solution.py:101
  3.7 2.6 %collective-permute-start.2 = (bf16[128,512]{1,0:T(8,128)(2,1)}, bf16[128,512]{1,0:T(8,128)(2,1)S(1)}, u32[]{:S(2)}, u32[]{:S(2)}) collective-permute-start(bf16[128,512]{1,0:T(8,128)(2,1)} %param.4), channel_id=1, source_target_pairs={{0,4},{1,5},{2,6},{3,7},{4,0},{5,1},{6,2},{7,3},{8,12},{9,13},{10,... | collective-permute-start | bytes 393224 | tf_op jit(solution)/shard_map/ppermute | solution.py:101
  6.3 3.3 %shard_map.58 = f32[8,512]{1,0:T(8,128)} custom-call(bf16[512,4096]{1,0:T(8,128)(2,1)} %tok.3, bf16[512,512]{1,0:T(8,128)(2,1)} %cot.3), custom_call_target="tpu_custom_call" | custom-call | flops 4194304 | bytes 4718592 | tf_op jit(solution)/shard_map/pallas_call | solution.py:70
  9.8 1.3 %collective-permute-done.1 = f32[8,512]{1,0:T(8,128)S(1)} collective-permute-done((f32[8,512]{1,0:T(8,128)}, f32[8,512]{1,0:T(8,128)S(1)}, u32[]{:S(2)}, u32[]{:S(2)}) %collective-permute-start.1) | collective-permute-done | bytes 16416 | tf_op jit(solution)/shard_map/ppermute | solution.py:101
  11.1 0.7 convert_reduce_fusion.3
  11.8 4.6 %multiply_convert_fusion = f16[4096,512]{1,0:T(8,128)(2,1)S(1)} fusion(bf16[512,4096]{1,0:T(8,128)(2,1)} %tok.3, bf16[512,512]{1,0:T(8,128)(2,1)S(1)} %copy-done.1, f32[512]{0:T(512)S(1)} %bitcast.118), kind=kOutput, calls=%fused_computation | convolution fusion | flops 2151677952 | bytes 8914944 | tf_op jit(solution)/shard_map/dot_general | solution.py:151
  17.7 1.6 %collective-permute-start.6 = (bf16[264,512]{1,0:T(8,128)(2,1)S(1)}, bf16[264,512]{1,0:T(8,128)(2,1)S(1)}, u32[]{:S(2)}, u32[]{:S(2)}) collective-permute-start(bf16[264,512]{1,0:T(8,128)(2,1)S(1)} %get-tuple-element.69), channel_id=1, source_target_pairs={{0,16},{1,17},{2,18},{3,19},{4,20},{5,21},{6,22},{7,23},{8,24},{9,... | collective-permute-start | bytes 811016 | tf_op jit(solution)/shard_map/ppermute | solution.py:101
  19.2 1.5 %collective-permute-start.5 = (bf16[264,512]{1,0:T(8,128)(2,1)S(1)}, bf16[264,512]{1,0:T(8,128)(2,1)S(1)}, u32[]{:S(2)}, u32[]{:S(2)}) collective-permute-start(bf16[264,512]{1,0:T(8,128)(2,1)S(1)} %get-tuple-element.70), channel_id=1, source_target_pairs={{0,1},{1,0},{2,3},{3,2},{4,5},{5,4},{6,7},{7,6},{8,9},{9,8},{10,11... | collective-permute-start | bytes 811016 | tf_op jit(solution)/shard_map/ppermute | solution.py:101
  20.9 5.7 %collective-permute-done.6 = bf16[264,512]{1,0:T(8,128)(2,1)S(1)} collective-permute-done((bf16[264,512]{1,0:T(8,128)(2,1)S(1)}, bf16[264,512]{1,0:T(8,128)(2,1)S(1)}, u32[]{:S(2)}, u32[]{:S(2)}) %collective-permute-start.6) | collective-permute-done | bytes 270368 | tf_op jit(solution)/shard_map/ppermute | solution.py:101
  26.6 1.2 %collective-permute-done.5 = bf16[264,512]{1,0:T(8,128)(2,1)S(1)} collective-permute-done((bf16[264,512]{1,0:T(8,128)(2,1)S(1)}, bf16[264,512]{1,0:T(8,128)(2,1)S(1)}, u32[]{:S(2)}, u32[]{:S(2)}) %collective-permute-start.5) | collective-permute-done | bytes 270368 | tf_op jit(solution)/shard_map/ppermute | solution.py:101
  28.0 0.8 %add_convert_fusion = f16[16,1,128,512]{3,2,0,1:T(8,128)(2,1)S(1)} fusion(f16[16,1,128,512]{3,2,0,1:T(8,128)(2,1)S(1)} %collective-permute-done.4, s32[]{:T(128)S(6)} %select_n.54, f16[16,2,128,512]{3,2,1,0:T(8,128)(2,1)S(1)} %bitcast.97), kind=kLoop, calls=%fused_computation.1 | loop fusion | flops 4194304 | bytes 6291460 | tf_op jit(solution)/shard_map/convert_element_type | solution.py:159
  29.2 1.6 %collective-permute-start.8 = (bf16[520,512]{1,0:T(8,128)(2,1)S(1)}, bf16[520,512]{1,0:T(8,128)(2,1)S(1)}, u32[]{:S(2)}, u32[]{:S(2)}) collective-permute-start(bf16[520,512]{1,0:T(8,128)(2,1)S(1)} %pad_maximum_fusion.2), channel_id=1, source_target_pairs={{0,1},{1,0},{2,3},{3,2},{4,5},{5,4},{6,7},{7,6},{8,9},{9,8},{10,11... | collective-permute-start | bytes 1597448 | tf_op jit(solution)/shard_map/ppermute | solution.py:101
  32.2 1.5 %collective-permute-start.12 = (f16[4,2,1,64,512]{4,3,2,1,0:T(8,128)(2,1)S(1)}, f16[4,2,1,64,512]{4,3,2,1,0:T(8,128)(2,1)S(1)}, u32[]{:S(2)}, u32[]{:S(2)}) collective-permute-start(f16[4,2,1,64,512]{4,3,2,1,0:T(8,128)(2,1)S(1)} %constant_dynamic-slice_fusion.2), channel_id=1, source_target_pairs={{0,16},{1,17},{2,18},{3,19},{4,20},{5,21},{6,22},{7,23},{8,24},{9,... | collective-permute-start | bytes 1572872 | tf_op jit(solution)/shard_map/ppermute | solution.py:101
  33.8 10.5 %collective-permute-done.8 = bf16[520,512]{1,0:T(8,128)(2,1)S(1)} collective-permute-done((bf16[520,512]{1,0:T(8,128)(2,1)S(1)}, bf16[520,512]{1,0:T(8,128)(2,1)S(1)}, u32[]{:S(2)}, u32[]{:S(2)}) %collective-permute-start.8) | collective-permute-done | bytes 532512 | tf_op jit(solution)/shard_map/ppermute | solution.py:101
  44.4 1.5 %collective-permute-done.7 = bf16[520,512]{1,0:T(8,128)(2,1)S(1)} collective-permute-done((bf16[520,512]{1,0:T(8,128)(2,1)S(1)}, bf16[520,512]{1,0:T(8,128)(2,1)S(1)}, u32[]{:S(2)}, u32[]{:S(2)}) %collective-permute-start.7) | collective-permute-done | bytes 532512 | tf_op jit(solution)/shard_map/ppermute | solution.py:101
  46.3 7.6 %collective-permute-done.10 = f16[4,1,2,64,512]{4,3,2,1,0:T(8,128)(2,1)S(1)} collective-permute-done((f16[4,1,2,64,512]{4,3,2,1,0:T(8,128)(2,1)S(1)}, f16[4,1,2,64,512]{4,3,2,1,0:T(8,128)(2,1)S(1)}, u32[]{:S(2)}, u32[]{:S(2)}) %collective-permute-start.10) | collective-permute-done | bytes 524320 | tf_op jit(solution)/shard_map/ppermute | solution.py:101
  54.2 0.7 collective-permute-start.11
  55.6 1.2 %collective-permute-start.13 = (f16[4,1,1,64,512]{4,3,2,1,0:T(8,128)(2,1)S(1)}, f16[4,1,1,64,512]{4,3,2,1,0:T(8,128)(2,1)S(1)}, u32[]{:S(2)}, u32[]{:S(2)}) collective-permute-start(f16[4,1,1,64,512]{4,3,2,1,0:T(8,128)(2,1)S(1)} %constant_dynamic-slice_fusion), channel_id=1, source_target_pairs={{0,1},{1,0},{2,3},{3,2},{4,5},{5,4},{6,7},{7,6},{8,9},{9,8},{10,11... | collective-permute-start | bytes 786440 | tf_op jit(solution)/shard_map/ppermute | solution.py:101
  57.7 4.4 %collective-permute-done.13 = f16[4,1,1,64,512]{4,3,2,1,0:T(8,128)(2,1)S(1)} collective-permute-done((f16[4,1,1,64,512]{4,3,2,1,0:T(8,128)(2,1)S(1)}, f16[4,1,1,64,512]{4,3,2,1,0:T(8,128)(2,1)S(1)}, u32[]{:S(2)}, u32[]{:S(2)}) %collective-permute-start.13) | collective-permute-done | bytes 262176 | tf_op jit(solution)/shard_map/ppermute | solution.py:101
  62.5 3.3 %collective-permute-start.16 = (f16[136,512]{1,0:T(8,128)(2,1)S(1)}, f16[136,512]{1,0:T(8,128)(2,1)S(1)}, u32[]{:S(2)}, u32[]{:S(2)}) collective-permute-start(f16[136,512]{1,0:T(8,128)(2,1)S(1)} %get-tuple-element.66), channel_id=1, source_target_pairs={{0,6},{1,7},{2,4},{3,5},{4,2},{5,3},{6,0},{7,1},{8,14},{9,15},{10,... | collective-permute-start | bytes 417800 | tf_op jit(solution)/shard_map/ppermute | solution.py:101
  66.0 1.0 %collective-permute-start.14 = (f16[136,512]{1,0:T(8,128)(2,1)S(1)}, f16[136,512]{1,0:T(8,128)(2,1)S(1)}, u32[]{:S(2)}, u32[]{:S(2)}) collective-permute-start(f16[136,512]{1,0:T(8,128)(2,1)S(1)} %get-tuple-element.68), channel_id=1, source_target_pairs={{0,2},{1,3},{2,0},{3,1},{4,6},{5,7},{6,4},{7,5},{8,10},{9,11},{10,... | collective-permute-start | bytes 417800 | tf_op jit(solution)/shard_map/ppermute | solution.py:101
  67.3 6.6 %shard_map.59 = (bf16[512,512]{1,0:T(8,128)(2,1)}, bf16[512,4096]{1,0:T(8,128)(2,1)}) custom-call(bf16[512,4096]{1,0:T(8,128)(2,1)S(1)} %copy-done, bf16[512,512]{1,0:T(8,128)(2,1)S(1)} %copy-done.1, bf16[4,1024,512]{2,1,0:T(8,128)(2,1)S(1)} %bitcast.86), custom_call_target="tpu_custom_call" | custom-call | tf_op jit(solution)/shard_map/pallas_call | solution.py:35
  73.9 1.9 %collective-permute-done.15 = f16[136,512]{1,0:T(8,128)(2,1)S(1)} collective-permute-done((f16[136,512]{1,0:T(8,128)(2,1)S(1)}, f16[136,512]{1,0:T(8,128)(2,1)S(1)}, u32[]{:S(2)}, u32[]{:S(2)}) %collective-permute-start.15) | collective-permute-done | bytes 139296 | tf_op jit(solution)/shard_map/ppermute | solution.py:101
  75.9 0.8 %fusion.3 = f32[128,512]{1,0:T(8,128)} fusion(s32[]{:T(128)S(6)} %select_n.58, f16[4,1,1,64,512]{4,3,2,1,0:T(8,128)(2,1)S(1)} %add_convert_fusion.4, f16[4,1,1,64,512]{4,3,2,1,0:T(8,128)(2,1)S(1)} %add_convert_fusion.3, f32[512]{0:T(512)S(1)} %bitcast.114, f16[136,512]{1,0:T(8,128)(2,1)S(1)} %collective-permute-done.16, f32[512]{0:T(512)S(1)} %bitcast.113, ...), kind=kLoop, calls=%fused_computation.30 | loop fusion | flops 851968 | bytes 1187844 | tf_op jit(solution)/shard_map/mul | solution.py:195
  (79 shorter events, 6.6 us)
Async XLA Ops:
  0.6 9.1 %copy-start.2 = (bf16[128,512]{1,0:T(8,128)(2,1)S(1)}, bf16[128,512]{1,0:T(8,128)(2,1)}, u32[]{:S(2)}) copy-start(bf16[128,512]{1,0:T(8,128)(2,1)} %param.4) | copy-start | bytes 393220
  0.6 11.2 %copy-start.1 = (bf16[512,512]{1,0:T(8,128)(2,1)S(1)}, bf16[512,512]{1,0:T(8,128)(2,1)}, u32[]{:S(2)}) copy-start(bf16[512,512]{1,0:T(8,128)(2,1)} %cot.3) | copy-start | bytes 1572868
  0.7 9.0 %collective-permute-start = (bf16[128,512]{1,0:T(8,128)(2,1)}, bf16[128,512]{1,0:T(8,128)(2,1)S(1)}, u32[]{:S(2)}, u32[]{:S(2)}) collective-permute-start(bf16[128,512]{1,0:T(8,128)(2,1)} %param.4), channel_id=1, source_target_pairs={{0,2},{1,3},{2,0},{3,1},{4,6},{5,7},{6,4},{7,5},{8,10},{9,11},{10,... | collective-permute-start | bytes 393224 | tf_op jit(solution)/shard_map/ppermute | solution.py:101
  3.7 13.2 %collective-permute-start.2 = (bf16[128,512]{1,0:T(8,128)(2,1)}, bf16[128,512]{1,0:T(8,128)(2,1)S(1)}, u32[]{:S(2)}, u32[]{:S(2)}) collective-permute-start(bf16[128,512]{1,0:T(8,128)(2,1)} %param.4), channel_id=1, source_target_pairs={{0,4},{1,5},{2,6},{3,7},{4,0},{5,1},{6,2},{7,3},{8,12},{9,13},{10,... | collective-permute-start | bytes 393224 | tf_op jit(solution)/shard_map/ppermute | solution.py:101
  6.3 10.6 %collective-permute-start.3 = (bf16[128,512]{1,0:T(8,128)(2,1)}, bf16[128,512]{1,0:T(8,128)(2,1)S(1)}, u32[]{:S(2)}, u32[]{:S(2)}) collective-permute-start(bf16[128,512]{1,0:T(8,128)(2,1)} %param.4), channel_id=1, source_target_pairs={{0,6},{1,7},{2,4},{3,5},{4,2},{5,3},{6,0},{7,1},{8,14},{9,15},{10,... | collective-permute-start | bytes 393224 | tf_op jit(solution)/shard_map/ppermute | solution.py:101
  9.7 1.4 %collective-permute-start.1 = (f32[8,512]{1,0:T(8,128)}, f32[8,512]{1,0:T(8,128)S(1)}, u32[]{:S(2)}, u32[]{:S(2)}) collective-permute-start(f32[8,512]{1,0:T(8,128)} %shard_map.58), channel_id=1, source_target_pairs={{0,8},{1,9},{2,10},{3,11},{4,12},{5,13},{6,14},{7,15},{8,0},{9,1},... | collective-permute-start | bytes 49160 | tf_op jit(solution)/shard_map/ppermute | solution.py:101
  17.4 10.6 %collective-permute-start.4 = (f16[16,1,128,512]{3,2,0,1:T(8,128)(2,1)S(1)}, f16[16,1,128,512]{3,2,0,1:T(8,128)(2,1)S(1)}, u32[]{:S(2)}, u32[]{:S(2)}) collective-permute-start(f16[16,1,128,512]{3,2,0,1:T(8,128)(2,1)S(1)} %dynamic-slice_bitcast_fusion), channel_id=1, source_target_pairs={{0,8},{1,9},{2,10},{3,11},{4,12},{5,13},{6,14},{7,15},{8,0},{9,1},... | collective-permute-start | bytes 6291464 | tf_op jit(solution)/shard_map/ppermute | solution.py:101
  17.7 8.9 %collective-permute-start.6 = (bf16[264,512]{1,0:T(8,128)(2,1)S(1)}, bf16[264,512]{1,0:T(8,128)(2,1)S(1)}, u32[]{:S(2)}, u32[]{:S(2)}) collective-permute-start(bf16[264,512]{1,0:T(8,128)(2,1)S(1)} %get-tuple-element.69), channel_id=1, source_target_pairs={{0,16},{1,17},{2,18},{3,19},{4,20},{5,21},{6,22},{7,23},{8,24},{9,... | collective-permute-start | bytes 811016 | tf_op jit(solution)/shard_map/ppermute | solution.py:101
  19.2 8.6 %collective-permute-start.5 = (bf16[264,512]{1,0:T(8,128)(2,1)S(1)}, bf16[264,512]{1,0:T(8,128)(2,1)S(1)}, u32[]{:S(2)}, u32[]{:S(2)}) collective-permute-start(bf16[264,512]{1,0:T(8,128)(2,1)S(1)} %get-tuple-element.70), channel_id=1, source_target_pairs={{0,1},{1,0},{2,3},{3,2},{4,5},{5,4},{6,7},{7,6},{8,9},{9,8},{10,11... | collective-permute-start | bytes 811016 | tf_op jit(solution)/shard_map/ppermute | solution.py:101
  29.2 15.1 %collective-permute-start.8 = (bf16[520,512]{1,0:T(8,128)(2,1)S(1)}, bf16[520,512]{1,0:T(8,128)(2,1)S(1)}, u32[]{:S(2)}, u32[]{:S(2)}) collective-permute-start(bf16[520,512]{1,0:T(8,128)(2,1)S(1)} %pad_maximum_fusion.2), channel_id=1, source_target_pairs={{0,1},{1,0},{2,3},{3,2},{4,5},{5,4},{6,7},{7,6},{8,9},{9,8},{10,11... | collective-permute-start | bytes 1597448 | tf_op jit(solution)/shard_map/ppermute | solution.py:101
  30.8 15.1 %collective-permute-start.7 = (bf16[520,512]{1,0:T(8,128)(2,1)S(1)}, bf16[520,512]{1,0:T(8,128)(2,1)S(1)}, u32[]{:S(2)}, u32[]{:S(2)}) collective-permute-start(bf16[520,512]{1,0:T(8,128)(2,1)S(1)} %pad_maximum_fusion.1), channel_id=1, source_target_pairs={{0,16},{1,17},{2,18},{3,19},{4,20},{5,21},{6,22},{7,23},{8,24},{9,... | collective-permute-start | bytes 1597448 | tf_op jit(solution)/shard_map/ppermute | solution.py:101
  31.6 22.4 %collective-permute-start.10 = (f16[4,1,2,64,512]{4,3,2,1,0:T(8,128)(2,1)S(1)}, f16[4,1,2,64,512]{4,3,2,1,0:T(8,128)(2,1)S(1)}, u32[]{:S(2)}, u32[]{:S(2)}) collective-permute-start(f16[4,1,2,64,512]{4,3,2,1,0:T(8,128)(2,1)S(1)} %constant_dynamic-slice_fusion.3), channel_id=1, source_target_pairs={{0,1},{1,0},{2,3},{3,2},{4,5},{5,4},{6,7},{7,6},{8,9},{9,8},{10,11... | collective-permute-start | bytes 1572872 | tf_op jit(solution)/shard_map/ppermute | solution.py:101
  32.2 23.1 %collective-permute-start.12 = (f16[4,2,1,64,512]{4,3,2,1,0:T(8,128)(2,1)S(1)}, f16[4,2,1,64,512]{4,3,2,1,0:T(8,128)(2,1)S(1)}, u32[]{:S(2)}, u32[]{:S(2)}) collective-permute-start(f16[4,2,1,64,512]{4,3,2,1,0:T(8,128)(2,1)S(1)} %constant_dynamic-slice_fusion.2), channel_id=1, source_target_pairs={{0,16},{1,17},{2,18},{3,19},{4,20},{5,21},{6,22},{7,23},{8,24},{9,... | collective-permute-start | bytes 1572872 | tf_op jit(solution)/shard_map/ppermute | solution.py:101
  46.2 20.7 %collective-permute-start.9 = (bf16[4,2,2,2,64,512]{5,4,3,2,1,0:T(8,128)(2,1)S(1)}, bf16[4,2,2,2,64,512]{5,4,3,2,1,0:T(8,128)(2,1)S(1)}, u32[]{:S(2)}, u32[]{:S(2)}) collective-permute-start(bf16[4,2,2,2,64,512]{5,4,3,2,1,0:T(8,128)(2,1)S(1)} %pad_maximum_fusion), channel_id=1, source_target_pairs={{0,8},{1,9},{2,10},{3,11},{4,12},{5,13},{6,14},{7,15},{8,0},{9,1},... | collective-permute-start | bytes 6291464 | tf_op jit(solution)/shard_map/ppermute | solution.py:101
  54.2 7.9 %collective-permute-start.11 = (f16[4,1,1,64,512]{4,3,2,1,0:T(8,128)(2,1)S(1)}, f16[4,1,1,64,512]{4,3,2,1,0:T(8,128)(2,1)S(1)}, u32[]{:S(2)}, u32[]{:S(2)}) collective-permute-start(f16[4,1,1,64,512]{4,3,2,1,0:T(8,128)(2,1)S(1)} %constant_dynamic-slice_fusion.1), channel_id=1, source_target_pairs={{0,16},{1,17},{2,18},{3,19},{4,20},{5,21},{6,22},{7,23},{8,24},{9,... | collective-permute-start | bytes 786440 | tf_op jit(solution)/shard_map/ppermute | solution.py:101
  55.6 6.5 %collective-permute-start.13 = (f16[4,1,1,64,512]{4,3,2,1,0:T(8,128)(2,1)S(1)}, f16[4,1,1,64,512]{4,3,2,1,0:T(8,128)(2,1)S(1)}, u32[]{:S(2)}, u32[]{:S(2)}) collective-permute-start(f16[4,1,1,64,512]{4,3,2,1,0:T(8,128)(2,1)S(1)} %constant_dynamic-slice_fusion), channel_id=1, source_target_pairs={{0,1},{1,0},{2,3},{3,2},{4,5},{5,4},{6,7},{7,6},{8,9},{9,8},{10,11... | collective-permute-start | bytes 786440 | tf_op jit(solution)/shard_map/ppermute | solution.py:101
  57.6 9.7 %copy-start = (bf16[512,4096]{1,0:T(8,128)(2,1)S(1)}, bf16[512,4096]{1,0:T(8,128)(2,1)}, u32[]{:S(2)}) copy-start(bf16[512,4096]{1,0:T(8,128)(2,1)} %tok.3) | copy-start | bytes 12582916
  62.5 11.4 %collective-permute-start.16 = (f16[136,512]{1,0:T(8,128)(2,1)S(1)}, f16[136,512]{1,0:T(8,128)(2,1)S(1)}, u32[]{:S(2)}, u32[]{:S(2)}) collective-permute-start(f16[136,512]{1,0:T(8,128)(2,1)S(1)} %get-tuple-element.66), channel_id=1, source_target_pairs={{0,6},{1,7},{2,4},{3,5},{4,2},{5,3},{6,0},{7,1},{8,14},{9,15},{10,... | collective-permute-start | bytes 417800 | tf_op jit(solution)/shard_map/ppermute | solution.py:101
  65.8 10.0 %collective-permute-start.15 = (f16[136,512]{1,0:T(8,128)(2,1)S(1)}, f16[136,512]{1,0:T(8,128)(2,1)S(1)}, u32[]{:S(2)}, u32[]{:S(2)}) collective-permute-start(f16[136,512]{1,0:T(8,128)(2,1)S(1)} %get-tuple-element.67), channel_id=1, source_target_pairs={{0,4},{1,5},{2,6},{3,7},{4,0},{5,1},{6,2},{7,3},{8,12},{9,13},{10,... | collective-permute-start | bytes 417800 | tf_op jit(solution)/shard_map/ppermute | solution.py:101
  66.0 9.8 %collective-permute-start.14 = (f16[136,512]{1,0:T(8,128)(2,1)S(1)}, f16[136,512]{1,0:T(8,128)(2,1)S(1)}, u32[]{:S(2)}, u32[]{:S(2)}) collective-permute-start(f16[136,512]{1,0:T(8,128)(2,1)S(1)} %get-tuple-element.68), channel_id=1, source_target_pairs={{0,2},{1,3},{2,0},{3,1},{4,6},{5,7},{6,4},{7,5},{8,10},{9,11},{10,... | collective-permute-start | bytes 417800 | tf_op jit(solution)/shard_map/ppermute | solution.py:101
